TPU v7x, 32 devices: a whole 2x2x4 slice. The times are simulated.
32 devices in a mesh: groups: 2 (over x), rows: 16 (over z, y, core).
Axes of the slice: x: 2, y: 2, z: 4, core: 2. Of those that a mesh axis runs over, the one named last changes fastest.
Arguments:
- queries: bfloat16 [1024, 4096], P(('groups', 'rows')), parts along dimension 0, may hold values from -200 to 200
- cache_keys: bfloat16 [1024, 2, 128, 128], P(('groups', 'rows')), parts along dimension 0, may hold values from -6 to 6
- cache_values: bfloat16 [1024, 2, 128, 128], P(('groups', 'rows')), parts along dimension 0, may hold values from -6 to 6
- lengths: int32 [1024], P(('groups', 'rows')), parts along dimension 0, may hold values from 2 to 128, as said below
- hidden: bfloat16 [1024, 2048], P(('groups', 'rows')), parts along dimension 0, may hold values from -6 to 6
- out_weight: bfloat16 [4096, 2048], P('rows'), may hold values from -0.1875 to 0.1875
- norm_gain: float32 [2048], replicated, may hold values from 0.25 to 1.75
- w_gate: bfloat16 [16, 2048, 768], P('rows'), may hold values from -0.125 to 0.125
- w_up: bfloat16 [16, 2048, 768], P('rows'), may hold values from -0.125 to 0.125
- w_down: bfloat16 [16, 768, 2048], P('rows'), may hold values from -0.3125 to 0.3125
- expert_ids: int32 [1024, 8], P(('groups', 'rows')), parts along dimension 0, may hold values from 0 to 15, all different within a row; in each aligned block of 32 rows (0 to 31, 32 to 63, ...) at most 32 rows name the same one
- gate_numer: int32 [1024, 8], P(('groups', 'rows')), parts along dimension 0, may hold values from 1 to 384, 1024 in all within a row
Outputs:
- layer_out: bfloat16 [1024, 2048], P(('groups', 'rows')), parts along dimension 0
There are 2 independent parts, one for each index of `groups`. A program takes and returns all parts, laid end to end along the dimension named above; an argument that names none is the same for every part. Nothing has to cross between parts.
Inputs may be any that keep to these rules, and one draw needn't show every extreme that they name: `expert_ids`: in the rows of one device no expert is named more than 32 times; in some device's rows some expert is named exactly 32 times. The 8 experts of a row differ. `gate_numer`: the 8 numerators of a row sum to 1024; the largest is 384. `lengths`: some row has all 128 slots live.
All inputs are finite; a program needn't handle non-finite values.
Results may differ from a plain program's by a relative error of at most 0.006.
Values may be sent and summed in bfloat16 or wider, within the bound.
No kernel may reach another device: no remote copies, remote signals or barrier semaphores. Data moves between devices by JAX's collectives and lax.ppermute only.
A program may use at most 128 MiB of HBM per device.

v0:
```python
import math

import jax
import jax.numpy as jnp
from jax import lax
from jax.sharding import PartitionSpec as P

TOPK = 8


gate_scale = 1.0 / 1024.0


def attend(queries, cache_keys, cache_values, lengths):
    row_count, kv_count, cache_len, head_size = cache_keys.shape
    grouped = queries.reshape(row_count, kv_count, -1, head_size)
    scores = jnp.einsum(
        "rkgh,rkch->rkgc", grouped, cache_keys, preferred_element_type=jnp.float32
    ) * (1.0 / math.sqrt(head_size))
    visible = (
        lax.broadcasted_iota(jnp.int32, (1, 1, 1, cache_len), 3) < lengths[:, None, None, None]
    )
    scores = jnp.where(visible, scores, -1e30)
    highest = jnp.max(scores, axis=3, keepdims=True)
    weights = jnp.exp(scores - highest)
    shares = (weights / jnp.sum(weights, axis=3, keepdims=True)).astype(jnp.bfloat16)
    blended = jnp.einsum(
        "rkgc,rkch->rkgh", shares, cache_values, preferred_element_type=jnp.float32
    )
    return blended.reshape(row_count, -1).astype(jnp.bfloat16)


def rms_scale(features, norm_gain):
    mean_square = jnp.mean(features * features, axis=-1, keepdims=True)
    return features * lax.rsqrt(mean_square + 1e-06) * norm_gain


def expert_block(arrived, w_gate, w_up, w_down):
    gate_proj = jnp.einsum("secd,edf->secf", arrived, w_gate, preferred_element_type=jnp.float32)
    raised = jnp.einsum("secd,edf->secf", arrived, w_up, preferred_element_type=jnp.float32)
    inner_act = (jax.nn.silu(gate_proj) * raised).astype(jnp.bfloat16)
    return jnp.einsum(
        "secf,efd->secd", inner_act, w_down, preferred_element_type=jnp.float32
    ).astype(jnp.bfloat16)


def on_device(
    queries,
    cache_keys,
    cache_values,
    lengths,
    hidden,
    out_weight,
    norm_gain,
    w_gate,
    w_up,
    w_down,
    expert_ids,
    gate_numer,
):
    row_count = queries.shape[0]
    width = hidden.shape[1]
    devices = lax.axis_size("rows")
    local_experts = w_gate.shape[0]
    expert_total = local_experts * devices
    slot_count = 2 * row_count * TOPK // expert_total
    attended = attend(queries, cache_keys, cache_values, lengths)
    head_parts = lax.all_to_all(attended, "rows", split_axis=1, concat_axis=0, tiled=True)
    projected = lax.psum_scatter(
        jnp.dot(head_parts, out_weight, preferred_element_type=jnp.float32),
        "rows",
        scatter_dimension=0,
        tiled=True,
    )
    residual = (hidden.astype(jnp.float32) + projected).astype(jnp.bfloat16)
    normed = rms_scale(residual.astype(jnp.float32), norm_gain).astype(jnp.bfloat16)
    pair_total = row_count * TOPK
    flat_ids = expert_ids.reshape(pair_total)
    one_hot = (flat_ids[:, None] == lax.broadcasted_iota(jnp.int32, (1, expert_total), 1)).astype(
        jnp.int32
    )
    position = jnp.sum(jnp.cumsum(one_hot, axis=0) * one_hot, axis=1) - 1
    target = flat_ids * slot_count + position
    target_rows = target.reshape(row_count, TOPK)
    slot_iota = lax.broadcasted_iota(jnp.int32, (expert_total * slot_count, 1, 1), 0)
    selector = jnp.any(target_rows[None, :, :] == slot_iota, axis=2).astype(jnp.bfloat16)
    outgoing = jnp.dot(selector, normed, preferred_element_type=jnp.float32).astype(jnp.bfloat16)
    outgoing = outgoing.reshape(devices, local_experts, slot_count, width)
    arrived = lax.all_to_all(outgoing, "rows", split_axis=0, concat_axis=0, tiled=True)
    finished = expert_block(arrived, w_gate, w_up, w_down)
    returned = lax.all_to_all(finished, "rows", split_axis=0, concat_axis=0, tiled=True)
    flat_back = returned.reshape(expert_total * slot_count, width)
    picked = jnp.take(flat_back, target, axis=0).reshape(row_count, TOPK, width)
    gate_values = gate_numer.astype(jnp.float32) * gate_scale
    combined = jnp.zeros((row_count, width), jnp.float32)
    for slot_index in range(TOPK):
        combined = combined + gate_values[:, slot_index, None] * picked[:, slot_index].astype(
            jnp.float32
        )
    return (residual.astype(jnp.float32) + combined).astype(jnp.bfloat16)


def solution(mesh):
    in_specs = (
        P(("groups", "rows"), None),
        P(("groups", "rows"), None, None, None),
        P(("groups", "rows"), None, None, None),
        P(("groups", "rows")),
        P(("groups", "rows"), None),
        P("rows", None),
        P(),
        P("rows", None, None),
        P("rows", None, None),
        P("rows", None, None),
        P(("groups", "rows"), None),
        P(("groups", "rows"), None),
    )
    out_specs = P(("groups", "rows"), None)
    return jax.shard_map(
        on_device, mesh=mesh, in_specs=in_specs, out_specs=out_specs, check_vma=False
    )
```

profile of v0, /device:TPU:13, one launch (start us, length us, event | category | flops | bytes accessed | tf_op | source)
XLA Modules:
  0.0 243.4 jit_solution(11596069235949879717)
XLA Ops:
  6.5 0.0 copy-start
  6.5 0.0 reduce-scatter.2.cloned.1.call-start
  6.5 1.1 copy.50
  7.7 0.7 iota_compare_fusion.3
  8.4 2.8 %fusion.30 = f32[32,2,16,128]{3,2,1,0:T(8,128)S(1)} fusion(bf16[32,2,16,128]{3,2,1,0:T(8,128)(2,1)S(1)} %bitcast.175, bf16[32,2,128,128]{3,2,1,0:T(8,128)(2,1)} %param.13, pred[32,128]{1,0:T(8,128)(4,1)S(1)} %iota_compare_fusion.3), kind=kOutput, calls=%fused_computation.24 | convolution fusion | flops 33816576 | bytes 2887680 | tf_op jit(solution)/shard_map/rkgh,rkch->rkgc/dot_general | solution.py:17
  11.2 0.0 copy-start.2
  11.2 0.8 copy-done.2
  12.0 0.4 fusion.59
  12.4 4.5 %convolution_convert_fusion.1 = bf16[32,2,16,128]{3,2,1,0:T(8,128)(2,1)} fusion(bf16[32,2,128,128]{3,2,1,0:T(8,128)(2,1)} %param.14, f32[32,2,16]{2,1,0:T(2,128)S(1)} %fusion.59, f32[32,2,16,128]{3,2,1,0:T(8,128)} %copy-done.2), kind=kOutput, calls=%fused_computation.25 | convolution fusion | flops 34079872 | bytes 2887680 | tf_op jit(solution)/shard_map/rkgc,rkch->rkgh/dot_general | solution.py:27
  16.9 1.0 convert_element_type.104
  17.9 0.1 copy.39
  18.0 14.3 %all_to_all.26 = bf16[32,16,256]{2,0,1:T(8,128)(2,1)S(1)} all-to-all(bf16[32,16,256]{2,0,1:T(8,128)(2,1)S(1)} %copy.39), channel_id=1, replica_groups=mesh['groups'=2,'rows'=16] {'rows'}, dimensions={1} | all-to-all | bytes 524288 | tf_op jit(solution)/shard_map/all_to_all | solution.py:68
  32.3 3.9 %fusion.60 = f32[512,2048]{1,0:T(8,128)} fusion(bf16[512,256]{1,0:T(8,128)(2,1)S(1)} %bitcast.174, bf16[256,2048]{1,0:T(8,128)(2,1)} %param.17), kind=kOutput, calls=%fused_computation.94 | convolution fusion | flops 536870912 | bytes 5505024 | tf_op jit(solution)/shard_map/dot_general | solution.py:70
  36.2 0.0 copy-start.4
  36.2 0.0 copy-start.3
  36.2 0.0 copy-start.5
  36.2 0.0 reduce-scatter.2.cloned.1.call-update
  36.2 0.7 copy-done.4
  36.9 0.1 copy.40
  37.0 0.1 eq.39
  37.1 0.1 reshape.160
  37.2 0.6 reduce-window.6
  37.7 0.2 slice_reduce_fusion
  38.0 0.1 fusion.53
  38.1 0.1 sub.19
  38.2 0.1 copy.43
  38.2 0.1 copy.44
  38.3 0.2 fusion.36
  38.6 67.9 %reduce-scatter.2.cloned.1.call-done = f32[32,2048]{1,0:T(8,128)} async-done(((f32[512,2048]{1,0:T(8,128)}), f32[32,2048]{1,0:T(8,128)}) %reduce-scatter.2.cloned.1.call-update) | async-done | bytes 262160 | tf_op jit(solution)/shard_map/reduce_scatter | solution.py:69
  106.5 0.0 copy-done.3
  106.5 1.1 fusion.37
  107.6 0.0 copy-done.5
  107.6 0.8 convolution_convert_fusion
  108.4 0.0 copy-start.7
  108.4 54.1 %all_to_all.27 = bf16[16,1,32,2048]{3,2,1,0:T(8,128)(2,1)S(1)} all-to-all(bf16[16,1,32,2048]{3,2,1,0:T(8,128)(2,1)S(1)} %bitcast.172), channel_id=1, replica_groups=mesh['groups'=2,'rows'=16] {'rows'}, dimensions={0} | all-to-all | bytes 4194304 | tf_op jit(solution)/shard_map/all_to_all | solution.py:89
  162.5 0.0 copy-start.1
  162.5 1.3 copy-done.1
  163.8 0.0 copy-done.7
  163.8 3.0 %fusion.5 = f32[16,32,768]{2,1,0:T(8,128)} fusion(bf16[1,2048,768]{2,1,0:T(8,128)(2,1)S(1)} %copy-done.7, bf16[16,1,32,2048]{3,2,1,0:T(8,128)(2,1)S(1)} %all_to_all.27), kind=kOutput, calls=%fused_computation.6 | convolution fusion | flops 1610612736 | bytes 6815744 | tf_op jit(solution)/shard_map/secd,edf->secf/dot_general | solution.py:39
  166.8 0.0 copy-done
  166.8 8.3 %fusion.10 = bf16[16,1,32,2048]{3,2,1,0:T(8,128)(2,1)} fusion(bf16[1,768,2048]{2,1,0:T(8,128)(2,1)S(1)} %copy-done, bf16[1,2048,768]{2,1,0:T(8,128)(2,1)} %param.20, bf16[16,1,32,2048]{3,2,1,0:T(8,128)(2,1)} %copy-done.1, f32[16,32,768]{2,1,0:T(8,128)} %fusion.5), kind=kOutput, calls=%fused_computation.10 | convolution fusion | flops 3224633344 | bytes 12058624 | tf_op jit(solution)/shard_map/secf,efd->secd/dot_general | solution.py:42
  175.1 0.0 copy-start.6
  175.1 5.3 %all-to-all-start.2 = ((bf16[16,1,32,2048]{3,2,1,0:T(8,128)(2,1)}), bf16[16,1,32,2048]{3,2,1,0:T(8,128)(2,1)}, u32[]{:S(2)}, u32[]{:S(2)}) async-start(bf16[16,1,32,2048]{3,2,1,0:T(8,128)(2,1)} %fusion.10), calls=%async_computation.3 | async-start | bytes 4194304 | tf_op jit(solution)/shard_map/all_to_all | solution.py:91
  180.3 0.1 copy.47
  180.4 0.1 mul.158
  180.5 0.0 copy-done.6
  180.6 47.3 %all-to-all-done.2 = bf16[16,1,32,2048]{3,2,1,0:T(8,128)(2,1)} async-done(((bf16[16,1,32,2048]{3,2,1,0:T(8,128)(2,1)}), bf16[16,1,32,2048]{3,2,1,0:T(8,128)(2,1)}, u32[]{:S(2)}, u32[]{:S(2)}) %all-to-all-start.2) | async-done | bytes 2097184 | tf_op jit(solution)/shard_map/all_to_all | solution.py:91
  227.9 5.2 %gather_fusion = bf16[256,2048]{1,0:T(8,128)(2,1)} fusion(bf16[512,2048]{1,0:T(8,128)(2,1)} %bitcast.26, s32[1024]{0:T(1024)S(1)} %pad_clamp_fusion), kind=kCustom, calls=%fused_computation | custom fusion | bytes 2098176 | tf_op jit(solution)/shard_map/jit(_take)/gather | solution.py:93
  233.1 2.4 %copy_select_fusion = bf16[32,8,2048]{2,0,1:T(8,128)(2,1)S(1)} fusion(bf16[32,8,2048]{2,1,0:T(8,128)(2,1)} %bitcast.173, pred[32,8]{0,1:T(8,128)(4,1)S(1)} %get-tuple-element.5), kind=kLoop, calls=%fused_computation.26 | loop fusion | flops 524288 | bytes 2097408 | tf_op jit(solution)/shard_map/jit(_take)/select_n | solution.py:93
  235.5 1.0 fusion.40
  (11 shorter events, 0.1 us)
Async XLA Ops:
  6.5 160.3 %copy-start = (bf16[1,768,2048]{2,1,0:T(8,128)(2,1)S(1)}, bf16[1,768,2048]{2,1,0:T(8,128)(2,1)}, u32[]{:S(2)}) copy-start(bf16[1,768,2048]{2,1,0:T(8,128)(2,1)} %param.21) | copy-start | bytes 9437188
  6.5 100.0 %reduce-scatter.2.cloned.1.call-start = ((), (), s32[]{:S(2)}) async-start(), calls=%async_computation.4 | async-start | bytes 4456448 | tf_op jit(solution)/shard_map/reduce_scatter | solution.py:69
  11.2 0.8 copy-start.2
  36.2 0.7 copy-start.4
  36.2 70.3 %copy-start.3 = (bf16[32,2048]{1,0:T(8,128)(2,1)S(1)}, bf16[32,2048]{1,0:T(8,128)(2,1)}, u32[]{:S(2)}) copy-start(bf16[32,2048]{1,0:T(8,128)(2,1)} %param.16) | copy-start | bytes 393220
  36.2 71.4 %copy-start.5 = (f32[2048]{0:T(1024)S(1)}, f32[2048]{0:T(1024)}, u32[]{:S(2)}) copy-start(f32[2048]{0:T(1024)} %param.18) | copy-start | bytes 24580
  108.4 55.4 %copy-start.7 = (bf16[1,2048,768]{2,1,0:T(8,128)(2,1)S(1)}, bf16[1,2048,768]{2,1,0:T(8,128)(2,1)}, u32[]{:S(2)}) copy-start(bf16[1,2048,768]{2,1,0:T(8,128)(2,1)} %param.19) | copy-start | bytes 9437188
  162.5 1.3 copy-start.1
  175.1 5.5 %copy-start.6 = (s32[32,8]{0,1:T(8,128)S(1)}, s32[32,8]{0,1:T(8,128)}, u32[]{:S(2)}) copy-start(s32[32,8]{0,1:T(8,128)} %param.23) | copy-start | bytes 3076
  175.1 52.8 %all-to-all-start.2 = ((bf16[16,1,32,2048]{3,2,1,0:T(8,128)(2,1)}), bf16[16,1,32,2048]{3,2,1,0:T(8,128)(2,1)}, u32[]{:S(2)}, u32[]{:S(2)}) async-start(bf16[16,1,32,2048]{3,2,1,0:T(8,128)(2,1)} %fusion.10), calls=%async_computation.3 | async-start | bytes 4194304 | tf_op jit(solution)/shard_map/all_to_all | solution.py:91
Sparse Core Ops, SparseCore 0:
  36.4 70.1 reduce-scatter.1
where the time goes:
time: 244 us; the launch traced here: 243 us
  waiting for transfers between devices  115 us (47%)
  blocking collectives  68.4 us (28%)
  matrix products  23.2 us (10%)
  between operations  13.5 us (6%)
  local copies, waits for them, and re-layouts  11.1 us (5%)
  other arithmetic  6.68 us (3%)
  starting transfers between devices  5.26 us (2%)
    reduce_scatter x1, waiting for transfers between devices, on_device(): lax.psum_scatter(jnp.dot(head_parts, out_weight, preferred_element_type=j...  67.9 us
    all_to_all x1, blocking collectives, on_device(): lax.all_to_all(outgoing, 'rows', split_axis=0, concat_axis=0, tiled=True)  54.1 us
    all_to_all x1, waiting for transfers between devices, on_device(): lax.all_to_all(finished, 'rows', split_axis=0, concat_axis=0, tiled=True)  47.3 us
    all_to_all x1, blocking collectives, on_device(): lax.all_to_all(attended, 'rows', split_axis=1, concat_axis=0, tiled=True)  14.3 us
    dot_general x1, matrix products, expert_block(): jnp.einsum('secf,efd->secd', inner_act, w_down, preferred_element_type=jn...  8.28 us
    all_to_all x1, starting transfers between devices, on_device(): lax.all_to_all(finished, 'rows', split_axis=0, concat_axis=0, tiled=True)  5.26 us
    gather x1, local copies, waits for them, and re-layouts, on_device(): picked = jnp.take(flat_back, target, axis=0).reshape(row_count, TOPK, width)  5.21 us
  transfers between devices with their start and end apart: 2, of which 2 were waited for; matrix products, arithmetic and copies ran while one was open for 1% of the time, Pallas kernels for 0%

commit v1 on v0

v1 whole, which is shorter than its diff:
```python
import math

import jax
import jax.numpy as jnp
from jax import lax
from jax.sharding import PartitionSpec as P

TOPK = 8
BF16 = jnp.bfloat16
F32 = jnp.float32


gate_scale = 1.0 / 1024.0


def attend(queries, cache_keys, cache_values, lengths):
    row_count, kv_count, cache_len, head_size = cache_keys.shape
    grouped = queries.reshape(row_count, kv_count, -1, head_size)
    scores = jnp.einsum(
        "rkgh,rkch->rkgc", grouped, cache_keys, preferred_element_type=jnp.float32
    ) * (1.0 / math.sqrt(head_size))
    visible = (
        lax.broadcasted_iota(jnp.int32, (1, 1, 1, cache_len), 3) < lengths[:, None, None, None]
    )
    scores = jnp.where(visible, scores, -1e30)
    highest = jnp.max(scores, axis=3, keepdims=True)
    weights = jnp.exp(scores - highest)
    shares = (weights / jnp.sum(weights, axis=3, keepdims=True)).astype(jnp.bfloat16)
    blended = jnp.einsum(
        "rkgc,rkch->rkgh", shares, cache_values, preferred_element_type=jnp.float32
    )
    return blended.reshape(row_count, -1).astype(jnp.bfloat16)


def rms_scale(features, norm_gain):
    mean_square = jnp.mean(features * features, axis=-1, keepdims=True)
    return features * lax.rsqrt(mean_square + 1e-06) * norm_gain


def ring_plan(devices):
    chips = devices // 2
    order = list(range(0, chips, 2)) + list(range(chips - 1, 0, -2))
    ahead, swap = [], []
    for place in range(chips):
        here, after = order[place], order[(place + 1) % chips]
        ahead += [(2 * here, 2 * after), (2 * after + 1, 2 * here + 1)]
        swap += [(2 * here, 2 * here + 1), (2 * here + 1, 2 * here)]
    back = [(target, source) for source, target in ahead]
    return order, ahead, back, swap


def ring_sum(parts, perm):
    message = parts[0].astype(BF16)
    half = message.shape[0]
    for part in parts[1:]:
        message = lax.ppermute(message, "rows", perm).astype(F32)
        if message.shape[0] == half:
            message = jnp.concatenate([message + part[:half], part[half:]], axis=0)
        else:
            message = message + part
        message = message.astype(BF16)
    return lax.ppermute(message, "rows", perm).astype(F32)


def on_device(
    queries,
    cache_keys,
    cache_values,
    lengths,
    hidden,
    out_weight,
    norm_gain,
    w_gate,
    w_up,
    w_down,
    expert_ids,
    gate_numer,
):
    rows, width = hidden.shape
    devices = lax.axis_size("rows")
    chips, hops = devices // 2, devices // 4
    local_experts = w_gate.shape[0]
    expert_total = local_experts * devices
    order, ahead, back, swap = ring_plan(devices)
    spot = [0] * chips
    for place, chip in enumerate(order):
        spot[chip] = place
    me = lax.axis_index("rows")
    chip, core = me // 2, me % 2
    place = jnp.asarray(spot, jnp.int32)[chip]
    sign = 1 - 2 * core

    def chip_at(offset):
        return jnp.asarray(order, jnp.int32)[(place + sign * offset) % chips]

    def paired(array):
        other = lax.ppermute(array, "rows", swap)
        return other

    weight_other = paired(out_weight)
    experts_own = (w_gate, w_up, w_down)
    experts_other = tuple(paired(w) for w in experts_own)
    hidden_other = paired(hidden)

    choice = lax.broadcasted_iota(jnp.int32, (1, 1, expert_total), 2)
    gates = jnp.sum(
        jnp.where(expert_ids[:, :, None] == choice, gate_numer[:, :, None], 0), axis=1
    ).astype(F32) * gate_scale
    all_gates = lax.all_gather(gates, "rows", axis=0, tiled=True)
    all_gates = all_gates.reshape(chips, 2, rows, expert_total)

    attended = attend(queries, cache_keys, cache_values, lengths)
    chip_feats = attended.shape[1] // chips
    feats = chip_feats // 2
    tokens = attended.reshape(rows, chips, chip_feats).transpose(1, 0, 2)
    groups = [[2 * c + k for c in range(chips)] for k in range(2)]
    tokens = lax.all_to_all(
        tokens, "rows", split_axis=0, concat_axis=0, tiled=True, axis_index_groups=groups
    )
    mine = jnp.take(tokens, jnp.stack([chip_at(o) for o in range(hops, -1, -1)]), axis=0)
    give = jnp.take(tokens, jnp.stack([chip_at(-o) for o in range(hops - 1, 0, -1)]), axis=0)
    got = paired(give)
    pieces = [mine[0]]
    for step in range(1, hops):
        pieces += [mine[step], got[step - 1]]
    pieces.append(mine[hops])
    lhs = jnp.concatenate(pieces, axis=0)
    weight = jnp.where(
        core == 0,
        jnp.concatenate([out_weight, weight_other], axis=0),
        jnp.concatenate([weight_other, out_weight], axis=0),
    )
    partial = jnp.dot(lhs, weight, preferred_element_type=F32)

    def blocks_of(array):
        out = [array[:rows]]
        for step in range(1, hops):
            start = rows + (step - 1) * 2 * rows
            out.append(array[start : start + 2 * rows])
        return out, array[rows + (hops - 1) * 2 * rows :]

    far, own = blocks_of(partial)
    total = ring_sum(far, ahead)
    total = jnp.concatenate([total[:rows] + own, total[rows:]], axis=0)
    got = paired(total)
    projected = total + jnp.concatenate([got[rows:], got[:rows]], axis=0)
    hidden_pair = jnp.concatenate([hidden, hidden_other], axis=0)
    residual = (hidden_pair.astype(F32) + projected).astype(BF16)
    normed = rms_scale(residual.astype(F32), norm_gain).astype(BF16)

    held = normed
    arrived = [normed[:rows]]
    for step in range(1, hops + 1):
        if step == hops:
            held = held[:rows]
        held = lax.ppermute(held, "rows", ahead)
        arrived.append(held)
    lhs = jnp.concatenate(arrived[::-1], axis=0)

    def gate_block(offset, parity):
        return all_gates[chip_at(-offset), parity]

    gate_rows = [gate_block(hops, core)]
    for step in range(hops - 1, 0, -1):
        gate_rows += [gate_block(step, core), gate_block(step, 1 - core)]
    gate_rows.append(gate_block(0, core))
    gate_rows = jnp.concatenate(gate_rows, axis=0)
    expert_iota = lax.broadcasted_iota(jnp.int32, (1, expert_total), 1)

    served = 0.0
    for owner, group in ((me, experts_own), (chip * 2 + 1 - core, experts_other)):
        for k in range(local_experts):
            w_g, w_u, w_d = (w[k] for w in group)
            gate_proj = jnp.dot(lhs, w_g, preferred_element_type=F32)
            raised = jnp.dot(lhs, w_u, preferred_element_type=F32)
            inner = (jax.nn.silu(gate_proj) * raised).astype(BF16)
            done = jnp.dot(inner, w_d, preferred_element_type=F32).astype(BF16)
            share = jnp.sum(
                jnp.where(expert_iota == owner * local_experts + k, gate_rows, 0.0),
                axis=1,
                keepdims=True,
            )
            served = served + share * done.astype(F32)

    far, own = blocks_of(served)
    total = ring_sum(far, back)
    got = paired(total[rows:])
    combined = total[:rows] + own + got
    return (residual[:rows].astype(F32) + combined).astype(BF16)


def solution(mesh):
    in_specs = (
        P(("groups", "rows"), None),
        P(("groups", "rows"), None, None, None),
        P(("groups", "rows"), None, None, None),
        P(("groups", "rows")),
        P(("groups", "rows"), None),
        P("rows", None),
        P(),
        P("rows", None, None),
        P("rows", None, None),
        P("rows", None, None),
        P(("groups", "rows"), None),
        P(("groups", "rows"), None),
    )
    out_specs = P(("groups", "rows"), None)
    return jax.shard_map(
        on_device, mesh=mesh, in_specs=in_specs, out_specs=out_specs, check_vma=False
    )
```

time: 244 us -> 171 us (0.70)
  the two profiles are of different devices: /device:TPU:13 before, /device:TPU:0 now
where the time goes in v1:
time: 171 us; the launch traced here: 170 us
  waiting for transfers between devices  54 us (32%)
  matrix products  29 us (17%)
  starting transfers between devices  23.7 us (14%)
  blocking collectives  20.7 us (12%)
  between operations  17 us (10%)
  local copies, waits for them, and re-layouts  13.2 us (8%)
  other arithmetic  12.8 us (7%)
    ppermute x6, waiting for transfers between devices, ring_sum(): message = lax.ppermute(message, 'rows', perm).astype(F32)  29.3 us
    all_gather x1, blocking collectives, on_device(): all_gates = lax.all_gather(gates, 'rows', axis=0, tiled=True)  20.7 us
    dot_general x2, matrix products, on_device(): done = jnp.dot(inner, w_d, preferred_element_type=F32).astype(BF16)  14.2 us
    ppermute x2, waiting for transfers between devices, ring_sum(): return lax.ppermute(message, 'rows', perm).astype(F32)  10.7 us
    ppermute x4, waiting for transfers between devices, on_device(): held = lax.ppermute(held, 'rows', ahead)  10.6 us
    all_to_all x1, starting transfers between devices, on_device(): lax.all_to_all(tokens, 'rows', split_axis=0, concat_axis=0, tiled=True, a...  7.28 us
    dot_general x2, matrix products, on_device(): raised = jnp.dot(lhs, w_u, preferred_element_type=F32)  6.99 us
    ppermute x6, starting transfers between devices, ring_sum(): message = lax.ppermute(message, 'rows', perm).astype(F32)  6.4 us
  transfers between devices with their start and end apart: 21, of which 15 were waited for; matrix products, arithmetic and copies ran while one was open for 18% of the time, Pallas kernels for 0%

profile of v1, /device:TPU:0, one launch (start us, length us, event | category | flops | bytes accessed | tf_op | source)
XLA Modules:
  0.0 170.3 jit_solution(2433574155905273739)
XLA Ops:
  0.0 0.9 iota_compare_fusion.1
  0.9 1.0 copy.41
  1.9 1.2 fusion.43
  3.1 0.4 fusion.88
  3.5 3.5 %convolution_convert_fusion = bf16[32,2,16,128]{3,2,1,0:T(8,128)(2,1)S(1)} fusion(bf16[32,2,128,128]{3,2,1,0:T(8,128)(2,1)} %param.31, f32[32,2,16]{2,1,0:T(2,128)S(1)} %fusion.88, f32[32,2,16,128]{3,2,1,0:T(8,128)S(1)} %fusion.43), kind=kOutput, calls=%fused_computation.34 | convolution fusion | flops 34079872 | bytes 2887680 | tf_op jit(solution)/shard_map/rkgc,rkch->rkgh/dot_general | solution.py:29
  7.0 0.2 convert_element_type.92
  7.2 0.8 copy.43
  7.9 7.3 %all-to-all-start = ((bf16[8,32,512]{2,1,0:T(8,128)(2,1)}), bf16[8,32,512]{2,1,0:T(8,128)(2,1)S(1)}, u32[]{:S(2)}, u32[]{:S(2)}) async-start(bf16[8,32,512]{2,1,0:T(8,128)(2,1)} %bitcast.130), calls=%async_computation | async-start | bytes 524288 | tf_op jit(solution)/shard_map/all_to_all | solution.py:117
  15.3 0.6 dynamic_slice.75
  23.2 0.7 fusion.87
  23.8 3.2 %stack.32 = s32[5,1]{0,1:T(1,128)S(1)} concatenate(s32[1,1]{0,1:T(1,128)} %bitcast.2, s32[1,1]{0,1:T(1,128)} %bitcast.3, s32[1,1]{0,1:T(1,128)} %bitcast.4, s32[1,1]{0,1:T(1,128)} %bitcast.5, s32[1,1]{0,1:T(1,128)} %bitcast.6), dimensions={0} | concatenate | bytes 40 | tf_op jit(solution)/shard_map/stack | solution.py:120
  27.0 1.9 %compare_and_fusion = pred[3]{0:T(512)(128)(4,1)S(1)} fusion(s32[1]{0:T(128)} %get-tuple-element.31, s32[1]{0:T(128)} %get-tuple-element.24, s32[1]{0:T(128)} %get-tuple-element.25), kind=kLoop, calls=%fused_computation.113 | loop fusion | flops 24 | bytes 15 | tf_op jit(solution)/shard_map/jit(_take)/and | solution.py:121
  29.0 1.9 %fusion.78 = s32[3]{0:T(128)S(1)} fusion(s32[1,1]{0,1:T(1,128)} %bitcast.12, s32[1,1]{0,1:T(1,128)} %bitcast.11, s32[1,1]{0,1:T(1,128)} %bitcast.10), kind=kLoop, calls=%fused_computation.116 | loop fusion | flops 15 | bytes 24 | tf_op jit(solution)/shard_map/jit(_take)/jit(_where)/select_n | solution.py:121
  30.9 3.2 %stack.26 = s32[5]{0:T(128)S(1)} concatenate(s32[1]{0:T(128)} %get-tuple-element.29, s32[1]{0:T(128)} %get-tuple-element.28, s32[1]{0:T(128)} %get-tuple-element.27, s32[1]{0:T(128)} %get-tuple-element.23, s32[1]{0:T(128)} %get-tuple-element.26), dimensions={0} | concatenate | bytes 40 | tf_op jit(solution)/shard_map/stack | solution.py:120
  34.1 0.6 gather_fusion.1
  34.7 0.1 broadcast_select_fusion.1
  34.8 0.5 collective-permute-start.1
  35.3 0.6 gather_fusion
  35.9 0.1 broadcast_select_fusion
  36.0 0.3 collective-permute-done.1
  36.3 3.2 %fusion.89 = (bf16[256,2048]{1,0:T(8,128)(2,1)S(1)}, f32[256,2048]{1,0:T(8,128)S(1)}) fusion(bf16[256,512]{1,0:T(8,128)(2,1)S(1)} %fusion.69, bf16[256,2048]{1,0:T(8,128)(2,1)} %collective-permute-done.2, bf16[256,2048]{1,0:T(8,128)(2,1)} %param.34, pred[]{:T(512)S(6)} %eq.56), kind=kOutput, calls=%fused_computation.129 | convolution fusion | flops 546832384 | bytes 5505025 | tf_op jit(solution)/shard_map/dot_general | solution.py:133
  39.5 2.1 %collective-permute-start.3 = (bf16[32,2048]{1,0:T(8,128)(2,1)S(1)}, bf16[32,2048]{1,0:T(8,128)(2,1)S(1)}, u32[]{:S(2)}, u32[]{:S(2)}) collective-permute-start(bf16[32,2048]{1,0:T(8,128)(2,1)S(1)} %get-tuple-element.11), channel_id=1, source_target_pairs={{0,4},{5,1},{4,8},{9,5},{8,12},{13,9},{12,14},{15,13},{14,10},{11,... | collective-permute-start | bytes 393224 | tf_op jit(solution)/shard_map/ppermute | solution.py:56
  41.6 2.9 %collective-permute-done.3 = bf16[32,2048]{1,0:T(8,128)(2,1)S(1)} collective-permute-done((bf16[32,2048]{1,0:T(8,128)(2,1)S(1)}, bf16[32,2048]{1,0:T(8,128)(2,1)S(1)}, u32[]{:S(2)}, u32[]{:S(2)}) %collective-permute-start.3) | collective-permute-done | bytes 131104 | tf_op jit(solution)/shard_map/ppermute | solution.py:56
  44.6 2.1 %collective-permute-start.4 = (bf16[64,2048]{1,0:T(8,128)(2,1)S(1)}, bf16[64,2048]{1,0:T(8,128)(2,1)S(1)}, u32[]{:S(2)}, u32[]{:S(2)}) collective-permute-start(bf16[64,2048]{1,0:T(8,128)(2,1)S(1)} %pad_maximum_fusion.1), channel_id=1, source_target_pairs={{0,4},{5,1},{4,8},{9,5},{8,12},{13,9},{12,14},{15,13},{14,10},{11,... | collective-permute-start | bytes 786440 | tf_op jit(solution)/shard_map/ppermute | solution.py:56
  46.7 4.4 %collective-permute-done.4 = bf16[64,2048]{1,0:T(8,128)(2,1)S(1)} collective-permute-done((bf16[64,2048]{1,0:T(8,128)(2,1)S(1)}, bf16[64,2048]{1,0:T(8,128)(2,1)S(1)}, u32[]{:S(2)}, u32[]{:S(2)}) %collective-permute-start.4) | collective-permute-done | bytes 262176 | tf_op jit(solution)/shard_map/ppermute | solution.py:56
  51.0 0.1 fusion.50
  51.1 2.1 %collective-permute-start.5 = (bf16[64,2048]{1,0:T(8,128)(2,1)S(1)}, bf16[64,2048]{1,0:T(8,128)(2,1)S(1)}, u32[]{:S(2)}, u32[]{:S(2)}) collective-permute-start(bf16[64,2048]{1,0:T(8,128)(2,1)S(1)} %fusion.50), channel_id=1, source_target_pairs={{0,4},{5,1},{4,8},{9,5},{8,12},{13,9},{12,14},{15,13},{14,10},{11,... | collective-permute-start | bytes 786440 | tf_op jit(solution)/shard_map/ppermute | solution.py:56
  53.2 4.4 %collective-permute-done.5 = bf16[64,2048]{1,0:T(8,128)(2,1)S(1)} collective-permute-done((bf16[64,2048]{1,0:T(8,128)(2,1)S(1)}, bf16[64,2048]{1,0:T(8,128)(2,1)S(1)}, u32[]{:S(2)}, u32[]{:S(2)}) %collective-permute-start.5) | collective-permute-done | bytes 262176 | tf_op jit(solution)/shard_map/ppermute | solution.py:56
  57.6 2.1 %collective-permute-start.6 = (bf16[64,2048]{1,0:T(8,128)(2,1)S(1)}, bf16[64,2048]{1,0:T(8,128)(2,1)S(1)}, u32[]{:S(2)}, u32[]{:S(2)}) collective-permute-start(bf16[64,2048]{1,0:T(8,128)(2,1)S(1)} %fusion.49), channel_id=1, source_target_pairs={{0,4},{5,1},{4,8},{9,5},{8,12},{13,9},{12,14},{15,13},{14,10},{11,... | collective-permute-start | bytes 786440 | tf_op jit(solution)/shard_map/ppermute | solution.py:62
  59.7 4.4 %collective-permute-done.6 = bf16[64,2048]{1,0:T(8,128)(2,1)S(1)} collective-permute-done((bf16[64,2048]{1,0:T(8,128)(2,1)S(1)}, bf16[64,2048]{1,0:T(8,128)(2,1)S(1)}, u32[]{:S(2)}, u32[]{:S(2)}) %collective-permute-start.6) | collective-permute-done | bytes 262176 | tf_op jit(solution)/shard_map/ppermute | solution.py:62
  64.2 0.1 collective-permute-start.7
  64.3 0.5 collective-permute-start
  64.8 0.1 collective-permute-start.13
  64.9 1.3 collective-permute-done.7
  66.2 0.3 collective-permute-done
  66.6 0.2 fusion.44
  66.8 0.1 fusion.46
  66.9 2.1 %collective-permute-start.8 = (bf16[64,2048]{1,0:T(8,128)(2,1)S(1)}, bf16[64,2048]{1,0:T(8,128)(2,1)S(1)}, u32[]{:S(2)}, u32[]{:S(2)}) collective-permute-start(bf16[64,2048]{1,0:T(8,128)(2,1)S(1)} %fusion.46), channel_id=1, source_target_pairs={{0,4},{5,1},{4,8},{9,5},{8,12},{13,9},{12,14},{15,13},{14,10},{11,... | collective-permute-start | bytes 786440 | tf_op jit(solution)/shard_map/ppermute | solution.py:156
  69.0 4.4 %collective-permute-done.8 = bf16[64,2048]{1,0:T(8,128)(2,1)S(1)} collective-permute-done((bf16[64,2048]{1,0:T(8,128)(2,1)S(1)}, bf16[64,2048]{1,0:T(8,128)(2,1)S(1)}, u32[]{:S(2)}, u32[]{:S(2)}) %collective-permute-start.8) | collective-permute-done | bytes 262176 | tf_op jit(solution)/shard_map/ppermute | solution.py:156
  73.3 2.0 %collective-permute-start.9 = (bf16[64,2048]{1,0:T(8,128)(2,1)S(1)}, bf16[64,2048]{1,0:T(8,128)(2,1)S(1)}, u32[]{:S(2)}, u32[]{:S(2)}) collective-permute-start(bf16[64,2048]{1,0:T(8,128)(2,1)S(1)} %collective-permute-done.8), channel_id=1, source_target_pairs={{0,4},{5,1},{4,8},{9,5},{8,12},{13,9},{12,14},{15,13},{14,10},{11,... | collective-permute-start | bytes 786440 | tf_op jit(solution)/shard_map/ppermute | solution.py:156
  75.4 0.5 collective-permute-start.14
  75.9 3.8 %collective-permute-done.9 = bf16[64,2048]{1,0:T(8,128)(2,1)S(1)} collective-permute-done((bf16[64,2048]{1,0:T(8,128)(2,1)S(1)}, bf16[64,2048]{1,0:T(8,128)(2,1)S(1)}, u32[]{:S(2)}, u32[]{:S(2)}) %collective-permute-start.9) | collective-permute-done | bytes 262176 | tf_op jit(solution)/shard_map/ppermute | solution.py:156
  79.7 2.0 %collective-permute-start.10 = (bf16[64,2048]{1,0:T(8,128)(2,1)S(1)}, bf16[64,2048]{1,0:T(8,128)(2,1)S(1)}, u32[]{:S(2)}, u32[]{:S(2)}) collective-permute-start(bf16[64,2048]{1,0:T(8,128)(2,1)S(1)} %collective-permute-done.9), channel_id=1, source_target_pairs={{0,4},{5,1},{4,8},{9,5},{8,12},{13,9},{12,14},{15,13},{14,10},{11,... | collective-permute-start | bytes 786440 | tf_op jit(solution)/shard_map/ppermute | solution.py:156
  90.9 20.7 %all-gather = f32[16,32,16]{1,2,0:T(8,128)S(1)} all-gather(f32[1,32,16]{1,2,0:T(8,128)S(1)} %multiply_bitcast_fusion), channel_id=1, replica_groups=mesh['groups'=2,'rows'=16] {'rows'}, dimensions={0}, use_global_device_ids=true | all-gather | bytes 34816 | tf_op jit(solution)/shard_map/all_gather | solution.py:109
  111.7 0.6 dynamic-slice_bitcast_fusion
  112.3 0.7 slice.149
  113.0 0.6 iota_compare_fusion.2
  113.5 0.9 concatenate.81
  114.4 1.3 select_reduce_fusion.1
  115.7 2.4 %collective-permute-done.11 = bf16[32,2048]{1,0:T(8,128)(2,1)S(1)} collective-permute-done((bf16[32,2048]{1,0:T(8,128)(2,1)}, bf16[32,2048]{1,0:T(8,128)(2,1)S(1)}, u32[]{:S(2)}, u32[]{:S(2)}) %collective-permute-start.11) | collective-permute-done | bytes 131104 | tf_op jit(solution)/shard_map/ppermute | solution.py:156
  118.3 3.2 %fusion.9 = f32[256,768]{1,0:T(8,128)S(1)} fusion(bf16[256,2048]{1,0:T(8,128)(2,1)S(1)} %slice_dynamic-update-slice_fusion, bf16[1,2048,768]{2,1,0:T(8,128)(2,1)} %param.37), kind=kOutput, calls=%fused_computation.11 | convolution fusion | flops 805306368 | bytes 4980736 | tf_op jit(solution)/shard_map/dot_general | solution.py:175
  121.5 3.7 %fusion.3 = f32[256,768]{1,0:T(8,128)} fusion(bf16[256,2048]{1,0:T(8,128)(2,1)S(1)} %slice_dynamic-update-slice_fusion, bf16[1,2048,768]{2,1,0:T(8,128)(2,1)} %collective-permute-done.13), kind=kOutput, calls=%fused_computation.5 | convolution fusion | flops 805306368 | bytes 4980736 | tf_op jit(solution)/shard_map/dot_general | solution.py:175
  125.3 6.7 %fusion.19 = f32[256,2048]{1,0:T(8,128)} fusion(bf16[1,768,2048]{2,1,0:T(8,128)(2,1)} %param.38, f32[256]{0:T(256)S(1)} %copy-done.8, f32[256,768]{1,0:T(8,128)S(1)} %fusion.9, bf16[256,2048]{1,0:T(8,128)(2,1)} %copy-done.3, bf16[1,2048,768]{2,1,0:T(8,128)(2,1)} %param.36), kind=kOutput, calls=%fused_computation.17 | convolution fusion | flops 1613365248 | bytes 10224640 | tf_op jit(solution)/shard_map/dot_general | solution.py:177
  132.0 7.5 %fusion.90 = (bf16[256,2048]{1,0:T(8,128)(2,1)S(1)}, f32[256,2048]{1,0:T(8,128)}) fusion(f32[256,2048]{1,0:T(8,128)} %fusion.19, bf16[1,768,2048]{2,1,0:T(8,128)(2,1)} %collective-permute-done.14, f32[256,768]{1,0:T(8,128)} %fusion.3, bf16[256,2048]{1,0:T(8,128)(2,1)} %copy-done.3, bf16[1,2048,768]{2,1,0:T(8,128)(2,1)} %collective-permute-done.12, ...), kind=kOutput, calls=%fused_computation.130 | convolution fusion | flops 1614413824 | bytes 13370368 | tf_op jit(solution)/shard_map/dot_general | solution.py:177
  139.6 5.0 %collective-permute-done.15 = bf16[32,2048]{1,0:T(8,128)(2,1)S(1)} collective-permute-done((bf16[32,2048]{1,0:T(8,128)(2,1)S(1)}, bf16[32,2048]{1,0:T(8,128)(2,1)S(1)}, u32[]{:S(2)}, u32[]{:S(2)}) %collective-permute-start.15) | collective-permute-done | bytes 131104 | tf_op jit(solution)/shard_map/ppermute | solution.py:56
  144.5 1.0 fusion.66
  145.6 6.4 %collective-permute-done.16 = bf16[64,2048]{1,0:T(8,128)(2,1)S(1)} collective-permute-done((bf16[64,2048]{1,0:T(8,128)(2,1)S(1)}, bf16[64,2048]{1,0:T(8,128)(2,1)S(1)}, u32[]{:S(2)}, u32[]{:S(2)}) %collective-permute-start.16) | collective-permute-done | bytes 262176 | tf_op jit(solution)/shard_map/ppermute | solution.py:56
  152.0 1.1 fusion.48
  153.2 6.4 %collective-permute-done.17 = bf16[64,2048]{1,0:T(8,128)(2,1)S(1)} collective-permute-done((bf16[64,2048]{1,0:T(8,128)(2,1)S(1)}, bf16[64,2048]{1,0:T(8,128)(2,1)S(1)}, u32[]{:S(2)}, u32[]{:S(2)}) %collective-permute-start.17) | collective-permute-done | bytes 262176 | tf_op jit(solution)/shard_map/ppermute | solution.py:56
  159.5 1.1 fusion.47
  160.7 6.4 %collective-permute-done.18 = bf16[64,2048]{1,0:T(8,128)(2,1)S(1)} collective-permute-done((bf16[64,2048]{1,0:T(8,128)(2,1)S(1)}, bf16[64,2048]{1,0:T(8,128)(2,1)S(1)}, u32[]{:S(2)}, u32[]{:S(2)}) %collective-permute-start.18) | collective-permute-done | bytes 262176 | tf_op jit(solution)/shard_map/ppermute | solution.py:62
  167.1 0.1 collective-permute-start.19
  167.2 1.5 collective-permute-done.19
  168.7 1.7 fusion.65
  (66 shorter events, 0.9 us)
Async XLA Ops:
  0.0 1.9 %copy-start = (bf16[32,2,128,128]{3,2,1,0:T(8,128)(2,1)S(1)}, bf16[32,2,128,128]{3,2,1,0:T(8,128)(2,1)}, u32[]{:S(2)}) copy-start(bf16[32,2,128,128]{3,2,1,0:T(8,128)(2,1)} %param.30) | copy-start | bytes 6291460
  3.5 11.8 %copy-start.9 = (s32[8]{0:T(128)S(1)}, s32[8]{0:T(128)}, u32[]{:S(2)}) copy-start(s32[8]{0:T(128)} %constant.146.clone) | copy-start | bytes 100
  3.5 19.6 %copy-start.2 = (s32[8]{0:T(128)S(1)}, s32[8]{0:T(128)}, u32[]{:S(2)}) copy-start(s32[8]{0:T(128)} %constant.147.clone) | copy-start | bytes 100
  7.9 26.2 %all-to-all-start = ((bf16[8,32,512]{2,1,0:T(8,128)(2,1)}), bf16[8,32,512]{2,1,0:T(8,128)(2,1)S(1)}, u32[]{:S(2)}, u32[]{:S(2)}) async-start(bf16[8,32,512]{2,1,0:T(8,128)(2,1)} %bitcast.130), calls=%async_computation | async-start | bytes 524288 | tf_op jit(solution)/shard_map/all_to_all | solution.py:117
  15.2 21.1 %collective-permute-start.2 = (bf16[256,2048]{1,0:T(8,128)(2,1)}, bf16[256,2048]{1,0:T(8,128)(2,1)}, u32[]{:S(2)}, u32[]{:S(2)}) collective-permute-start(bf16[256,2048]{1,0:T(8,128)(2,1)} %param.34), channel_id=1, source_target_pairs={{0,1},{1,0},{4,5},{5,4},{8,9},{9,8},{12,13},{13,12},{14,15},{15,14... | collective-permute-start | bytes 3145736 | tf_op jit(solution)/shard_map/ppermute | solution.py:97
  34.8 1.5 collective-permute-start.1
  39.5 5.0 %collective-permute-start.3 = (bf16[32,2048]{1,0:T(8,128)(2,1)S(1)}, bf16[32,2048]{1,0:T(8,128)(2,1)S(1)}, u32[]{:S(2)}, u32[]{:S(2)}) collective-permute-start(bf16[32,2048]{1,0:T(8,128)(2,1)S(1)} %get-tuple-element.11), channel_id=1, source_target_pairs={{0,4},{5,1},{4,8},{9,5},{8,12},{13,9},{12,14},{15,13},{14,10},{11,... | collective-permute-start | bytes 393224 | tf_op jit(solution)/shard_map/ppermute | solution.py:56
  44.6 6.4 %collective-permute-start.4 = (bf16[64,2048]{1,0:T(8,128)(2,1)S(1)}, bf16[64,2048]{1,0:T(8,128)(2,1)S(1)}, u32[]{:S(2)}, u32[]{:S(2)}) collective-permute-start(bf16[64,2048]{1,0:T(8,128)(2,1)S(1)} %pad_maximum_fusion.1), channel_id=1, source_target_pairs={{0,4},{5,1},{4,8},{9,5},{8,12},{13,9},{12,14},{15,13},{14,10},{11,... | collective-permute-start | bytes 786440 | tf_op jit(solution)/shard_map/ppermute | solution.py:56
  51.1 13.2 %copy-start.1 = (bf16[32,2048]{1,0:T(8,128)(2,1)S(1)}, bf16[32,2048]{1,0:T(8,128)(2,1)}, u32[]{:S(2)}) copy-start(bf16[32,2048]{1,0:T(8,128)(2,1)} %param.33) | copy-start | bytes 393220
  51.1 6.4 %collective-permute-start.5 = (bf16[64,2048]{1,0:T(8,128)(2,1)S(1)}, bf16[64,2048]{1,0:T(8,128)(2,1)S(1)}, u32[]{:S(2)}, u32[]{:S(2)}) collective-permute-start(bf16[64,2048]{1,0:T(8,128)(2,1)S(1)} %fusion.50), channel_id=1, source_target_pairs={{0,4},{5,1},{4,8},{9,5},{8,12},{13,9},{12,14},{15,13},{14,10},{11,... | collective-permute-start | bytes 786440 | tf_op jit(solution)/shard_map/ppermute | solution.py:56
  57.6 6.4 %collective-permute-start.6 = (bf16[64,2048]{1,0:T(8,128)(2,1)S(1)}, bf16[64,2048]{1,0:T(8,128)(2,1)S(1)}, u32[]{:S(2)}, u32[]{:S(2)}) collective-permute-start(bf16[64,2048]{1,0:T(8,128)(2,1)S(1)} %fusion.49), channel_id=1, source_target_pairs={{0,4},{5,1},{4,8},{9,5},{8,12},{13,9},{12,14},{15,13},{14,10},{11,... | collective-permute-start | bytes 786440 | tf_op jit(solution)/shard_map/ppermute | solution.py:62
  64.1 2.7 %copy-start.4 = (f32[2048]{0:T(1024)S(1)}, f32[2048]{0:T(1024)}, u32[]{:S(2)}) copy-start(f32[2048]{0:T(1024)} %param.35) | copy-start | bytes 24580
  64.2 11.7 %copy-start.5 = (s32[32,8]{0,1:T(8,128)S(1)}, s32[32,8]{0,1:T(8,128)}, u32[]{:S(2)}) copy-start(s32[32,8]{0,1:T(8,128)} %param.40) | copy-start | bytes 3076
  64.2 11.7 %copy-start.6 = (s32[32,8]{0,1:T(8,128)S(1)}, s32[32,8]{0,1:T(8,128)}, u32[]{:S(2)}) copy-start(s32[32,8]{0,1:T(8,128)} %param.39) | copy-start | bytes 3076
  64.2 2.0 %collective-permute-start.7 = (f32[64,2048]{1,0:T(8,128)S(1)}, f32[64,2048]{1,0:T(8,128)S(1)}, u32[]{:S(2)}, u32[]{:S(2)}) collective-permute-start(f32[64,2048]{1,0:T(8,128)S(1)} %pad_maximum_fusion), channel_id=1, source_target_pairs={{0,1},{1,0},{4,5},{5,4},{8,9},{9,8},{12,13},{13,12},{14,15},{15,14... | collective-permute-start | bytes 1572872 | tf_op jit(solution)/shard_map/ppermute | solution.py:97
  64.3 2.3 %collective-permute-start = (bf16[32,2048]{1,0:T(8,128)(2,1)S(1)}, bf16[32,2048]{1,0:T(8,128)(2,1)S(1)}, u32[]{:S(2)}, u32[]{:S(2)}) collective-permute-start(bf16[32,2048]{1,0:T(8,128)(2,1)S(1)} %copy-done.1), channel_id=1, source_target_pairs={{0,1},{1,0},{4,5},{5,4},{8,9},{9,8},{12,13},{13,12},{14,15},{15,14... | collective-permute-start | bytes 393224 | tf_op jit(solution)/shard_map/ppermute | solution.py:97
  64.8 56.7 %collective-permute-start.13 = (bf16[1,2048,768]{2,1,0:T(8,128)(2,1)}, bf16[1,2048,768]{2,1,0:T(8,128)(2,1)}, u32[]{:S(2)}, u32[]{:S(2)}) collective-permute-start(bf16[1,2048,768]{2,1,0:T(8,128)(2,1)} %param.37), channel_id=1, source_target_pairs={{0,1},{1,0},{4,5},{5,4},{8,9},{9,8},{12,13},{13,12},{14,15},{15,14... | collective-permute-start | bytes 9437192 | tf_op jit(solution)/shard_map/ppermute | solution.py:97
  66.9 6.4 %collective-permute-start.8 = (bf16[64,2048]{1,0:T(8,128)(2,1)S(1)}, bf16[64,2048]{1,0:T(8,128)(2,1)S(1)}, u32[]{:S(2)}, u32[]{:S(2)}) collective-permute-start(bf16[64,2048]{1,0:T(8,128)(2,1)S(1)} %fusion.46), channel_id=1, source_target_pairs={{0,4},{5,1},{4,8},{9,5},{8,12},{13,9},{12,14},{15,13},{14,10},{11,... | collective-permute-start | bytes 786440 | tf_op jit(solution)/shard_map/ppermute | solution.py:156
  73.3 6.4 %collective-permute-start.9 = (bf16[64,2048]{1,0:T(8,128)(2,1)S(1)}, bf16[64,2048]{1,0:T(8,128)(2,1)S(1)}, u32[]{:S(2)}, u32[]{:S(2)}) collective-permute-start(bf16[64,2048]{1,0:T(8,128)(2,1)S(1)} %collective-permute-done.8), channel_id=1, source_target_pairs={{0,4},{5,1},{4,8},{9,5},{8,12},{13,9},{12,14},{15,13},{14,10},{11,... | collective-permute-start | bytes 786440 | tf_op jit(solution)/shard_map/ppermute | solution.py:156
  75.4 56.6 %collective-permute-start.12 = (bf16[1,2048,768]{2,1,0:T(8,128)(2,1)}, bf16[1,2048,768]{2,1,0:T(8,128)(2,1)}, u32[]{:S(2)}, u32[]{:S(2)}) collective-permute-start(bf16[1,2048,768]{2,1,0:T(8,128)(2,1)} %param.36), channel_id=1, source_target_pairs={{0,1},{1,0},{4,5},{5,4},{8,9},{9,8},{12,13},{13,12},{14,15},{15,14... | collective-permute-start | bytes 9437192 | tf_op jit(solution)/shard_map/ppermute | solution.py:97
  75.4 56.6 %collective-permute-start.14 = (bf16[1,768,2048]{2,1,0:T(8,128)(2,1)}, bf16[1,768,2048]{2,1,0:T(8,128)(2,1)}, u32[]{:S(2)}, u32[]{:S(2)}) collective-permute-start(bf16[1,768,2048]{2,1,0:T(8,128)(2,1)} %param.38), channel_id=1, source_target_pairs={{0,1},{1,0},{4,5},{5,4},{8,9},{9,8},{12,13},{13,12},{14,15},{15,14... | collective-permute-start | bytes 9437192 | tf_op jit(solution)/shard_map/ppermute | solution.py:97
  79.7 32.6 %collective-permute-start.10 = (bf16[64,2048]{1,0:T(8,128)(2,1)S(1)}, bf16[64,2048]{1,0:T(8,128)(2,1)S(1)}, u32[]{:S(2)}, u32[]{:S(2)}) collective-permute-start(bf16[64,2048]{1,0:T(8,128)(2,1)S(1)} %collective-permute-done.9), channel_id=1, source_target_pairs={{0,4},{5,1},{4,8},{9,5},{8,12},{13,9},{12,14},{15,13},{14,10},{11,... | collective-permute-start | bytes 786440 | tf_op jit(solution)/shard_map/ppermute | solution.py:156
  113.0 5.2 %collective-permute-start.11 = (bf16[32,2048]{1,0:T(8,128)(2,1)}, bf16[32,2048]{1,0:T(8,128)(2,1)S(1)}, u32[]{:S(2)}, u32[]{:S(2)}) collective-permute-start(bf16[32,2048]{1,0:T(8,128)(2,1)} %slice.149), channel_id=1, source_target_pairs={{0,4},{5,1},{4,8},{9,5},{8,12},{13,9},{12,14},{15,13},{14,10},{11,... | collective-permute-start | bytes 393224 | tf_op jit(solution)/shard_map/ppermute | solution.py:156
  118.3 3.3 %copy-start.3 = (bf16[256,2048]{1,0:T(8,128)(2,1)}, bf16[256,2048]{1,0:T(8,128)(2,1)S(1)}, u32[]{:S(2)}) copy-start(bf16[256,2048]{1,0:T(8,128)(2,1)S(1)} %slice_dynamic-update-slice_fusion) | copy-start | bytes 3145732
  121.5 3.8 %copy-start.8 = (f32[256]{0:T(256)S(1)}, f32[256]{0:T(256)}, u32[]{:S(2)}) copy-start(f32[256]{0:T(256)} %get-tuple-element.6) | copy-start | bytes 3076
  125.3 6.7 %copy-start.7 = (f32[256]{0:T(256)S(1)}, f32[256]{0:T(256)}, u32[]{:S(2)}) copy-start(f32[256]{0:T(256)} %get-tuple-element.5) | copy-start | bytes 3076
  139.5 5.0 %collective-permute-start.15 = (bf16[32,2048]{1,0:T(8,128)(2,1)S(1)}, bf16[32,2048]{1,0:T(8,128)(2,1)S(1)}, u32[]{:S(2)}, u32[]{:S(2)}) collective-permute-start(bf16[32,2048]{1,0:T(8,128)(2,1)S(1)} %get-tuple-element.9), channel_id=1, source_target_pairs={{4,0},{1,5},{8,4},{5,9},{12,8},{9,13},{14,12},{13,15},{10,14},{15,... | collective-permute-start | bytes 393224 | tf_op jit(solution)/shard_map/ppermute | solution.py:56
  145.6 6.4 %collective-permute-start.16 = (bf16[64,2048]{1,0:T(8,128)(2,1)S(1)}, bf16[64,2048]{1,0:T(8,128)(2,1)S(1)}, u32[]{:S(2)}, u32[]{:S(2)}) collective-permute-start(bf16[64,2048]{1,0:T(8,128)(2,1)S(1)} %pad_maximum_fusion.2), channel_id=1, source_target_pairs={{4,0},{1,5},{8,4},{5,9},{12,8},{9,13},{14,12},{13,15},{10,14},{15,... | collective-permute-start | bytes 786440 | tf_op jit(solution)/shard_map/ppermute | solution.py:56
  153.1 6.4 %collective-permute-start.17 = (bf16[64,2048]{1,0:T(8,128)(2,1)S(1)}, bf16[64,2048]{1,0:T(8,128)(2,1)S(1)}, u32[]{:S(2)}, u32[]{:S(2)}) collective-permute-start(bf16[64,2048]{1,0:T(8,128)(2,1)S(1)} %fusion.48), channel_id=1, source_target_pairs={{4,0},{1,5},{8,4},{5,9},{12,8},{9,13},{14,12},{13,15},{10,14},{15,... | collective-permute-start | bytes 786440 | tf_op jit(solution)/shard_map/ppermute | solution.py:56
  160.6 6.4 %collective-permute-start.18 = (bf16[64,2048]{1,0:T(8,128)(2,1)S(1)}, bf16[64,2048]{1,0:T(8,128)(2,1)S(1)}, u32[]{:S(2)}, u32[]{:S(2)}) collective-permute-start(bf16[64,2048]{1,0:T(8,128)(2,1)S(1)} %fusion.47), channel_id=1, source_target_pairs={{4,0},{1,5},{8,4},{5,9},{12,8},{9,13},{14,12},{13,15},{10,14},{15,... | collective-permute-start | bytes 786440 | tf_op jit(solution)/shard_map/ppermute | solution.py:62
  167.1 1.6 collective-permute-start.19

commit v2 on v0

v2 whole, which is shorter than its diff:
```python
import functools
import math

import jax
import jax.numpy as jnp
from jax import lax
from jax.experimental import pallas as pl
from jax.experimental.pallas import tpu as pltpu
from jax.sharding import PartitionSpec as P

TOPK = 8
BF16 = jnp.bfloat16
F32 = jnp.float32


gate_scale = 1.0 / 1024.0


def attend(queries, cache_keys, cache_values, lengths):
    row_count, kv_count, cache_len, head_size = cache_keys.shape
    grouped = queries.reshape(row_count, kv_count, -1, head_size)
    scores = jnp.einsum(
        "rkgh,rkch->rkgc", grouped, cache_keys, preferred_element_type=jnp.float32
    ) * (1.0 / math.sqrt(head_size))
    visible = (
        lax.broadcasted_iota(jnp.int32, (1, 1, 1, cache_len), 3) < lengths[:, None, None, None]
    )
    scores = jnp.where(visible, scores, -1e30)
    highest = jnp.max(scores, axis=3, keepdims=True)
    weights = jnp.exp(scores - highest)
    shares = (weights / jnp.sum(weights, axis=3, keepdims=True)).astype(jnp.bfloat16)
    blended = jnp.einsum(
        "rkgc,rkch->rkgh", shares, cache_values, preferred_element_type=jnp.float32
    )
    return blended.reshape(row_count, -1).astype(jnp.bfloat16)


def rms_scale(features, norm_gain):
    mean_square = jnp.mean(features * features, axis=-1, keepdims=True)
    return features * lax.rsqrt(mean_square + 1e-06) * norm_gain


def ring_plan(devices):
    chips = devices // 2
    order = list(range(0, chips, 2)) + list(range(chips - 1, 0, -2))
    swap = [(device, device ^ 1) for device in range(devices)]

    def toward(step):
        pairs = []
        for place in range(chips):
            for core in range(2):
                target = order[(place + step * (1 - 2 * core)) % chips]
                pairs.append((2 * order[place] + core, 2 * target + core))
        return pairs

    return order, toward, swap


def project_kernel(core_ref, x_ref, own_ref, other_ref, out_ref):
    feats = own_ref.shape[0]

    def both(first, second):
        out_ref[...] = jnp.dot(
            x_ref[:, :feats], first[...], preferred_element_type=F32
        ) + jnp.dot(x_ref[:, feats : 2 * feats], second[...], preferred_element_type=F32)

    @pl.when(core_ref[0] == 0)
    def _():
        both(own_ref, other_ref)

    @pl.when(core_ref[0] == 1)
    def _():
        both(other_ref, own_ref)


def project(core, tokens, own, other):
    rows, feats, width = tokens.shape[0], own.shape[0], own.shape[1]
    vmem = pl.BlockSpec(memory_space=pltpu.VMEM)
    return pl.pallas_call(
        project_kernel,
        out_shape=jax.ShapeDtypeStruct((rows, width), F32),
        in_specs=[pl.BlockSpec(memory_space=pltpu.SMEM), vmem, vmem, vmem],
        out_specs=vmem,
        compiler_params=pltpu.CompilerParams(vmem_limit_bytes=24 * 1024 * 1024),
        cost_estimate=pl.CostEstimate(
            flops=4 * rows * feats * width, bytes_accessed=4 * feats * width, transcendentals=0
        ),
    )(core, tokens, own, other)


def expert_kernel(tiles, pieces, *refs):
    piece_refs, refs = refs[:pieces], refs[pieces:]
    gates_ref, own_refs, other_refs = refs[0], refs[1:4], refs[4:7]
    out_ref, far_ref, x_ref = refs[7:]
    step = pl.program_id(0)

    @pl.when(step == 0)
    def _():
        start = 0
        for piece in piece_refs:
            x_ref[start : start + piece.shape[0], :] = piece[...]
            start += piece.shape[0]
        out_ref[...] = jnp.zeros_like(out_ref)

    def serve(weight_refs, column):
        w_gate, w_up, w_down = weight_refs
        gate_proj = jnp.dot(x_ref[...], w_gate[0], preferred_element_type=F32)
        raised = jnp.dot(x_ref[...], w_up[0], preferred_element_type=F32)
        inner = (jax.nn.silu(gate_proj) * raised).astype(BF16)
        done = jnp.dot(inner, w_down[0], preferred_element_type=F32)
        out_ref[...] += gates_ref[:, column : column + 1] * done

    @pl.when(step < tiles)
    def _():
        serve(own_refs, 0)

    @pl.when(step >= tiles)
    def _():
        serve(other_refs, 1)

    @pl.when(step == 2 * tiles - 1)
    def _():
        far_ref[...] = out_ref[: far_ref.shape[0], :].astype(BF16)


def experts(pieces, gates, own, other, local):
    width, hidden_units = own[0].shape[1:]
    rows = sum(piece.shape[0] for piece in pieces)
    far = pieces[0].shape[0]
    tile = 256
    tiles = hidden_units // tile

    def specs(place):
        wide = pl.BlockSpec((1, width, tile), lambda t: (local, 0, place(t)))
        tall = pl.BlockSpec((1, tile, width), lambda t: (local, place(t), 0))
        return [wide, wide, tall]

    whole = pl.BlockSpec(memory_space=pltpu.VMEM)
    return pl.pallas_call(
        functools.partial(expert_kernel, tiles, len(pieces)),
        out_shape=(
            jax.ShapeDtypeStruct((rows, width), F32),
            jax.ShapeDtypeStruct((far, width), BF16),
        ),
        grid=(2 * tiles,),
        in_specs=[whole] * (len(pieces) + 1)
        + specs(lambda t: jnp.minimum(t, tiles - 1))
        + specs(lambda t: jnp.maximum(t - tiles, 0)),
        out_specs=(whole, whole),
        scratch_shapes=[pltpu.VMEM((rows, width), BF16)],
        compiler_params=pltpu.CompilerParams(vmem_limit_bytes=48 * 1024 * 1024),
        cost_estimate=pl.CostEstimate(
            flops=12 * rows * hidden_units * width,
            bytes_accessed=12 * hidden_units * width,
            transcendentals=2 * rows * hidden_units,
        ),
    )(*pieces, gates, *own, *other)


def on_device(
    queries,
    cache_keys,
    cache_values,
    lengths,
    hidden,
    out_weight,
    norm_gain,
    w_gate,
    w_up,
    w_down,
    expert_ids,
    gate_numer,
):
    rows, width = hidden.shape
    devices = lax.axis_size("rows")
    chips, hops = devices // 2, devices // 4
    local_experts = w_gate.shape[0]
    chip_experts = 2 * local_experts
    expert_total = local_experts * devices
    order, toward, swap = ring_plan(devices)
    spot = [0] * chips
    for place, chip in enumerate(order):
        spot[chip] = place
    me = lax.axis_index("rows")
    chip, core = me // 2, me % 2
    place = jnp.asarray(spot, jnp.int32)[chip]
    sign = 1 - 2 * core
    core_word = core.astype(jnp.int32).reshape(1)

    def chip_at(offset):
        return jnp.asarray(order, jnp.int32)[(place + sign * offset) % chips]

    def pass_on(array, step):
        return lax.ppermute(array, "rows", toward(step))

    def swapped(array):
        return lax.ppermute(array, "rows", swap)

    weight_other = swapped(out_weight)
    own_experts = (w_gate, w_up, w_down)
    other_experts = tuple(swapped(w) for w in own_experts)

    choice = lax.broadcasted_iota(jnp.int32, (1, 1, expert_total), 2)
    numer = jnp.sum(
        jnp.where(expert_ids[:, :, None] == choice, gate_numer[:, :, None], 0), axis=1
    ).reshape(rows, chips, chip_experts)
    digits = jnp.concatenate([numer // 16, numer % 16], axis=2).astype(BF16)
    extra = -(-2 * chip_experts // 128) * 128
    digits = jnp.pad(digits, ((0, 0), (0, 0), (0, extra - 2 * chip_experts)))

    attended = attend(queries, cache_keys, cache_values, lengths)
    chip_feats = attended.shape[1] // chips
    tokens = jnp.concatenate([attended.reshape(rows, chips, chip_feats), digits], axis=2)
    tokens = tokens.transpose(1, 0, 2)
    got = swapped(jnp.take(tokens, jnp.stack([chip_at(o) for o in range(1, hops)]), axis=0))
    arrived = {}
    for offset in range(hops, 0, -1):
        message = lax.dynamic_index_in_dim(tokens, chip_at(-offset), 0, keepdims=False)
        if offset < hops:
            message = jnp.concatenate([message, got[offset - 1]], axis=0)
        arrived[offset] = pass_on(message, -offset)
    arrived[0] = lax.dynamic_index_in_dim(tokens, chip, 0, keepdims=False)

    partial = {}
    for offset in range(hops, -1, -1):
        partial[offset] = project(core_word, arrived[offset], out_weight, weight_other)

    def ring_sums(partial, message):
        own, other = message, partial[hops - 1][rows:].astype(BF16)
        for offset in range(hops - 1, 0, -1):
            if offset < hops - 1:
                other = (pass_on(other, 1).astype(F32) + partial[offset][rows:]).astype(BF16)
            own = (pass_on(own, 1).astype(F32) + partial[offset][:rows]).astype(BF16)
        other = swapped(pass_on(other, 1)).astype(F32)
        return pass_on(own, 1).astype(F32) + partial[0] + other

    projected = ring_sums(partial, partial[hops].astype(BF16))
    residual = (hidden.astype(F32) + projected).astype(BF16)
    normed = rms_scale(residual.astype(F32), norm_gain).astype(BF16)

    own, other = normed, swapped(normed)
    pieces, bounds = [own], []
    for offset in range(1, hops + 1):
        own = pass_on(own, -1)
        if offset < hops:
            other = pass_on(other, -1)
            pieces = [own, other] + pieces
        else:
            pieces = [own] + pieces

    digits = jnp.concatenate(
        [arrived[offset][:, chip_feats : chip_feats + 2 * chip_experts] for offset in range(hops, -1, -1)],
        axis=0,
    ).astype(F32)
    gates = (digits[:, :chip_experts] * 16.0 + digits[:, chip_experts:]) * gate_scale
    gates = jnp.stack([gates[:, :local_experts], gates[:, local_experts:]], axis=1)
    gates = jnp.where(core == 0, gates, gates[:, ::-1])

    for local in range(local_experts):
        served, far = experts(pieces, gates[:, :, local], own_experts, other_experts, local)
        if local == 0:
            total, first = served, far
        else:
            total = total + served
            first = total[:rows].astype(BF16)

    partial = {0: total[-rows:]}
    for offset in range(1, hops):
        start = rows + (hops - 1 - offset) * 2 * rows
        partial[offset] = total[start : start + 2 * rows]
    combined = ring_sums(partial, first)
    return (residual.astype(F32) + combined).astype(BF16)


def solution(mesh):
    in_specs = (
        P(("groups", "rows"), None),
        P(("groups", "rows"), None, None, None),
        P(("groups", "rows"), None, None, None),
        P(("groups", "rows")),
        P(("groups", "rows"), None),
        P("rows", None),
        P(),
        P("rows", None, None),
        P("rows", None, None),
        P("rows", None, None),
        P(("groups", "rows"), None),
        P(("groups", "rows"), None),
    )
    out_specs = P(("groups", "rows"), None)
    return jax.shard_map(
        on_device, mesh=mesh, in_specs=in_specs, out_specs=out_specs, check_vma=False
    )
```

time: 244 us -> 140 us (0.57)
  the two profiles are of different devices: /device:TPU:13 before, /device:TPU:0 now
where the time goes in v2:
time: 140 us; the launch traced here: 139 us
  waiting for transfers between devices  43.7 us (31%)
  starting transfers between devices  36.9 us (26%)
  Pallas kernels  20 us (14%)
  between operations  12.4 us (9%)
  other arithmetic  10.5 us (8%)
  local copies, waits for them, and re-layouts  9.75 us (7%)
  matrix products  5.34 us (4%)
    ppermute x25, waiting for transfers between devices, pass_on(): return lax.ppermute(array, 'rows', toward(step))  43.4 us
    ppermute x25, starting transfers between devices, pass_on(): return lax.ppermute(array, 'rows', toward(step))  35.8 us
    pallas_call x1, Pallas kernels, experts(): pl.pallas_call(functools.partial(expert_kernel, tiles, len(pieces)), out_...  11.6 us
    pallas_call x5, Pallas kernels, project(): pl.pallas_call(project_kernel, out_shape=jax.ShapeDtypeStruct((rows, widt...  8.47 us
    dot_general x1, matrix products, attend(): jnp.einsum('rkgc,rkch->rkgh', shares, cache_values, preferred_element_typ...  4.15 us
    select_n x2, other arithmetic, on_device(): jnp.take(tokens, jnp.stack([chip_at(o) for o in range(1, hops)]), axis=0)  3.53 us
  transfers between devices with their start and end apart: 33, of which 21 were waited for; matrix products, arithmetic and copies ran while one was open for 18% of the time, Pallas kernels for 5%

profile of v2, /device:TPU:0, one launch (start us, length us, event | category | flops | bytes accessed | tf_op | source)
XLA Modules:
  0.0 138.7 jit_solution(14353388854183547784)
XLA Ops:
  0.0 0.5 collective-permute-start.1
  0.5 1.4 %dynamic_slice.30 = s32[1]{0:T(128)} dynamic-slice(s32[8]{0:T(128)} %constant.146.clone, s32[]{:T(128)S(6)} %select_n.130), dynamic_slice_sizes={1} | dynamic-slice | bytes 12 | tf_op jit(solution)/shard_map/dynamic_slice | solution.py:186
  5.9 0.7 iota_compare_fusion.2
  6.6 0.7 select_reduce_fusion
  7.4 1.0 copy.49
  8.4 1.2 fusion.3
  9.6 0.4 fusion.23
  10.0 4.1 %convolution_convert_fusion = bf16[32,2,16,128]{3,2,1,0:T(8,128)(2,1)} fusion(bf16[32,2,128,128]{3,2,1,0:T(8,128)(2,1)} %param.22, f32[32,2,16]{2,1,0:T(2,128)S(1)} %fusion.23, f32[32,2,16,128]{3,2,1,0:T(8,128)S(1)} %fusion.3), kind=kOutput, calls=%fused_computation.6 | convolution fusion | flops 34079872 | bytes 2887680 | tf_op jit(solution)/shard_map/rkgc,rkch->rkgh/dot_general | solution.py:32
  14.9 0.8 copy.48
  15.7 1.1 convert_element_type.112
  16.8 0.8 copy.39
  17.6 0.7 fusion.22
  18.3 1.9 %fusion.19 = s32[3]{0:T(128)S(1)} fusion(s32[1,1]{0,1:T(1,128)} %bitcast.10, s32[1,1]{0,1:T(1,128)} %bitcast.9, s32[1,1]{0,1:T(1,128)} %bitcast.8), kind=kLoop, calls=%fused_computation.73 | loop fusion | flops 15 | bytes 24 | tf_op jit(solution)/shard_map/jit(_take)/jit(_where)/select_n | solution.py:215
  20.2 1.8 %fusion.5 = (bf16[32,8,640]{2,0,1:T(8,128)(2,1)S(1)}, bf16[8,32,640]{2,1,0:T(8,128)(2,1)}) fusion(bf16[32,8,4]{2,0,1:T(8,128)(2,1)} %copy.48, bf16[32,8,512]{2,0,1:T(8,128)(2,1)} %copy.39), kind=kLoop, calls=%fused_computation.13 | loop fusion | flops 983040 | bytes 919552 | tf_op jit(solution)/shard_map/concatenate | solution.py:213
  21.9 2.2 %gather_fusion = bf16[3,32,640]{2,1,0:T(8,128)(2,1)} fusion(bf16[8,32,640]{2,1,0:T(8,128)(2,1)} %get-tuple-element.25, s32[1024]{0:T(1024)S(1)} %pad_clamp_fusion), kind=kCustom, calls=%fused_computation | custom fusion | bytes 245772 | tf_op jit(solution)/shard_map/jit(_take)/gather | solution.py:215
  24.1 1.9 %compare_and_fusion = pred[3]{0:T(512)(128)(4,1)S(1)} fusion(s32[1]{0:T(128)} %get-tuple-element.34, s32[1]{0:T(128)} %get-tuple-element.35, s32[1]{0:T(128)} %get-tuple-element.36), kind=kLoop, calls=%fused_computation.70 | loop fusion | flops 24 | bytes 15 | tf_op jit(solution)/shard_map/jit(_take)/and | solution.py:215
  26.0 1.6 %broadcast_select_fusion = bf16[3,32,640]{2,1,0:T(8,128)(2,1)} fusion(bf16[3,32,640]{2,1,0:T(8,128)(2,1)} %gather_fusion, pred[3]{0:T(512)(128)(4,1)S(1)} %compare_and_fusion), kind=kLoop, calls=%fused_computation.38 | loop fusion | flops 61440 | bytes 245763 | tf_op jit(solution)/shard_map/jit(_take)/select_n | solution.py:215
  35.1 5.9 %collective-permute-start = (bf16[32,640]{1,0:T(8,128)(2,1)S(1)}, bf16[32,640]{1,0:T(8,128)(2,1)S(1)}, u32[]{:S(2)}, u32[]{:S(2)}) collective-permute-start(bf16[32,640]{1,0:T(8,128)(2,1)S(1)} %get-tuple-element.19), channel_id=1, source_target_pairs={{0,14},{1,15},{4,10},{5,11},{8,6},{9,7},{12,2},{13,3},{14,0},{15,1... | collective-permute-start | bytes 122888 | tf_op jit(solution)/shard_map/ppermute | solution.py:194
  41.1 0.8 slice_bitcast_fusion.2
  41.9 1.2 collective-permute-done.x_ref
  43.1 1.7 %shard_map.190 = f32[32,2048]{1,0:T(8,128)S(1)} custom-call(s32[1]{0:T(128)} %bitcast.core_ref, bf16[32,640]{1,0:T(8,128)(2,1)S(1)} %collective-permute-done.x_ref, bf16[256,2048]{1,0:T(8,128)(2,1)S(1)} %copy-done.1, bf16[256,2048]{1,0:T(8,128)(2,1)} %collective-permute-done.1.other_ref), custom_call_target="tpu_custom_call" | custom-call | flops 67108864 | bytes 2097152 | tf_op jit(solution)/shard_map/pallas_call | solution.py:79
  44.8 0.8 collective-permute-start.2
  45.7 2.5 %collective-permute-start.4 = (bf16[64,640]{1,0:T(8,128)(2,1)S(1)}, bf16[64,640]{1,0:T(8,128)(2,1)S(1)}, u32[]{:S(2)}, u32[]{:S(2)}) collective-permute-start(bf16[64,640]{1,0:T(8,128)(2,1)S(1)} %pad_maximum_fusion), channel_id=1, source_target_pairs={{0,10},{1,13},{4,6},{5,15},{8,2},{9,11},{12,0},{13,7},{14,4},{15,3... | collective-permute-start | bytes 245768 | tf_op jit(solution)/shard_map/ppermute | solution.py:194
  48.1 0.5 collective-permute-start.23
  48.6 4.0 %collective-permute-done.4.x_ref = bf16[64,640]{1,0:T(8,128)(2,1)S(1)} collective-permute-done((bf16[64,640]{1,0:T(8,128)(2,1)S(1)}, bf16[64,640]{1,0:T(8,128)(2,1)S(1)}, u32[]{:S(2)}, u32[]{:S(2)}) %collective-permute-start.4) | collective-permute-done | bytes 81952 | tf_op jit(solution)/shard_map/ppermute | solution.py:194
  52.6 1.7 %shard_map.191 = f32[64,2048]{1,0:T(8,128)S(1)} custom-call(s32[1]{0:T(128)} %bitcast.core_ref, bf16[64,640]{1,0:T(8,128)(2,1)S(1)} %collective-permute-done.4.x_ref, bf16[256,2048]{1,0:T(8,128)(2,1)S(1)} %copy-done.1, bf16[256,2048]{1,0:T(8,128)(2,1)} %collective-permute-done.1.other_ref), custom_call_target="tpu_custom_call" | custom-call | flops 134217728 | bytes 2097152 | tf_op jit(solution)/shard_map/pallas_call | solution.py:79
  54.3 1.5 %collective-permute-start.10 = (bf16[32,2048]{1,0:T(8,128)(2,1)S(1)}, bf16[32,2048]{1,0:T(8,128)(2,1)S(1)}, u32[]{:S(2)}, u32[]{:S(2)}) collective-permute-start(bf16[32,2048]{1,0:T(8,128)(2,1)S(1)} %slice.167), channel_id=1, source_target_pairs={{0,4},{1,3},{4,8},{5,1},{8,12},{9,5},{12,14},{13,9},{14,10},{15,13... | collective-permute-start | bytes 393224 | tf_op jit(solution)/shard_map/ppermute | solution.py:194
  56.1 1.9 %collective-permute-start.6 = (bf16[64,640]{1,0:T(8,128)(2,1)S(1)}, bf16[64,640]{1,0:T(8,128)(2,1)S(1)}, u32[]{:S(2)}, u32[]{:S(2)}) collective-permute-start(bf16[64,640]{1,0:T(8,128)(2,1)S(1)} %pad_maximum_fusion.1), channel_id=1, source_target_pairs={{0,6},{1,9},{4,2},{5,13},{8,0},{9,15},{12,4},{13,11},{14,8},{15,7}... | collective-permute-start | bytes 245768 | tf_op jit(solution)/shard_map/ppermute | solution.py:194
  58.1 3.7 %collective-permute-done.6.x_ref = bf16[64,640]{1,0:T(8,128)(2,1)S(1)} collective-permute-done((bf16[64,640]{1,0:T(8,128)(2,1)S(1)}, bf16[64,640]{1,0:T(8,128)(2,1)S(1)}, u32[]{:S(2)}, u32[]{:S(2)}) %collective-permute-start.6) | collective-permute-done | bytes 81952 | tf_op jit(solution)/shard_map/ppermute | solution.py:194
  61.8 1.7 %shard_map.192 = f32[64,2048]{1,0:T(8,128)S(1)} custom-call(s32[1]{0:T(128)} %bitcast.core_ref, bf16[64,640]{1,0:T(8,128)(2,1)S(1)} %collective-permute-done.6.x_ref, bf16[256,2048]{1,0:T(8,128)(2,1)S(1)} %copy-done.1, bf16[256,2048]{1,0:T(8,128)(2,1)} %collective-permute-done.1.other_ref), custom_call_target="tpu_custom_call" | custom-call | flops 134217728 | bytes 2097152 | tf_op jit(solution)/shard_map/pallas_call | solution.py:79
  63.5 2.3 %collective-permute-start.8 = (bf16[64,640]{1,0:T(8,128)(2,1)S(1)}, bf16[64,640]{1,0:T(8,128)(2,1)S(1)}, u32[]{:S(2)}, u32[]{:S(2)}) collective-permute-start(bf16[64,640]{1,0:T(8,128)(2,1)S(1)} %pad_maximum_fusion.2), channel_id=1, source_target_pairs={{0,2},{1,5},{4,0},{5,9},{8,4},{9,13},{12,8},{13,15},{14,12},{15,11... | collective-permute-start | bytes 245768 | tf_op jit(solution)/shard_map/ppermute | solution.py:194
  65.9 1.2 collective-permute-start.7
  67.1 2.3 %collective-permute-done.8.x_ref = bf16[64,640]{1,0:T(8,128)(2,1)S(1)} collective-permute-done((bf16[64,640]{1,0:T(8,128)(2,1)S(1)}, bf16[64,640]{1,0:T(8,128)(2,1)S(1)}, u32[]{:S(2)}, u32[]{:S(2)}) %collective-permute-start.8) | collective-permute-done | bytes 81952 | tf_op jit(solution)/shard_map/ppermute | solution.py:194
  69.4 2.9 %collective-permute-start.11 = (bf16[32,2048]{1,0:T(8,128)(2,1)S(1)}, bf16[32,2048]{1,0:T(8,128)(2,1)S(1)}, u32[]{:S(2)}, u32[]{:S(2)}) collective-permute-start(bf16[32,2048]{1,0:T(8,128)(2,1)S(1)} %get-tuple-element.18), channel_id=1, source_target_pairs={{0,4},{1,3},{4,8},{5,1},{8,12},{9,5},{12,14},{13,9},{14,10},{15,13... | collective-permute-start | bytes 393224 | tf_op jit(solution)/shard_map/ppermute | solution.py:194
  72.3 1.7 %shard_map.193 = f32[64,2048]{1,0:T(8,128)S(1)} custom-call(s32[1]{0:T(128)} %bitcast.core_ref, bf16[64,640]{1,0:T(8,128)(2,1)S(1)} %collective-permute-done.8.x_ref, bf16[256,2048]{1,0:T(8,128)(2,1)S(1)} %copy-done.1, bf16[256,2048]{1,0:T(8,128)(2,1)} %collective-permute-done.1.other_ref), custom_call_target="tpu_custom_call" | custom-call | flops 134217728 | bytes 2097152 | tf_op jit(solution)/shard_map/pallas_call | solution.py:79
  74.0 0.8 collective-permute-done.11
  74.8 2.5 %collective-permute-start.12 = (bf16[32,2048]{1,0:T(8,128)(2,1)S(1)}, bf16[32,2048]{1,0:T(8,128)(2,1)S(1)}, u32[]{:S(2)}, u32[]{:S(2)}) collective-permute-start(bf16[32,2048]{1,0:T(8,128)(2,1)S(1)} %get-tuple-element.16), channel_id=1, source_target_pairs={{0,4},{1,3},{4,8},{5,1},{8,12},{9,5},{12,14},{13,9},{14,10},{15,13... | collective-permute-start | bytes 393224 | tf_op jit(solution)/shard_map/ppermute | solution.py:194
  77.4 2.5 %collective-permute-done.12 = bf16[32,2048]{1,0:T(8,128)(2,1)S(1)} collective-permute-done((bf16[32,2048]{1,0:T(8,128)(2,1)S(1)}, bf16[32,2048]{1,0:T(8,128)(2,1)S(1)}, u32[]{:S(2)}, u32[]{:S(2)}) %collective-permute-start.12) | collective-permute-done | bytes 131104 | tf_op jit(solution)/shard_map/ppermute | solution.py:194
  79.9 1.7 %shard_map.194 = f32[32,2048]{1,0:T(8,128)S(1)} custom-call(s32[1]{0:T(128)} %bitcast.core_ref, bf16[32,640]{1,0:T(8,128)(2,1)S(1)} %get-tuple-element.22.x_ref, bf16[256,2048]{1,0:T(8,128)(2,1)S(1)} %copy-done.1, bf16[256,2048]{1,0:T(8,128)(2,1)} %collective-permute-done.1.other_ref), custom_call_target="tpu_custom_call" | custom-call | flops 67108864 | bytes 2097152 | tf_op jit(solution)/shard_map/pallas_call | solution.py:79
  81.5 0.8 collective-permute-done.9
  82.7 0.4 collective-permute-start.14
  83.7 0.3 collective-permute-done.18
  84.0 1.8 %collective-permute-start.19 = (bf16[32,2048]{1,0:T(8,128)(2,1)S(1)}, bf16[32,2048]{1,0:T(8,128)(2,1)S(1)}, u32[]{:S(2)}, u32[]{:S(2)}) collective-permute-start(bf16[32,2048]{1,0:T(8,128)(2,1)S(1)} %collective-permute-done.18), channel_id=1, source_target_pairs={{0,2},{1,5},{4,0},{5,9},{8,4},{9,13},{12,8},{13,15},{14,12},{15,11... | collective-permute-start | bytes 393224 | tf_op jit(solution)/shard_map/ppermute | solution.py:194
  85.8 2.0 %collective-permute-done.14.refs_5_ = bf16[32,2048]{1,0:T(8,128)(2,1)S(1)} collective-permute-done((bf16[32,2048]{1,0:T(8,128)(2,1)S(1)}, bf16[32,2048]{1,0:T(8,128)(2,1)S(1)}, u32[]{:S(2)}, u32[]{:S(2)}) %collective-permute-start.14) | collective-permute-done | bytes 131104 | tf_op jit(solution)/shard_map/ppermute | solution.py:194
  88.1 1.1 collective-permute-done.19.refs_6_
  89.3 1.5 %collective-permute-start.20 = (bf16[32,2048]{1,0:T(8,128)(2,1)S(1)}, bf16[32,2048]{1,0:T(8,128)(2,1)S(1)}, u32[]{:S(2)}, u32[]{:S(2)}) collective-permute-start(bf16[32,2048]{1,0:T(8,128)(2,1)S(1)} %collective-permute-done.19.refs_6_), channel_id=1, source_target_pairs={{0,2},{1,5},{4,0},{5,9},{8,4},{9,13},{12,8},{13,15},{14,12},{15,11... | collective-permute-start | bytes 393224 | tf_op jit(solution)/shard_map/ppermute | solution.py:194
  90.8 2.0 %collective-permute-done.15.refs_3_ = bf16[32,2048]{1,0:T(8,128)(2,1)S(1)} collective-permute-done((bf16[32,2048]{1,0:T(8,128)(2,1)S(1)}, bf16[32,2048]{1,0:T(8,128)(2,1)S(1)}, u32[]{:S(2)}, u32[]{:S(2)}) %collective-permute-start.15) | collective-permute-done | bytes 131104 | tf_op jit(solution)/shard_map/ppermute | solution.py:194
  93.4 0.8 collective-permute-done.20.refs_4_
  94.2 1.5 %collective-permute-start.21 = (bf16[32,2048]{1,0:T(8,128)(2,1)S(1)}, bf16[32,2048]{1,0:T(8,128)(2,1)S(1)}, u32[]{:S(2)}, u32[]{:S(2)}) collective-permute-start(bf16[32,2048]{1,0:T(8,128)(2,1)S(1)} %collective-permute-done.20.refs_4_), channel_id=1, source_target_pairs={{0,2},{1,5},{4,0},{5,9},{8,4},{9,13},{12,8},{13,15},{14,12},{15,11... | collective-permute-start | bytes 393224 | tf_op jit(solution)/shard_map/ppermute | solution.py:194
  95.8 2.0 %collective-permute-done.16.refs_1_ = bf16[32,2048]{1,0:T(8,128)(2,1)S(1)} collective-permute-done((bf16[32,2048]{1,0:T(8,128)(2,1)S(1)}, bf16[32,2048]{1,0:T(8,128)(2,1)S(1)}, u32[]{:S(2)}, u32[]{:S(2)}) %collective-permute-start.16) | collective-permute-done | bytes 131104 | tf_op jit(solution)/shard_map/ppermute | solution.py:194
  98.1 1.1 collective-permute-done.21.refs_2_
  99.2 3.6 %collective-permute-done.17.refs_0_ = bf16[32,2048]{1,0:T(8,128)(2,1)S(1)} collective-permute-done((bf16[32,2048]{1,0:T(8,128)(2,1)S(1)}, bf16[32,2048]{1,0:T(8,128)(2,1)S(1)}, u32[]{:S(2)}, u32[]{:S(2)}) %collective-permute-start.17) | collective-permute-done | bytes 131104 | tf_op jit(solution)/shard_map/ppermute | solution.py:194
  102.8 11.6 %shard_map.195 = (f32[256,2048]{1,0:T(8,128)S(1)}, bf16[32,2048]{1,0:T(8,128)(2,1)S(1)}) custom-call(bf16[32,2048]{1,0:T(8,128)(2,1)S(1)} %collective-permute-done.17.refs_0_, bf16[32,2048]{1,0:T(8,128)(2,1)S(1)} %collective-permute-done.16.refs_1_, bf16[32,2048]{1,0:T(8,128)(2,1)S(1)} %collective-permute-done.21.refs_2_, ...), custom_call_target="tpu_custom_call" | custom-call | flops 4831838208 | bytes 18874368 | tf_op jit(solution)/shard_map/pallas_call | solution.py:139
  114.3 2.1 %collective-permute-start.25 = (bf16[32,2048]{1,0:T(8,128)(2,1)S(1)}, bf16[32,2048]{1,0:T(8,128)(2,1)S(1)}, u32[]{:S(2)}, u32[]{:S(2)}) collective-permute-start(bf16[32,2048]{1,0:T(8,128)(2,1)S(1)} %get-tuple-element.7), channel_id=1, source_target_pairs={{0,4},{1,3},{4,8},{5,1},{8,12},{9,5},{12,14},{13,9},{14,10},{15,13... | collective-permute-start | bytes 393224 | tf_op jit(solution)/shard_map/ppermute | solution.py:194
  116.5 2.8 %collective-permute-done.25 = bf16[32,2048]{1,0:T(8,128)(2,1)S(1)} collective-permute-done((bf16[32,2048]{1,0:T(8,128)(2,1)S(1)}, bf16[32,2048]{1,0:T(8,128)(2,1)S(1)}, u32[]{:S(2)}, u32[]{:S(2)}) %collective-permute-start.25) | collective-permute-done | bytes 131104 | tf_op jit(solution)/shard_map/ppermute | solution.py:194
  119.4 2.1 %collective-permute-start.26 = (bf16[32,2048]{1,0:T(8,128)(2,1)S(1)}, bf16[32,2048]{1,0:T(8,128)(2,1)S(1)}, u32[]{:S(2)}, u32[]{:S(2)}) collective-permute-start(bf16[32,2048]{1,0:T(8,128)(2,1)S(1)} %add_convert_fusion.4), channel_id=1, source_target_pairs={{0,4},{1,3},{4,8},{5,1},{8,12},{9,5},{12,14},{13,9},{14,10},{15,13... | collective-permute-start | bytes 393224 | tf_op jit(solution)/shard_map/ppermute | solution.py:194
  121.5 2.9 %collective-permute-done.26 = bf16[32,2048]{1,0:T(8,128)(2,1)S(1)} collective-permute-done((bf16[32,2048]{1,0:T(8,128)(2,1)S(1)}, bf16[32,2048]{1,0:T(8,128)(2,1)S(1)}, u32[]{:S(2)}, u32[]{:S(2)}) %collective-permute-start.26) | collective-permute-done | bytes 131104 | tf_op jit(solution)/shard_map/ppermute | solution.py:194
  124.5 2.1 %collective-permute-start.27 = (bf16[32,2048]{1,0:T(8,128)(2,1)S(1)}, bf16[32,2048]{1,0:T(8,128)(2,1)S(1)}, u32[]{:S(2)}, u32[]{:S(2)}) collective-permute-start(bf16[32,2048]{1,0:T(8,128)(2,1)S(1)} %get-tuple-element.13), channel_id=1, source_target_pairs={{0,4},{1,3},{4,8},{5,1},{8,12},{9,5},{12,14},{13,9},{14,10},{15,13... | collective-permute-start | bytes 393224 | tf_op jit(solution)/shard_map/ppermute | solution.py:194
  126.6 2.9 %collective-permute-done.27 = bf16[32,2048]{1,0:T(8,128)(2,1)S(1)} collective-permute-done((bf16[32,2048]{1,0:T(8,128)(2,1)S(1)}, bf16[32,2048]{1,0:T(8,128)(2,1)S(1)}, u32[]{:S(2)}, u32[]{:S(2)}) %collective-permute-start.27) | collective-permute-done | bytes 131104 | tf_op jit(solution)/shard_map/ppermute | solution.py:194
  129.5 2.0 %collective-permute-done.30 = bf16[32,2048]{1,0:T(8,128)(2,1)S(1)} collective-permute-done((bf16[32,2048]{1,0:T(8,128)(2,1)S(1)}, bf16[32,2048]{1,0:T(8,128)(2,1)S(1)}, u32[]{:S(2)}, u32[]{:S(2)}) %collective-permute-start.30) | collective-permute-done | bytes 131104 | tf_op jit(solution)/shard_map/ppermute | solution.py:194
  131.6 1.5 %collective-permute-start.31 = (bf16[32,2048]{1,0:T(8,128)(2,1)S(1)}, bf16[32,2048]{1,0:T(8,128)(2,1)S(1)}, u32[]{:S(2)}, u32[]{:S(2)}) collective-permute-start(bf16[32,2048]{1,0:T(8,128)(2,1)S(1)} %get-tuple-element.12), channel_id=1, source_target_pairs={{0,4},{1,3},{4,8},{5,1},{8,12},{9,5},{12,14},{13,9},{14,10},{15,13... | collective-permute-start | bytes 393224 | tf_op jit(solution)/shard_map/ppermute | solution.py:194
  133.1 3.5 %collective-permute-done.31 = bf16[32,2048]{1,0:T(8,128)(2,1)S(1)} collective-permute-done((bf16[32,2048]{1,0:T(8,128)(2,1)S(1)}, bf16[32,2048]{1,0:T(8,128)(2,1)S(1)}, u32[]{:S(2)}, u32[]{:S(2)}) %collective-permute-start.31) | collective-permute-done | bytes 131104 | tf_op jit(solution)/shard_map/ppermute | solution.py:194
  136.6 1.4 %collective-permute-done.28 = bf16[32,2048]{1,0:T(8,128)(2,1)S(1)} collective-permute-done((bf16[32,2048]{1,0:T(8,128)(2,1)S(1)}, bf16[32,2048]{1,0:T(8,128)(2,1)S(1)}, u32[]{:S(2)}, u32[]{:S(2)}) %collective-permute-start.28) | collective-permute-done | bytes 131104 | tf_op jit(solution)/shard_map/ppermute | solution.py:194
  138.0 0.7 fusion.9
  (73 shorter events, 3.2 us)
Async XLA Ops:
  0.0 8.4 %copy-start = (bf16[32,2,128,128]{3,2,1,0:T(8,128)(2,1)S(1)}, bf16[32,2,128,128]{3,2,1,0:T(8,128)(2,1)}, u32[]{:S(2)}) copy-start(bf16[32,2,128,128]{3,2,1,0:T(8,128)(2,1)} %param.21) | copy-start | bytes 6291460
  0.0 43.1 %collective-permute-start.1 = (bf16[256,2048]{1,0:T(8,128)(2,1)}, bf16[256,2048]{1,0:T(8,128)(2,1)}, u32[]{:S(2)}, u32[]{:S(2)}) collective-permute-start(bf16[256,2048]{1,0:T(8,128)(2,1)} %own_ref.9), channel_id=1, source_target_pairs={{0,1},{1,0},{2,3},{3,2},{4,5},{5,4},{6,7},{7,6},{8,9},{9,8},{10,11... | collective-permute-start | bytes 3145736 | tf_op jit(solution)/shard_map/ppermute | solution.py:197
  10.0 7.6 %copy-start.3 = (s32[8]{0:T(128)S(1)}, s32[8]{0:T(128)}, u32[]{:S(2)}) copy-start(s32[8]{0:T(128)} %constant.147.clone) | copy-start | bytes 100
  14.2 28.9 %copy-start.1 = (bf16[256,2048]{1,0:T(8,128)(2,1)S(1)}, bf16[256,2048]{1,0:T(8,128)(2,1)}, u32[]{:S(2)}) copy-start(bf16[256,2048]{1,0:T(8,128)(2,1)} %own_ref.9) | copy-start | bytes 3145732
  27.7 13.4 %collective-permute-start.3 = (bf16[3,32,640]{2,1,0:T(8,128)(2,1)}, bf16[3,32,640]{2,1,0:T(8,128)(2,1)}, u32[]{:S(2)}, u32[]{:S(2)}) collective-permute-start(bf16[3,32,640]{2,1,0:T(8,128)(2,1)} %broadcast_select_fusion), channel_id=1, source_target_pairs={{0,1},{1,0},{2,3},{3,2},{4,5},{5,4},{6,7},{7,6},{8,9},{9,8},{10,11... | collective-permute-start | bytes 368648 | tf_op jit(solution)/shard_map/ppermute | solution.py:197
  35.1 7.9 %collective-permute-start = (bf16[32,640]{1,0:T(8,128)(2,1)S(1)}, bf16[32,640]{1,0:T(8,128)(2,1)S(1)}, u32[]{:S(2)}, u32[]{:S(2)}) collective-permute-start(bf16[32,640]{1,0:T(8,128)(2,1)S(1)} %get-tuple-element.19), channel_id=1, source_target_pairs={{0,14},{1,15},{4,10},{5,11},{8,6},{9,7},{12,2},{13,3},{14,0},{15,1... | collective-permute-start | bytes 122888 | tf_op jit(solution)/shard_map/ppermute | solution.py:194
  44.8 11.0 %collective-permute-start.2 = (bf16[32,2048]{1,0:T(8,128)(2,1)S(1)}, bf16[32,2048]{1,0:T(8,128)(2,1)S(1)}, u32[]{:S(2)}, u32[]{:S(2)}) collective-permute-start(bf16[32,2048]{1,0:T(8,128)(2,1)S(1)} %convert_element_type.113), channel_id=1, source_target_pairs={{0,4},{1,3},{4,8},{5,1},{8,12},{9,5},{12,14},{13,9},{14,10},{15,13... | collective-permute-start | bytes 393224 | tf_op jit(solution)/shard_map/ppermute | solution.py:194
  45.7 6.9 %collective-permute-start.4 = (bf16[64,640]{1,0:T(8,128)(2,1)S(1)}, bf16[64,640]{1,0:T(8,128)(2,1)S(1)}, u32[]{:S(2)}, u32[]{:S(2)}) collective-permute-start(bf16[64,640]{1,0:T(8,128)(2,1)S(1)} %pad_maximum_fusion), channel_id=1, source_target_pairs={{0,10},{1,13},{4,6},{5,15},{8,2},{9,11},{12,0},{13,7},{14,4},{15,3... | collective-permute-start | bytes 245768 | tf_op jit(solution)/shard_map/ppermute | solution.py:194
  48.1 54.6 %collective-permute-start.22 = (bf16[1,2048,768]{2,1,0:T(8,128)(2,1)}, bf16[1,2048,768]{2,1,0:T(8,128)(2,1)}, u32[]{:S(2)}, u32[]{:S(2)}) collective-permute-start(bf16[1,2048,768]{2,1,0:T(8,128)(2,1)} %refs_9_.1), channel_id=1, source_target_pairs={{0,1},{1,0},{2,3},{3,2},{4,5},{5,4},{6,7},{7,6},{8,9},{9,8},{10,11... | collective-permute-start | bytes 9437192 | tf_op jit(solution)/shard_map/ppermute | solution.py:197
  48.1 54.6 %collective-permute-start.23 = (bf16[1,2048,768]{2,1,0:T(8,128)(2,1)}, bf16[1,2048,768]{2,1,0:T(8,128)(2,1)}, u32[]{:S(2)}, u32[]{:S(2)}) collective-permute-start(bf16[1,2048,768]{2,1,0:T(8,128)(2,1)} %refs_10_.1), channel_id=1, source_target_pairs={{0,1},{1,0},{2,3},{3,2},{4,5},{5,4},{6,7},{7,6},{8,9},{9,8},{10,11... | collective-permute-start | bytes 9437192 | tf_op jit(solution)/shard_map/ppermute | solution.py:197
  54.3 9.2 %collective-permute-start.10 = (bf16[32,2048]{1,0:T(8,128)(2,1)S(1)}, bf16[32,2048]{1,0:T(8,128)(2,1)S(1)}, u32[]{:S(2)}, u32[]{:S(2)}) collective-permute-start(bf16[32,2048]{1,0:T(8,128)(2,1)S(1)} %slice.167), channel_id=1, source_target_pairs={{0,4},{1,3},{4,8},{5,1},{8,12},{9,5},{12,14},{13,9},{14,10},{15,13... | collective-permute-start | bytes 393224 | tf_op jit(solution)/shard_map/ppermute | solution.py:194
  55.9 9.9 %collective-permute-start.5 = (bf16[32,2048]{1,0:T(8,128)(2,1)S(1)}, bf16[32,2048]{1,0:T(8,128)(2,1)S(1)}, u32[]{:S(2)}, u32[]{:S(2)}) collective-permute-start(bf16[32,2048]{1,0:T(8,128)(2,1)S(1)} %fusion.14), channel_id=1, source_target_pairs={{0,4},{1,3},{4,8},{5,1},{8,12},{9,5},{12,14},{13,9},{14,10},{15,13... | collective-permute-start | bytes 393224 | tf_op jit(solution)/shard_map/ppermute | solution.py:194
  56.1 5.6 %collective-permute-start.6 = (bf16[64,640]{1,0:T(8,128)(2,1)S(1)}, bf16[64,640]{1,0:T(8,128)(2,1)S(1)}, u32[]{:S(2)}, u32[]{:S(2)}) collective-permute-start(bf16[64,640]{1,0:T(8,128)(2,1)S(1)} %pad_maximum_fusion.1), channel_id=1, source_target_pairs={{0,6},{1,9},{4,2},{5,13},{8,0},{9,15},{12,4},{13,11},{14,8},{15,7}... | collective-permute-start | bytes 245768 | tf_op jit(solution)/shard_map/ppermute | solution.py:194
  61.7 41.0 %collective-permute-start.24 = (bf16[1,768,2048]{2,1,0:T(8,128)(2,1)}, bf16[1,768,2048]{2,1,0:T(8,128)(2,1)}, u32[]{:S(2)}, u32[]{:S(2)}) collective-permute-start(bf16[1,768,2048]{2,1,0:T(8,128)(2,1)} %refs_11_.1), channel_id=1, source_target_pairs={{0,1},{1,0},{2,3},{3,2},{4,5},{5,4},{6,7},{7,6},{8,9},{9,8},{10,11... | collective-permute-start | bytes 9437192 | tf_op jit(solution)/shard_map/ppermute | solution.py:197
  63.5 5.8 %collective-permute-start.8 = (bf16[64,640]{1,0:T(8,128)(2,1)S(1)}, bf16[64,640]{1,0:T(8,128)(2,1)S(1)}, u32[]{:S(2)}, u32[]{:S(2)}) collective-permute-start(bf16[64,640]{1,0:T(8,128)(2,1)S(1)} %pad_maximum_fusion.2), channel_id=1, source_target_pairs={{0,2},{1,5},{4,0},{5,9},{8,4},{9,13},{12,8},{13,15},{14,12},{15,11... | collective-permute-start | bytes 245768 | tf_op jit(solution)/shard_map/ppermute | solution.py:194
  65.9 8.1 %collective-permute-start.7 = (bf16[32,2048]{1,0:T(8,128)(2,1)S(1)}, bf16[32,2048]{1,0:T(8,128)(2,1)S(1)}, u32[]{:S(2)}, u32[]{:S(2)}) collective-permute-start(bf16[32,2048]{1,0:T(8,128)(2,1)S(1)} %get-tuple-element.17), channel_id=1, source_target_pairs={{0,4},{1,3},{4,8},{5,1},{8,12},{9,5},{12,14},{13,9},{14,10},{15,13... | collective-permute-start | bytes 393224 | tf_op jit(solution)/shard_map/ppermute | solution.py:194
  69.4 5.4 %collective-permute-start.11 = (bf16[32,2048]{1,0:T(8,128)(2,1)S(1)}, bf16[32,2048]{1,0:T(8,128)(2,1)S(1)}, u32[]{:S(2)}, u32[]{:S(2)}) collective-permute-start(bf16[32,2048]{1,0:T(8,128)(2,1)S(1)} %get-tuple-element.18), channel_id=1, source_target_pairs={{0,4},{1,3},{4,8},{5,1},{8,12},{9,5},{12,14},{13,9},{14,10},{15,13... | collective-permute-start | bytes 393224 | tf_op jit(solution)/shard_map/ppermute | solution.py:194
  74.0 8.3 %copy-start.2 = (bf16[32,2048]{1,0:T(8,128)(2,1)S(1)}, bf16[32,2048]{1,0:T(8,128)(2,1)}, u32[]{:S(2)}) copy-start(bf16[32,2048]{1,0:T(8,128)(2,1)} %param.24) | copy-start | bytes 393220
  74.0 8.5 %copy-start.4 = (f32[2048]{0:T(1024)S(1)}, f32[2048]{0:T(1024)}, u32[]{:S(2)}) copy-start(f32[2048]{0:T(1024)} %param.26) | copy-start | bytes 24580
  74.8 5.0 %collective-permute-start.12 = (bf16[32,2048]{1,0:T(8,128)(2,1)S(1)}, bf16[32,2048]{1,0:T(8,128)(2,1)S(1)}, u32[]{:S(2)}, u32[]{:S(2)}) collective-permute-start(bf16[32,2048]{1,0:T(8,128)(2,1)S(1)} %get-tuple-element.16), channel_id=1, source_target_pairs={{0,4},{1,3},{4,8},{5,1},{8,12},{9,5},{12,14},{13,9},{14,10},{15,13... | collective-permute-start | bytes 393224 | tf_op jit(solution)/shard_map/ppermute | solution.py:194
  77.3 5.0 %collective-permute-start.9 = (bf16[32,2048]{1,0:T(8,128)(2,1)S(1)}, bf16[32,2048]{1,0:T(8,128)(2,1)S(1)}, u32[]{:S(2)}, u32[]{:S(2)}) collective-permute-start(bf16[32,2048]{1,0:T(8,128)(2,1)S(1)} %get-tuple-element.15), channel_id=1, source_target_pairs={{0,4},{1,3},{4,8},{5,1},{8,12},{9,5},{12,14},{13,9},{14,10},{15,13... | collective-permute-start | bytes 393224 | tf_op jit(solution)/shard_map/ppermute | solution.py:194
  79.9 2.4 %collective-permute-start.13 = (bf16[32,2048]{1,0:T(8,128)(2,1)S(1)}, bf16[32,2048]{1,0:T(8,128)(2,1)S(1)}, u32[]{:S(2)}, u32[]{:S(2)}) collective-permute-start(bf16[32,2048]{1,0:T(8,128)(2,1)S(1)} %collective-permute-done.12), channel_id=1, source_target_pairs={{0,1},{1,0},{2,3},{3,2},{4,5},{5,4},{6,7},{7,6},{8,9},{9,8},{10,11... | collective-permute-start | bytes 393224 | tf_op jit(solution)/shard_map/ppermute | solution.py:197
  82.6 1.4 %collective-permute-start.18 = (bf16[32,2048]{1,0:T(8,128)(2,1)S(1)}, bf16[32,2048]{1,0:T(8,128)(2,1)S(1)}, u32[]{:S(2)}, u32[]{:S(2)}) collective-permute-start(bf16[32,2048]{1,0:T(8,128)(2,1)S(1)} %fusion.8.refs_7_), channel_id=1, source_target_pairs={{0,1},{1,0},{2,3},{3,2},{4,5},{5,4},{6,7},{7,6},{8,9},{9,8},{10,11... | collective-permute-start | bytes 393224 | tf_op jit(solution)/shard_map/ppermute | solution.py:197
  82.7 5.1 %collective-permute-start.14 = (bf16[32,2048]{1,0:T(8,128)(2,1)S(1)}, bf16[32,2048]{1,0:T(8,128)(2,1)S(1)}, u32[]{:S(2)}, u32[]{:S(2)}) collective-permute-start(bf16[32,2048]{1,0:T(8,128)(2,1)S(1)} %fusion.8.refs_7_), channel_id=1, source_target_pairs={{0,2},{1,5},{4,0},{5,9},{8,4},{9,13},{12,8},{13,15},{14,12},{15,11... | collective-permute-start | bytes 393224 | tf_op jit(solution)/shard_map/ppermute | solution.py:194
  84.0 5.2 %collective-permute-start.19 = (bf16[32,2048]{1,0:T(8,128)(2,1)S(1)}, bf16[32,2048]{1,0:T(8,128)(2,1)S(1)}, u32[]{:S(2)}, u32[]{:S(2)}) collective-permute-start(bf16[32,2048]{1,0:T(8,128)(2,1)S(1)} %collective-permute-done.18), channel_id=1, source_target_pairs={{0,2},{1,5},{4,0},{5,9},{8,4},{9,13},{12,8},{13,15},{14,12},{15,11... | collective-permute-start | bytes 393224 | tf_op jit(solution)/shard_map/ppermute | solution.py:194
  87.9 5.0 %collective-permute-start.15 = (bf16[32,2048]{1,0:T(8,128)(2,1)S(1)}, bf16[32,2048]{1,0:T(8,128)(2,1)S(1)}, u32[]{:S(2)}, u32[]{:S(2)}) collective-permute-start(bf16[32,2048]{1,0:T(8,128)(2,1)S(1)} %collective-permute-done.14.refs_5_), channel_id=1, source_target_pairs={{0,2},{1,5},{4,0},{5,9},{8,4},{9,13},{12,8},{13,15},{14,12},{15,11... | collective-permute-start | bytes 393224 | tf_op jit(solution)/shard_map/ppermute | solution.py:194
  89.3 5.0 %collective-permute-start.20 = (bf16[32,2048]{1,0:T(8,128)(2,1)S(1)}, bf16[32,2048]{1,0:T(8,128)(2,1)S(1)}, u32[]{:S(2)}, u32[]{:S(2)}) collective-permute-start(bf16[32,2048]{1,0:T(8,128)(2,1)S(1)} %collective-permute-done.19.refs_6_), channel_id=1, source_target_pairs={{0,2},{1,5},{4,0},{5,9},{8,4},{9,13},{12,8},{13,15},{14,12},{15,11... | collective-permute-start | bytes 393224 | tf_op jit(solution)/shard_map/ppermute | solution.py:194
  92.8 5.0 %collective-permute-start.16 = (bf16[32,2048]{1,0:T(8,128)(2,1)S(1)}, bf16[32,2048]{1,0:T(8,128)(2,1)S(1)}, u32[]{:S(2)}, u32[]{:S(2)}) collective-permute-start(bf16[32,2048]{1,0:T(8,128)(2,1)S(1)} %collective-permute-done.15.refs_3_), channel_id=1, source_target_pairs={{0,2},{1,5},{4,0},{5,9},{8,4},{9,13},{12,8},{13,15},{14,12},{15,11... | collective-permute-start | bytes 393224 | tf_op jit(solution)/shard_map/ppermute | solution.py:194
  94.2 5.0 %collective-permute-start.21 = (bf16[32,2048]{1,0:T(8,128)(2,1)S(1)}, bf16[32,2048]{1,0:T(8,128)(2,1)S(1)}, u32[]{:S(2)}, u32[]{:S(2)}) collective-permute-start(bf16[32,2048]{1,0:T(8,128)(2,1)S(1)} %collective-permute-done.20.refs_4_), channel_id=1, source_target_pairs={{0,2},{1,5},{4,0},{5,9},{8,4},{9,13},{12,8},{13,15},{14,12},{15,11... | collective-permute-start | bytes 393224 | tf_op jit(solution)/shard_map/ppermute | solution.py:194
  97.8 5.0 %collective-permute-start.17 = (bf16[32,2048]{1,0:T(8,128)(2,1)S(1)}, bf16[32,2048]{1,0:T(8,128)(2,1)S(1)}, u32[]{:S(2)}, u32[]{:S(2)}) collective-permute-start(bf16[32,2048]{1,0:T(8,128)(2,1)S(1)} %collective-permute-done.16.refs_1_), channel_id=1, source_target_pairs={{0,2},{1,5},{4,0},{5,9},{8,4},{9,13},{12,8},{13,15},{14,12},{15,11... | collective-permute-start | bytes 393224 | tf_op jit(solution)/shard_map/ppermute | solution.py:194
  114.3 5.0 %collective-permute-start.25 = (bf16[32,2048]{1,0:T(8,128)(2,1)S(1)}, bf16[32,2048]{1,0:T(8,128)(2,1)S(1)}, u32[]{:S(2)}, u32[]{:S(2)}) collective-permute-start(bf16[32,2048]{1,0:T(8,128)(2,1)S(1)} %get-tuple-element.7), channel_id=1, source_target_pairs={{0,4},{1,3},{4,8},{5,1},{8,12},{9,5},{12,14},{13,9},{14,10},{15,13... | collective-permute-start | bytes 393224 | tf_op jit(solution)/shard_map/ppermute | solution.py:194
  116.4 5.0 %collective-permute-start.29 = (bf16[32,2048]{1,0:T(8,128)(2,1)S(1)}, bf16[32,2048]{1,0:T(8,128)(2,1)S(1)}, u32[]{:S(2)}, u32[]{:S(2)}) collective-permute-start(bf16[32,2048]{1,0:T(8,128)(2,1)S(1)} %slice.166), channel_id=1, source_target_pairs={{0,4},{1,3},{4,8},{5,1},{8,12},{9,5},{12,14},{13,9},{14,10},{15,13... | collective-permute-start | bytes 393224 | tf_op jit(solution)/shard_map/ppermute | solution.py:194
  119.4 5.0 %collective-permute-start.26 = (bf16[32,2048]{1,0:T(8,128)(2,1)S(1)}, bf16[32,2048]{1,0:T(8,128)(2,1)S(1)}, u32[]{:S(2)}, u32[]{:S(2)}) collective-permute-start(bf16[32,2048]{1,0:T(8,128)(2,1)S(1)} %add_convert_fusion.4), channel_id=1, source_target_pairs={{0,4},{1,3},{4,8},{5,1},{8,12},{9,5},{12,14},{13,9},{14,10},{15,13... | collective-permute-start | bytes 393224 | tf_op jit(solution)/shard_map/ppermute | solution.py:194
  124.5 5.0 %collective-permute-start.27 = (bf16[32,2048]{1,0:T(8,128)(2,1)S(1)}, bf16[32,2048]{1,0:T(8,128)(2,1)S(1)}, u32[]{:S(2)}, u32[]{:S(2)}) collective-permute-start(bf16[32,2048]{1,0:T(8,128)(2,1)S(1)} %get-tuple-element.13), channel_id=1, source_target_pairs={{0,4},{1,3},{4,8},{5,1},{8,12},{9,5},{12,14},{13,9},{14,10},{15,13... | collective-permute-start | bytes 393224 | tf_op jit(solution)/shard_map/ppermute | solution.py:194
  126.5 5.0 %collective-permute-start.30 = (bf16[32,2048]{1,0:T(8,128)(2,1)S(1)}, bf16[32,2048]{1,0:T(8,128)(2,1)S(1)}, u32[]{:S(2)}, u32[]{:S(2)}) collective-permute-start(bf16[32,2048]{1,0:T(8,128)(2,1)S(1)} %get-tuple-element.14), channel_id=1, source_target_pairs={{0,4},{1,3},{4,8},{5,1},{8,12},{9,5},{12,14},{13,9},{14,10},{15,13... | collective-permute-start | bytes 393224 | tf_op jit(solution)/shard_map/ppermute | solution.py:194
  131.6 5.0 %collective-permute-start.31 = (bf16[32,2048]{1,0:T(8,128)(2,1)S(1)}, bf16[32,2048]{1,0:T(8,128)(2,1)S(1)}, u32[]{:S(2)}, u32[]{:S(2)}) collective-permute-start(bf16[32,2048]{1,0:T(8,128)(2,1)S(1)} %get-tuple-element.12), channel_id=1, source_target_pairs={{0,4},{1,3},{4,8},{5,1},{8,12},{9,5},{12,14},{13,9},{14,10},{15,13... | collective-permute-start | bytes 393224 | tf_op jit(solution)/shard_map/ppermute | solution.py:194
  133.0 5.0 %collective-permute-start.28 = (bf16[32,2048]{1,0:T(8,128)(2,1)S(1)}, bf16[32,2048]{1,0:T(8,128)(2,1)S(1)}, u32[]{:S(2)}, u32[]{:S(2)}) collective-permute-start(bf16[32,2048]{1,0:T(8,128)(2,1)S(1)} %get-tuple-element.11), channel_id=1, source_target_pairs={{0,4},{1,3},{4,8},{5,1},{8,12},{9,5},{12,14},{13,9},{14,10},{15,13... | collective-permute-start | bytes 393224 | tf_op jit(solution)/shard_map/ppermute | solution.py:194
  136.6 1.4 %collective-permute-start.32 = (bf16[32,2048]{1,0:T(8,128)(2,1)S(1)}, bf16[32,2048]{1,0:T(8,128)(2,1)S(1)}, u32[]{:S(2)}, u32[]{:S(2)}) collective-permute-start(bf16[32,2048]{1,0:T(8,128)(2,1)S(1)} %collective-permute-done.31), channel_id=1, source_target_pairs={{0,1},{1,0},{2,3},{3,2},{4,5},{5,4},{6,7},{7,6},{8,9},{9,8},{10,11... | collective-permute-start | bytes 393224 | tf_op jit(solution)/shard_map/ppermute | solution.py:197

commit v3 on v0

v3 whole, which is shorter than its diff:
```python
import functools
import math

import jax
import jax.numpy as jnp
from jax import lax
from jax.experimental import pallas as pl
from jax.experimental.pallas import tpu as pltpu
from jax.sharding import PartitionSpec as P

TOPK = 8
BF16 = jnp.bfloat16
F32 = jnp.float32


gate_scale = 1.0 / 1024.0


def rms_scale(features, norm_gain):
    mean_square = jnp.mean(features * features, axis=-1, keepdims=True)
    return features * lax.rsqrt(mean_square + 1e-06) * norm_gain


def ring_plan(devices):
    chips = devices // 2
    order = list(range(0, chips, 2)) + list(range(chips - 1, 0, -2))
    swap = [(device, device ^ 1) for device in range(devices)]

    def toward(step):
        pairs = []
        for place in range(chips):
            for core in range(2):
                target = order[(place + step * (1 - 2 * core)) % chips]
                pairs.append((2 * order[place] + core, 2 * target + core))
        return pairs

    return order, toward, swap


VMEM = pl.BlockSpec(memory_space=pltpu.VMEM)
SMEM = pl.BlockSpec(memory_space=pltpu.SMEM)


def ring_view(chips):
    me = lax.axis_index("rows")
    chip, core = lax.div(me, 2), lax.rem(me, 2)
    half = lax.div(chip, 2)
    place = jnp.where(lax.rem(chip, 2) == 0, half, chips - 1 - half)

    def chip_at(offset):
        there = lax.rem(place + (1 - 2 * core) * offset + chips, chips)
        return jnp.where(there < chips // 2, 2 * there, 2 * (chips - 1 - there) + 1)

    return chip, core, chip_at


def attend_kernel(
    chips,
    hops,
    chip_experts,
    lengths_ref,
    q_ref,
    k_ref,
    v_ref,
    ids_ref,
    numer_ref,
    far_ref,
    mine_ref,
    give_ref,
    own_ref,
    q_rows,
    out_rows,
    tokens,
):
    step, steps = pl.program_id(0), pl.num_programs(0)
    block, kv_count, cache_len, head_size = k_ref.shape
    rows, feats = q_ref.shape
    heads = feats // head_size
    group = heads // kv_count

    @pl.when(step == 0)
    def _():
        for head in range(heads):
            q_rows[pl.ds(head, rows, stride=heads), :] = q_ref[
                :, head * head_size : (head + 1) * head_size
            ].astype(F32)

    head_of = lax.broadcasted_iota(jnp.int32, (heads, cache_len), 0) // group
    slot = lax.broadcasted_iota(jnp.int32, (heads, cache_len), 1)
    for i in range(block):
        row = step * block + i
        span = pl.ds(pl.multiple_of(row * heads, heads), heads)
        keys = k_ref[i].reshape(kv_count * cache_len, head_size)
        scores = lax.dot_general(
            q_rows[span, :].astype(BF16),
            keys,
            (((1,), (1,)), ((), ())),
            preferred_element_type=F32,
        )
        picked = scores[:, :cache_len]
        for kv in range(1, kv_count):
            picked = jnp.where(
                head_of == kv, scores[:, kv * cache_len : (kv + 1) * cache_len], picked
            )
        picked = picked * (1.0 / math.sqrt(head_size))
        picked = jnp.where(slot < lengths_ref[row], picked, -1e30)
        weights = jnp.exp(picked - jnp.max(picked, axis=1, keepdims=True))
        shares = weights / jnp.sum(weights, axis=1, keepdims=True)
        spread = jnp.concatenate(
            [jnp.where(head_of == kv, shares, 0.0) for kv in range(kv_count)], axis=1
        ).astype(BF16)
        values = v_ref[i].reshape(kv_count * cache_len, head_size)
        out_rows[span, :] = jnp.dot(spread, values, preferred_element_type=F32)

    @pl.when(step == steps - 1)
    def _():
        chip_heads = heads // chips
        chip_feats = chip_heads * head_size
        for head in range(heads):
            start = (head % chip_heads) * head_size
            tokens[head // chip_heads, :, start : start + head_size] = out_rows[
                pl.ds(head, rows, stride=heads), :
            ].astype(BF16)
        extra = tokens.shape[2] - chip_feats
        lane = lax.broadcasted_iota(jnp.int32, (rows, extra), 1)
        expert = jnp.where(lane < chip_experts, lane, lane - chip_experts)
        choices = ids_ref.shape[1]
        named = [jnp.broadcast_to(ids_ref[:, j : j + 1], (rows, extra)) for j in range(choices)]
        numers = [jnp.broadcast_to(numer_ref[:, j : j + 1], (rows, extra)) for j in range(choices)]
        for there in range(chips):
            found = jnp.zeros((rows, extra), jnp.int32)
            for j in range(choices):
                found += jnp.where(named[j] == expert + there * chip_experts, numers[j], 0)
            digit = jnp.where(lane < chip_experts, found >> 4, found & 15)
            digit = jnp.where(lane < 2 * chip_experts, digit, 0)
            tokens[there, :, chip_feats:] = digit.astype(F32).astype(BF16)
        chip, _, chip_at = ring_view(chips)
        far_ref[...] = tokens[chip_at(-hops)]
        own_ref[...] = tokens[chip]
        for offset in range(1, hops):
            mine_ref[offset - 1] = tokens[chip_at(-offset)]
            give_ref[offset - 1] = tokens[chip_at(offset)]


def attend(devices, chip_experts, queries, cache_keys, cache_values, lengths, ids, numer):
    chips, hops = devices // 2, devices // 4
    rows, feats = queries.shape
    kv_count, cache_len, head_size = cache_keys.shape[1:]
    heads = feats // head_size
    extra = -(-2 * chip_experts // 128) * 128
    wide = feats // chips + extra
    block = 8
    cache = pl.BlockSpec((block, kv_count, cache_len, head_size), lambda t: (t, 0, 0, 0))
    one = jax.ShapeDtypeStruct((rows, wide), BF16)
    several = jax.ShapeDtypeStruct((hops - 1, rows, wide), BF16)
    return pl.pallas_call(
        functools.partial(attend_kernel, chips, hops, chip_experts),
        out_shape=(one, several, several, one),
        grid=(rows // block,),
        in_specs=[SMEM, VMEM, cache, cache, VMEM, VMEM],
        out_specs=(VMEM,) * 4,
        scratch_shapes=[
            pltpu.VMEM((rows * heads, head_size), F32),
            pltpu.VMEM((rows * heads, head_size), F32),
            pltpu.VMEM((chips, rows, wide), BF16),
        ],
        compiler_params=pltpu.CompilerParams(vmem_limit_bytes=24 * 1024 * 1024),
        cost_estimate=pl.CostEstimate(
            flops=4 * rows * heads * cache_len * head_size,
            bytes_accessed=4 * rows * kv_count * cache_len * head_size,
            transcendentals=rows * heads * cache_len,
        ),
    )(lengths, queries, cache_keys, cache_values, ids, numer)


def project_kernel(pieces, *refs):
    piece_refs, own_ref, other_ref = refs[:pieces], refs[pieces], refs[pieces + 1]
    out_refs, x_ref = refs[pieces + 2 : -1], refs[-1]
    feats, width = own_ref.shape
    start = 0
    for piece in piece_refs:
        x_ref[start : start + piece.shape[0], :] = piece[:, : 2 * feats]
        start += piece.shape[0]

    def both(first, second):
        tile = 512
        for column in range(0, width, tile):
            done = jnp.dot(
                x_ref[:, :feats], first[:, column : column + tile], preferred_element_type=F32
            ) + jnp.dot(
                x_ref[:, feats:], second[:, column : column + tile], preferred_element_type=F32
            )
            start = 0
            for out in out_refs:
                out[:, column : column + tile] = done[start : start + out.shape[0]].astype(
                    out.dtype
                )
                start += out.shape[0]

    core = lax.rem(lax.axis_index("rows"), 2)

    @pl.when(core == 0)
    def _():
        both(own_ref, other_ref)

    @pl.when(core == 1)
    def _():
        both(other_ref, own_ref)


def project(pieces, kinds, own, other):
    feats, width = own.shape
    rows = sum(piece.shape[0] for piece in pieces)
    return pl.pallas_call(
        functools.partial(project_kernel, len(pieces)),
        out_shape=tuple(
            jax.ShapeDtypeStruct((rows // len(kinds), width), kind) for kind in kinds
        ),
        in_specs=[VMEM] * (len(pieces) + 2),
        out_specs=(VMEM,) * len(kinds),
        scratch_shapes=[pltpu.VMEM((rows, 2 * feats), BF16)],
        compiler_params=pltpu.CompilerParams(vmem_limit_bytes=32 * 1024 * 1024),
        cost_estimate=pl.CostEstimate(
            flops=4 * rows * feats * width, bytes_accessed=4 * feats * width, transcendentals=0
        ),
    )(*pieces, own, other)


def expert_kernel(tiles, hops, local, local_experts, *refs):
    pieces = 2 * hops
    piece_refs, refs = refs[:pieces], refs[pieces:]
    digit_refs, refs = refs[: hops + 1], refs[hops + 1 :]
    own_refs, other_refs, refs = refs[:3], refs[3:6], refs[6:]
    out_refs, (x_ref, gates_ref, inner_ref) = refs[:pieces], refs[pieces:]
    step = pl.program_id(0)
    tile = own_refs[0].shape[2]

    @pl.when(step == 0)
    def _():
        start = 0
        for piece in piece_refs:
            x_ref[start : start + piece.shape[0], :] = piece[...]
            start += piece.shape[0]
        core = lax.rem(lax.axis_index("rows"), 2)
        chip_experts = 2 * local_experts
        start = 0
        for digits in digit_refs:
            feats = digits.shape[1] - 128 * (-(-2 * chip_experts // 128))
            taken = digits[:, feats:].astype(F32)

            def gate(k):
                high, low = taken[:, k : k + 1], taken[:, chip_experts + k : chip_experts + k + 1]
                return (high * 16.0 + low) * gate_scale

            first, second = gate(local), gate(local_experts + local)
            size = digits.shape[0]
            gates_ref[0, start : start + size, :] = jnp.where(core == 0, first, second)
            gates_ref[1, start : start + size, :] = jnp.where(core == 0, second, first)
            start += size

    def raise_up(w_gate, w_up, which):
        gate_proj = jnp.dot(x_ref[...], w_gate[0], preferred_element_type=F32)
        raised = jnp.dot(x_ref[...], w_up[0], preferred_element_type=F32)
        inner = jax.nn.silu(gate_proj) * raised * gates_ref[which]
        span = pl.ds(pl.multiple_of(step * tile, tile), tile)
        inner_ref[:, span] = inner.astype(BF16)

    @pl.when(step < tiles)
    def _():
        raise_up(own_refs[0], own_refs[1], 0)

    @pl.when((step >= tiles) & (step < 2 * tiles))
    def _():
        raise_up(other_refs[0], other_refs[1], 1)

    @pl.when(step >= 2 * tiles)
    def _():
        depth, wide = own_refs[2].shape[1:]
        done = jnp.dot(
            inner_ref[:, :depth], own_refs[2][0], preferred_element_type=F32
        ) + jnp.dot(inner_ref[:, depth:], other_refs[2][0], preferred_element_type=F32)
        span = pl.ds(pl.multiple_of((step - 2 * tiles) * wide, wide), wide)
        start = 0
        for out in out_refs:
            out[:, span] = done[start : start + out.shape[0]].astype(out.dtype)
            start += out.shape[0]


def experts(pieces, kinds, digits, own, other, local):
    local_experts, width, hidden_units = own[0].shape
    rows = sum(piece.shape[0] for piece in pieces)
    tile, wide = 256, 512
    tiles, columns = hidden_units // tile, width // wide

    def specs(turn):
        def place(t):
            return jnp.clip(t - turn * tiles, 0, tiles - 1)

        up = pl.BlockSpec((1, width, tile), lambda t: (local, 0, place(t)))
        down = pl.BlockSpec(
            (1, hidden_units, wide), lambda t: (local, 0, jnp.maximum(t - 2 * tiles, 0))
        )
        return [up, up, down]

    return pl.pallas_call(
        functools.partial(expert_kernel, tiles, len(pieces) // 2, local, local_experts),
        out_shape=tuple(
            jax.ShapeDtypeStruct((piece.shape[0], width), kind)
            for piece, kind in zip(pieces, kinds)
        ),
        grid=(2 * tiles + columns,),
        in_specs=[VMEM] * (len(pieces) + len(digits)) + specs(0) + specs(1),
        out_specs=(VMEM,) * len(pieces),
        scratch_shapes=[
            pltpu.VMEM((rows, width), BF16),
            pltpu.VMEM((2, rows, 1), F32),
            pltpu.VMEM((rows, 2 * hidden_units), BF16),
        ],
        compiler_params=pltpu.CompilerParams(vmem_limit_bytes=48 * 1024 * 1024),
        cost_estimate=pl.CostEstimate(
            flops=12 * rows * hidden_units * width,
            bytes_accessed=12 * hidden_units * width,
            transcendentals=2 * rows * hidden_units,
        ),
    )(*pieces, *digits, *own, *other)


def on_device(
    queries,
    cache_keys,
    cache_values,
    lengths,
    hidden,
    out_weight,
    norm_gain,
    w_gate,
    w_up,
    w_down,
    expert_ids,
    gate_numer,
):
    devices = lax.axis_size("rows")
    hops = devices // 4
    local_experts = w_gate.shape[0]
    order, toward, swap = ring_plan(devices)

    def pass_on(array, step):
        return lax.ppermute(array, "rows", toward(step))

    def swapped(array):
        return lax.ppermute(array, "rows", swap)

    weight_other = swapped(out_weight)
    own_experts = (w_gate, w_up, w_down)
    other_experts = tuple(swapped(w) for w in own_experts)

    far, mine, give, here = attend(
        devices,
        2 * local_experts,
        queries,
        cache_keys,
        cache_values,
        lengths,
        expert_ids,
        gate_numer,
    )
    got = swapped(give)
    arrived = {0: here, hops: pass_on(far, -hops)}
    for offset in range(hops - 1, 0, -1):
        message = jnp.concatenate([mine[offset - 1], got[offset - 1]], axis=0)
        arrived[offset] = pass_on(message, -offset)

    kinds = [BF16, F32, BF16] + [F32] * (2 * hops - 3)
    partial = project([arrived[hops], arrived[hops - 1]], kinds[:3], out_weight, weight_other)
    partial += project(
        [arrived[offset] for offset in range(hops - 2, -1, -1)], kinds[3:], out_weight, weight_other
    )

    def ring_sums(partial):
        own, other = partial[0], partial[2]
        for offset in range(hops - 1, 0, -1):
            spot = 1 + 2 * (hops - 1 - offset)
            if offset < hops - 1:
                other = (pass_on(other, 1).astype(F32) + partial[spot + 1]).astype(BF16)
            own = (pass_on(own, 1).astype(F32) + partial[spot]).astype(BF16)
        other = swapped(pass_on(other, 1)).astype(F32)
        return pass_on(own, 1).astype(F32) + partial[-1] + other

    residual = (hidden.astype(F32) + ring_sums(partial)).astype(BF16)
    normed = rms_scale(residual.astype(F32), norm_gain).astype(BF16)

    own, other = normed, swapped(normed)
    pieces = [own]
    for offset in range(1, hops + 1):
        own = pass_on(own, -1)
        pieces = [own] + pieces
        if offset < hops:
            other = pass_on(other, -1)
            pieces = [own, other] + pieces[1:]

    digits = [arrived[offset] for offset in range(hops, -1, -1)]
    total = None
    for local in range(local_experts):
        plain = [F32] * (2 * hops)
        served = experts(
            pieces,
            kinds if local_experts == 1 else plain,
            digits,
            own_experts,
            other_experts,
            local,
        )
        total = served if local == 0 else [a + b for a, b in zip(total, served)]
    total = [part.astype(kind) for part, kind in zip(total, kinds)]
    return (residual.astype(F32) + ring_sums(total)).astype(BF16)


def solution(mesh):
    in_specs = (
        P(("groups", "rows"), None),
        P(("groups", "rows"), None, None, None),
        P(("groups", "rows"), None, None, None),
        P(("groups", "rows")),
        P(("groups", "rows"), None),
        P("rows", None),
        P(),
        P("rows", None, None),
        P("rows", None, None),
        P("rows", None, None),
        P(("groups", "rows"), None),
        P(("groups", "rows"), None),
    )
    out_specs = P(("groups", "rows"), None)
    return jax.shard_map(
        on_device, mesh=mesh, in_specs=in_specs, out_specs=out_specs, check_vma=False
    )
```

time: 244 us -> 113 us (0.46)
  the two profiles are of different devices: /device:TPU:13 before, /device:TPU:0 now
where the time goes in v3:
time: 113 us
  waiting for transfers between devices  49.2 us (44%)
  Pallas kernels  26.5 us (23%)
  starting transfers between devices  26.4 us (23%)
  local copies, waits for them, and re-layouts  8.91 us (8%)
  other arithmetic  1.36 us (1%)
    ppermute x25, waiting for transfers between devices, pass_on(): return lax.ppermute(array, 'rows', toward(step))  47.9 us
    ppermute x25, starting transfers between devices, pass_on(): return lax.ppermute(array, 'rows', toward(step))  24.8 us
    pallas_call x1, Pallas kernels, experts(): pl.pallas_call(functools.partial(expert_kernel, tiles, len(pieces) // 2,...  13.3 us
    pallas_call x1, Pallas kernels, attend(): pl.pallas_call(functools.partial(attend_kernel, chips, hops, chip_experts...  12.3 us
    unnamed x24, local copies, waits for them, and re-layouts  8.89 us
  transfers between devices with their start and end apart: 33, of which 23 were waited for; matrix products, arithmetic and copies ran while one was open for 2% of the time, Pallas kernels for 12%

profile of v3, /device:TPU:0, one launch (start us, length us, event | category | flops | bytes accessed | tf_op | source)
XLA Modules:
  0.0 112.5 jit_solution(7344620991448943410)
XLA Ops:
  0.0 0.5 collective-permute-start.3
  0.5 0.8 copy.13.ids_ref
  1.2 0.8 copy.14.numer_ref
  2.0 1.6 %copy-done.1 = bf16[32,2,128,128]{3,2,1,0:T(8,128)(2,1)S(1)} copy-done((bf16[32,2,128,128]{3,2,1,0:T(8,128)(2,1)S(1)}, bf16[32,2,128,128]{3,2,1,0:T(8,128)(2,1)}, u32[]{:S(2)}) %copy-start.1) | copy-done | bytes 2097176
  3.6 1.6 %copy-done.2 = bf16[32,2,128,128]{3,2,1,0:T(8,128)(2,1)S(1)} copy-done((bf16[32,2,128,128]{3,2,1,0:T(8,128)(2,1)S(1)}, bf16[32,2,128,128]{3,2,1,0:T(8,128)(2,1)}, u32[]{:S(2)}) %copy-start.2) | copy-done | bytes 2097176
  5.2 0.9 copy-done.3
  6.1 0.7 copy-done.4
  6.8 12.3 %shard_map.118 = (bf16[32,640]{1,0:T(8,128)(2,1)S(1)}, bf16[3,32,640]{2,1,0:T(8,128)(2,1)S(1)}, bf16[3,32,640]{2,1,0:T(8,128)(2,1)S(1)}, bf16[32,640]{1,0:T(8,128)(2,1)S(1)}) custom-call(s32[32]{0:T(128)S(1)} %copy-done.4, bf16[32,4096]{1,0:T(8,128)(2,1)S(1)} %copy-done.3, bf16[32,2,128,128]{3,2,1,0:T(8,128)(2,1)S(1)} %copy-done.1, ...), custom_call_target="tpu_custom_call" | custom-call | flops 67108864 | bytes 4194304 | tf_op jit(solution)/shard_map/pallas_call | solution.py:156
  19.0 5.7 %collective-permute-start = (bf16[32,640]{1,0:T(8,128)(2,1)S(1)}, bf16[32,640]{1,0:T(8,128)(2,1)S(1)}, u32[]{:S(2)}, u32[]{:S(2)}) collective-permute-start(bf16[32,640]{1,0:T(8,128)(2,1)S(1)} %get-tuple-element.25), channel_id=1, source_target_pairs={{0,14},{1,15},{4,10},{5,11},{8,6},{9,7},{12,2},{13,3},{14,0},{15,1... | collective-permute-start | bytes 122888 | tf_op jit(solution)/shard_map/ppermute | solution.py:348
  24.7 0.2 collective-permute-start.1
  24.9 1.2 %collective-permute-done.1 = bf16[3,32,640]{2,1,0:T(8,128)(2,1)S(1)} collective-permute-done((bf16[3,32,640]{2,1,0:T(8,128)(2,1)S(1)}, bf16[3,32,640]{2,1,0:T(8,128)(2,1)S(1)}, u32[]{:S(2)}, u32[]{:S(2)}) %collective-permute-start.1) | collective-permute-done | bytes 122912 | tf_op jit(solution)/shard_map/ppermute | solution.py:351
  26.2 1.7 %collective-permute-start.6 = (bf16[64,640]{1,0:T(8,128)(2,1)S(1)}, bf16[64,640]{1,0:T(8,128)(2,1)S(1)}, u32[]{:S(2)}, u32[]{:S(2)}) collective-permute-start(bf16[64,640]{1,0:T(8,128)(2,1)S(1)} %pad_maximum_fusion.1), channel_id=1, source_target_pairs={{0,6},{1,9},{4,2},{5,13},{8,0},{9,15},{12,4},{13,11},{14,8},{15,7}... | collective-permute-start | bytes 245768 | tf_op jit(solution)/shard_map/ppermute | solution.py:348
  27.9 5.0 %collective-permute-done.2.refs_1_.refs_9_ = bf16[64,640]{1,0:T(8,128)(2,1)S(1)} collective-permute-done((bf16[64,640]{1,0:T(8,128)(2,1)S(1)}, bf16[64,640]{1,0:T(8,128)(2,1)S(1)}, u32[]{:S(2)}, u32[]{:S(2)}) %collective-permute-start.2) | collective-permute-done | bytes 81952 | tf_op jit(solution)/shard_map/ppermute | solution.py:348
  33.0 0.5 shard_map.119
  33.6 2.1 %collective-permute-start.7 = (bf16[64,640]{1,0:T(8,128)(2,1)S(1)}, bf16[64,640]{1,0:T(8,128)(2,1)S(1)}, u32[]{:S(2)}, u32[]{:S(2)}) collective-permute-start(bf16[64,640]{1,0:T(8,128)(2,1)S(1)} %pad_maximum_fusion.2), channel_id=1, source_target_pairs={{0,2},{1,5},{4,0},{5,9},{8,4},{9,13},{12,8},{13,15},{14,12},{15,11... | collective-permute-start | bytes 245768 | tf_op jit(solution)/shard_map/ppermute | solution.py:348
  35.6 0.3 collective-permute-start.22
  35.9 0.2 collective-permute-start.23
  36.1 0.3 collective-permute-start.24
  36.5 2.5 %collective-permute-done.7.refs_1_.refs_11_ = bf16[64,640]{1,0:T(8,128)(2,1)S(1)} collective-permute-done((bf16[64,640]{1,0:T(8,128)(2,1)S(1)}, bf16[64,640]{1,0:T(8,128)(2,1)S(1)}, u32[]{:S(2)}, u32[]{:S(2)}) %collective-permute-start.7) | collective-permute-done | bytes 81952 | tf_op jit(solution)/shard_map/ppermute | solution.py:348
  38.9 0.5 shard_map.120
  39.5 1.3 %collective-permute-start.5 = (bf16[32,2048]{1,0:T(8,128)(2,1)S(1)}, bf16[32,2048]{1,0:T(8,128)(2,1)S(1)}, u32[]{:S(2)}, u32[]{:S(2)}) collective-permute-start(bf16[32,2048]{1,0:T(8,128)(2,1)S(1)} %add_convert_fusion.10), channel_id=1, source_target_pairs={{0,4},{1,3},{4,8},{5,1},{8,12},{9,5},{12,14},{13,9},{14,10},{15,13... | collective-permute-start | bytes 393224 | tf_op jit(solution)/shard_map/ppermute | solution.py:348
  40.8 3.1 %collective-permute-done.10 = bf16[32,2048]{1,0:T(8,128)(2,1)S(1)} collective-permute-done((bf16[32,2048]{1,0:T(8,128)(2,1)S(1)}, bf16[32,2048]{1,0:T(8,128)(2,1)S(1)}, u32[]{:S(2)}, u32[]{:S(2)}) %collective-permute-start.10) | collective-permute-done | bytes 131104 | tf_op jit(solution)/shard_map/ppermute | solution.py:348
  44.0 1.3 %collective-permute-done.5 = bf16[32,2048]{1,0:T(8,128)(2,1)S(1)} collective-permute-done((bf16[32,2048]{1,0:T(8,128)(2,1)S(1)}, bf16[32,2048]{1,0:T(8,128)(2,1)S(1)}, u32[]{:S(2)}, u32[]{:S(2)}) %collective-permute-start.5) | collective-permute-done | bytes 131104 | tf_op jit(solution)/shard_map/ppermute | solution.py:348
  45.3 0.6 collective-permute-start.8
  45.9 3.1 %collective-permute-done.11 = bf16[32,2048]{1,0:T(8,128)(2,1)S(1)} collective-permute-done((bf16[32,2048]{1,0:T(8,128)(2,1)S(1)}, bf16[32,2048]{1,0:T(8,128)(2,1)S(1)}, u32[]{:S(2)}, u32[]{:S(2)}) %collective-permute-start.11) | collective-permute-done | bytes 131104 | tf_op jit(solution)/shard_map/ppermute | solution.py:348
  49.1 1.3 %collective-permute-done.8 = bf16[32,2048]{1,0:T(8,128)(2,1)S(1)} collective-permute-done((bf16[32,2048]{1,0:T(8,128)(2,1)S(1)}, bf16[32,2048]{1,0:T(8,128)(2,1)S(1)}, u32[]{:S(2)}, u32[]{:S(2)}) %collective-permute-start.8) | collective-permute-done | bytes 131104 | tf_op jit(solution)/shard_map/ppermute | solution.py:348
  50.4 0.6 collective-permute-start.9
  51.0 3.1 %collective-permute-done.12 = bf16[32,2048]{1,0:T(8,128)(2,1)S(1)} collective-permute-done((bf16[32,2048]{1,0:T(8,128)(2,1)S(1)}, bf16[32,2048]{1,0:T(8,128)(2,1)S(1)}, u32[]{:S(2)}, u32[]{:S(2)}) %collective-permute-start.12) | collective-permute-done | bytes 131104 | tf_op jit(solution)/shard_map/ppermute | solution.py:348
  54.0 1.4 %collective-permute-done.9 = bf16[32,2048]{1,0:T(8,128)(2,1)S(1)} collective-permute-done((bf16[32,2048]{1,0:T(8,128)(2,1)S(1)}, bf16[32,2048]{1,0:T(8,128)(2,1)S(1)}, u32[]{:S(2)}, u32[]{:S(2)}) %collective-permute-start.9) | collective-permute-done | bytes 131104 | tf_op jit(solution)/shard_map/ppermute | solution.py:348
  55.4 0.2 fusion
  55.6 0.1 fusion.2.refs_7_
  55.7 0.2 collective-permute-start.18
  55.9 1.2 %collective-permute-start.14 = (bf16[32,2048]{1,0:T(8,128)(2,1)S(1)}, bf16[32,2048]{1,0:T(8,128)(2,1)S(1)}, u32[]{:S(2)}, u32[]{:S(2)}) collective-permute-start(bf16[32,2048]{1,0:T(8,128)(2,1)S(1)} %fusion.2.refs_7_), channel_id=1, source_target_pairs={{0,2},{1,5},{4,0},{5,9},{8,4},{9,13},{12,8},{13,15},{14,12},{15,11... | collective-permute-start | bytes 393224 | tf_op jit(solution)/shard_map/ppermute | solution.py:348
  57.1 1.3 %collective-permute-start.19 = (bf16[32,2048]{1,0:T(8,128)(2,1)S(1)}, bf16[32,2048]{1,0:T(8,128)(2,1)S(1)}, u32[]{:S(2)}, u32[]{:S(2)}) collective-permute-start(bf16[32,2048]{1,0:T(8,128)(2,1)S(1)} %collective-permute-done.18), channel_id=1, source_target_pairs={{0,2},{1,5},{4,0},{5,9},{8,4},{9,13},{12,8},{13,15},{14,12},{15,11... | collective-permute-start | bytes 393224 | tf_op jit(solution)/shard_map/ppermute | solution.py:348
  58.4 2.5 %collective-permute-done.14.refs_5_ = bf16[32,2048]{1,0:T(8,128)(2,1)S(1)} collective-permute-done((bf16[32,2048]{1,0:T(8,128)(2,1)S(1)}, bf16[32,2048]{1,0:T(8,128)(2,1)S(1)}, u32[]{:S(2)}, u32[]{:S(2)}) %collective-permute-start.14) | collective-permute-done | bytes 131104 | tf_op jit(solution)/shard_map/ppermute | solution.py:348
  60.9 1.2 %collective-permute-start.15 = (bf16[32,2048]{1,0:T(8,128)(2,1)S(1)}, bf16[32,2048]{1,0:T(8,128)(2,1)S(1)}, u32[]{:S(2)}, u32[]{:S(2)}) collective-permute-start(bf16[32,2048]{1,0:T(8,128)(2,1)S(1)} %collective-permute-done.14.refs_5_), channel_id=1, source_target_pairs={{0,2},{1,5},{4,0},{5,9},{8,4},{9,13},{12,8},{13,15},{14,12},{15,11... | collective-permute-start | bytes 393224 | tf_op jit(solution)/shard_map/ppermute | solution.py:348
  62.1 0.2 collective-permute-done.19.refs_6_
  62.3 1.2 %collective-permute-start.20 = (bf16[32,2048]{1,0:T(8,128)(2,1)S(1)}, bf16[32,2048]{1,0:T(8,128)(2,1)S(1)}, u32[]{:S(2)}, u32[]{:S(2)}) collective-permute-start(bf16[32,2048]{1,0:T(8,128)(2,1)S(1)} %collective-permute-done.19.refs_6_), channel_id=1, source_target_pairs={{0,2},{1,5},{4,0},{5,9},{8,4},{9,13},{12,8},{13,15},{14,12},{15,11... | collective-permute-start | bytes 393224 | tf_op jit(solution)/shard_map/ppermute | solution.py:348
  63.5 2.3 %collective-permute-done.15.refs_3_ = bf16[32,2048]{1,0:T(8,128)(2,1)S(1)} collective-permute-done((bf16[32,2048]{1,0:T(8,128)(2,1)S(1)}, bf16[32,2048]{1,0:T(8,128)(2,1)S(1)}, u32[]{:S(2)}, u32[]{:S(2)}) %collective-permute-start.15) | collective-permute-done | bytes 131104 | tf_op jit(solution)/shard_map/ppermute | solution.py:348
  65.8 1.2 %collective-permute-start.16 = (bf16[32,2048]{1,0:T(8,128)(2,1)S(1)}, bf16[32,2048]{1,0:T(8,128)(2,1)S(1)}, u32[]{:S(2)}, u32[]{:S(2)}) collective-permute-start(bf16[32,2048]{1,0:T(8,128)(2,1)S(1)} %collective-permute-done.15.refs_3_), channel_id=1, source_target_pairs={{0,2},{1,5},{4,0},{5,9},{8,4},{9,13},{12,8},{13,15},{14,12},{15,11... | collective-permute-start | bytes 393224 | tf_op jit(solution)/shard_map/ppermute | solution.py:348
  67.1 0.2 collective-permute-done.20.refs_4_
  67.2 1.2 %collective-permute-start.21 = (bf16[32,2048]{1,0:T(8,128)(2,1)S(1)}, bf16[32,2048]{1,0:T(8,128)(2,1)S(1)}, u32[]{:S(2)}, u32[]{:S(2)}) collective-permute-start(bf16[32,2048]{1,0:T(8,128)(2,1)S(1)} %collective-permute-done.20.refs_4_), channel_id=1, source_target_pairs={{0,2},{1,5},{4,0},{5,9},{8,4},{9,13},{12,8},{13,15},{14,12},{15,11... | collective-permute-start | bytes 393224 | tf_op jit(solution)/shard_map/ppermute | solution.py:348
  68.5 2.3 %collective-permute-done.16.refs_1_ = bf16[32,2048]{1,0:T(8,128)(2,1)S(1)} collective-permute-done((bf16[32,2048]{1,0:T(8,128)(2,1)S(1)}, bf16[32,2048]{1,0:T(8,128)(2,1)S(1)}, u32[]{:S(2)}, u32[]{:S(2)}) %collective-permute-start.16) | collective-permute-done | bytes 131104 | tf_op jit(solution)/shard_map/ppermute | solution.py:348
  70.8 1.2 %collective-permute-start.17 = (bf16[32,2048]{1,0:T(8,128)(2,1)S(1)}, bf16[32,2048]{1,0:T(8,128)(2,1)S(1)}, u32[]{:S(2)}, u32[]{:S(2)}) collective-permute-start(bf16[32,2048]{1,0:T(8,128)(2,1)S(1)} %collective-permute-done.16.refs_1_), channel_id=1, source_target_pairs={{0,2},{1,5},{4,0},{5,9},{8,4},{9,13},{12,8},{13,15},{14,12},{15,11... | collective-permute-start | bytes 393224 | tf_op jit(solution)/shard_map/ppermute | solution.py:348
  72.0 0.2 collective-permute-done.21.refs_2_
  72.2 3.6 %collective-permute-done.17.refs_0_ = bf16[32,2048]{1,0:T(8,128)(2,1)S(1)} collective-permute-done((bf16[32,2048]{1,0:T(8,128)(2,1)S(1)}, bf16[32,2048]{1,0:T(8,128)(2,1)S(1)}, u32[]{:S(2)}, u32[]{:S(2)}) %collective-permute-start.17) | collective-permute-done | bytes 131104 | tf_op jit(solution)/shard_map/ppermute | solution.py:348
  75.8 1.7 %copy-done.8 = bf16[1,2048,768]{2,1,0:T(8,128)(2,1)} copy-done((bf16[1,2048,768]{2,1,0:T(8,128)(2,1)}, bf16[1,2048,768]{2,1,0:T(8,128)(2,1)S(1)}, u32[]{:S(2)}) %copy-start.8) | copy-done | bytes 3145752
  77.5 0.9 copy-done.7
  78.3 13.3 %shard_map.121 = (bf16[32,2048]{1,0:T(8,128)(2,1)S(1)}, f32[32,2048]{1,0:T(8,128)S(1)}, bf16[32,2048]{1,0:T(8,128)(2,1)S(1)}, f32[32,2048]{1,0:T(8,128)S(1)}, f3...) custom-call(bf16[32,2048]{1,0:T(8,128)(2,1)S(1)} %collective-permute-done.17.ref, ...), custom_call_target="tpu_custom_call" | custom-call | flops 4831838208 | bytes 18874368 | tf_op jit(solution)/shard_map/pallas_call | solution.py:305
  91.6 0.5 collective-permute-start.25
  92.1 0.8 collective-permute-start.29
  92.9 3.7 %collective-permute-done.25 = bf16[32,2048]{1,0:T(8,128)(2,1)S(1)} collective-permute-done((bf16[32,2048]{1,0:T(8,128)(2,1)S(1)}, bf16[32,2048]{1,0:T(8,128)(2,1)S(1)}, u32[]{:S(2)}, u32[]{:S(2)}) %collective-permute-start.25) | collective-permute-done | bytes 131104 | tf_op jit(solution)/shard_map/ppermute | solution.py:348
  96.7 0.5 collective-permute-start.26
  97.2 0.8 collective-permute-done.29
  98.1 0.5 collective-permute-start.30
  98.6 3.1 %collective-permute-done.26 = bf16[32,2048]{1,0:T(8,128)(2,1)S(1)} collective-permute-done((bf16[32,2048]{1,0:T(8,128)(2,1)S(1)}, bf16[32,2048]{1,0:T(8,128)(2,1)S(1)}, u32[]{:S(2)}, u32[]{:S(2)}) %collective-permute-start.26) | collective-permute-done | bytes 131104 | tf_op jit(solution)/shard_map/ppermute | solution.py:348
  101.7 0.5 collective-permute-start.27
  102.3 0.8 collective-permute-done.30
  103.1 0.5 collective-permute-start.31
  103.7 3.1 %collective-permute-done.27 = bf16[32,2048]{1,0:T(8,128)(2,1)S(1)} collective-permute-done((bf16[32,2048]{1,0:T(8,128)(2,1)S(1)}, bf16[32,2048]{1,0:T(8,128)(2,1)S(1)}, u32[]{:S(2)}, u32[]{:S(2)}) %collective-permute-start.27) | collective-permute-done | bytes 131104 | tf_op jit(solution)/shard_map/ppermute | solution.py:348
  106.8 0.5 collective-permute-start.28
  107.3 0.8 collective-permute-done.31
  108.2 3.7 %collective-permute-done.28 = bf16[32,2048]{1,0:T(8,128)(2,1)S(1)} collective-permute-done((bf16[32,2048]{1,0:T(8,128)(2,1)S(1)}, bf16[32,2048]{1,0:T(8,128)(2,1)S(1)}, u32[]{:S(2)}, u32[]{:S(2)}) %collective-permute-start.28) | collective-permute-done | bytes 131104 | tf_op jit(solution)/shard_map/ppermute | solution.py:348
  111.8 0.7 fusion.3
  (49 shorter events, 0.7 us)
Async XLA Ops:
  0.0 33.0 %copy-start = (bf16[256,2048]{1,0:T(8,128)(2,1)S(1)}, bf16[256,2048]{1,0:T(8,128)(2,1)}, u32[]{:S(2)}) copy-start(bf16[256,2048]{1,0:T(8,128)(2,1)} %refs_3_.1) | copy-start | bytes 3145732
  0.0 33.0 %collective-permute-start.3 = (bf16[256,2048]{1,0:T(8,128)(2,1)}, bf16[256,2048]{1,0:T(8,128)(2,1)S(1)}, u32[]{:S(2)}, u32[]{:S(2)}) collective-permute-start(bf16[256,2048]{1,0:T(8,128)(2,1)} %refs_3_.1), channel_id=1, source_target_pairs={{0,1},{1,0},{2,3},{3,2},{4,5},{5,4},{6,7},{7,6},{8,9},{9,8},{10,11... | collective-permute-start | bytes 3145736 | tf_op jit(solution)/shard_map/ppermute | solution.py:351
  2.0 1.6 %copy-start.1 = (bf16[32,2,128,128]{3,2,1,0:T(8,128)(2,1)S(1)}, bf16[32,2,128,128]{3,2,1,0:T(8,128)(2,1)}, u32[]{:S(2)}) copy-start(bf16[32,2,128,128]{3,2,1,0:T(8,128)(2,1)} %k_ref.1) | copy-start | bytes 6291460
  3.6 1.6 %copy-start.2 = (bf16[32,2,128,128]{3,2,1,0:T(8,128)(2,1)S(1)}, bf16[32,2,128,128]{3,2,1,0:T(8,128)(2,1)}, u32[]{:S(2)}) copy-start(bf16[32,2,128,128]{3,2,1,0:T(8,128)(2,1)} %v_ref.1) | copy-start | bytes 6291460
  5.2 0.9 copy-start.3
  6.1 0.7 copy-start.4
  6.8 28.9 %copy-start.5 = (bf16[1,2048,768]{2,1,0:T(8,128)(2,1)S(1)}, bf16[1,2048,768]{2,1,0:T(8,128)(2,1)}, u32[]{:S(2)}) copy-start(bf16[1,2048,768]{2,1,0:T(8,128)(2,1)} %refs_13_.1) | copy-start | bytes 9437188
  6.8 29.2 %copy-start.6 = (bf16[1,2048,768]{2,1,0:T(8,128)(2,1)S(1)}, bf16[1,2048,768]{2,1,0:T(8,128)(2,1)}, u32[]{:S(2)}) copy-start(bf16[1,2048,768]{2,1,0:T(8,128)(2,1)} %refs_14_.1) | copy-start | bytes 9437188
  19.0 8.9 %collective-permute-start = (bf16[32,640]{1,0:T(8,128)(2,1)S(1)}, bf16[32,640]{1,0:T(8,128)(2,1)S(1)}, u32[]{:S(2)}, u32[]{:S(2)}) collective-permute-start(bf16[32,640]{1,0:T(8,128)(2,1)S(1)} %get-tuple-element.25), channel_id=1, source_target_pairs={{0,14},{1,15},{4,10},{5,11},{8,6},{9,7},{12,2},{13,3},{14,0},{15,1... | collective-permute-start | bytes 122888 | tf_op jit(solution)/shard_map/ppermute | solution.py:348
  24.7 1.3 %collective-permute-start.1 = (bf16[3,32,640]{2,1,0:T(8,128)(2,1)S(1)}, bf16[3,32,640]{2,1,0:T(8,128)(2,1)S(1)}, u32[]{:S(2)}, u32[]{:S(2)}) collective-permute-start(bf16[3,32,640]{2,1,0:T(8,128)(2,1)S(1)} %get-tuple-element.27), channel_id=1, source_target_pairs={{0,1},{1,0},{2,3},{3,2},{4,5},{5,4},{6,7},{7,6},{8,9},{9,8},{10,11... | collective-permute-start | bytes 368648 | tf_op jit(solution)/shard_map/ppermute | solution.py:351
  26.1 6.9 %collective-permute-start.2 = (bf16[64,640]{1,0:T(8,128)(2,1)S(1)}, bf16[64,640]{1,0:T(8,128)(2,1)S(1)}, u32[]{:S(2)}, u32[]{:S(2)}) collective-permute-start(bf16[64,640]{1,0:T(8,128)(2,1)S(1)} %pad_maximum_fusion), channel_id=1, source_target_pairs={{0,10},{1,13},{4,6},{5,15},{8,2},{9,11},{12,0},{13,7},{14,4},{15,3... | collective-permute-start | bytes 245768 | tf_op jit(solution)/shard_map/ppermute | solution.py:348
  26.2 29.2 %copy-start.9 = (bf16[32,2048]{1,0:T(8,128)(2,1)S(1)}, bf16[32,2048]{1,0:T(8,128)(2,1)}, u32[]{:S(2)}) copy-start(bf16[32,2048]{1,0:T(8,128)(2,1)} %param.16) | copy-start | bytes 393220
  26.2 9.9 %collective-permute-start.6 = (bf16[64,640]{1,0:T(8,128)(2,1)S(1)}, bf16[64,640]{1,0:T(8,128)(2,1)S(1)}, u32[]{:S(2)}, u32[]{:S(2)}) collective-permute-start(bf16[64,640]{1,0:T(8,128)(2,1)S(1)} %pad_maximum_fusion.1), channel_id=1, source_target_pairs={{0,6},{1,9},{4,2},{5,13},{8,0},{9,15},{12,4},{13,11},{14,8},{15,7}... | collective-permute-start | bytes 245768 | tf_op jit(solution)/shard_map/ppermute | solution.py:348
  33.5 22.1 %copy-start.10 = (f32[2048]{0:T(1024)S(1)}, f32[2048]{0:T(1024)}, u32[]{:S(2)}) copy-start(f32[2048]{0:T(1024)} %param.18) | copy-start | bytes 24580
  33.5 6.0 %collective-permute-start.4 = (bf16[32,2048]{1,0:T(8,128)(2,1)S(1)}, bf16[32,2048]{1,0:T(8,128)(2,1)S(1)}, u32[]{:S(2)}, u32[]{:S(2)}) collective-permute-start(bf16[32,2048]{1,0:T(8,128)(2,1)S(1)} %get-tuple-element.28), channel_id=1, source_target_pairs={{0,4},{1,3},{4,8},{5,1},{8,12},{9,5},{12,14},{13,9},{14,10},{15,13... | collective-permute-start | bytes 393224 | tf_op jit(solution)/shard_map/ppermute | solution.py:348
  33.6 5.4 %collective-permute-start.7 = (bf16[64,640]{1,0:T(8,128)(2,1)S(1)}, bf16[64,640]{1,0:T(8,128)(2,1)S(1)}, u32[]{:S(2)}, u32[]{:S(2)}) collective-permute-start(bf16[64,640]{1,0:T(8,128)(2,1)S(1)} %pad_maximum_fusion.2), channel_id=1, source_target_pairs={{0,2},{1,5},{4,0},{5,9},{8,4},{9,13},{12,8},{13,15},{14,12},{15,11... | collective-permute-start | bytes 245768 | tf_op jit(solution)/shard_map/ppermute | solution.py:348
  35.6 40.1 %collective-permute-start.22 = (bf16[1,2048,768]{2,1,0:T(8,128)(2,1)S(1)}, bf16[1,2048,768]{2,1,0:T(8,128)(2,1)S(1)}, u32[]{:S(2)}, u32[]{:S(2)}) collective-permute-start(bf16[1,2048,768]{2,1,0:T(8,128)(2,1)S(1)} %copy-done.5), channel_id=1, source_target_pairs={{0,1},{1,0},{2,3},{3,2},{4,5},{5,4},{6,7},{7,6},{8,9},{9,8},{10,11... | collective-permute-start | bytes 9437192 | tf_op jit(solution)/shard_map/ppermute | solution.py:351
  35.9 39.8 %collective-permute-start.23 = (bf16[1,2048,768]{2,1,0:T(8,128)(2,1)S(1)}, bf16[1,2048,768]{2,1,0:T(8,128)(2,1)S(1)}, u32[]{:S(2)}, u32[]{:S(2)}) collective-permute-start(bf16[1,2048,768]{2,1,0:T(8,128)(2,1)S(1)} %copy-done.6), channel_id=1, source_target_pairs={{0,1},{1,0},{2,3},{3,2},{4,5},{5,4},{6,7},{7,6},{8,9},{9,8},{10,11... | collective-permute-start | bytes 9437192 | tf_op jit(solution)/shard_map/ppermute | solution.py:351
  36.1 41.3 %collective-permute-start.24 = (bf16[1,768,2048]{2,1,0:T(8,128)(2,1)}, bf16[1,768,2048]{2,1,0:T(8,128)(2,1)}, u32[]{:S(2)}, u32[]{:S(2)}) collective-permute-start(bf16[1,768,2048]{2,1,0:T(8,128)(2,1)} %refs_15_.1), channel_id=1, source_target_pairs={{0,1},{1,0},{2,3},{3,2},{4,5},{5,4},{6,7},{7,6},{8,9},{9,8},{10,11... | collective-permute-start | bytes 9437192 | tf_op jit(solution)/shard_map/ppermute | solution.py:351
  38.9 5.0 %collective-permute-start.10 = (bf16[32,2048]{1,0:T(8,128)(2,1)S(1)}, bf16[32,2048]{1,0:T(8,128)(2,1)S(1)}, u32[]{:S(2)}, u32[]{:S(2)}) collective-permute-start(bf16[32,2048]{1,0:T(8,128)(2,1)S(1)} %get-tuple-element.34), channel_id=1, source_target_pairs={{0,4},{1,3},{4,8},{5,1},{8,12},{9,5},{12,14},{13,9},{14,10},{15,13... | collective-permute-start | bytes 393224 | tf_op jit(solution)/shard_map/ppermute | solution.py:348
  39.5 5.8 %collective-permute-start.5 = (bf16[32,2048]{1,0:T(8,128)(2,1)S(1)}, bf16[32,2048]{1,0:T(8,128)(2,1)S(1)}, u32[]{:S(2)}, u32[]{:S(2)}) collective-permute-start(bf16[32,2048]{1,0:T(8,128)(2,1)S(1)} %add_convert_fusion.10), channel_id=1, source_target_pairs={{0,4},{1,3},{4,8},{5,1},{8,12},{9,5},{12,14},{13,9},{14,10},{15,13... | collective-permute-start | bytes 393224 | tf_op jit(solution)/shard_map/ppermute | solution.py:348
  43.9 5.0 %collective-permute-start.11 = (bf16[32,2048]{1,0:T(8,128)(2,1)S(1)}, bf16[32,2048]{1,0:T(8,128)(2,1)S(1)}, u32[]{:S(2)}, u32[]{:S(2)}) collective-permute-start(bf16[32,2048]{1,0:T(8,128)(2,1)S(1)} %add_convert_fusion.7), channel_id=1, source_target_pairs={{0,4},{1,3},{4,8},{5,1},{8,12},{9,5},{12,14},{13,9},{14,10},{15,13... | collective-permute-start | bytes 393224 | tf_op jit(solution)/shard_map/ppermute | solution.py:348
  45.3 5.0 %collective-permute-start.8 = (bf16[32,2048]{1,0:T(8,128)(2,1)S(1)}, bf16[32,2048]{1,0:T(8,128)(2,1)S(1)}, u32[]{:S(2)}, u32[]{:S(2)}) collective-permute-start(bf16[32,2048]{1,0:T(8,128)(2,1)S(1)} %add_convert_fusion.9), channel_id=1, source_target_pairs={{0,4},{1,3},{4,8},{5,1},{8,12},{9,5},{12,14},{13,9},{14,10},{15,13... | collective-permute-start | bytes 393224 | tf_op jit(solution)/shard_map/ppermute | solution.py:348
  49.0 5.0 %collective-permute-start.12 = (bf16[32,2048]{1,0:T(8,128)(2,1)S(1)}, bf16[32,2048]{1,0:T(8,128)(2,1)S(1)}, u32[]{:S(2)}, u32[]{:S(2)}) collective-permute-start(bf16[32,2048]{1,0:T(8,128)(2,1)S(1)} %add_convert_fusion.6), channel_id=1, source_target_pairs={{0,4},{1,3},{4,8},{5,1},{8,12},{9,5},{12,14},{13,9},{14,10},{15,13... | collective-permute-start | bytes 393224 | tf_op jit(solution)/shard_map/ppermute | solution.py:348
  50.4 5.0 %collective-permute-start.9 = (bf16[32,2048]{1,0:T(8,128)(2,1)S(1)}, bf16[32,2048]{1,0:T(8,128)(2,1)S(1)}, u32[]{:S(2)}, u32[]{:S(2)}) collective-permute-start(bf16[32,2048]{1,0:T(8,128)(2,1)S(1)} %add_convert_fusion.8), channel_id=1, source_target_pairs={{0,4},{1,3},{4,8},{5,1},{8,12},{9,5},{12,14},{13,9},{14,10},{15,13... | collective-permute-start | bytes 393224 | tf_op jit(solution)/shard_map/ppermute | solution.py:348
  54.0 1.4 %collective-permute-start.13 = (bf16[32,2048]{1,0:T(8,128)(2,1)S(1)}, bf16[32,2048]{1,0:T(8,128)(2,1)S(1)}, u32[]{:S(2)}, u32[]{:S(2)}) collective-permute-start(bf16[32,2048]{1,0:T(8,128)(2,1)S(1)} %collective-permute-done.12), channel_id=1, source_target_pairs={{0,1},{1,0},{2,3},{3,2},{4,5},{5,4},{6,7},{7,6},{8,9},{9,8},{10,11... | collective-permute-start | bytes 393224 | tf_op jit(solution)/shard_map/ppermute | solution.py:351
  55.7 1.4 %collective-permute-start.18 = (bf16[32,2048]{1,0:T(8,128)(2,1)S(1)}, bf16[32,2048]{1,0:T(8,128)(2,1)S(1)}, u32[]{:S(2)}, u32[]{:S(2)}) collective-permute-start(bf16[32,2048]{1,0:T(8,128)(2,1)S(1)} %fusion.2.refs_7_), channel_id=1, source_target_pairs={{0,1},{1,0},{2,3},{3,2},{4,5},{5,4},{6,7},{7,6},{8,9},{9,8},{10,11... | collective-permute-start | bytes 393224 | tf_op jit(solution)/shard_map/ppermute | solution.py:351
  55.9 5.0 %collective-permute-start.14 = (bf16[32,2048]{1,0:T(8,128)(2,1)S(1)}, bf16[32,2048]{1,0:T(8,128)(2,1)S(1)}, u32[]{:S(2)}, u32[]{:S(2)}) collective-permute-start(bf16[32,2048]{1,0:T(8,128)(2,1)S(1)} %fusion.2.refs_7_), channel_id=1, source_target_pairs={{0,2},{1,5},{4,0},{5,9},{8,4},{9,13},{12,8},{13,15},{14,12},{15,11... | collective-permute-start | bytes 393224 | tf_op jit(solution)/shard_map/ppermute | solution.py:348
  57.1 5.1 %collective-permute-start.19 = (bf16[32,2048]{1,0:T(8,128)(2,1)S(1)}, bf16[32,2048]{1,0:T(8,128)(2,1)S(1)}, u32[]{:S(2)}, u32[]{:S(2)}) collective-permute-start(bf16[32,2048]{1,0:T(8,128)(2,1)S(1)} %collective-permute-done.18), channel_id=1, source_target_pairs={{0,2},{1,5},{4,0},{5,9},{8,4},{9,13},{12,8},{13,15},{14,12},{15,11... | collective-permute-start | bytes 393224 | tf_op jit(solution)/shard_map/ppermute | solution.py:348
  60.9 5.0 %collective-permute-start.15 = (bf16[32,2048]{1,0:T(8,128)(2,1)S(1)}, bf16[32,2048]{1,0:T(8,128)(2,1)S(1)}, u32[]{:S(2)}, u32[]{:S(2)}) collective-permute-start(bf16[32,2048]{1,0:T(8,128)(2,1)S(1)} %collective-permute-done.14.refs_5_), channel_id=1, source_target_pairs={{0,2},{1,5},{4,0},{5,9},{8,4},{9,13},{12,8},{13,15},{14,12},{15,11... | collective-permute-start | bytes 393224 | tf_op jit(solution)/shard_map/ppermute | solution.py:348
  62.3 5.0 %collective-permute-start.20 = (bf16[32,2048]{1,0:T(8,128)(2,1)S(1)}, bf16[32,2048]{1,0:T(8,128)(2,1)S(1)}, u32[]{:S(2)}, u32[]{:S(2)}) collective-permute-start(bf16[32,2048]{1,0:T(8,128)(2,1)S(1)} %collective-permute-done.19.refs_6_), channel_id=1, source_target_pairs={{0,2},{1,5},{4,0},{5,9},{8,4},{9,13},{12,8},{13,15},{14,12},{15,11... | collective-permute-start | bytes 393224 | tf_op jit(solution)/shard_map/ppermute | solution.py:348
  65.8 5.0 %collective-permute-start.16 = (bf16[32,2048]{1,0:T(8,128)(2,1)S(1)}, bf16[32,2048]{1,0:T(8,128)(2,1)S(1)}, u32[]{:S(2)}, u32[]{:S(2)}) collective-permute-start(bf16[32,2048]{1,0:T(8,128)(2,1)S(1)} %collective-permute-done.15.refs_3_), channel_id=1, source_target_pairs={{0,2},{1,5},{4,0},{5,9},{8,4},{9,13},{12,8},{13,15},{14,12},{15,11... | collective-permute-start | bytes 393224 | tf_op jit(solution)/shard_map/ppermute | solution.py:348
  67.2 5.0 %collective-permute-start.21 = (bf16[32,2048]{1,0:T(8,128)(2,1)S(1)}, bf16[32,2048]{1,0:T(8,128)(2,1)S(1)}, u32[]{:S(2)}, u32[]{:S(2)}) collective-permute-start(bf16[32,2048]{1,0:T(8,128)(2,1)S(1)} %collective-permute-done.20.refs_4_), channel_id=1, source_target_pairs={{0,2},{1,5},{4,0},{5,9},{8,4},{9,13},{12,8},{13,15},{14,12},{15,11... | collective-permute-start | bytes 393224 | tf_op jit(solution)/shard_map/ppermute | solution.py:348
  70.8 5.0 %collective-permute-start.17 = (bf16[32,2048]{1,0:T(8,128)(2,1)S(1)}, bf16[32,2048]{1,0:T(8,128)(2,1)S(1)}, u32[]{:S(2)}, u32[]{:S(2)}) collective-permute-start(bf16[32,2048]{1,0:T(8,128)(2,1)S(1)} %collective-permute-done.16.refs_1_), channel_id=1, source_target_pairs={{0,2},{1,5},{4,0},{5,9},{8,4},{9,13},{12,8},{13,15},{14,12},{15,11... | collective-permute-start | bytes 393224 | tf_op jit(solution)/shard_map/ppermute | solution.py:348
  75.8 2.6 %copy-start.7 = (bf16[1,2048,768]{2,1,0:T(8,128)(2,1)}, bf16[1,2048,768]{2,1,0:T(8,128)(2,1)S(1)}, u32[]{:S(2)}) copy-start(bf16[1,2048,768]{2,1,0:T(8,128)(2,1)S(1)} %collective-permute-done.22.refs_16_) | copy-start | bytes 9437188
  75.8 1.7 %copy-start.8 = (bf16[1,2048,768]{2,1,0:T(8,128)(2,1)}, bf16[1,2048,768]{2,1,0:T(8,128)(2,1)S(1)}, u32[]{:S(2)}) copy-start(bf16[1,2048,768]{2,1,0:T(8,128)(2,1)S(1)} %collective-permute-done.23.refs_17_) | copy-start | bytes 9437188
  91.6 5.0 %collective-permute-start.25 = (bf16[32,2048]{1,0:T(8,128)(2,1)S(1)}, bf16[32,2048]{1,0:T(8,128)(2,1)S(1)}, u32[]{:S(2)}, u32[]{:S(2)}) collective-permute-start(bf16[32,2048]{1,0:T(8,128)(2,1)S(1)} %get-tuple-element.37), channel_id=1, source_target_pairs={{0,4},{1,3},{4,8},{5,1},{8,12},{9,5},{12,14},{13,9},{14,10},{15,13... | collective-permute-start | bytes 393224 | tf_op jit(solution)/shard_map/ppermute | solution.py:348
  92.1 5.9 %collective-permute-start.29 = (bf16[32,2048]{1,0:T(8,128)(2,1)S(1)}, bf16[32,2048]{1,0:T(8,128)(2,1)S(1)}, u32[]{:S(2)}, u32[]{:S(2)}) collective-permute-start(bf16[32,2048]{1,0:T(8,128)(2,1)S(1)} %get-tuple-element.42), channel_id=1, source_target_pairs={{0,4},{1,3},{4,8},{5,1},{8,12},{9,5},{12,14},{13,9},{14,10},{15,13... | collective-permute-start | bytes 393224 | tf_op jit(solution)/shard_map/ppermute | solution.py:348
  96.7 5.0 %collective-permute-start.26 = (bf16[32,2048]{1,0:T(8,128)(2,1)S(1)}, bf16[32,2048]{1,0:T(8,128)(2,1)S(1)}, u32[]{:S(2)}, u32[]{:S(2)}) collective-permute-start(bf16[32,2048]{1,0:T(8,128)(2,1)S(1)} %add_convert_fusion.4), channel_id=1, source_target_pairs={{0,4},{1,3},{4,8},{5,1},{8,12},{9,5},{12,14},{13,9},{14,10},{15,13... | collective-permute-start | bytes 393224 | tf_op jit(solution)/shard_map/ppermute | solution.py:348
  98.1 5.0 %collective-permute-start.30 = (bf16[32,2048]{1,0:T(8,128)(2,1)S(1)}, bf16[32,2048]{1,0:T(8,128)(2,1)S(1)}, u32[]{:S(2)}, u32[]{:S(2)}) collective-permute-start(bf16[32,2048]{1,0:T(8,128)(2,1)S(1)} %add_convert_fusion.1), channel_id=1, source_target_pairs={{0,4},{1,3},{4,8},{5,1},{8,12},{9,5},{12,14},{13,9},{14,10},{15,13... | collective-permute-start | bytes 393224 | tf_op jit(solution)/shard_map/ppermute | solution.py:348
  101.7 5.0 %collective-permute-start.27 = (bf16[32,2048]{1,0:T(8,128)(2,1)S(1)}, bf16[32,2048]{1,0:T(8,128)(2,1)S(1)}, u32[]{:S(2)}, u32[]{:S(2)}) collective-permute-start(bf16[32,2048]{1,0:T(8,128)(2,1)S(1)} %add_convert_fusion.3), channel_id=1, source_target_pairs={{0,4},{1,3},{4,8},{5,1},{8,12},{9,5},{12,14},{13,9},{14,10},{15,13... | collective-permute-start | bytes 393224 | tf_op jit(solution)/shard_map/ppermute | solution.py:348
  103.1 5.0 %collective-permute-start.31 = (bf16[32,2048]{1,0:T(8,128)(2,1)S(1)}, bf16[32,2048]{1,0:T(8,128)(2,1)S(1)}, u32[]{:S(2)}, u32[]{:S(2)}) collective-permute-start(bf16[32,2048]{1,0:T(8,128)(2,1)S(1)} %add_convert_fusion), channel_id=1, source_target_pairs={{0,4},{1,3},{4,8},{5,1},{8,12},{9,5},{12,14},{13,9},{14,10},{15,13... | collective-permute-start | bytes 393224 | tf_op jit(solution)/shard_map/ppermute | solution.py:348
  106.8 5.0 %collective-permute-start.28 = (bf16[32,2048]{1,0:T(8,128)(2,1)S(1)}, bf16[32,2048]{1,0:T(8,128)(2,1)S(1)}, u32[]{:S(2)}, u32[]{:S(2)}) collective-permute-start(bf16[32,2048]{1,0:T(8,128)(2,1)S(1)} %add_convert_fusion.2), channel_id=1, source_target_pairs={{0,4},{1,3},{4,8},{5,1},{8,12},{9,5},{12,14},{13,9},{14,10},{15,13... | collective-permute-start | bytes 393224 | tf_op jit(solution)/shard_map/ppermute | solution.py:348
  108.1 3.7 %collective-permute-start.32 = (bf16[32,2048]{1,0:T(8,128)(2,1)S(1)}, bf16[32,2048]{1,0:T(8,128)(2,1)S(1)}, u32[]{:S(2)}, u32[]{:S(2)}) collective-permute-start(bf16[32,2048]{1,0:T(8,128)(2,1)S(1)} %collective-permute-done.31), channel_id=1, source_target_pairs={{0,1},{1,0},{2,3},{3,2},{4,5},{5,4},{6,7},{7,6},{8,9},{9,8},{10,11... | collective-permute-start | bytes 393224 | tf_op jit(solution)/shard_map/ppermute | solution.py:351

commit v4 on v3

--- a/solution.py
+++ b/solution.py
@@ -85,32 +85,37 @@
                 :, head * head_size : (head + 1) * head_size
             ].astype(F32)
 
-    head_of = lax.broadcasted_iota(jnp.int32, (heads, cache_len), 0) // group
+    head_of = lax.broadcasted_iota(jnp.int32, (block, heads, cache_len), 1) // group
     slot = lax.broadcasted_iota(jnp.int32, (heads, cache_len), 1)
-    for i in range(block):
-        row = step * block + i
-        span = pl.ds(pl.multiple_of(row * heads, heads), heads)
-        keys = k_ref[i].reshape(kv_count * cache_len, head_size)
-        scores = lax.dot_general(
-            q_rows[span, :].astype(BF16),
-            keys,
+    first = pl.multiple_of(step * block * heads, block * heads)
+    asked = q_rows[pl.ds(first, block * heads), :].astype(BF16)
+    scores = [
+        lax.dot_general(
+            asked[i * heads : (i + 1) * heads],
+            k_ref[i].reshape(kv_count * cache_len, head_size),
             (((1,), (1,)), ((), ())),
             preferred_element_type=F32,
         )
-        picked = scores[:, :cache_len]
-        for kv in range(1, kv_count):
-            picked = jnp.where(
-                head_of == kv, scores[:, kv * cache_len : (kv + 1) * cache_len], picked
-            )
-        picked = picked * (1.0 / math.sqrt(head_size))
-        picked = jnp.where(slot < lengths_ref[row], picked, -1e30)
-        weights = jnp.exp(picked - jnp.max(picked, axis=1, keepdims=True))
-        shares = weights / jnp.sum(weights, axis=1, keepdims=True)
-        spread = jnp.concatenate(
-            [jnp.where(head_of == kv, shares, 0.0) for kv in range(kv_count)], axis=1
-        ).astype(BF16)
+        for i in range(block)
+    ]
+    scores = jnp.stack(scores)
+    live = jnp.stack([slot < lengths_ref[step * block + i] for i in range(block)])
+    picked = scores[:, :, :cache_len]
+    for kv in range(1, kv_count):
+        picked = jnp.where(
+            head_of == kv, scores[:, :, kv * cache_len : (kv + 1) * cache_len], picked
+        )
+    picked = jnp.where(live, picked * (1.0 / math.sqrt(head_size)), -1e30)
+    weights = jnp.exp(picked - jnp.max(picked, axis=2, keepdims=True))
+    shares = weights / jnp.sum(weights, axis=2, keepdims=True)
+    spread = jnp.concatenate(
+        [jnp.where(head_of == kv, shares, 0.0) for kv in range(kv_count)], axis=2
+    ).astype(BF16)
+    for i in range(block):
         values = v_ref[i].reshape(kv_count * cache_len, head_size)
-        out_rows[span, :] = jnp.dot(spread, values, preferred_element_type=F32)
+        out_rows[pl.ds(first + i * heads, heads), :] = jnp.dot(
+            spread[i], values, preferred_element_type=F32
+        )
 
     @pl.when(step == steps - 1)
     def _():
@@ -122,18 +127,25 @@
                 pl.ds(head, rows, stride=heads), :
             ].astype(BF16)
         extra = tokens.shape[2] - chip_feats
-        lane = lax.broadcasted_iota(jnp.int32, (rows, extra), 1)
-        expert = jnp.where(lane < chip_experts, lane, lane - chip_experts)
-        choices = ids_ref.shape[1]
-        named = [jnp.broadcast_to(ids_ref[:, j : j + 1], (rows, extra)) for j in range(choices)]
-        numers = [jnp.broadcast_to(numer_ref[:, j : j + 1], (rows, extra)) for j in range(choices)]
+        choices = ids_ref.shape[0]
+        total = chips * chip_experts
+        expert = lax.broadcasted_iota(jnp.int32, (total, rows), 0)
+        found = jnp.zeros((total, rows), jnp.int32)
+        for j in range(choices):
+            found += jnp.where(ids_ref[j : j + 1, :] == expert, numer_ref[j : j + 1, :], 0)
+        digits = jnp.concatenate([found >> 4, found & 15], axis=0).astype(F32).astype(BF16)
+        source = lax.broadcasted_iota(jnp.int32, (2 * total, extra), 0)
+        lane = lax.broadcasted_iota(jnp.int32, (2 * total, extra), 1)
         for there in range(chips):
-            found = jnp.zeros((rows, extra), jnp.int32)
-            for j in range(choices):
-                found += jnp.where(named[j] == expert + there * chip_experts, numers[j], 0)
-            digit = jnp.where(lane < chip_experts, found >> 4, found & 15)
-            digit = jnp.where(lane < 2 * chip_experts, digit, 0)
-            tokens[there, :, chip_feats:] = digit.astype(F32).astype(BF16)
+            base = there * chip_experts
+            wanted = jnp.where(lane < chip_experts, base + lane, total + base + lane - chip_experts)
+            pick = (source == wanted) & (lane < 2 * chip_experts)
+            tokens[there, :, chip_feats:] = lax.dot_general(
+                digits,
+                jnp.where(pick, 1.0, 0.0).astype(BF16),
+                (((0,), (0,)), ((), ())),
+                preferred_element_type=F32,
+            ).astype(BF16)
         chip, _, chip_at = ring_view(chips)
         far_ref[...] = tokens[chip_at(-hops)]
         own_ref[...] = tokens[chip]
@@ -149,7 +161,7 @@
     heads = feats // head_size
     extra = -(-2 * chip_experts // 128) * 128
     wide = feats // chips + extra
-    block = 8
+    block = 16
     cache = pl.BlockSpec((block, kv_count, cache_len, head_size), lambda t: (t, 0, 0, 0))
     one = jax.ShapeDtypeStruct((rows, wide), BF16)
     several = jax.ShapeDtypeStruct((hops - 1, rows, wide), BF16)
@@ -164,13 +176,13 @@
             pltpu.VMEM((rows * heads, head_size), F32),
             pltpu.VMEM((chips, rows, wide), BF16),
         ],
-        compiler_params=pltpu.CompilerParams(vmem_limit_bytes=24 * 1024 * 1024),
+        compiler_params=pltpu.CompilerParams(vmem_limit_bytes=56 * 1024 * 1024),
         cost_estimate=pl.CostEstimate(
             flops=4 * rows * heads * cache_len * head_size,
             bytes_accessed=4 * rows * kv_count * cache_len * head_size,
             transcendentals=rows * heads * cache_len,
         ),
-    )(lengths, queries, cache_keys, cache_values, ids, numer)
+    )(lengths, queries, cache_keys, cache_values, ids.T, numer.T)
 
 
 def project_kernel(pieces, *refs):
@@ -316,7 +328,7 @@
             pltpu.VMEM((2, rows, 1), F32),
             pltpu.VMEM((rows, 2 * hidden_units), BF16),
         ],
-        compiler_params=pltpu.CompilerParams(vmem_limit_bytes=48 * 1024 * 1024),
+        compiler_params=pltpu.CompilerParams(vmem_limit_bytes=56 * 1024 * 1024),
         cost_estimate=pl.CostEstimate(
             flops=12 * rows * hidden_units * width,
             bytes_accessed=12 * hidden_units * width,

time: 113 us -> 107 us (0.947)
  other arithmetic: 1.36 us -> 7.03 us
  Pallas kernels: 26.5 us -> 21.5 us
  local copies, waits for them, and re-layouts: 8.91 us -> 4.22 us
  waiting for transfers between devices: 49.2 us -> 45.4 us
  starting transfers between devices: 26.4 us -> 27.7 us
    pallas_call x1, Pallas kernels: 12.3 us -> 5.04 us  [attend(): pl.pallas_call(functools.partial(attend_kernel, chips, hops, chip_experts...]
    unnamed x24 -> x40, local copies, waits for them, and re-layouts: 8.89 us -> 3.38 us
    ppermute x25, waiting for transfers between devices: 47.9 us -> 44.8 us  [pass_on(): return lax.ppermute(array, 'rows', toward(step))]
    convert_element_type x6, other arithmetic: 0.2 us -> 3.03 us  [ring_sums(): own = (pass_on(own, 1).astype(F32) + partial[spot]).astype(BF16)]
    pallas_call x1, Pallas kernels: 13.3 us -> 15.4 us  [experts(): pl.pallas_call(functools.partial(expert_kernel, tiles, len(pieces) // 2,...]
    convert_element_type x4, other arithmetic: 0.11 us -> 2.02 us  [ring_sums(): other = (pass_on(other, 1).astype(F32) + partial[spot + 1]).astype(BF16)]
    ppermute x25, starting transfers between devices: 24.8 us -> 26 us  [pass_on(): return lax.ppermute(array, 'rows', toward(step))]
  transfers between devices with their start and end apart: 33 -> 33, of which waited for: 23 -> 20; matrix products, arithmetic and copies ran while one was open for 2% -> 6% of each run, Pallas kernels for 12% -> 6%
where the time goes in v4:
time: 107 us; the launch traced here: 106 us
  waiting for transfers between devices  45.4 us (42%)
  starting transfers between devices  27.7 us (26%)
  Pallas kernels  21.5 us (20%)
  other arithmetic  7.03 us (7%)
  local copies, waits for them, and re-layouts  4.22 us (4%)
    ppermute x25, waiting for transfers between devices, pass_on(): return lax.ppermute(array, 'rows', toward(step))  44.8 us
    ppermute x25, starting transfers between devices, pass_on(): return lax.ppermute(array, 'rows', toward(step))  26 us
    pallas_call x1, Pallas kernels, experts(): pl.pallas_call(functools.partial(expert_kernel, tiles, len(pieces) // 2,...  15.4 us
    pallas_call x1, Pallas kernels, attend(): pl.pallas_call(functools.partial(attend_kernel, chips, hops, chip_experts...  5.04 us
    unnamed x40, local copies, waits for them, and re-layouts  3.38 us
    convert_element_type x6, other arithmetic, ring_sums(): own = (pass_on(own, 1).astype(F32) + partial[spot]).astype(BF16)  3.03 us
  transfers between devices with their start and end apart: 33, of which 20 were waited for; matrix products, arithmetic and copies ran while one was open for 6% of the time, Pallas kernels for 6%

profile of v4, /device:TPU:0, one launch (start us, length us, event | category | flops | bytes accessed | tf_op | source)
XLA Modules:
  0.0 106.1 jit_solution(9759790587994546835)
XLA Ops:
  0.0 0.5 collective-permute-start.3
  0.5 5.0 %shard_map.118 = (bf16[32,640]{1,0:T(8,128)(2,1)}, bf16[3,32,640]{2,1,0:T(8,128)(2,1)}, bf16[3,32,640]{2,1,0:T(8,128)(2,1)}, bf16[32,640]{1,0:T(8,128)(2,1)}) custom-call(s32[32]{0:T(128)} %lengths_ref.1, bf16[32,4096]{1,0:T(8,128)(2,1)} %q_ref.1, bf16[32,2,128,128]{3,2,1,0:T(8,128)(2,1)} %k_ref.1, bf16[32,2,128,128]{3,2,1,0:T(8,128)(2,1)} %v_ref.1, ...), custom_call_target="tpu_custom_call" | custom-call | flops 67108864 | bytes 4194304 | tf_op jit(solution)/shard_map/pallas_call | solution.py:168
  5.5 5.6 %collective-permute-start = (bf16[32,640]{1,0:T(8,128)(2,1)}, bf16[32,640]{1,0:T(8,128)(2,1)S(1)}, u32[]{:S(2)}, u32[]{:S(2)}) collective-permute-start(bf16[32,640]{1,0:T(8,128)(2,1)} %get-tuple-element.25), channel_id=1, source_target_pairs={{0,14},{1,15},{4,10},{5,11},{8,6},{9,7},{12,2},{13,3},{14,0},{15,1... | collective-permute-start | bytes 122888 | tf_op jit(solution)/shard_map/ppermute | solution.py:360
  11.2 0.2 collective-permute-start.1
  11.4 0.8 slice_bitcast_fusion.5
  12.2 0.5 collective-permute-done.1
  12.7 0.1 collective-permute-start.2
  12.8 1.7 %collective-permute-start.6 = (bf16[64,640]{1,0:T(8,128)(2,1)S(1)}, bf16[64,640]{1,0:T(8,128)(2,1)S(1)}, u32[]{:S(2)}, u32[]{:S(2)}) collective-permute-start(bf16[64,640]{1,0:T(8,128)(2,1)S(1)} %pad_maximum_fusion.1), channel_id=1, source_target_pairs={{0,6},{1,9},{4,2},{5,13},{8,0},{9,15},{12,4},{13,11},{14,8},{15,7}... | collective-permute-start | bytes 245768 | tf_op jit(solution)/shard_map/ppermute | solution.py:360
  14.6 5.0 %collective-permute-done.2.refs_1_.refs_9_ = bf16[64,640]{1,0:T(8,128)(2,1)S(1)} collective-permute-done((bf16[64,640]{1,0:T(8,128)(2,1)S(1)}, bf16[64,640]{1,0:T(8,128)(2,1)S(1)}, u32[]{:S(2)}, u32[]{:S(2)}) %collective-permute-start.2) | collective-permute-done | bytes 81952 | tf_op jit(solution)/shard_map/ppermute | solution.py:360
  19.5 0.5 shard_map.119
  20.0 0.1 collective-permute-start.4
  20.1 2.1 %collective-permute-start.7 = (bf16[64,640]{1,0:T(8,128)(2,1)S(1)}, bf16[64,640]{1,0:T(8,128)(2,1)S(1)}, u32[]{:S(2)}, u32[]{:S(2)}) collective-permute-start(bf16[64,640]{1,0:T(8,128)(2,1)S(1)} %pad_maximum_fusion.2), channel_id=1, source_target_pairs={{0,2},{1,5},{4,0},{5,9},{8,4},{9,13},{12,8},{13,15},{14,12},{15,11... | collective-permute-start | bytes 245768 | tf_op jit(solution)/shard_map/ppermute | solution.py:360
  22.2 0.4 collective-permute-start.22
  22.6 0.1 collective-permute-start.23
  22.7 0.4 collective-permute-start.24
  23.1 2.4 %collective-permute-done.7.refs_1_.refs_11_ = bf16[64,640]{1,0:T(8,128)(2,1)S(1)} collective-permute-done((bf16[64,640]{1,0:T(8,128)(2,1)S(1)}, bf16[64,640]{1,0:T(8,128)(2,1)S(1)}, u32[]{:S(2)}, u32[]{:S(2)}) %collective-permute-start.7) | collective-permute-done | bytes 81952 | tf_op jit(solution)/shard_map/ppermute | solution.py:360
  25.5 0.5 shard_map.120
  26.1 1.4 %collective-permute-start.5 = (bf16[32,2048]{1,0:T(8,128)(2,1)S(1)}, bf16[32,2048]{1,0:T(8,128)(2,1)S(1)}, u32[]{:S(2)}, u32[]{:S(2)}) collective-permute-start(bf16[32,2048]{1,0:T(8,128)(2,1)S(1)} %add_convert_fusion.10), channel_id=1, source_target_pairs={{0,4},{1,3},{4,8},{5,1},{8,12},{9,5},{12,14},{13,9},{14,10},{15,13... | collective-permute-start | bytes 393224 | tf_op jit(solution)/shard_map/ppermute | solution.py:360
  27.5 2.9 %collective-permute-done.10 = bf16[32,2048]{1,0:T(8,128)(2,1)S(1)} collective-permute-done((bf16[32,2048]{1,0:T(8,128)(2,1)S(1)}, bf16[32,2048]{1,0:T(8,128)(2,1)S(1)}, u32[]{:S(2)}, u32[]{:S(2)}) %collective-permute-start.10) | collective-permute-done | bytes 131104 | tf_op jit(solution)/shard_map/ppermute | solution.py:360
  30.5 0.1 collective-permute-start.11
  30.6 1.3 %collective-permute-done.5 = bf16[32,2048]{1,0:T(8,128)(2,1)S(1)} collective-permute-done((bf16[32,2048]{1,0:T(8,128)(2,1)S(1)}, bf16[32,2048]{1,0:T(8,128)(2,1)S(1)}, u32[]{:S(2)}, u32[]{:S(2)}) %collective-permute-start.5) | collective-permute-done | bytes 131104 | tf_op jit(solution)/shard_map/ppermute | solution.py:360
  31.9 0.7 collective-permute-start.8
  32.6 2.9 %collective-permute-done.11 = bf16[32,2048]{1,0:T(8,128)(2,1)S(1)} collective-permute-done((bf16[32,2048]{1,0:T(8,128)(2,1)S(1)}, bf16[32,2048]{1,0:T(8,128)(2,1)S(1)}, u32[]{:S(2)}, u32[]{:S(2)}) %collective-permute-start.11) | collective-permute-done | bytes 131104 | tf_op jit(solution)/shard_map/ppermute | solution.py:360
  35.6 1.3 %collective-permute-done.8 = bf16[32,2048]{1,0:T(8,128)(2,1)S(1)} collective-permute-done((bf16[32,2048]{1,0:T(8,128)(2,1)S(1)}, bf16[32,2048]{1,0:T(8,128)(2,1)S(1)}, u32[]{:S(2)}, u32[]{:S(2)}) %collective-permute-start.8) | collective-permute-done | bytes 131104 | tf_op jit(solution)/shard_map/ppermute | solution.py:360
  36.9 0.7 collective-permute-start.9
  37.6 3.0 %collective-permute-done.12 = bf16[32,2048]{1,0:T(8,128)(2,1)S(1)} collective-permute-done((bf16[32,2048]{1,0:T(8,128)(2,1)S(1)}, bf16[32,2048]{1,0:T(8,128)(2,1)S(1)}, u32[]{:S(2)}, u32[]{:S(2)}) %collective-permute-start.12) | collective-permute-done | bytes 131104 | tf_op jit(solution)/shard_map/ppermute | solution.py:360
  40.6 1.4 %collective-permute-done.9 = bf16[32,2048]{1,0:T(8,128)(2,1)S(1)} collective-permute-done((bf16[32,2048]{1,0:T(8,128)(2,1)S(1)}, bf16[32,2048]{1,0:T(8,128)(2,1)S(1)}, u32[]{:S(2)}, u32[]{:S(2)}) %collective-permute-start.9) | collective-permute-done | bytes 131104 | tf_op jit(solution)/shard_map/ppermute | solution.py:360
  42.0 0.2 fusion
  42.2 0.1 fusion.2.refs_7_
  42.3 0.2 collective-permute-start.18
  42.5 1.2 %collective-permute-start.14 = (bf16[32,2048]{1,0:T(8,128)(2,1)S(1)}, bf16[32,2048]{1,0:T(8,128)(2,1)S(1)}, u32[]{:S(2)}, u32[]{:S(2)}) collective-permute-start(bf16[32,2048]{1,0:T(8,128)(2,1)S(1)} %fusion.2.refs_7_), channel_id=1, source_target_pairs={{0,2},{1,5},{4,0},{5,9},{8,4},{9,13},{12,8},{13,15},{14,12},{15,11... | collective-permute-start | bytes 393224 | tf_op jit(solution)/shard_map/ppermute | solution.py:360
  43.7 1.2 %collective-permute-start.19 = (bf16[32,2048]{1,0:T(8,128)(2,1)S(1)}, bf16[32,2048]{1,0:T(8,128)(2,1)S(1)}, u32[]{:S(2)}, u32[]{:S(2)}) collective-permute-start(bf16[32,2048]{1,0:T(8,128)(2,1)S(1)} %collective-permute-done.18), channel_id=1, source_target_pairs={{0,2},{1,5},{4,0},{5,9},{8,4},{9,13},{12,8},{13,15},{14,12},{15,11... | collective-permute-start | bytes 393224 | tf_op jit(solution)/shard_map/ppermute | solution.py:360
  45.0 2.5 %collective-permute-done.14.refs_5_ = bf16[32,2048]{1,0:T(8,128)(2,1)S(1)} collective-permute-done((bf16[32,2048]{1,0:T(8,128)(2,1)S(1)}, bf16[32,2048]{1,0:T(8,128)(2,1)S(1)}, u32[]{:S(2)}, u32[]{:S(2)}) %collective-permute-start.14) | collective-permute-done | bytes 131104 | tf_op jit(solution)/shard_map/ppermute | solution.py:360
  47.4 1.2 %collective-permute-start.15 = (bf16[32,2048]{1,0:T(8,128)(2,1)S(1)}, bf16[32,2048]{1,0:T(8,128)(2,1)S(1)}, u32[]{:S(2)}, u32[]{:S(2)}) collective-permute-start(bf16[32,2048]{1,0:T(8,128)(2,1)S(1)} %collective-permute-done.14.refs_5_), channel_id=1, source_target_pairs={{0,2},{1,5},{4,0},{5,9},{8,4},{9,13},{12,8},{13,15},{14,12},{15,11... | collective-permute-start | bytes 393224 | tf_op jit(solution)/shard_map/ppermute | solution.py:360
  48.6 0.2 collective-permute-done.19.refs_6_
  48.8 1.2 %collective-permute-start.20 = (bf16[32,2048]{1,0:T(8,128)(2,1)S(1)}, bf16[32,2048]{1,0:T(8,128)(2,1)S(1)}, u32[]{:S(2)}, u32[]{:S(2)}) collective-permute-start(bf16[32,2048]{1,0:T(8,128)(2,1)S(1)} %collective-permute-done.19.refs_6_), channel_id=1, source_target_pairs={{0,2},{1,5},{4,0},{5,9},{8,4},{9,13},{12,8},{13,15},{14,12},{15,11... | collective-permute-start | bytes 393224 | tf_op jit(solution)/shard_map/ppermute | solution.py:360
  50.0 2.4 %collective-permute-done.15.refs_3_ = bf16[32,2048]{1,0:T(8,128)(2,1)S(1)} collective-permute-done((bf16[32,2048]{1,0:T(8,128)(2,1)S(1)}, bf16[32,2048]{1,0:T(8,128)(2,1)S(1)}, u32[]{:S(2)}, u32[]{:S(2)}) %collective-permute-start.15) | collective-permute-done | bytes 131104 | tf_op jit(solution)/shard_map/ppermute | solution.py:360
  52.4 1.2 %collective-permute-start.16 = (bf16[32,2048]{1,0:T(8,128)(2,1)S(1)}, bf16[32,2048]{1,0:T(8,128)(2,1)S(1)}, u32[]{:S(2)}, u32[]{:S(2)}) collective-permute-start(bf16[32,2048]{1,0:T(8,128)(2,1)S(1)} %collective-permute-done.15.refs_3_), channel_id=1, source_target_pairs={{0,2},{1,5},{4,0},{5,9},{8,4},{9,13},{12,8},{13,15},{14,12},{15,11... | collective-permute-start | bytes 393224 | tf_op jit(solution)/shard_map/ppermute | solution.py:360
  53.6 0.2 collective-permute-done.20.refs_4_
  53.8 1.2 %collective-permute-start.21 = (bf16[32,2048]{1,0:T(8,128)(2,1)S(1)}, bf16[32,2048]{1,0:T(8,128)(2,1)S(1)}, u32[]{:S(2)}, u32[]{:S(2)}) collective-permute-start(bf16[32,2048]{1,0:T(8,128)(2,1)S(1)} %collective-permute-done.20.refs_4_), channel_id=1, source_target_pairs={{0,2},{1,5},{4,0},{5,9},{8,4},{9,13},{12,8},{13,15},{14,12},{15,11... | collective-permute-start | bytes 393224 | tf_op jit(solution)/shard_map/ppermute | solution.py:360
  55.0 2.4 %collective-permute-done.16.refs_1_ = bf16[32,2048]{1,0:T(8,128)(2,1)S(1)} collective-permute-done((bf16[32,2048]{1,0:T(8,128)(2,1)S(1)}, bf16[32,2048]{1,0:T(8,128)(2,1)S(1)}, u32[]{:S(2)}, u32[]{:S(2)}) %collective-permute-start.16) | collective-permute-done | bytes 131104 | tf_op jit(solution)/shard_map/ppermute | solution.py:360
  57.4 1.2 %collective-permute-start.17 = (bf16[32,2048]{1,0:T(8,128)(2,1)S(1)}, bf16[32,2048]{1,0:T(8,128)(2,1)S(1)}, u32[]{:S(2)}, u32[]{:S(2)}) collective-permute-start(bf16[32,2048]{1,0:T(8,128)(2,1)S(1)} %collective-permute-done.16.refs_1_), channel_id=1, source_target_pairs={{0,2},{1,5},{4,0},{5,9},{8,4},{9,13},{12,8},{13,15},{14,12},{15,11... | collective-permute-start | bytes 393224 | tf_op jit(solution)/shard_map/ppermute | solution.py:360
  58.6 0.2 collective-permute-done.21.refs_2_
  58.8 3.6 %collective-permute-done.17.refs_0_ = bf16[32,2048]{1,0:T(8,128)(2,1)S(1)} collective-permute-done((bf16[32,2048]{1,0:T(8,128)(2,1)S(1)}, bf16[32,2048]{1,0:T(8,128)(2,1)S(1)}, u32[]{:S(2)}, u32[]{:S(2)}) %collective-permute-start.17) | collective-permute-done | bytes 131104 | tf_op jit(solution)/shard_map/ppermute | solution.py:360
  62.4 1.6 %copy-done.8 = bf16[1,2048,768]{2,1,0:T(8,128)(2,1)} copy-done((bf16[1,2048,768]{2,1,0:T(8,128)(2,1)}, bf16[1,2048,768]{2,1,0:T(8,128)(2,1)S(1)}, u32[]{:S(2)}) %copy-start.8) | copy-done | bytes 3145752
  64.0 1.7 %copy-done.9 = bf16[1,2048,768]{2,1,0:T(8,128)(2,1)} copy-done((bf16[1,2048,768]{2,1,0:T(8,128)(2,1)}, bf16[1,2048,768]{2,1,0:T(8,128)(2,1)S(1)}, u32[]{:S(2)}) %copy-start.9) | copy-done | bytes 3145752
  65.8 15.4 %shard_map.121 = (bf16[32,2048]{1,0:T(8,128)(2,1)}, f32[32,2048]{1,0:T(8,128)}, bf16[32,2048]{1,0:T(8,128)(2,1)}, f32[32,2048]{1,0:T(8,128)}, f32[32,2048]{1,0:T...) custom-call(bf16[32,2048]{1,0:T(8,128)(2,1)} %copy-done.17, bf16[32,2048]{1,0:T(8,128)(2,1)} %copy-done.15, ...), custom_call_target="tpu_custom_call" | custom-call | flops 4831838208 | bytes 18874368 | tf_op jit(solution)/shard_map/pallas_call | solution.py:317
  81.2 0.6 collective-permute-start.25
  81.8 0.8 collective-permute-start.29
  82.6 3.8 %collective-permute-done.25 = bf16[32,2048]{1,0:T(8,128)(2,1)S(1)} collective-permute-done((bf16[32,2048]{1,0:T(8,128)(2,1)}, bf16[32,2048]{1,0:T(8,128)(2,1)S(1)}, u32[]{:S(2)}, u32[]{:S(2)}) %collective-permute-start.25) | collective-permute-done | bytes 131104 | tf_op jit(solution)/shard_map/ppermute | solution.py:360
  86.4 1.0 add_convert_fusion.4
  87.4 0.6 collective-permute-start.26
  88.0 1.0 add_convert_fusion.1
  89.0 0.9 collective-permute-start.30
  89.9 2.5 %collective-permute-done.26 = bf16[32,2048]{1,0:T(8,128)(2,1)S(1)} collective-permute-done((bf16[32,2048]{1,0:T(8,128)(2,1)S(1)}, bf16[32,2048]{1,0:T(8,128)(2,1)S(1)}, u32[]{:S(2)}, u32[]{:S(2)}) %collective-permute-start.26) | collective-permute-done | bytes 131104 | tf_op jit(solution)/shard_map/ppermute | solution.py:360
  92.4 1.0 add_convert_fusion.3
  93.4 0.6 collective-permute-start.27
  94.0 1.0 add_convert_fusion
  95.0 0.9 collective-permute-start.31
  95.9 2.5 %collective-permute-done.27 = bf16[32,2048]{1,0:T(8,128)(2,1)S(1)} collective-permute-done((bf16[32,2048]{1,0:T(8,128)(2,1)S(1)}, bf16[32,2048]{1,0:T(8,128)(2,1)S(1)}, u32[]{:S(2)}, u32[]{:S(2)}) %collective-permute-start.27) | collective-permute-done | bytes 131104 | tf_op jit(solution)/shard_map/ppermute | solution.py:360
  98.4 1.0 add_convert_fusion.2
  99.4 0.6 collective-permute-start.28
  100.0 4.4 %collective-permute-done.28 = bf16[32,2048]{1,0:T(8,128)(2,1)S(1)} collective-permute-done((bf16[32,2048]{1,0:T(8,128)(2,1)S(1)}, bf16[32,2048]{1,0:T(8,128)(2,1)S(1)}, u32[]{:S(2)}, u32[]{:S(2)}) %collective-permute-start.28) | collective-permute-done | bytes 131104 | tf_op jit(solution)/shard_map/ppermute | solution.py:360
  104.4 1.7 %fusion.3 = bf16[32,2048]{1,0:T(8,128)(2,1)} fusion(bf16[32,2048]{1,0:T(8,128)(2,1)S(1)} %get-tuple-element.46, bf16[32,2048]{1,0:T(8,128)(2,1)S(1)} %collective-permute-done.32, f32[32,2048]{1,0:T(8,128)} %get-tuple-element.41, bf16[32,2048]{1,0:T(8,128)(2,1)S(1)} %collective-permute-done.28), kind=kLoop, calls=%fused_computation.6 | loop fusion | flops 458752 | bytes 786432 | tf_op jit(solution)/shard_map/convert_element_type | solution.py:427
  (65 shorter events, 0.4 us)
Async XLA Ops:
  0.0 19.5 %copy-start = (bf16[256,2048]{1,0:T(8,128)(2,1)S(1)}, bf16[256,2048]{1,0:T(8,128)(2,1)}, u32[]{:S(2)}) copy-start(bf16[256,2048]{1,0:T(8,128)(2,1)} %refs_3_.1) | copy-start | bytes 3145732
  0.0 19.5 %collective-permute-start.3 = (bf16[256,2048]{1,0:T(8,128)(2,1)}, bf16[256,2048]{1,0:T(8,128)(2,1)S(1)}, u32[]{:S(2)}, u32[]{:S(2)}) collective-permute-start(bf16[256,2048]{1,0:T(8,128)(2,1)} %refs_3_.1), channel_id=1, source_target_pairs={{0,1},{1,0},{2,3},{3,2},{4,5},{5,4},{6,7},{7,6},{8,9},{9,8},{10,11... | collective-permute-start | bytes 3145736 | tf_op jit(solution)/shard_map/ppermute | solution.py:363
  0.5 21.7 %copy-start.6 = (bf16[1,2048,768]{2,1,0:T(8,128)(2,1)S(1)}, bf16[1,2048,768]{2,1,0:T(8,128)(2,1)}, u32[]{:S(2)}) copy-start(bf16[1,2048,768]{2,1,0:T(8,128)(2,1)} %refs_13_.1) | copy-start | bytes 9437188
  5.5 17.1 %copy-start.7 = (bf16[1,2048,768]{2,1,0:T(8,128)(2,1)S(1)}, bf16[1,2048,768]{2,1,0:T(8,128)(2,1)}, u32[]{:S(2)}) copy-start(bf16[1,2048,768]{2,1,0:T(8,128)(2,1)} %refs_14_.1) | copy-start | bytes 9437188
  5.5 20.0 %copy-start.4 = (bf16[32,640]{1,0:T(8,128)(2,1)S(1)}, bf16[32,640]{1,0:T(8,128)(2,1)}, u32[]{:S(2)}) copy-start(bf16[32,640]{1,0:T(8,128)(2,1)} %get-tuple-element.30.refs_2_.refs_12_) | copy-start | bytes 122884
  5.5 9.0 %collective-permute-start = (bf16[32,640]{1,0:T(8,128)(2,1)}, bf16[32,640]{1,0:T(8,128)(2,1)S(1)}, u32[]{:S(2)}, u32[]{:S(2)}) collective-permute-start(bf16[32,640]{1,0:T(8,128)(2,1)} %get-tuple-element.25), channel_id=1, source_target_pairs={{0,14},{1,15},{4,10},{5,11},{8,6},{9,7},{12,2},{13,3},{14,0},{15,1... | collective-permute-start | bytes 122888 | tf_op jit(solution)/shard_map/ppermute | solution.py:360
  11.2 1.5 %collective-permute-start.1 = (bf16[3,32,640]{2,1,0:T(8,128)(2,1)}, bf16[3,32,640]{2,1,0:T(8,128)(2,1)S(1)}, u32[]{:S(2)}, u32[]{:S(2)}) collective-permute-start(bf16[3,32,640]{2,1,0:T(8,128)(2,1)} %get-tuple-element.27), channel_id=1, source_target_pairs={{0,1},{1,0},{2,3},{3,2},{4,5},{5,4},{6,7},{7,6},{8,9},{9,8},{10,11... | collective-permute-start | bytes 368648 | tf_op jit(solution)/shard_map/ppermute | solution.py:363
  12.7 6.8 %collective-permute-start.2 = (bf16[64,640]{1,0:T(8,128)(2,1)S(1)}, bf16[64,640]{1,0:T(8,128)(2,1)S(1)}, u32[]{:S(2)}, u32[]{:S(2)}) collective-permute-start(bf16[64,640]{1,0:T(8,128)(2,1)S(1)} %pad_maximum_fusion), channel_id=1, source_target_pairs={{0,10},{1,13},{4,6},{5,15},{8,2},{9,11},{12,0},{13,7},{14,4},{15,3... | collective-permute-start | bytes 245768 | tf_op jit(solution)/shard_map/ppermute | solution.py:360
  12.8 29.2 %copy-start.18 = (bf16[32,2048]{1,0:T(8,128)(2,1)S(1)}, bf16[32,2048]{1,0:T(8,128)(2,1)}, u32[]{:S(2)}) copy-start(bf16[32,2048]{1,0:T(8,128)(2,1)} %param.16) | copy-start | bytes 393220
  12.8 9.9 %collective-permute-start.6 = (bf16[64,640]{1,0:T(8,128)(2,1)S(1)}, bf16[64,640]{1,0:T(8,128)(2,1)S(1)}, u32[]{:S(2)}, u32[]{:S(2)}) collective-permute-start(bf16[64,640]{1,0:T(8,128)(2,1)S(1)} %pad_maximum_fusion.1), channel_id=1, source_target_pairs={{0,6},{1,9},{4,2},{5,13},{8,0},{9,15},{12,4},{13,11},{14,8},{15,7}... | collective-permute-start | bytes 245768 | tf_op jit(solution)/shard_map/ppermute | solution.py:360
  14.5 21.0 %copy-start.5 = (bf16[32,640]{1,0:T(8,128)(2,1)}, bf16[32,640]{1,0:T(8,128)(2,1)S(1)}, u32[]{:S(2)}) copy-start(bf16[32,640]{1,0:T(8,128)(2,1)S(1)} %collective-permute-done.refs_0_.refs_8_) | copy-start | bytes 122884
  19.5 16.0 %copy-start.1 = (bf16[64,640]{1,0:T(8,128)(2,1)}, bf16[64,640]{1,0:T(8,128)(2,1)S(1)}, u32[]{:S(2)}) copy-start(bf16[64,640]{1,0:T(8,128)(2,1)S(1)} %collective-permute-done.2.refs_1_.refs_9_) | copy-start | bytes 245764
  20.0 22.2 %copy-start.19 = (f32[2048]{0:T(1024)S(1)}, f32[2048]{0:T(1024)}, u32[]{:S(2)}) copy-start(f32[2048]{0:T(1024)} %param.18) | copy-start | bytes 24580
  20.0 6.0 %collective-permute-start.4 = (bf16[32,2048]{1,0:T(8,128)(2,1)S(1)}, bf16[32,2048]{1,0:T(8,128)(2,1)S(1)}, u32[]{:S(2)}, u32[]{:S(2)}) collective-permute-start(bf16[32,2048]{1,0:T(8,128)(2,1)S(1)} %get-tuple-element.28), channel_id=1, source_target_pairs={{0,4},{1,3},{4,8},{5,1},{8,12},{9,5},{12,14},{13,9},{14,10},{15,13... | collective-permute-start | bytes 393224 | tf_op jit(solution)/shard_map/ppermute | solution.py:360
  20.1 5.4 %collective-permute-start.7 = (bf16[64,640]{1,0:T(8,128)(2,1)S(1)}, bf16[64,640]{1,0:T(8,128)(2,1)S(1)}, u32[]{:S(2)}, u32[]{:S(2)}) collective-permute-start(bf16[64,640]{1,0:T(8,128)(2,1)S(1)} %pad_maximum_fusion.2), channel_id=1, source_target_pairs={{0,2},{1,5},{4,0},{5,9},{8,4},{9,13},{12,8},{13,15},{14,12},{15,11... | collective-permute-start | bytes 245768 | tf_op jit(solution)/shard_map/ppermute | solution.py:360
  22.2 40.2 %collective-permute-start.22 = (bf16[1,2048,768]{2,1,0:T(8,128)(2,1)S(1)}, bf16[1,2048,768]{2,1,0:T(8,128)(2,1)S(1)}, u32[]{:S(2)}, u32[]{:S(2)}) collective-permute-start(bf16[1,2048,768]{2,1,0:T(8,128)(2,1)S(1)} %copy-done.6), channel_id=1, source_target_pairs={{0,1},{1,0},{2,3},{3,2},{4,5},{5,4},{6,7},{7,6},{8,9},{9,8},{10,11... | collective-permute-start | bytes 9437192 | tf_op jit(solution)/shard_map/ppermute | solution.py:363
  22.6 39.8 %collective-permute-start.23 = (bf16[1,2048,768]{2,1,0:T(8,128)(2,1)S(1)}, bf16[1,2048,768]{2,1,0:T(8,128)(2,1)S(1)}, u32[]{:S(2)}, u32[]{:S(2)}) collective-permute-start(bf16[1,2048,768]{2,1,0:T(8,128)(2,1)S(1)} %copy-done.7), channel_id=1, source_target_pairs={{0,1},{1,0},{2,3},{3,2},{4,5},{5,4},{6,7},{7,6},{8,9},{9,8},{10,11... | collective-permute-start | bytes 9437192 | tf_op jit(solution)/shard_map/ppermute | solution.py:363
  22.7 43.0 %copy-start.2 = (bf16[64,640]{1,0:T(8,128)(2,1)}, bf16[64,640]{1,0:T(8,128)(2,1)S(1)}, u32[]{:S(2)}) copy-start(bf16[64,640]{1,0:T(8,128)(2,1)S(1)} %collective-permute-done.6.refs_0_.refs_10_) | copy-start | bytes 245764
  22.7 43.0 %collective-permute-start.24 = (bf16[1,768,2048]{2,1,0:T(8,128)(2,1)}, bf16[1,768,2048]{2,1,0:T(8,128)(2,1)}, u32[]{:S(2)}, u32[]{:S(2)}) collective-permute-start(bf16[1,768,2048]{2,1,0:T(8,128)(2,1)} %refs_15_.1), channel_id=1, source_target_pairs={{0,1},{1,0},{2,3},{3,2},{4,5},{5,4},{6,7},{7,6},{8,9},{9,8},{10,11... | collective-permute-start | bytes 9437192 | tf_op jit(solution)/shard_map/ppermute | solution.py:363
  25.5 40.2 %copy-start.3 = (bf16[64,640]{1,0:T(8,128)(2,1)}, bf16[64,640]{1,0:T(8,128)(2,1)S(1)}, u32[]{:S(2)}) copy-start(bf16[64,640]{1,0:T(8,128)(2,1)S(1)} %collective-permute-done.7.refs_1_.refs_11_) | copy-start | bytes 245764
  25.5 5.0 %collective-permute-start.10 = (bf16[32,2048]{1,0:T(8,128)(2,1)S(1)}, bf16[32,2048]{1,0:T(8,128)(2,1)S(1)}, u32[]{:S(2)}, u32[]{:S(2)}) collective-permute-start(bf16[32,2048]{1,0:T(8,128)(2,1)S(1)} %get-tuple-element.34), channel_id=1, source_target_pairs={{0,4},{1,3},{4,8},{5,1},{8,12},{9,5},{12,14},{13,9},{14,10},{15,13... | collective-permute-start | bytes 393224 | tf_op jit(solution)/shard_map/ppermute | solution.py:360
  26.1 5.8 %collective-permute-start.5 = (bf16[32,2048]{1,0:T(8,128)(2,1)S(1)}, bf16[32,2048]{1,0:T(8,128)(2,1)S(1)}, u32[]{:S(2)}, u32[]{:S(2)}) collective-permute-start(bf16[32,2048]{1,0:T(8,128)(2,1)S(1)} %add_convert_fusion.10), channel_id=1, source_target_pairs={{0,4},{1,3},{4,8},{5,1},{8,12},{9,5},{12,14},{13,9},{14,10},{15,13... | collective-permute-start | bytes 393224 | tf_op jit(solution)/shard_map/ppermute | solution.py:360
  30.5 5.0 %collective-permute-start.11 = (bf16[32,2048]{1,0:T(8,128)(2,1)S(1)}, bf16[32,2048]{1,0:T(8,128)(2,1)S(1)}, u32[]{:S(2)}, u32[]{:S(2)}) collective-permute-start(bf16[32,2048]{1,0:T(8,128)(2,1)S(1)} %add_convert_fusion.7), channel_id=1, source_target_pairs={{0,4},{1,3},{4,8},{5,1},{8,12},{9,5},{12,14},{13,9},{14,10},{15,13... | collective-permute-start | bytes 393224 | tf_op jit(solution)/shard_map/ppermute | solution.py:360
  31.9 5.0 %collective-permute-start.8 = (bf16[32,2048]{1,0:T(8,128)(2,1)S(1)}, bf16[32,2048]{1,0:T(8,128)(2,1)S(1)}, u32[]{:S(2)}, u32[]{:S(2)}) collective-permute-start(bf16[32,2048]{1,0:T(8,128)(2,1)S(1)} %add_convert_fusion.9), channel_id=1, source_target_pairs={{0,4},{1,3},{4,8},{5,1},{8,12},{9,5},{12,14},{13,9},{14,10},{15,13... | collective-permute-start | bytes 393224 | tf_op jit(solution)/shard_map/ppermute | solution.py:360
  35.6 5.0 %collective-permute-start.12 = (bf16[32,2048]{1,0:T(8,128)(2,1)S(1)}, bf16[32,2048]{1,0:T(8,128)(2,1)S(1)}, u32[]{:S(2)}, u32[]{:S(2)}) collective-permute-start(bf16[32,2048]{1,0:T(8,128)(2,1)S(1)} %add_convert_fusion.6), channel_id=1, source_target_pairs={{0,4},{1,3},{4,8},{5,1},{8,12},{9,5},{12,14},{13,9},{14,10},{15,13... | collective-permute-start | bytes 393224 | tf_op jit(solution)/shard_map/ppermute | solution.py:360
  36.9 5.0 %collective-permute-start.9 = (bf16[32,2048]{1,0:T(8,128)(2,1)S(1)}, bf16[32,2048]{1,0:T(8,128)(2,1)S(1)}, u32[]{:S(2)}, u32[]{:S(2)}) collective-permute-start(bf16[32,2048]{1,0:T(8,128)(2,1)S(1)} %add_convert_fusion.8), channel_id=1, source_target_pairs={{0,4},{1,3},{4,8},{5,1},{8,12},{9,5},{12,14},{13,9},{14,10},{15,13... | collective-permute-start | bytes 393224 | tf_op jit(solution)/shard_map/ppermute | solution.py:360
  40.6 1.4 %collective-permute-start.13 = (bf16[32,2048]{1,0:T(8,128)(2,1)S(1)}, bf16[32,2048]{1,0:T(8,128)(2,1)S(1)}, u32[]{:S(2)}, u32[]{:S(2)}) collective-permute-start(bf16[32,2048]{1,0:T(8,128)(2,1)S(1)} %collective-permute-done.12), channel_id=1, source_target_pairs={{0,1},{1,0},{2,3},{3,2},{4,5},{5,4},{6,7},{7,6},{8,9},{9,8},{10,11... | collective-permute-start | bytes 393224 | tf_op jit(solution)/shard_map/ppermute | solution.py:363
  42.3 23.4 %copy-start.10 = (bf16[32,2048]{1,0:T(8,128)(2,1)}, bf16[32,2048]{1,0:T(8,128)(2,1)S(1)}, u32[]{:S(2)}) copy-start(bf16[32,2048]{1,0:T(8,128)(2,1)S(1)} %fusion.2.refs_7_) | copy-start | bytes 393220
  42.3 1.4 %collective-permute-start.18 = (bf16[32,2048]{1,0:T(8,128)(2,1)S(1)}, bf16[32,2048]{1,0:T(8,128)(2,1)S(1)}, u32[]{:S(2)}, u32[]{:S(2)}) collective-permute-start(bf16[32,2048]{1,0:T(8,128)(2,1)S(1)} %fusion.2.refs_7_), channel_id=1, source_target_pairs={{0,1},{1,0},{2,3},{3,2},{4,5},{5,4},{6,7},{7,6},{8,9},{9,8},{10,11... | collective-permute-start | bytes 393224 | tf_op jit(solution)/shard_map/ppermute | solution.py:363
  42.5 5.0 %collective-permute-start.14 = (bf16[32,2048]{1,0:T(8,128)(2,1)S(1)}, bf16[32,2048]{1,0:T(8,128)(2,1)S(1)}, u32[]{:S(2)}, u32[]{:S(2)}) collective-permute-start(bf16[32,2048]{1,0:T(8,128)(2,1)S(1)} %fusion.2.refs_7_), channel_id=1, source_target_pairs={{0,2},{1,5},{4,0},{5,9},{8,4},{9,13},{12,8},{13,15},{14,12},{15,11... | collective-permute-start | bytes 393224 | tf_op jit(solution)/shard_map/ppermute | solution.py:360
  43.7 5.1 %collective-permute-start.19 = (bf16[32,2048]{1,0:T(8,128)(2,1)S(1)}, bf16[32,2048]{1,0:T(8,128)(2,1)S(1)}, u32[]{:S(2)}, u32[]{:S(2)}) collective-permute-start(bf16[32,2048]{1,0:T(8,128)(2,1)S(1)} %collective-permute-done.18), channel_id=1, source_target_pairs={{0,2},{1,5},{4,0},{5,9},{8,4},{9,13},{12,8},{13,15},{14,12},{15,11... | collective-permute-start | bytes 393224 | tf_op jit(solution)/shard_map/ppermute | solution.py:360
  47.4 18.3 %copy-start.11 = (bf16[32,2048]{1,0:T(8,128)(2,1)}, bf16[32,2048]{1,0:T(8,128)(2,1)S(1)}, u32[]{:S(2)}) copy-start(bf16[32,2048]{1,0:T(8,128)(2,1)S(1)} %collective-permute-done.14.refs_5_) | copy-start | bytes 393220
  47.4 5.0 %collective-permute-start.15 = (bf16[32,2048]{1,0:T(8,128)(2,1)S(1)}, bf16[32,2048]{1,0:T(8,128)(2,1)S(1)}, u32[]{:S(2)}, u32[]{:S(2)}) collective-permute-start(bf16[32,2048]{1,0:T(8,128)(2,1)S(1)} %collective-permute-done.14.refs_5_), channel_id=1, source_target_pairs={{0,2},{1,5},{4,0},{5,9},{8,4},{9,13},{12,8},{13,15},{14,12},{15,11... | collective-permute-start | bytes 393224 | tf_op jit(solution)/shard_map/ppermute | solution.py:360
  48.8 16.9 %copy-start.12 = (bf16[32,2048]{1,0:T(8,128)(2,1)}, bf16[32,2048]{1,0:T(8,128)(2,1)S(1)}, u32[]{:S(2)}) copy-start(bf16[32,2048]{1,0:T(8,128)(2,1)S(1)} %collective-permute-done.19.refs_6_) | copy-start | bytes 393220
  48.8 5.0 %collective-permute-start.20 = (bf16[32,2048]{1,0:T(8,128)(2,1)S(1)}, bf16[32,2048]{1,0:T(8,128)(2,1)S(1)}, u32[]{:S(2)}, u32[]{:S(2)}) collective-permute-start(bf16[32,2048]{1,0:T(8,128)(2,1)S(1)} %collective-permute-done.19.refs_6_), channel_id=1, source_target_pairs={{0,2},{1,5},{4,0},{5,9},{8,4},{9,13},{12,8},{13,15},{14,12},{15,11... | collective-permute-start | bytes 393224 | tf_op jit(solution)/shard_map/ppermute | solution.py:360
  52.4 13.3 %copy-start.13 = (bf16[32,2048]{1,0:T(8,128)(2,1)}, bf16[32,2048]{1,0:T(8,128)(2,1)S(1)}, u32[]{:S(2)}) copy-start(bf16[32,2048]{1,0:T(8,128)(2,1)S(1)} %collective-permute-done.15.refs_3_) | copy-start | bytes 393220
  52.4 5.0 %collective-permute-start.16 = (bf16[32,2048]{1,0:T(8,128)(2,1)S(1)}, bf16[32,2048]{1,0:T(8,128)(2,1)S(1)}, u32[]{:S(2)}, u32[]{:S(2)}) collective-permute-start(bf16[32,2048]{1,0:T(8,128)(2,1)S(1)} %collective-permute-done.15.refs_3_), channel_id=1, source_target_pairs={{0,2},{1,5},{4,0},{5,9},{8,4},{9,13},{12,8},{13,15},{14,12},{15,11... | collective-permute-start | bytes 393224 | tf_op jit(solution)/shard_map/ppermute | solution.py:360
  53.8 11.9 %copy-start.14 = (bf16[32,2048]{1,0:T(8,128)(2,1)}, bf16[32,2048]{1,0:T(8,128)(2,1)S(1)}, u32[]{:S(2)}) copy-start(bf16[32,2048]{1,0:T(8,128)(2,1)S(1)} %collective-permute-done.20.refs_4_) | copy-start | bytes 393220
  53.8 5.0 %collective-permute-start.21 = (bf16[32,2048]{1,0:T(8,128)(2,1)S(1)}, bf16[32,2048]{1,0:T(8,128)(2,1)S(1)}, u32[]{:S(2)}, u32[]{:S(2)}) collective-permute-start(bf16[32,2048]{1,0:T(8,128)(2,1)S(1)} %collective-permute-done.20.refs_4_), channel_id=1, source_target_pairs={{0,2},{1,5},{4,0},{5,9},{8,4},{9,13},{12,8},{13,15},{14,12},{15,11... | collective-permute-start | bytes 393224 | tf_op jit(solution)/shard_map/ppermute | solution.py:360
  57.4 8.4 %copy-start.15 = (bf16[32,2048]{1,0:T(8,128)(2,1)}, bf16[32,2048]{1,0:T(8,128)(2,1)S(1)}, u32[]{:S(2)}) copy-start(bf16[32,2048]{1,0:T(8,128)(2,1)S(1)} %collective-permute-done.16.refs_1_) | copy-start | bytes 393220
  57.4 5.0 %collective-permute-start.17 = (bf16[32,2048]{1,0:T(8,128)(2,1)S(1)}, bf16[32,2048]{1,0:T(8,128)(2,1)S(1)}, u32[]{:S(2)}, u32[]{:S(2)}) collective-permute-start(bf16[32,2048]{1,0:T(8,128)(2,1)S(1)} %collective-permute-done.16.refs_1_), channel_id=1, source_target_pairs={{0,2},{1,5},{4,0},{5,9},{8,4},{9,13},{12,8},{13,15},{14,12},{15,11... | collective-permute-start | bytes 393224 | tf_op jit(solution)/shard_map/ppermute | solution.py:360
  58.8 7.0 %copy-start.16 = (bf16[32,2048]{1,0:T(8,128)(2,1)}, bf16[32,2048]{1,0:T(8,128)(2,1)S(1)}, u32[]{:S(2)}) copy-start(bf16[32,2048]{1,0:T(8,128)(2,1)S(1)} %collective-permute-done.21.refs_2_) | copy-start | bytes 393220
  62.3 3.4 %copy-start.17 = (bf16[32,2048]{1,0:T(8,128)(2,1)}, bf16[32,2048]{1,0:T(8,128)(2,1)S(1)}, u32[]{:S(2)}) copy-start(bf16[32,2048]{1,0:T(8,128)(2,1)S(1)} %collective-permute-done.17.refs_0_) | copy-start | bytes 393220
  62.3 1.6 %copy-start.8 = (bf16[1,2048,768]{2,1,0:T(8,128)(2,1)}, bf16[1,2048,768]{2,1,0:T(8,128)(2,1)S(1)}, u32[]{:S(2)}) copy-start(bf16[1,2048,768]{2,1,0:T(8,128)(2,1)S(1)} %collective-permute-done.22.refs_16_) | copy-start | bytes 9437188
  64.0 1.7 %copy-start.9 = (bf16[1,2048,768]{2,1,0:T(8,128)(2,1)}, bf16[1,2048,768]{2,1,0:T(8,128)(2,1)S(1)}, u32[]{:S(2)}) copy-start(bf16[1,2048,768]{2,1,0:T(8,128)(2,1)S(1)} %collective-permute-done.23.refs_17_) | copy-start | bytes 9437188
  81.2 5.2 %collective-permute-start.25 = (bf16[32,2048]{1,0:T(8,128)(2,1)}, bf16[32,2048]{1,0:T(8,128)(2,1)S(1)}, u32[]{:S(2)}, u32[]{:S(2)}) collective-permute-start(bf16[32,2048]{1,0:T(8,128)(2,1)} %get-tuple-element.37), channel_id=1, source_target_pairs={{0,4},{1,3},{4,8},{5,1},{8,12},{9,5},{12,14},{13,9},{14,10},{15,13... | collective-permute-start | bytes 393224 | tf_op jit(solution)/shard_map/ppermute | solution.py:360
  81.8 6.2 %collective-permute-start.29 = (bf16[32,2048]{1,0:T(8,128)(2,1)}, bf16[32,2048]{1,0:T(8,128)(2,1)S(1)}, u32[]{:S(2)}, u32[]{:S(2)}) collective-permute-start(bf16[32,2048]{1,0:T(8,128)(2,1)} %get-tuple-element.42), channel_id=1, source_target_pairs={{0,4},{1,3},{4,8},{5,1},{8,12},{9,5},{12,14},{13,9},{14,10},{15,13... | collective-permute-start | bytes 393224 | tf_op jit(solution)/shard_map/ppermute | solution.py:360
  87.4 5.0 %collective-permute-start.26 = (bf16[32,2048]{1,0:T(8,128)(2,1)S(1)}, bf16[32,2048]{1,0:T(8,128)(2,1)S(1)}, u32[]{:S(2)}, u32[]{:S(2)}) collective-permute-start(bf16[32,2048]{1,0:T(8,128)(2,1)S(1)} %add_convert_fusion.4), channel_id=1, source_target_pairs={{0,4},{1,3},{4,8},{5,1},{8,12},{9,5},{12,14},{13,9},{14,10},{15,13... | collective-permute-start | bytes 393224 | tf_op jit(solution)/shard_map/ppermute | solution.py:360
  89.0 5.0 %collective-permute-start.30 = (bf16[32,2048]{1,0:T(8,128)(2,1)S(1)}, bf16[32,2048]{1,0:T(8,128)(2,1)S(1)}, u32[]{:S(2)}, u32[]{:S(2)}) collective-permute-start(bf16[32,2048]{1,0:T(8,128)(2,1)S(1)} %add_convert_fusion.1), channel_id=1, source_target_pairs={{0,4},{1,3},{4,8},{5,1},{8,12},{9,5},{12,14},{13,9},{14,10},{15,13... | collective-permute-start | bytes 393224 | tf_op jit(solution)/shard_map/ppermute | solution.py:360
  93.4 5.0 %collective-permute-start.27 = (bf16[32,2048]{1,0:T(8,128)(2,1)S(1)}, bf16[32,2048]{1,0:T(8,128)(2,1)S(1)}, u32[]{:S(2)}, u32[]{:S(2)}) collective-permute-start(bf16[32,2048]{1,0:T(8,128)(2,1)S(1)} %add_convert_fusion.3), channel_id=1, source_target_pairs={{0,4},{1,3},{4,8},{5,1},{8,12},{9,5},{12,14},{13,9},{14,10},{15,13... | collective-permute-start | bytes 393224 | tf_op jit(solution)/shard_map/ppermute | solution.py:360
  95.0 5.0 %collective-permute-start.31 = (bf16[32,2048]{1,0:T(8,128)(2,1)S(1)}, bf16[32,2048]{1,0:T(8,128)(2,1)S(1)}, u32[]{:S(2)}, u32[]{:S(2)}) collective-permute-start(bf16[32,2048]{1,0:T(8,128)(2,1)S(1)} %add_convert_fusion), channel_id=1, source_target_pairs={{0,4},{1,3},{4,8},{5,1},{8,12},{9,5},{12,14},{13,9},{14,10},{15,13... | collective-permute-start | bytes 393224 | tf_op jit(solution)/shard_map/ppermute | solution.py:360
  99.4 5.0 %collective-permute-start.28 = (bf16[32,2048]{1,0:T(8,128)(2,1)S(1)}, bf16[32,2048]{1,0:T(8,128)(2,1)S(1)}, u32[]{:S(2)}, u32[]{:S(2)}) collective-permute-start(bf16[32,2048]{1,0:T(8,128)(2,1)S(1)} %add_convert_fusion.2), channel_id=1, source_target_pairs={{0,4},{1,3},{4,8},{5,1},{8,12},{9,5},{12,14},{13,9},{14,10},{15,13... | collective-permute-start | bytes 393224 | tf_op jit(solution)/shard_map/ppermute | solution.py:360
  100.0 4.4 %collective-permute-start.32 = (bf16[32,2048]{1,0:T(8,128)(2,1)S(1)}, bf16[32,2048]{1,0:T(8,128)(2,1)S(1)}, u32[]{:S(2)}, u32[]{:S(2)}) collective-permute-start(bf16[32,2048]{1,0:T(8,128)(2,1)S(1)} %collective-permute-done.31), channel_id=1, source_target_pairs={{0,1},{1,0},{2,3},{3,2},{4,5},{5,4},{6,7},{7,6},{8,9},{9,8},{10,11... | collective-permute-start | bytes 393224 | tf_op jit(solution)/shard_map/ppermute | solution.py:363

commit v5 on v4

--- a/solution.py
+++ b/solution.py
@@ -238,103 +238,77 @@
     )(*pieces, own, other)
 
 
-def expert_kernel(tiles, hops, local, local_experts, *refs):
-    pieces = 2 * hops
-    piece_refs, refs = refs[:pieces], refs[pieces:]
-    digit_refs, refs = refs[: hops + 1], refs[hops + 1 :]
-    own_refs, other_refs, refs = refs[:3], refs[3:6], refs[6:]
-    out_refs, (x_ref, gates_ref, inner_ref) = refs[:pieces], refs[pieces:]
-    step = pl.program_id(0)
-    tile = own_refs[0].shape[2]
-
-    @pl.when(step == 0)
-    def _():
-        start = 0
-        for piece in piece_refs:
-            x_ref[start : start + piece.shape[0], :] = piece[...]
-            start += piece.shape[0]
-        core = lax.rem(lax.axis_index("rows"), 2)
-        chip_experts = 2 * local_experts
-        start = 0
-        for digits in digit_refs:
-            feats = digits.shape[1] - 128 * (-(-2 * chip_experts // 128))
-            taken = digits[:, feats:].astype(F32)
-
-            def gate(k):
-                high, low = taken[:, k : k + 1], taken[:, chip_experts + k : chip_experts + k + 1]
-                return (high * 16.0 + low) * gate_scale
-
-            first, second = gate(local), gate(local_experts + local)
-            size = digits.shape[0]
-            gates_ref[0, start : start + size, :] = jnp.where(core == 0, first, second)
-            gates_ref[1, start : start + size, :] = jnp.where(core == 0, second, first)
-            start += size
-
-    def raise_up(w_gate, w_up, which):
-        gate_proj = jnp.dot(x_ref[...], w_gate[0], preferred_element_type=F32)
-        raised = jnp.dot(x_ref[...], w_up[0], preferred_element_type=F32)
-        inner = jax.nn.silu(gate_proj) * raised * gates_ref[which]
-        span = pl.ds(pl.multiple_of(step * tile, tile), tile)
-        inner_ref[:, span] = inner.astype(BF16)
-
-    @pl.when(step < tiles)
-    def _():
-        raise_up(own_refs[0], own_refs[1], 0)
-
-    @pl.when((step >= tiles) & (step < 2 * tiles))
-    def _():
-        raise_up(other_refs[0], other_refs[1], 1)
-
-    @pl.when(step >= 2 * tiles)
-    def _():
-        depth, wide = own_refs[2].shape[1:]
+def expert_kernel(pieces, local, local_experts, *refs):
+    piece_refs, digits_ref, refs = refs[:pieces], refs[pieces], refs[pieces + 1 :]
+    weight_refs, refs = refs[:6], refs[6:]
+    out_refs, (x_ref, inner_ref) = refs[:pieces], refs[pieces:]
+    size = piece_refs[0].shape[0]
+    for index, piece in enumerate(piece_refs):
+        x_ref[index * size : (index + 1) * size, :] = piece[...]
+    core = lax.rem(lax.axis_index("rows"), 2)
+    chip_experts = 2 * local_experts
+    feats = digits_ref.shape[1] - 128 * (-(-2 * chip_experts // 128))
+    taken = digits_ref[:, feats:].astype(F32)
+
+    def gate(k):
+        high, low = taken[:, k : k + 1], taken[:, chip_experts + k : chip_experts + k + 1]
+        return (high * 16.0 + low) * gate_scale
+
+    first, second = gate(local), gate(local_experts + local)
+    gates = (jnp.where(core == 0, first, second), jnp.where(core == 0, second, first))
+    hidden_units, width = weight_refs[2].shape[1:]
+    tile = 256
+    for which in range(2):
+        w_gate, w_up = weight_refs[3 * which], weight_refs[3 * which + 1]
+        for start in range(0, hidden_units, tile):
+            gate_proj = jnp.dot(
+                x_ref[...], w_gate[local, :, start : start + tile], preferred_element_type=F32
+            )
+            raised = jnp.dot(
+                x_ref[...], w_up[local, :, start : start + tile], preferred_element_type=F32
+            )
+            inner = jax.nn.silu(gate_proj) * raised * gates[which]
+            place = which * hidden_units + start
+            inner_ref[:, place : place + tile] = inner.astype(BF16)
+    tile = 512
+    for start in range(0, width, tile):
         done = jnp.dot(
-            inner_ref[:, :depth], own_refs[2][0], preferred_element_type=F32
-        ) + jnp.dot(inner_ref[:, depth:], other_refs[2][0], preferred_element_type=F32)
-        span = pl.ds(pl.multiple_of((step - 2 * tiles) * wide, wide), wide)
-        start = 0
-        for out in out_refs:
-            out[:, span] = done[start : start + out.shape[0]].astype(out.dtype)
-            start += out.shape[0]
+            inner_ref[:, :hidden_units],
+            weight_refs[2][local, :, start : start + tile],
+            preferred_element_type=F32,
+        ) + jnp.dot(
+            inner_ref[:, hidden_units:],
+            weight_refs[5][local, :, start : start + tile],
+            preferred_element_type=F32,
+        )
+        for index, out in enumerate(out_refs):
+            out[:, start : start + tile] = done[index * size : (index + 1) * size].astype(
+                out.dtype
+            )
 
 
 def experts(pieces, kinds, digits, own, other, local):
     local_experts, width, hidden_units = own[0].shape
     rows = sum(piece.shape[0] for piece in pieces)
-    tile, wide = 256, 512
-    tiles, columns = hidden_units // tile, width // wide
-
-    def specs(turn):
-        def place(t):
-            return jnp.clip(t - turn * tiles, 0, tiles - 1)
-
-        up = pl.BlockSpec((1, width, tile), lambda t: (local, 0, place(t)))
-        down = pl.BlockSpec(
-            (1, hidden_units, wide), lambda t: (local, 0, jnp.maximum(t - 2 * tiles, 0))
-        )
-        return [up, up, down]
-
     return pl.pallas_call(
-        functools.partial(expert_kernel, tiles, len(pieces) // 2, local, local_experts),
+        functools.partial(expert_kernel, len(pieces), local, local_experts),
         out_shape=tuple(
             jax.ShapeDtypeStruct((piece.shape[0], width), kind)
             for piece, kind in zip(pieces, kinds)
         ),
-        grid=(2 * tiles + columns,),
-        in_specs=[VMEM] * (len(pieces) + len(digits)) + specs(0) + specs(1),
+        in_specs=[VMEM] * (len(pieces) + 7),
         out_specs=(VMEM,) * len(pieces),
         scratch_shapes=[
             pltpu.VMEM((rows, width), BF16),
-            pltpu.VMEM((2, rows, 1), F32),
             pltpu.VMEM((rows, 2 * hidden_units), BF16),
         ],
-        compiler_params=pltpu.CompilerParams(vmem_limit_bytes=56 * 1024 * 1024),
+        compiler_params=pltpu.CompilerParams(vmem_limit_bytes=16 * 1024 * 1024),
         cost_estimate=pl.CostEstimate(
-            flops=12 * rows * hidden_units * width,
-            bytes_accessed=12 * hidden_units * width,
+            flops=24 * rows * hidden_units * width,
+            bytes_accessed=rows * width,
             transcendentals=2 * rows * hidden_units,
         ),
-    )(*pieces, *digits, *own, *other)
+    )(*pieces, digits, *own, *other)
 
 
 def on_device(
@@ -401,29 +375,21 @@
     residual = (hidden.astype(F32) + ring_sums(partial)).astype(BF16)
     normed = rms_scale(residual.astype(F32), norm_gain).astype(BF16)
 
+    def serve(pieces, kinds, digits):
+        total = None
+        for local in range(local_experts):
+            plain = kinds if local_experts == 1 else [F32] * len(kinds)
+            served = experts(pieces, plain, digits, own_experts, other_experts, local)
+            total = served if local == 0 else [a + b for a, b in zip(total, served)]
+        return [part.astype(kind) for part, kind in zip(total, kinds)]
+
     own, other = normed, swapped(normed)
-    pieces = [own]
-    for offset in range(1, hops + 1):
-        own = pass_on(own, -1)
-        pieces = [own] + pieces
-        if offset < hops:
-            other = pass_on(other, -1)
-            pieces = [own, other] + pieces[1:]
-
-    digits = [arrived[offset] for offset in range(hops, -1, -1)]
-    total = None
-    for local in range(local_experts):
-        plain = [F32] * (2 * hops)
-        served = experts(
-            pieces,
-            kinds if local_experts == 1 else plain,
-            digits,
-            own_experts,
-            other_experts,
-            local,
-        )
-        total = served if local == 0 else [a + b for a, b in zip(total, served)]
-    total = [part.astype(kind) for part, kind in zip(total, kinds)]
+    total = serve([own], [F32], arrived[0])
+    for offset in range(1, hops):
+        own, other = pass_on(own, -1), pass_on(other, -1)
+        kinds = [F32, BF16 if offset == hops - 1 else F32]
+        total = serve([own, other], kinds, arrived[offset]) + total
+    total = serve([pass_on(own, -1)], [BF16], arrived[hops]) + total
     return (residual.astype(F32) + ring_sums(total)).astype(BF16)
 
 

time: 107 us -> 96.8 us (0.905)
  waiting for transfers between devices: 45.4 us -> 29.6 us
  starting transfers between devices: 27.7 us -> 39.1 us
  other arithmetic: 7.03 us -> 1.32 us
  Pallas kernels: 21.5 us -> 25.4 us
  local copies, waits for them, and re-layouts: 4.22 us -> 0.88 us
    ppermute x25, waiting for transfers between devices: 44.8 us -> 29.5 us  [pass_on(): return lax.ppermute(array, 'rows', toward(step))]
    ppermute x25, starting transfers between devices: 26 us -> 38 us  [pass_on(): return lax.ppermute(array, 'rows', toward(step))]
    unnamed x40 -> x14, local copies, waits for them, and re-layouts: 3.38 us -> 0.03 us
    convert_element_type x6, other arithmetic: 3.03 us -> 0.17 us  [ring_sums(): own = (pass_on(own, 1).astype(F32) + partial[spot]).astype(BF16)]
    pallas_call x2, Pallas kernels: 1 us -> 3.44 us  [project(): pl.pallas_call(functools.partial(project_kernel, len(pieces)), out_shape=...]
    convert_element_type x4, other arithmetic: 2.02 us -> 0.11 us  [ring_sums(): other = (pass_on(other, 1).astype(F32) + partial[spot + 1]).astype(BF16)]
    pallas_call x1 -> x5, Pallas kernels: 15.4 us -> 16.9 us  [experts(): pl.pallas_call(functools.partial(expert_kernel, len(pieces), local, local...]
  transfers between devices with their start and end apart: 33 -> 33, of which waited for: 20 -> 15; matrix products, arithmetic and copies ran while one was open for 6% -> 1% of each run, Pallas kernels for 6% -> 26%
where the time goes in v5:
time: 96.8 us; the launch traced here: 96.5 us
  starting transfers between devices  39.1 us (40%)
  waiting for transfers between devices  29.6 us (31%)
  Pallas kernels  25.4 us (26%)
  other arithmetic  1.32 us (1%)
    ppermute x25, starting transfers between devices, pass_on(): return lax.ppermute(array, 'rows', toward(step))  38 us
    ppermute x25, waiting for transfers between devices, pass_on(): return lax.ppermute(array, 'rows', toward(step))  29.5 us
    pallas_call x5, Pallas kernels, experts(): pl.pallas_call(functools.partial(expert_kernel, len(pieces), local, local...  16.9 us
    pallas_call x1, Pallas kernels, attend(): pl.pallas_call(functools.partial(attend_kernel, chips, hops, chip_experts...  5.06 us
    pallas_call x2, Pallas kernels, project(): pl.pallas_call(functools.partial(project_kernel, len(pieces)), out_shape=...  3.44 us
  transfers between devices with their start and end apart: 33, of which 15 were waited for; matrix products, arithmetic and copies ran while one was open for 1% of the time, Pallas kernels for 26%

profile of v5, /device:TPU:0, one launch (start us, length us, event | category | flops | bytes accessed | tf_op | source)
XLA Modules:
  0.0 96.5 jit_solution(4060387923395314620)
XLA Ops:
  0.0 0.5 collective-permute-start.3
  0.5 5.1 %shard_map.118 = (bf16[32,640]{1,0:T(8,128)(2,1)}, bf16[3,32,640]{2,1,0:T(8,128)(2,1)}, bf16[3,32,640]{2,1,0:T(8,128)(2,1)}, bf16[32,640]{1,0:T(8,128)(2,1)}) custom-call(s32[32]{0:T(128)} %lengths_ref.1, bf16[32,4096]{1,0:T(8,128)(2,1)} %q_ref.1, bf16[32,2,128,128]{3,2,1,0:T(8,128)(2,1)} %k_ref.1, bf16[32,2,128,128]{3,2,1,0:T(8,128)(2,1)} %v_ref.1, ...), custom_call_target="tpu_custom_call" | custom-call | flops 67108864 | bytes 4194304 | tf_op jit(solution)/shard_map/pallas_call | solution.py:168
  5.5 0.1 collective-permute-start.1
  5.6 6.0 %collective-permute-start = (bf16[32,640]{1,0:T(8,128)(2,1)}, bf16[32,640]{1,0:T(8,128)(2,1)S(1)}, u32[]{:S(2)}, u32[]{:S(2)}) collective-permute-start(bf16[32,640]{1,0:T(8,128)(2,1)} %get-tuple-element.23), channel_id=1, source_target_pairs={{0,14},{1,15},{4,10},{5,11},{8,6},{9,7},{12,2},{13,3},{14,0},{15,1... | collective-permute-start | bytes 122888 | tf_op jit(solution)/shard_map/ppermute | solution.py:334
  11.6 0.8 slice_bitcast_fusion.5
  12.5 0.1 collective-permute-start.2
  12.6 0.0 copy-start.5
  12.6 0.9 collective-permute-start.7
  13.5 0.4 collective-permute-done.refs_0_.refs_1_
  13.9 5.0 %collective-permute-done.2.refs_1_.refs_2_ = bf16[64,640]{1,0:T(8,128)(2,1)S(1)} collective-permute-done((bf16[64,640]{1,0:T(8,128)(2,1)S(1)}, bf16[64,640]{1,0:T(8,128)(2,1)S(1)}, u32[]{:S(2)}, u32[]{:S(2)}) %collective-permute-start.2) | collective-permute-done | bytes 81952 | tf_op jit(solution)/shard_map/ppermute | solution.py:334
  18.9 1.7 %shard_map.119 = (bf16[32,2048]{1,0:T(8,128)(2,1)S(1)}, f32[32,2048]{1,0:T(8,128)S(1)}, bf16[32,2048]{1,0:T(8,128)(2,1)S(1)}) custom-call(bf16[32,640]{1,0:T(8,128)(2,1)S(1)} %collective-permute-done.refs_0_.refs_1_, bf16[64,640]{1,0:T(8,128)(2,1)S(1)} %collective-permute-done.2.refs_1_.refs_2_, bf16[256,2048]{1,0:T(8,128)(2,1)S(1)} %copy-done.3, ...), custom_call_target="tpu_custom_call" | custom-call | flops 201326592 | bytes 2097152 | tf_op jit(solution)/shard_map/pallas_call | solution.py:226
  20.6 0.0 copy-start.6
  20.6 0.0 copy-start.2
  20.6 0.4 collective-permute-start.4
  21.0 1.7 %collective-permute-start.6 = (bf16[64,640]{1,0:T(8,128)(2,1)S(1)}, bf16[64,640]{1,0:T(8,128)(2,1)S(1)}, u32[]{:S(2)}, u32[]{:S(2)}) collective-permute-start(bf16[64,640]{1,0:T(8,128)(2,1)S(1)} %pad_maximum_fusion.1), channel_id=1, source_target_pairs={{0,6},{1,9},{4,2},{5,13},{8,0},{9,15},{12,4},{13,11},{14,8},{15,7}... | collective-permute-start | bytes 245768 | tf_op jit(solution)/shard_map/ppermute | solution.py:334
  22.7 0.5 collective-permute-start.19
  23.3 0.1 collective-permute-start.20
  23.3 3.7 %collective-permute-done.6.refs_0_.refs_2_ = bf16[64,640]{1,0:T(8,128)(2,1)S(1)} collective-permute-done((bf16[64,640]{1,0:T(8,128)(2,1)S(1)}, bf16[64,640]{1,0:T(8,128)(2,1)S(1)}, u32[]{:S(2)}, u32[]{:S(2)}) %collective-permute-start.6) | collective-permute-done | bytes 81952 | tf_op jit(solution)/shard_map/ppermute | solution.py:334
  27.0 0.0 collective-permute-start.10
  27.1 1.7 %shard_map.120 = (f32[32,2048]{1,0:T(8,128)S(1)}, f32[32,2048]{1,0:T(8,128)S(1)}, f32[32,2048]{1,0:T(8,128)S(1)}, f32[32,2048]{1,0:T(8,128)S(1)}, f32[32,2048]{1,0:T(8,128)S(1)}) custom-call(bf16[64,640]{1,0:T(8,128)(2,1)S(1)} %collective-permute-done.6.refs_0_.refs_2_, bf16[64,640]{1,0:T(8,128)(2,1)S(1)} %collective-permute-done.7.refs_1_.refs_2_, ...), custom_call_target="tpu_custom_call" | custom-call | flops 335544320 | bytes 2097152 | tf_op jit(solution)/shard_map/pallas_call | solution.py:226
  28.9 1.6 %collective-permute-start.5 = (bf16[32,2048]{1,0:T(8,128)(2,1)S(1)}, bf16[32,2048]{1,0:T(8,128)(2,1)S(1)}, u32[]{:S(2)}, u32[]{:S(2)}) collective-permute-start(bf16[32,2048]{1,0:T(8,128)(2,1)S(1)} %add_convert_fusion.10), channel_id=1, source_target_pairs={{0,4},{1,3},{4,8},{5,1},{8,12},{9,5},{12,14},{13,9},{14,10},{15,13... | collective-permute-start | bytes 393224 | tf_op jit(solution)/shard_map/ppermute | solution.py:334
  30.5 1.5 %collective-permute-done.10 = bf16[32,2048]{1,0:T(8,128)(2,1)S(1)} collective-permute-done((bf16[32,2048]{1,0:T(8,128)(2,1)S(1)}, bf16[32,2048]{1,0:T(8,128)(2,1)S(1)}, u32[]{:S(2)}, u32[]{:S(2)}) %collective-permute-start.10) | collective-permute-done | bytes 131104 | tf_op jit(solution)/shard_map/ppermute | solution.py:334
  32.0 0.1 collective-permute-start.11
  32.1 1.8 %collective-permute-done.5 = bf16[32,2048]{1,0:T(8,128)(2,1)S(1)} collective-permute-done((bf16[32,2048]{1,0:T(8,128)(2,1)S(1)}, bf16[32,2048]{1,0:T(8,128)(2,1)S(1)}, u32[]{:S(2)}, u32[]{:S(2)}) %collective-permute-start.5) | collective-permute-done | bytes 131104 | tf_op jit(solution)/shard_map/ppermute | solution.py:334
  33.9 1.6 %collective-permute-start.8 = (bf16[32,2048]{1,0:T(8,128)(2,1)S(1)}, bf16[32,2048]{1,0:T(8,128)(2,1)S(1)}, u32[]{:S(2)}, u32[]{:S(2)}) collective-permute-start(bf16[32,2048]{1,0:T(8,128)(2,1)S(1)} %add_convert_fusion.9), channel_id=1, source_target_pairs={{0,4},{1,3},{4,8},{5,1},{8,12},{9,5},{12,14},{13,9},{14,10},{15,13... | collective-permute-start | bytes 393224 | tf_op jit(solution)/shard_map/ppermute | solution.py:334
  35.5 1.5 %collective-permute-done.11 = bf16[32,2048]{1,0:T(8,128)(2,1)S(1)} collective-permute-done((bf16[32,2048]{1,0:T(8,128)(2,1)S(1)}, bf16[32,2048]{1,0:T(8,128)(2,1)S(1)}, u32[]{:S(2)}, u32[]{:S(2)}) %collective-permute-start.11) | collective-permute-done | bytes 131104 | tf_op jit(solution)/shard_map/ppermute | solution.py:334
  37.1 0.1 collective-permute-start.12
  37.2 1.8 %collective-permute-done.8 = bf16[32,2048]{1,0:T(8,128)(2,1)S(1)} collective-permute-done((bf16[32,2048]{1,0:T(8,128)(2,1)S(1)}, bf16[32,2048]{1,0:T(8,128)(2,1)S(1)}, u32[]{:S(2)}, u32[]{:S(2)}) %collective-permute-start.8) | collective-permute-done | bytes 131104 | tf_op jit(solution)/shard_map/ppermute | solution.py:334
  39.0 1.6 %collective-permute-start.9 = (bf16[32,2048]{1,0:T(8,128)(2,1)S(1)}, bf16[32,2048]{1,0:T(8,128)(2,1)S(1)}, u32[]{:S(2)}, u32[]{:S(2)}) collective-permute-start(bf16[32,2048]{1,0:T(8,128)(2,1)S(1)} %add_convert_fusion.8), channel_id=1, source_target_pairs={{0,4},{1,3},{4,8},{5,1},{8,12},{9,5},{12,14},{13,9},{14,10},{15,13... | collective-permute-start | bytes 393224 | tf_op jit(solution)/shard_map/ppermute | solution.py:334
  40.6 1.5 %collective-permute-done.12 = bf16[32,2048]{1,0:T(8,128)(2,1)S(1)} collective-permute-done((bf16[32,2048]{1,0:T(8,128)(2,1)S(1)}, bf16[32,2048]{1,0:T(8,128)(2,1)S(1)}, u32[]{:S(2)}, u32[]{:S(2)}) %collective-permute-start.12) | collective-permute-done | bytes 131104 | tf_op jit(solution)/shard_map/ppermute | solution.py:334
  42.1 1.9 %collective-permute-done.9 = bf16[32,2048]{1,0:T(8,128)(2,1)S(1)} collective-permute-done((bf16[32,2048]{1,0:T(8,128)(2,1)S(1)}, bf16[32,2048]{1,0:T(8,128)(2,1)S(1)}, u32[]{:S(2)}, u32[]{:S(2)}) %collective-permute-start.9) | collective-permute-done | bytes 131104 | tf_op jit(solution)/shard_map/ppermute | solution.py:334
  44.0 0.2 fusion
  44.2 0.1 fusion.2.refs_0_
  44.3 2.0 %collective-permute-start.14 = (bf16[32,2048]{1,0:T(8,128)(2,1)S(1)}, bf16[32,2048]{1,0:T(8,128)(2,1)S(1)}, u32[]{:S(2)}, u32[]{:S(2)}) collective-permute-start(bf16[32,2048]{1,0:T(8,128)(2,1)S(1)} %fusion.2.refs_0_), channel_id=1, source_target_pairs={{0,2},{1,5},{4,0},{5,9},{8,4},{9,13},{12,8},{13,15},{14,12},{15,11... | collective-permute-start | bytes 393224 | tf_op jit(solution)/shard_map/ppermute | solution.py:334
  46.3 3.0 %collective-permute-done.14.refs_0_ = bf16[32,2048]{1,0:T(8,128)(2,1)S(1)} collective-permute-done((bf16[32,2048]{1,0:T(8,128)(2,1)S(1)}, bf16[32,2048]{1,0:T(8,128)(2,1)S(1)}, u32[]{:S(2)}, u32[]{:S(2)}) %collective-permute-start.14) | collective-permute-done | bytes 131104 | tf_op jit(solution)/shard_map/ppermute | solution.py:334
  49.3 2.0 %collective-permute-start.15 = (bf16[32,2048]{1,0:T(8,128)(2,1)S(1)}, bf16[32,2048]{1,0:T(8,128)(2,1)S(1)}, u32[]{:S(2)}, u32[]{:S(2)}) collective-permute-start(bf16[32,2048]{1,0:T(8,128)(2,1)S(1)} %collective-permute-done.14.refs_0_), channel_id=1, source_target_pairs={{0,2},{1,5},{4,0},{5,9},{8,4},{9,13},{12,8},{13,15},{14,12},{15,11... | collective-permute-start | bytes 393224 | tf_op jit(solution)/shard_map/ppermute | solution.py:334
  51.3 1.9 %collective-permute-start.23 = (bf16[32,2048]{1,0:T(8,128)(2,1)S(1)}, bf16[32,2048]{1,0:T(8,128)(2,1)S(1)}, u32[]{:S(2)}, u32[]{:S(2)}) collective-permute-start(bf16[32,2048]{1,0:T(8,128)(2,1)S(1)} %collective-permute-done.22), channel_id=1, source_target_pairs={{0,2},{1,5},{4,0},{5,9},{8,4},{9,13},{12,8},{13,15},{14,12},{15,11... | collective-permute-start | bytes 393224 | tf_op jit(solution)/shard_map/ppermute | solution.py:334
  53.2 1.1 %collective-permute-done.15.refs_0_ = bf16[32,2048]{1,0:T(8,128)(2,1)S(1)} collective-permute-done((bf16[32,2048]{1,0:T(8,128)(2,1)S(1)}, bf16[32,2048]{1,0:T(8,128)(2,1)S(1)}, u32[]{:S(2)}, u32[]{:S(2)}) %collective-permute-start.15) | collective-permute-done | bytes 131104 | tf_op jit(solution)/shard_map/ppermute | solution.py:334
  54.3 2.0 %collective-permute-start.16 = (bf16[32,2048]{1,0:T(8,128)(2,1)S(1)}, bf16[32,2048]{1,0:T(8,128)(2,1)S(1)}, u32[]{:S(2)}, u32[]{:S(2)}) collective-permute-start(bf16[32,2048]{1,0:T(8,128)(2,1)S(1)} %collective-permute-done.15.refs_0_), channel_id=1, source_target_pairs={{0,2},{1,5},{4,0},{5,9},{8,4},{9,13},{12,8},{13,15},{14,12},{15,11... | collective-permute-start | bytes 393224 | tf_op jit(solution)/shard_map/ppermute | solution.py:334
  56.3 0.0 collective-permute-done.23.refs_1_
  56.3 1.9 %collective-permute-start.24 = (bf16[32,2048]{1,0:T(8,128)(2,1)S(1)}, bf16[32,2048]{1,0:T(8,128)(2,1)S(1)}, u32[]{:S(2)}, u32[]{:S(2)}) collective-permute-start(bf16[32,2048]{1,0:T(8,128)(2,1)S(1)} %collective-permute-done.23.refs_1_), channel_id=1, source_target_pairs={{0,2},{1,5},{4,0},{5,9},{8,4},{9,13},{12,8},{13,15},{14,12},{15,11... | collective-permute-start | bytes 393224 | tf_op jit(solution)/shard_map/ppermute | solution.py:334
  58.1 1.1 %collective-permute-done.16.refs_0_ = bf16[32,2048]{1,0:T(8,128)(2,1)S(1)} collective-permute-done((bf16[32,2048]{1,0:T(8,128)(2,1)S(1)}, bf16[32,2048]{1,0:T(8,128)(2,1)S(1)}, u32[]{:S(2)}, u32[]{:S(2)}) %collective-permute-start.16) | collective-permute-done | bytes 131104 | tf_op jit(solution)/shard_map/ppermute | solution.py:334
  59.3 2.0 %collective-permute-start.17 = (bf16[32,2048]{1,0:T(8,128)(2,1)S(1)}, bf16[32,2048]{1,0:T(8,128)(2,1)S(1)}, u32[]{:S(2)}, u32[]{:S(2)}) collective-permute-start(bf16[32,2048]{1,0:T(8,128)(2,1)S(1)} %collective-permute-done.16.refs_0_), channel_id=1, source_target_pairs={{0,2},{1,5},{4,0},{5,9},{8,4},{9,13},{12,8},{13,15},{14,12},{15,11... | collective-permute-start | bytes 393224 | tf_op jit(solution)/shard_map/ppermute | solution.py:334
  61.2 0.0 collective-permute-done.24.refs_1_
  61.2 1.9 %collective-permute-start.25 = (bf16[32,2048]{1,0:T(8,128)(2,1)S(1)}, bf16[32,2048]{1,0:T(8,128)(2,1)S(1)}, u32[]{:S(2)}, u32[]{:S(2)}) collective-permute-start(bf16[32,2048]{1,0:T(8,128)(2,1)S(1)} %collective-permute-done.24.refs_1_), channel_id=1, source_target_pairs={{0,2},{1,5},{4,0},{5,9},{8,4},{9,13},{12,8},{13,15},{14,12},{15,11... | collective-permute-start | bytes 393224 | tf_op jit(solution)/shard_map/ppermute | solution.py:334
  63.1 1.1 %collective-permute-done.17.refs_0_ = bf16[32,2048]{1,0:T(8,128)(2,1)S(1)} collective-permute-done((bf16[32,2048]{1,0:T(8,128)(2,1)S(1)}, bf16[32,2048]{1,0:T(8,128)(2,1)S(1)}, u32[]{:S(2)}, u32[]{:S(2)}) %collective-permute-start.17) | collective-permute-done | bytes 131104 | tf_op jit(solution)/shard_map/ppermute | solution.py:334
  64.3 3.4 %shard_map.121 = bf16[32,2048]{1,0:T(8,128)(2,1)S(1)} custom-call(bf16[32,2048]{1,0:T(8,128)(2,1)S(1)} %collective-permute-done.17.refs_0_, bf16[32,640]{1,0:T(8,128)(2,1)S(1)} %collective-permute-done.refs_0_.refs_1_, bf16[1,2048,768]{2,1,0:T(8,128)(2,1)S(1)} %copy-done, bf16[1,2048,768]{2,1,0:T(8,128)(2,1)S(1)} %copy-done.1, ...), custom_call_target="tpu_custom_call" | custom-call | flops 1207959552 | bytes 65536 | tf_op jit(solution)/shard_map/pallas_call | solution.py:293
  67.6 1.5 %collective-permute-start.21 = (bf16[32,2048]{1,0:T(8,128)(2,1)S(1)}, bf16[32,2048]{1,0:T(8,128)(2,1)S(1)}, u32[]{:S(2)}, u32[]{:S(2)}) collective-permute-start(bf16[32,2048]{1,0:T(8,128)(2,1)S(1)} %shard_map.121), channel_id=1, source_target_pairs={{0,4},{1,3},{4,8},{5,1},{8,12},{9,5},{12,14},{13,9},{14,10},{15,13... | collective-permute-start | bytes 393224 | tf_op jit(solution)/shard_map/ppermute | solution.py:334
  69.2 3.4 %shard_map.122 = (f32[32,2048]{1,0:T(8,128)S(1)}, bf16[32,2048]{1,0:T(8,128)(2,1)S(1)}) custom-call(bf16[32,2048]{1,0:T(8,128)(2,1)S(1)} %collective-permute-done.16.refs_0_, bf16[32,2048]{1,0:T(8,128)(2,1)S(1)} %collective-permute-done.25.refs_1_, bf16[64,640]{1,0:T(8,128)(2,1)S(1)} %collective-permute-done.2.refs_1_.refs_2_, ...), custom_call_target="tpu_custom_call" | custom-call | flops 2415919104 | bytes 131072 | tf_op jit(solution)/shard_map/pallas_call | solution.py:293
  72.6 0.7 collective-permute-start.29
  73.2 3.4 %shard_map.123 = (f32[32,2048]{1,0:T(8,128)S(1)}, f32[32,2048]{1,0:T(8,128)S(1)}) custom-call(bf16[32,2048]{1,0:T(8,128)(2,1)S(1)} %collective-permute-done.15.refs_0_, bf16[32,2048]{1,0:T(8,128)(2,1)S(1)} %collective-permute-done.24.refs_1_, bf16[64,640]{1,0:T(8,128)(2,1)S(1)} %collective-permute-done.6.refs_0_.refs_2_, bf16[1,2048,768]{2,1,0:T(8,128)(2,1)S(1)} %copy-done, ...), custom_call_target="tpu_custom_call" | custom-call | flops 2415919104 | bytes 131072 | tf_op jit(solution)/shard_map/pallas_call | solution.py:293
  76.7 3.4 %shard_map.124 = (f32[32,2048]{1,0:T(8,128)S(1)}, f32[32,2048]{1,0:T(8,128)S(1)}) custom-call(bf16[32,2048]{1,0:T(8,128)(2,1)S(1)} %collective-permute-done.14.refs_0_, bf16[32,2048]{1,0:T(8,128)(2,1)S(1)} %collective-permute-done.23.refs_1_, bf16[64,640]{1,0:T(8,128)(2,1)S(1)} %collective-permute-done.7.refs_1_.refs_2_, bf16[1,2048,768]{2,1,0:T(8,128)(2,1)S(1)} %copy-done, ...), custom_call_target="tpu_custom_call" | custom-call | flops 2415919104 | bytes 131072 | tf_op jit(solution)/shard_map/pallas_call | solution.py:293
  80.1 2.2 %collective-permute-start.26 = (bf16[32,2048]{1,0:T(8,128)(2,1)S(1)}, bf16[32,2048]{1,0:T(8,128)(2,1)S(1)}, u32[]{:S(2)}, u32[]{:S(2)}) collective-permute-start(bf16[32,2048]{1,0:T(8,128)(2,1)S(1)} %add_convert_fusion.4), channel_id=1, source_target_pairs={{0,4},{1,3},{4,8},{5,1},{8,12},{9,5},{12,14},{13,9},{14,10},{15,13... | collective-permute-start | bytes 393224 | tf_op jit(solution)/shard_map/ppermute | solution.py:334
  82.4 0.1 collective-permute-start.30
  82.5 2.7 %collective-permute-done.26 = bf16[32,2048]{1,0:T(8,128)(2,1)S(1)} collective-permute-done((bf16[32,2048]{1,0:T(8,128)(2,1)S(1)}, bf16[32,2048]{1,0:T(8,128)(2,1)S(1)}, u32[]{:S(2)}, u32[]{:S(2)}) %collective-permute-start.26) | collective-permute-done | bytes 131104 | tf_op jit(solution)/shard_map/ppermute | solution.py:334
  85.2 2.2 %collective-permute-start.27 = (bf16[32,2048]{1,0:T(8,128)(2,1)S(1)}, bf16[32,2048]{1,0:T(8,128)(2,1)S(1)}, u32[]{:S(2)}, u32[]{:S(2)}) collective-permute-start(bf16[32,2048]{1,0:T(8,128)(2,1)S(1)} %add_convert_fusion.3), channel_id=1, source_target_pairs={{0,4},{1,3},{4,8},{5,1},{8,12},{9,5},{12,14},{13,9},{14,10},{15,13... | collective-permute-start | bytes 393224 | tf_op jit(solution)/shard_map/ppermute | solution.py:334
  87.4 0.0 collective-permute-done.30
  87.4 1.4 %collective-permute-start.31 = (bf16[32,2048]{1,0:T(8,128)(2,1)S(1)}, bf16[32,2048]{1,0:T(8,128)(2,1)S(1)}, u32[]{:S(2)}, u32[]{:S(2)}) collective-permute-start(bf16[32,2048]{1,0:T(8,128)(2,1)S(1)} %add_convert_fusion), channel_id=1, source_target_pairs={{0,4},{1,3},{4,8},{5,1},{8,12},{9,5},{12,14},{13,9},{14,10},{15,13... | collective-permute-start | bytes 393224 | tf_op jit(solution)/shard_map/ppermute | solution.py:334
  88.8 1.4 %collective-permute-done.27 = bf16[32,2048]{1,0:T(8,128)(2,1)S(1)} collective-permute-done((bf16[32,2048]{1,0:T(8,128)(2,1)S(1)}, bf16[32,2048]{1,0:T(8,128)(2,1)S(1)}, u32[]{:S(2)}, u32[]{:S(2)}) %collective-permute-start.27) | collective-permute-done | bytes 131104 | tf_op jit(solution)/shard_map/ppermute | solution.py:334
  90.2 2.2 %collective-permute-start.28 = (bf16[32,2048]{1,0:T(8,128)(2,1)S(1)}, bf16[32,2048]{1,0:T(8,128)(2,1)S(1)}, u32[]{:S(2)}, u32[]{:S(2)}) collective-permute-start(bf16[32,2048]{1,0:T(8,128)(2,1)S(1)} %add_convert_fusion.2), channel_id=1, source_target_pairs={{0,4},{1,3},{4,8},{5,1},{8,12},{9,5},{12,14},{13,9},{14,10},{15,13... | collective-permute-start | bytes 393224 | tf_op jit(solution)/shard_map/ppermute | solution.py:334
  92.5 0.0 collective-permute-done.31
  92.5 3.3 %shard_map.125 = f32[32,2048]{1,0:T(8,128)S(1)} custom-call(bf16[32,2048]{1,0:T(8,128)(2,1)S(1)} %fusion.2.refs_0_, bf16[32,640]{1,0:T(8,128)(2,1)S(1)} %copy-done.4, bf16[1,2048,768]{2,1,0:T(8,128)(2,1)S(1)} %copy-done, bf16[1,2048,768]{2,1,0:T(8,128)(2,1)S(1)} %copy-done.1, bf16[1,768,2048]{2,1,0:T(8,128)(2,1)S(1)} %copy-done.2, ...), custom_call_target="tpu_custom_call" | custom-call | flops 1207959552 | bytes 65536 | tf_op jit(solution)/shard_map/pallas_call | solution.py:293
  95.8 0.0 collective-permute-done.32
  95.8 0.7 fusion.3
  (43 shorter events, 0.4 us)
Async XLA Ops:
  0.0 18.9 %copy-start.3 = (bf16[256,2048]{1,0:T(8,128)(2,1)S(1)}, bf16[256,2048]{1,0:T(8,128)(2,1)}, u32[]{:S(2)}) copy-start(bf16[256,2048]{1,0:T(8,128)(2,1)} %refs_3_.6) | copy-start | bytes 3145732
  0.0 18.9 %collective-permute-start.3 = (bf16[256,2048]{1,0:T(8,128)(2,1)}, bf16[256,2048]{1,0:T(8,128)(2,1)}, u32[]{:S(2)}, u32[]{:S(2)}) collective-permute-start(bf16[256,2048]{1,0:T(8,128)(2,1)} %refs_3_.6), channel_id=1, source_target_pairs={{0,1},{1,0},{2,3},{3,2},{4,5},{5,4},{6,7},{7,6},{8,9},{9,8},{10,11... | collective-permute-start | bytes 3145736 | tf_op jit(solution)/shard_map/ppermute | solution.py:337
  0.5 22.3 %copy-start = (bf16[1,2048,768]{2,1,0:T(8,128)(2,1)S(1)}, bf16[1,2048,768]{2,1,0:T(8,128)(2,1)}, u32[]{:S(2)}) copy-start(bf16[1,2048,768]{2,1,0:T(8,128)(2,1)} %refs_2_.5) | copy-start | bytes 9437188
  0.5 22.3 %copy-start.1 = (bf16[1,2048,768]{2,1,0:T(8,128)(2,1)S(1)}, bf16[1,2048,768]{2,1,0:T(8,128)(2,1)}, u32[]{:S(2)}) copy-start(bf16[1,2048,768]{2,1,0:T(8,128)(2,1)} %refs_3_.11) | copy-start | bytes 9437188
  5.5 21.6 %copy-start.4 = (bf16[32,640]{1,0:T(8,128)(2,1)S(1)}, bf16[32,640]{1,0:T(8,128)(2,1)}, u32[]{:S(2)}) copy-start(bf16[32,640]{1,0:T(8,128)(2,1)} %get-tuple-element.28.refs_2_.refs_1_) | copy-start | bytes 122884
  5.5 6.9 %collective-permute-start.1 = (bf16[3,32,640]{2,1,0:T(8,128)(2,1)}, bf16[3,32,640]{2,1,0:T(8,128)(2,1)S(1)}, u32[]{:S(2)}, u32[]{:S(2)}) collective-permute-start(bf16[3,32,640]{2,1,0:T(8,128)(2,1)} %get-tuple-element.25), channel_id=1, source_target_pairs={{0,1},{1,0},{2,3},{3,2},{4,5},{5,4},{6,7},{7,6},{8,9},{9,8},{10,11... | collective-permute-start | bytes 368648 | tf_op jit(solution)/shard_map/ppermute | solution.py:337
  5.6 8.3 %collective-permute-start = (bf16[32,640]{1,0:T(8,128)(2,1)}, bf16[32,640]{1,0:T(8,128)(2,1)S(1)}, u32[]{:S(2)}, u32[]{:S(2)}) collective-permute-start(bf16[32,640]{1,0:T(8,128)(2,1)} %get-tuple-element.23), channel_id=1, source_target_pairs={{0,14},{1,15},{4,10},{5,11},{8,6},{9,7},{12,2},{13,3},{14,0},{15,1... | collective-permute-start | bytes 122888 | tf_op jit(solution)/shard_map/ppermute | solution.py:334
  12.5 6.4 %collective-permute-start.2 = (bf16[64,640]{1,0:T(8,128)(2,1)S(1)}, bf16[64,640]{1,0:T(8,128)(2,1)S(1)}, u32[]{:S(2)}, u32[]{:S(2)}) collective-permute-start(bf16[64,640]{1,0:T(8,128)(2,1)S(1)} %pad_maximum_fusion), channel_id=1, source_target_pairs={{0,10},{1,13},{4,6},{5,15},{8,2},{9,11},{12,0},{13,7},{14,4},{15,3... | collective-permute-start | bytes 245768 | tf_op jit(solution)/shard_map/ppermute | solution.py:334
  12.6 31.4 %copy-start.5 = (bf16[32,2048]{1,0:T(8,128)(2,1)S(1)}, bf16[32,2048]{1,0:T(8,128)(2,1)}, u32[]{:S(2)}) copy-start(bf16[32,2048]{1,0:T(8,128)(2,1)} %param.16) | copy-start | bytes 393220
  12.6 10.6 %collective-permute-start.7 = (bf16[64,640]{1,0:T(8,128)(2,1)S(1)}, bf16[64,640]{1,0:T(8,128)(2,1)S(1)}, u32[]{:S(2)}, u32[]{:S(2)}) collective-permute-start(bf16[64,640]{1,0:T(8,128)(2,1)S(1)} %pad_maximum_fusion.2), channel_id=1, source_target_pairs={{0,2},{1,5},{4,0},{5,9},{8,4},{9,13},{12,8},{13,15},{14,12},{15,11... | collective-permute-start | bytes 245768 | tf_op jit(solution)/shard_map/ppermute | solution.py:334
  20.6 23.6 %copy-start.6 = (f32[2048]{0:T(1024)S(1)}, f32[2048]{0:T(1024)}, u32[]{:S(2)}) copy-start(f32[2048]{0:T(1024)} %param.18) | copy-start | bytes 24580
  20.6 43.6 %copy-start.2 = (bf16[1,768,2048]{2,1,0:T(8,128)(2,1)S(1)}, bf16[1,768,2048]{2,1,0:T(8,128)(2,1)}, u32[]{:S(2)}) copy-start(bf16[1,768,2048]{2,1,0:T(8,128)(2,1)} %refs_4_.9) | copy-start | bytes 9437188
  20.6 8.2 %collective-permute-start.4 = (bf16[32,2048]{1,0:T(8,128)(2,1)S(1)}, bf16[32,2048]{1,0:T(8,128)(2,1)S(1)}, u32[]{:S(2)}, u32[]{:S(2)}) collective-permute-start(bf16[32,2048]{1,0:T(8,128)(2,1)S(1)} %get-tuple-element.26), channel_id=1, source_target_pairs={{0,4},{1,3},{4,8},{5,1},{8,12},{9,5},{12,14},{13,9},{14,10},{15,13... | collective-permute-start | bytes 393224 | tf_op jit(solution)/shard_map/ppermute | solution.py:334
  21.0 6.0 %collective-permute-start.6 = (bf16[64,640]{1,0:T(8,128)(2,1)S(1)}, bf16[64,640]{1,0:T(8,128)(2,1)S(1)}, u32[]{:S(2)}, u32[]{:S(2)}) collective-permute-start(bf16[64,640]{1,0:T(8,128)(2,1)S(1)} %pad_maximum_fusion.1), channel_id=1, source_target_pairs={{0,6},{1,9},{4,2},{5,13},{8,0},{9,15},{12,4},{13,11},{14,8},{15,7}... | collective-permute-start | bytes 245768 | tf_op jit(solution)/shard_map/ppermute | solution.py:334
  22.7 41.5 %collective-permute-start.18 = (bf16[1,2048,768]{2,1,0:T(8,128)(2,1)S(1)}, bf16[1,2048,768]{2,1,0:T(8,128)(2,1)S(1)}, u32[]{:S(2)}, u32[]{:S(2)}) collective-permute-start(bf16[1,2048,768]{2,1,0:T(8,128)(2,1)S(1)} %copy-done), channel_id=1, source_target_pairs={{0,1},{1,0},{2,3},{3,2},{4,5},{5,4},{6,7},{7,6},{8,9},{9,8},{10,11... | collective-permute-start | bytes 9437192 | tf_op jit(solution)/shard_map/ppermute | solution.py:337
  22.7 41.5 %collective-permute-start.19 = (bf16[1,2048,768]{2,1,0:T(8,128)(2,1)S(1)}, bf16[1,2048,768]{2,1,0:T(8,128)(2,1)S(1)}, u32[]{:S(2)}, u32[]{:S(2)}) collective-permute-start(bf16[1,2048,768]{2,1,0:T(8,128)(2,1)S(1)} %copy-done.1), channel_id=1, source_target_pairs={{0,1},{1,0},{2,3},{3,2},{4,5},{5,4},{6,7},{7,6},{8,9},{9,8},{10,11... | collective-permute-start | bytes 9437192 | tf_op jit(solution)/shard_map/ppermute | solution.py:337
  23.3 41.0 %collective-permute-start.20 = (bf16[1,768,2048]{2,1,0:T(8,128)(2,1)}, bf16[1,768,2048]{2,1,0:T(8,128)(2,1)S(1)}, u32[]{:S(2)}, u32[]{:S(2)}) collective-permute-start(bf16[1,768,2048]{2,1,0:T(8,128)(2,1)} %refs_4_.9), channel_id=1, source_target_pairs={{0,1},{1,0},{2,3},{3,2},{4,5},{5,4},{6,7},{7,6},{8,9},{9,8},{10,11... | collective-permute-start | bytes 9437192 | tf_op jit(solution)/shard_map/ppermute | solution.py:337
  27.0 5.0 %collective-permute-start.10 = (bf16[32,2048]{1,0:T(8,128)(2,1)S(1)}, bf16[32,2048]{1,0:T(8,128)(2,1)S(1)}, u32[]{:S(2)}, u32[]{:S(2)}) collective-permute-start(bf16[32,2048]{1,0:T(8,128)(2,1)S(1)} %get-tuple-element.32), channel_id=1, source_target_pairs={{0,4},{1,3},{4,8},{5,1},{8,12},{9,5},{12,14},{13,9},{14,10},{15,13... | collective-permute-start | bytes 393224 | tf_op jit(solution)/shard_map/ppermute | solution.py:334
  28.9 5.0 %collective-permute-start.5 = (bf16[32,2048]{1,0:T(8,128)(2,1)S(1)}, bf16[32,2048]{1,0:T(8,128)(2,1)S(1)}, u32[]{:S(2)}, u32[]{:S(2)}) collective-permute-start(bf16[32,2048]{1,0:T(8,128)(2,1)S(1)} %add_convert_fusion.10), channel_id=1, source_target_pairs={{0,4},{1,3},{4,8},{5,1},{8,12},{9,5},{12,14},{13,9},{14,10},{15,13... | collective-permute-start | bytes 393224 | tf_op jit(solution)/shard_map/ppermute | solution.py:334
  32.0 5.0 %collective-permute-start.11 = (bf16[32,2048]{1,0:T(8,128)(2,1)S(1)}, bf16[32,2048]{1,0:T(8,128)(2,1)S(1)}, u32[]{:S(2)}, u32[]{:S(2)}) collective-permute-start(bf16[32,2048]{1,0:T(8,128)(2,1)S(1)} %add_convert_fusion.7), channel_id=1, source_target_pairs={{0,4},{1,3},{4,8},{5,1},{8,12},{9,5},{12,14},{13,9},{14,10},{15,13... | collective-permute-start | bytes 393224 | tf_op jit(solution)/shard_map/ppermute | solution.py:334
  33.9 5.0 %collective-permute-start.8 = (bf16[32,2048]{1,0:T(8,128)(2,1)S(1)}, bf16[32,2048]{1,0:T(8,128)(2,1)S(1)}, u32[]{:S(2)}, u32[]{:S(2)}) collective-permute-start(bf16[32,2048]{1,0:T(8,128)(2,1)S(1)} %add_convert_fusion.9), channel_id=1, source_target_pairs={{0,4},{1,3},{4,8},{5,1},{8,12},{9,5},{12,14},{13,9},{14,10},{15,13... | collective-permute-start | bytes 393224 | tf_op jit(solution)/shard_map/ppermute | solution.py:334
  37.1 5.0 %collective-permute-start.12 = (bf16[32,2048]{1,0:T(8,128)(2,1)S(1)}, bf16[32,2048]{1,0:T(8,128)(2,1)S(1)}, u32[]{:S(2)}, u32[]{:S(2)}) collective-permute-start(bf16[32,2048]{1,0:T(8,128)(2,1)S(1)} %add_convert_fusion.6), channel_id=1, source_target_pairs={{0,4},{1,3},{4,8},{5,1},{8,12},{9,5},{12,14},{13,9},{14,10},{15,13... | collective-permute-start | bytes 393224 | tf_op jit(solution)/shard_map/ppermute | solution.py:334
  39.0 5.0 %collective-permute-start.9 = (bf16[32,2048]{1,0:T(8,128)(2,1)S(1)}, bf16[32,2048]{1,0:T(8,128)(2,1)S(1)}, u32[]{:S(2)}, u32[]{:S(2)}) collective-permute-start(bf16[32,2048]{1,0:T(8,128)(2,1)S(1)} %add_convert_fusion.8), channel_id=1, source_target_pairs={{0,4},{1,3},{4,8},{5,1},{8,12},{9,5},{12,14},{13,9},{14,10},{15,13... | collective-permute-start | bytes 393224 | tf_op jit(solution)/shard_map/ppermute | solution.py:334
  42.1 1.9 %collective-permute-start.13 = (bf16[32,2048]{1,0:T(8,128)(2,1)S(1)}, bf16[32,2048]{1,0:T(8,128)(2,1)S(1)}, u32[]{:S(2)}, u32[]{:S(2)}) collective-permute-start(bf16[32,2048]{1,0:T(8,128)(2,1)S(1)} %collective-permute-done.12), channel_id=1, source_target_pairs={{0,1},{1,0},{2,3},{3,2},{4,5},{5,4},{6,7},{7,6},{8,9},{9,8},{10,11... | collective-permute-start | bytes 393224 | tf_op jit(solution)/shard_map/ppermute | solution.py:337
  44.3 5.0 %collective-permute-start.14 = (bf16[32,2048]{1,0:T(8,128)(2,1)S(1)}, bf16[32,2048]{1,0:T(8,128)(2,1)S(1)}, u32[]{:S(2)}, u32[]{:S(2)}) collective-permute-start(bf16[32,2048]{1,0:T(8,128)(2,1)S(1)} %fusion.2.refs_0_), channel_id=1, source_target_pairs={{0,2},{1,5},{4,0},{5,9},{8,4},{9,13},{12,8},{13,15},{14,12},{15,11... | collective-permute-start | bytes 393224 | tf_op jit(solution)/shard_map/ppermute | solution.py:334
  46.3 5.0 %collective-permute-start.22 = (bf16[32,2048]{1,0:T(8,128)(2,1)S(1)}, bf16[32,2048]{1,0:T(8,128)(2,1)S(1)}, u32[]{:S(2)}, u32[]{:S(2)}) collective-permute-start(bf16[32,2048]{1,0:T(8,128)(2,1)S(1)} %fusion.2.refs_0_), channel_id=1, source_target_pairs={{0,1},{1,0},{2,3},{3,2},{4,5},{5,4},{6,7},{7,6},{8,9},{9,8},{10,11... | collective-permute-start | bytes 393224 | tf_op jit(solution)/shard_map/ppermute | solution.py:337
  49.3 5.0 %collective-permute-start.15 = (bf16[32,2048]{1,0:T(8,128)(2,1)S(1)}, bf16[32,2048]{1,0:T(8,128)(2,1)S(1)}, u32[]{:S(2)}, u32[]{:S(2)}) collective-permute-start(bf16[32,2048]{1,0:T(8,128)(2,1)S(1)} %collective-permute-done.14.refs_0_), channel_id=1, source_target_pairs={{0,2},{1,5},{4,0},{5,9},{8,4},{9,13},{12,8},{13,15},{14,12},{15,11... | collective-permute-start | bytes 393224 | tf_op jit(solution)/shard_map/ppermute | solution.py:334
  51.3 5.0 %collective-permute-start.23 = (bf16[32,2048]{1,0:T(8,128)(2,1)S(1)}, bf16[32,2048]{1,0:T(8,128)(2,1)S(1)}, u32[]{:S(2)}, u32[]{:S(2)}) collective-permute-start(bf16[32,2048]{1,0:T(8,128)(2,1)S(1)} %collective-permute-done.22), channel_id=1, source_target_pairs={{0,2},{1,5},{4,0},{5,9},{8,4},{9,13},{12,8},{13,15},{14,12},{15,11... | collective-permute-start | bytes 393224 | tf_op jit(solution)/shard_map/ppermute | solution.py:334
  54.3 5.0 %collective-permute-start.16 = (bf16[32,2048]{1,0:T(8,128)(2,1)S(1)}, bf16[32,2048]{1,0:T(8,128)(2,1)S(1)}, u32[]{:S(2)}, u32[]{:S(2)}) collective-permute-start(bf16[32,2048]{1,0:T(8,128)(2,1)S(1)} %collective-permute-done.15.refs_0_), channel_id=1, source_target_pairs={{0,2},{1,5},{4,0},{5,9},{8,4},{9,13},{12,8},{13,15},{14,12},{15,11... | collective-permute-start | bytes 393224 | tf_op jit(solution)/shard_map/ppermute | solution.py:334
  56.3 5.0 %collective-permute-start.24 = (bf16[32,2048]{1,0:T(8,128)(2,1)S(1)}, bf16[32,2048]{1,0:T(8,128)(2,1)S(1)}, u32[]{:S(2)}, u32[]{:S(2)}) collective-permute-start(bf16[32,2048]{1,0:T(8,128)(2,1)S(1)} %collective-permute-done.23.refs_1_), channel_id=1, source_target_pairs={{0,2},{1,5},{4,0},{5,9},{8,4},{9,13},{12,8},{13,15},{14,12},{15,11... | collective-permute-start | bytes 393224 | tf_op jit(solution)/shard_map/ppermute | solution.py:334
  59.3 5.0 %collective-permute-start.17 = (bf16[32,2048]{1,0:T(8,128)(2,1)S(1)}, bf16[32,2048]{1,0:T(8,128)(2,1)S(1)}, u32[]{:S(2)}, u32[]{:S(2)}) collective-permute-start(bf16[32,2048]{1,0:T(8,128)(2,1)S(1)} %collective-permute-done.16.refs_0_), channel_id=1, source_target_pairs={{0,2},{1,5},{4,0},{5,9},{8,4},{9,13},{12,8},{13,15},{14,12},{15,11... | collective-permute-start | bytes 393224 | tf_op jit(solution)/shard_map/ppermute | solution.py:334
  61.2 7.9 %collective-permute-start.25 = (bf16[32,2048]{1,0:T(8,128)(2,1)S(1)}, bf16[32,2048]{1,0:T(8,128)(2,1)S(1)}, u32[]{:S(2)}, u32[]{:S(2)}) collective-permute-start(bf16[32,2048]{1,0:T(8,128)(2,1)S(1)} %collective-permute-done.24.refs_1_), channel_id=1, source_target_pairs={{0,2},{1,5},{4,0},{5,9},{8,4},{9,13},{12,8},{13,15},{14,12},{15,11... | collective-permute-start | bytes 393224 | tf_op jit(solution)/shard_map/ppermute | solution.py:334
  67.6 12.5 %collective-permute-start.21 = (bf16[32,2048]{1,0:T(8,128)(2,1)S(1)}, bf16[32,2048]{1,0:T(8,128)(2,1)S(1)}, u32[]{:S(2)}, u32[]{:S(2)}) collective-permute-start(bf16[32,2048]{1,0:T(8,128)(2,1)S(1)} %shard_map.121), channel_id=1, source_target_pairs={{0,4},{1,3},{4,8},{5,1},{8,12},{9,5},{12,14},{13,9},{14,10},{15,13... | collective-permute-start | bytes 393224 | tf_op jit(solution)/shard_map/ppermute | solution.py:334
  72.6 9.8 %collective-permute-start.29 = (bf16[32,2048]{1,0:T(8,128)(2,1)S(1)}, bf16[32,2048]{1,0:T(8,128)(2,1)S(1)}, u32[]{:S(2)}, u32[]{:S(2)}) collective-permute-start(bf16[32,2048]{1,0:T(8,128)(2,1)S(1)} %get-tuple-element.38), channel_id=1, source_target_pairs={{0,4},{1,3},{4,8},{5,1},{8,12},{9,5},{12,14},{13,9},{14,10},{15,13... | collective-permute-start | bytes 393224 | tf_op jit(solution)/shard_map/ppermute | solution.py:334
  80.1 5.0 %collective-permute-start.26 = (bf16[32,2048]{1,0:T(8,128)(2,1)S(1)}, bf16[32,2048]{1,0:T(8,128)(2,1)S(1)}, u32[]{:S(2)}, u32[]{:S(2)}) collective-permute-start(bf16[32,2048]{1,0:T(8,128)(2,1)S(1)} %add_convert_fusion.4), channel_id=1, source_target_pairs={{0,4},{1,3},{4,8},{5,1},{8,12},{9,5},{12,14},{13,9},{14,10},{15,13... | collective-permute-start | bytes 393224 | tf_op jit(solution)/shard_map/ppermute | solution.py:334
  82.4 5.0 %collective-permute-start.30 = (bf16[32,2048]{1,0:T(8,128)(2,1)S(1)}, bf16[32,2048]{1,0:T(8,128)(2,1)S(1)}, u32[]{:S(2)}, u32[]{:S(2)}) collective-permute-start(bf16[32,2048]{1,0:T(8,128)(2,1)S(1)} %add_convert_fusion.1), channel_id=1, source_target_pairs={{0,4},{1,3},{4,8},{5,1},{8,12},{9,5},{12,14},{13,9},{14,10},{15,13... | collective-permute-start | bytes 393224 | tf_op jit(solution)/shard_map/ppermute | solution.py:334
  85.2 5.0 %collective-permute-start.27 = (bf16[32,2048]{1,0:T(8,128)(2,1)S(1)}, bf16[32,2048]{1,0:T(8,128)(2,1)S(1)}, u32[]{:S(2)}, u32[]{:S(2)}) collective-permute-start(bf16[32,2048]{1,0:T(8,128)(2,1)S(1)} %add_convert_fusion.3), channel_id=1, source_target_pairs={{0,4},{1,3},{4,8},{5,1},{8,12},{9,5},{12,14},{13,9},{14,10},{15,13... | collective-permute-start | bytes 393224 | tf_op jit(solution)/shard_map/ppermute | solution.py:334
  87.4 5.0 %collective-permute-start.31 = (bf16[32,2048]{1,0:T(8,128)(2,1)S(1)}, bf16[32,2048]{1,0:T(8,128)(2,1)S(1)}, u32[]{:S(2)}, u32[]{:S(2)}) collective-permute-start(bf16[32,2048]{1,0:T(8,128)(2,1)S(1)} %add_convert_fusion), channel_id=1, source_target_pairs={{0,4},{1,3},{4,8},{5,1},{8,12},{9,5},{12,14},{13,9},{14,10},{15,13... | collective-permute-start | bytes 393224 | tf_op jit(solution)/shard_map/ppermute | solution.py:334
  90.2 5.6 %collective-permute-start.28 = (bf16[32,2048]{1,0:T(8,128)(2,1)S(1)}, bf16[32,2048]{1,0:T(8,128)(2,1)S(1)}, u32[]{:S(2)}, u32[]{:S(2)}) collective-permute-start(bf16[32,2048]{1,0:T(8,128)(2,1)S(1)} %add_convert_fusion.2), channel_id=1, source_target_pairs={{0,4},{1,3},{4,8},{5,1},{8,12},{9,5},{12,14},{13,9},{14,10},{15,13... | collective-permute-start | bytes 393224 | tf_op jit(solution)/shard_map/ppermute | solution.py:334
  92.5 3.4 %collective-permute-start.32 = (bf16[32,2048]{1,0:T(8,128)(2,1)S(1)}, bf16[32,2048]{1,0:T(8,128)(2,1)S(1)}, u32[]{:S(2)}, u32[]{:S(2)}) collective-permute-start(bf16[32,2048]{1,0:T(8,128)(2,1)S(1)} %collective-permute-done.31), channel_id=1, source_target_pairs={{0,1},{1,0},{2,3},{3,2},{4,5},{5,4},{6,7},{7,6},{8,9},{9,8},{10,11... | collective-permute-start | bytes 393224 | tf_op jit(solution)/shard_map/ppermute | solution.py:337

commit v6 on v5

--- a/solution.py
+++ b/solution.py
@@ -176,7 +176,7 @@
             pltpu.VMEM((rows * heads, head_size), F32),
             pltpu.VMEM((chips, rows, wide), BF16),
         ],
-        compiler_params=pltpu.CompilerParams(vmem_limit_bytes=56 * 1024 * 1024),
+        compiler_params=pltpu.CompilerParams(vmem_limit_bytes=54 * 1024 * 1024),
         cost_estimate=pl.CostEstimate(
             flops=4 * rows * heads * cache_len * head_size,
             bytes_accessed=4 * rows * kv_count * cache_len * head_size,
@@ -238,24 +238,30 @@
     )(*pieces, own, other)
 
 
-def expert_kernel(pieces, local, local_experts, *refs):
-    piece_refs, digits_ref, refs = refs[:pieces], refs[pieces], refs[pieces + 1 :]
+def expert_kernel(pieces, blocks, local, local_experts, *refs):
+    piece_refs, digit_refs, refs = refs[:pieces], refs[pieces : pieces + blocks], refs[pieces + blocks :]
     weight_refs, refs = refs[:6], refs[6:]
-    out_refs, (x_ref, inner_ref) = refs[:pieces], refs[pieces:]
+    out_refs, (x_ref, inner_ref, gates_ref) = refs[:pieces], refs[pieces:]
     size = piece_refs[0].shape[0]
     for index, piece in enumerate(piece_refs):
         x_ref[index * size : (index + 1) * size, :] = piece[...]
     core = lax.rem(lax.axis_index("rows"), 2)
     chip_experts = 2 * local_experts
-    feats = digits_ref.shape[1] - 128 * (-(-2 * chip_experts // 128))
-    taken = digits_ref[:, feats:].astype(F32)
-
-    def gate(k):
-        high, low = taken[:, k : k + 1], taken[:, chip_experts + k : chip_experts + k + 1]
-        return (high * 16.0 + low) * gate_scale
-
-    first, second = gate(local), gate(local_experts + local)
-    gates = (jnp.where(core == 0, first, second), jnp.where(core == 0, second, first))
+    start = 0
+    for digits in digit_refs:
+        feats = digits.shape[1] - 128 * (-(-2 * chip_experts // 128))
+        taken = digits[:, feats:].astype(F32)
+
+        def gate(k):
+            high, low = taken[:, k : k + 1], taken[:, chip_experts + k : chip_experts + k + 1]
+            return (high * 16.0 + low) * gate_scale
+
+        first, second = gate(local), gate(local_experts + local)
+        stop = start + digits.shape[0]
+        gates_ref[0, start:stop, :] = jnp.where(core == 0, first, second)
+        gates_ref[1, start:stop, :] = jnp.where(core == 0, second, first)
+        start = stop
+    gates = (gates_ref[0], gates_ref[1])
     hidden_units, width = weight_refs[2].shape[1:]
     tile = 256
     for which in range(2):
@@ -291,24 +297,25 @@
     local_experts, width, hidden_units = own[0].shape
     rows = sum(piece.shape[0] for piece in pieces)
     return pl.pallas_call(
-        functools.partial(expert_kernel, len(pieces), local, local_experts),
+        functools.partial(expert_kernel, len(pieces), len(digits), local, local_experts),
         out_shape=tuple(
             jax.ShapeDtypeStruct((piece.shape[0], width), kind)
             for piece, kind in zip(pieces, kinds)
         ),
-        in_specs=[VMEM] * (len(pieces) + 7),
+        in_specs=[VMEM] * (len(pieces) + len(digits) + 6),
         out_specs=(VMEM,) * len(pieces),
         scratch_shapes=[
             pltpu.VMEM((rows, width), BF16),
             pltpu.VMEM((rows, 2 * hidden_units), BF16),
+            pltpu.VMEM((2, rows, 1), F32),
         ],
         compiler_params=pltpu.CompilerParams(vmem_limit_bytes=16 * 1024 * 1024),
         cost_estimate=pl.CostEstimate(
-            flops=24 * rows * hidden_units * width,
+            flops=12 * rows * hidden_units * width,
             bytes_accessed=rows * width,
             transcendentals=2 * rows * hidden_units,
         ),
-    )(*pieces, digits, *own, *other)
+    )(*pieces, *digits, *own, *other)
 
 
 def on_device(
@@ -384,12 +391,13 @@
         return [part.astype(kind) for part, kind in zip(total, kinds)]
 
     own, other = normed, swapped(normed)
-    total = serve([own], [F32], arrived[0])
+    pieces = [own]
     for offset in range(1, hops):
         own, other = pass_on(own, -1), pass_on(other, -1)
-        kinds = [F32, BF16 if offset == hops - 1 else F32]
-        total = serve([own, other], kinds, arrived[offset]) + total
-    total = serve([pass_on(own, -1)], [BF16], arrived[hops]) + total
+        pieces = [own, other] + pieces
+    pieces = [pass_on(own, -1)] + pieces
+    digits = [arrived[offset] for offset in range(hops, -1, -1)]
+    total = serve(pieces[:3], kinds[:3], digits[:2]) + serve(pieces[3:], kinds[3:], digits[2:])
     return (residual.astype(F32) + ring_sums(total)).astype(BF16)
 
 

time: 96.8 us -> 94.5 us (0.976)
  waiting for transfers between devices: 29.6 us -> 54 us
  starting transfers between devices: 39.1 us -> 25.3 us
  Pallas kernels: 25.4 us -> 12.6 us
    ppermute x25, waiting for transfers between devices: 29.5 us -> 54 us  [pass_on(): return lax.ppermute(array, 'rows', toward(step))]
    ppermute x25, starting transfers between devices: 38 us -> 24.2 us  [pass_on(): return lax.ppermute(array, 'rows', toward(step))]
    pallas_call x5 -> x2, Pallas kernels: 16.9 us -> 6.54 us  [experts(): pl.pallas_call(functools.partial(expert_kernel, len(pieces), len(digits),...]
    pallas_call x2, Pallas kernels: 3.44 us -> 1 us  [project(): pl.pallas_call(functools.partial(project_kernel, len(pieces)), out_shape=...]
  transfers between devices with their start and end apart: 33 -> 33, of which waited for: 15 -> 22; matrix products, arithmetic and copies ran while one was open for 1% -> 2% of each run, Pallas kernels for 26% -> 10%
where the time goes in v6:
time: 94.5 us; the launch traced here: 94.3 us
  waiting for transfers between devices  54 us (57%)
  starting transfers between devices  25.3 us (27%)
  Pallas kernels  12.6 us (13%)
  other arithmetic  1.3 us (1%)
    ppermute x25, waiting for transfers between devices, pass_on(): return lax.ppermute(array, 'rows', toward(step))  54 us
    ppermute x25, starting transfers between devices, pass_on(): return lax.ppermute(array, 'rows', toward(step))  24.2 us
    pallas_call x2, Pallas kernels, experts(): pl.pallas_call(functools.partial(expert_kernel, len(pieces), len(digits),...  6.54 us
    pallas_call x1, Pallas kernels, attend(): pl.pallas_call(functools.partial(attend_kernel, chips, hops, chip_experts...  5.05 us
  transfers between devices with their start and end apart: 33, of which 22 were waited for; matrix products, arithmetic and copies ran while one was open for 2% of the time, Pallas kernels for 10%

profile of v6, /device:TPU:0, one launch (start us, length us, event | category | flops | bytes accessed | tf_op | source)
XLA Modules:
  0.0 94.3 jit_solution(3641649341397937251)
XLA Ops:
  0.0 0.5 collective-permute-start.3
  0.5 5.1 %shard_map.118 = (bf16[32,640]{1,0:T(8,128)(2,1)}, bf16[3,32,640]{2,1,0:T(8,128)(2,1)}, bf16[3,32,640]{2,1,0:T(8,128)(2,1)}, bf16[32,640]{1,0:T(8,128)(2,1)}) custom-call(s32[32]{0:T(128)} %lengths_ref.1, bf16[32,4096]{1,0:T(8,128)(2,1)} %q_ref.1, bf16[32,2,128,128]{3,2,1,0:T(8,128)(2,1)} %k_ref.1, bf16[32,2,128,128]{3,2,1,0:T(8,128)(2,1)} %v_ref.1, ...), custom_call_target="tpu_custom_call" | custom-call | flops 67108864 | bytes 4194304 | tf_op jit(solution)/shard_map/pallas_call | solution.py:168
  5.5 0.1 collective-permute-start.1
  5.6 6.0 %collective-permute-start = (bf16[32,640]{1,0:T(8,128)(2,1)}, bf16[32,640]{1,0:T(8,128)(2,1)S(1)}, u32[]{:S(2)}, u32[]{:S(2)}) collective-permute-start(bf16[32,640]{1,0:T(8,128)(2,1)} %get-tuple-element.25), channel_id=1, source_target_pairs={{0,14},{1,15},{4,10},{5,11},{8,6},{9,7},{12,2},{13,3},{14,0},{15,1... | collective-permute-start | bytes 122888 | tf_op jit(solution)/shard_map/ppermute | solution.py:341
  11.6 0.8 slice_bitcast_fusion.5
  12.5 0.0 collective-permute-done.1
  12.5 0.1 collective-permute-start.2
  12.6 0.0 copy-start.5
  12.6 1.7 %collective-permute-start.6 = (bf16[64,640]{1,0:T(8,128)(2,1)S(1)}, bf16[64,640]{1,0:T(8,128)(2,1)S(1)}, u32[]{:S(2)}, u32[]{:S(2)}) collective-permute-start(bf16[64,640]{1,0:T(8,128)(2,1)S(1)} %pad_maximum_fusion.1), channel_id=1, source_target_pairs={{0,6},{1,9},{4,2},{5,13},{8,0},{9,15},{12,4},{13,11},{14,8},{15,7}... | collective-permute-start | bytes 245768 | tf_op jit(solution)/shard_map/ppermute | solution.py:341
  14.3 0.0 collective-permute-done.refs_0_.refs_3_
  14.3 5.3 %collective-permute-done.2.refs_1_.refs_4_ = bf16[64,640]{1,0:T(8,128)(2,1)S(1)} collective-permute-done((bf16[64,640]{1,0:T(8,128)(2,1)S(1)}, bf16[64,640]{1,0:T(8,128)(2,1)S(1)}, u32[]{:S(2)}, u32[]{:S(2)}) %collective-permute-start.2) | collective-permute-done | bytes 81952 | tf_op jit(solution)/shard_map/ppermute | solution.py:341
  19.7 0.5 shard_map.119
  20.1 0.0 copy-start.6
  20.1 0.0 copy-start.2
  20.2 0.1 collective-permute-start.10
  20.2 2.1 %collective-permute-start.7 = (bf16[64,640]{1,0:T(8,128)(2,1)S(1)}, bf16[64,640]{1,0:T(8,128)(2,1)S(1)}, u32[]{:S(2)}, u32[]{:S(2)}) collective-permute-start(bf16[64,640]{1,0:T(8,128)(2,1)S(1)} %pad_maximum_fusion.2), channel_id=1, source_target_pairs={{0,2},{1,5},{4,0},{5,9},{8,4},{9,13},{12,8},{13,15},{14,12},{15,11... | collective-permute-start | bytes 245768 | tf_op jit(solution)/shard_map/ppermute | solution.py:341
  22.3 0.5 collective-permute-start.23
  22.8 0.1 collective-permute-start.24
  22.9 2.6 %collective-permute-done.7.refs_1_.refs_6_ = bf16[64,640]{1,0:T(8,128)(2,1)S(1)} collective-permute-done((bf16[64,640]{1,0:T(8,128)(2,1)S(1)}, bf16[64,640]{1,0:T(8,128)(2,1)S(1)}, u32[]{:S(2)}, u32[]{:S(2)}) %collective-permute-start.7) | collective-permute-done | bytes 81952 | tf_op jit(solution)/shard_map/ppermute | solution.py:341
  25.5 0.5 shard_map.120
  26.0 1.4 %collective-permute-start.11 = (bf16[32,2048]{1,0:T(8,128)(2,1)S(1)}, bf16[32,2048]{1,0:T(8,128)(2,1)S(1)}, u32[]{:S(2)}, u32[]{:S(2)}) collective-permute-start(bf16[32,2048]{1,0:T(8,128)(2,1)S(1)} %add_convert_fusion.7), channel_id=1, source_target_pairs={{0,4},{1,3},{4,8},{5,1},{8,12},{9,5},{12,14},{13,9},{14,10},{15,13... | collective-permute-start | bytes 393224 | tf_op jit(solution)/shard_map/ppermute | solution.py:341
  27.4 3.0 %collective-permute-done.4 = bf16[32,2048]{1,0:T(8,128)(2,1)S(1)} collective-permute-done((bf16[32,2048]{1,0:T(8,128)(2,1)S(1)}, bf16[32,2048]{1,0:T(8,128)(2,1)S(1)}, u32[]{:S(2)}, u32[]{:S(2)}) %collective-permute-start.4) | collective-permute-done | bytes 131104 | tf_op jit(solution)/shard_map/ppermute | solution.py:341
  30.5 0.1 collective-permute-start.5
  30.5 1.3 %collective-permute-done.11 = bf16[32,2048]{1,0:T(8,128)(2,1)S(1)} collective-permute-done((bf16[32,2048]{1,0:T(8,128)(2,1)S(1)}, bf16[32,2048]{1,0:T(8,128)(2,1)S(1)}, u32[]{:S(2)}, u32[]{:S(2)}) %collective-permute-start.11) | collective-permute-done | bytes 131104 | tf_op jit(solution)/shard_map/ppermute | solution.py:341
  31.9 0.6 collective-permute-start.12
  32.5 3.0 %collective-permute-done.5 = bf16[32,2048]{1,0:T(8,128)(2,1)S(1)} collective-permute-done((bf16[32,2048]{1,0:T(8,128)(2,1)S(1)}, bf16[32,2048]{1,0:T(8,128)(2,1)S(1)}, u32[]{:S(2)}, u32[]{:S(2)}) %collective-permute-start.5) | collective-permute-done | bytes 131104 | tf_op jit(solution)/shard_map/ppermute | solution.py:341
  35.5 0.1 collective-permute-start.8
  35.6 1.3 %collective-permute-done.12 = bf16[32,2048]{1,0:T(8,128)(2,1)S(1)} collective-permute-done((bf16[32,2048]{1,0:T(8,128)(2,1)S(1)}, bf16[32,2048]{1,0:T(8,128)(2,1)S(1)}, u32[]{:S(2)}, u32[]{:S(2)}) %collective-permute-start.12) | collective-permute-done | bytes 131104 | tf_op jit(solution)/shard_map/ppermute | solution.py:341
  36.9 3.6 %collective-permute-done.8 = bf16[32,2048]{1,0:T(8,128)(2,1)S(1)} collective-permute-done((bf16[32,2048]{1,0:T(8,128)(2,1)S(1)}, bf16[32,2048]{1,0:T(8,128)(2,1)S(1)}, u32[]{:S(2)}, u32[]{:S(2)}) %collective-permute-start.8) | collective-permute-done | bytes 131104 | tf_op jit(solution)/shard_map/ppermute | solution.py:341
  40.6 0.1 collective-permute-start.9
  40.6 6.3 %collective-permute-done.9 = bf16[32,2048]{1,0:T(8,128)(2,1)S(1)} collective-permute-done((bf16[32,2048]{1,0:T(8,128)(2,1)S(1)}, bf16[32,2048]{1,0:T(8,128)(2,1)S(1)}, u32[]{:S(2)}, u32[]{:S(2)}) %collective-permute-start.9) | collective-permute-done | bytes 131104 | tf_op jit(solution)/shard_map/ppermute | solution.py:341
  46.9 0.2 fusion
  47.1 0.1 fusion.2.refs_4_
  47.2 1.3 %collective-permute-start.14 = (bf16[32,2048]{1,0:T(8,128)(2,1)S(1)}, bf16[32,2048]{1,0:T(8,128)(2,1)S(1)}, u32[]{:S(2)}, u32[]{:S(2)}) collective-permute-start(bf16[32,2048]{1,0:T(8,128)(2,1)S(1)} %fusion.2.refs_4_), channel_id=1, source_target_pairs={{0,2},{1,5},{4,0},{5,9},{8,4},{9,13},{12,8},{13,15},{14,12},{15,11... | collective-permute-start | bytes 393224 | tf_op jit(solution)/shard_map/ppermute | solution.py:341
  48.6 3.7 %collective-permute-done.14.refs_2_ = bf16[32,2048]{1,0:T(8,128)(2,1)S(1)} collective-permute-done((bf16[32,2048]{1,0:T(8,128)(2,1)S(1)}, bf16[32,2048]{1,0:T(8,128)(2,1)S(1)}, u32[]{:S(2)}, u32[]{:S(2)}) %collective-permute-start.14) | collective-permute-done | bytes 131104 | tf_op jit(solution)/shard_map/ppermute | solution.py:341
  52.2 1.3 %collective-permute-start.15 = (bf16[32,2048]{1,0:T(8,128)(2,1)S(1)}, bf16[32,2048]{1,0:T(8,128)(2,1)S(1)}, u32[]{:S(2)}, u32[]{:S(2)}) collective-permute-start(bf16[32,2048]{1,0:T(8,128)(2,1)S(1)} %collective-permute-done.14.refs_2_), channel_id=1, source_target_pairs={{0,2},{1,5},{4,0},{5,9},{8,4},{9,13},{12,8},{13,15},{14,12},{15,11... | collective-permute-start | bytes 393224 | tf_op jit(solution)/shard_map/ppermute | solution.py:341
  53.5 0.0 collective-permute-start.19
  53.5 3.7 %collective-permute-done.15.refs_0_ = bf16[32,2048]{1,0:T(8,128)(2,1)S(1)} collective-permute-done((bf16[32,2048]{1,0:T(8,128)(2,1)S(1)}, bf16[32,2048]{1,0:T(8,128)(2,1)S(1)}, u32[]{:S(2)}, u32[]{:S(2)}) %collective-permute-start.15) | collective-permute-done | bytes 131104 | tf_op jit(solution)/shard_map/ppermute | solution.py:341
  57.2 1.3 %collective-permute-start.16 = (bf16[32,2048]{1,0:T(8,128)(2,1)S(1)}, bf16[32,2048]{1,0:T(8,128)(2,1)S(1)}, u32[]{:S(2)}, u32[]{:S(2)}) collective-permute-start(bf16[32,2048]{1,0:T(8,128)(2,1)S(1)} %collective-permute-done.15.refs_0_), channel_id=1, source_target_pairs={{0,2},{1,5},{4,0},{5,9},{8,4},{9,13},{12,8},{13,15},{14,12},{15,11... | collective-permute-start | bytes 393224 | tf_op jit(solution)/shard_map/ppermute | solution.py:341
  58.5 0.1 collective-permute-done.19.refs_3_
  58.6 1.3 %collective-permute-start.20 = (bf16[32,2048]{1,0:T(8,128)(2,1)S(1)}, bf16[32,2048]{1,0:T(8,128)(2,1)S(1)}, u32[]{:S(2)}, u32[]{:S(2)}) collective-permute-start(bf16[32,2048]{1,0:T(8,128)(2,1)S(1)} %collective-permute-done.19.refs_3_), channel_id=1, source_target_pairs={{0,2},{1,5},{4,0},{5,9},{8,4},{9,13},{12,8},{13,15},{14,12},{15,11... | collective-permute-start | bytes 393224 | tf_op jit(solution)/shard_map/ppermute | solution.py:341
  59.9 2.3 %collective-permute-done.16.refs_1_ = bf16[32,2048]{1,0:T(8,128)(2,1)S(1)} collective-permute-done((bf16[32,2048]{1,0:T(8,128)(2,1)S(1)}, bf16[32,2048]{1,0:T(8,128)(2,1)S(1)}, u32[]{:S(2)}, u32[]{:S(2)}) %collective-permute-start.16) | collective-permute-done | bytes 131104 | tf_op jit(solution)/shard_map/ppermute | solution.py:341
  62.2 1.3 %collective-permute-start.17 = (bf16[32,2048]{1,0:T(8,128)(2,1)S(1)}, bf16[32,2048]{1,0:T(8,128)(2,1)S(1)}, u32[]{:S(2)}, u32[]{:S(2)}) collective-permute-start(bf16[32,2048]{1,0:T(8,128)(2,1)S(1)} %collective-permute-done.16.refs_1_), channel_id=1, source_target_pairs={{0,2},{1,5},{4,0},{5,9},{8,4},{9,13},{12,8},{13,15},{14,12},{15,11... | collective-permute-start | bytes 393224 | tf_op jit(solution)/shard_map/ppermute | solution.py:341
  63.5 0.1 collective-permute-done.20.refs_1_
  63.6 1.3 %collective-permute-start.21 = (bf16[32,2048]{1,0:T(8,128)(2,1)S(1)}, bf16[32,2048]{1,0:T(8,128)(2,1)S(1)}, u32[]{:S(2)}, u32[]{:S(2)}) collective-permute-start(bf16[32,2048]{1,0:T(8,128)(2,1)S(1)} %collective-permute-done.20.refs_1_), channel_id=1, source_target_pairs={{0,2},{1,5},{4,0},{5,9},{8,4},{9,13},{12,8},{13,15},{14,12},{15,11... | collective-permute-start | bytes 393224 | tf_op jit(solution)/shard_map/ppermute | solution.py:341
  64.9 2.3 %collective-permute-done.17.refs_0_ = bf16[32,2048]{1,0:T(8,128)(2,1)S(1)} collective-permute-done((bf16[32,2048]{1,0:T(8,128)(2,1)S(1)}, bf16[32,2048]{1,0:T(8,128)(2,1)S(1)}, u32[]{:S(2)}, u32[]{:S(2)}) %collective-permute-start.17) | collective-permute-done | bytes 131104 | tf_op jit(solution)/shard_map/ppermute | solution.py:341
  67.1 1.5 %collective-permute-done.21.refs_2_ = bf16[32,2048]{1,0:T(8,128)(2,1)S(1)} collective-permute-done((bf16[32,2048]{1,0:T(8,128)(2,1)S(1)}, bf16[32,2048]{1,0:T(8,128)(2,1)S(1)}, u32[]{:S(2)}, u32[]{:S(2)}) %collective-permute-start.21) | collective-permute-done | bytes 131104 | tf_op jit(solution)/shard_map/ppermute | solution.py:341
  68.7 3.2 %shard_map.121 = (bf16[32,2048]{1,0:T(8,128)(2,1)S(1)}, f32[32,2048]{1,0:T(8,128)S(1)}, bf16[32,2048]{1,0:T(8,128)(2,1)S(1)}) custom-call(bf16[32,2048]{1,0:T(8,128)(2,1)S(1)} %collective-permute-done.17.refs_0_, bf16[32,2048]{1,0:T(8,128)(2,1)S(1)} %collective-permute-done.16.refs_1_, bf16[32,2048]{1,0:T(8,128)(2,1)S(1)} %collective-permute-done.21.refs_2_, ...), custom_call_target="tpu_custom_call" | custom-call | flops 1811939328 | bytes 196608 | tf_op jit(solution)/shard_map/pallas_call | solution.py:299
  71.9 0.6 collective-permute-start.29
  72.5 1.1 %collective-permute-start.25 = (bf16[32,2048]{1,0:T(8,128)(2,1)S(1)}, bf16[32,2048]{1,0:T(8,128)(2,1)S(1)}, u32[]{:S(2)}, u32[]{:S(2)}) collective-permute-start(bf16[32,2048]{1,0:T(8,128)(2,1)S(1)} %get-tuple-element.37), channel_id=1, source_target_pairs={{0,4},{1,3},{4,8},{5,1},{8,12},{9,5},{12,14},{13,9},{14,10},{15,13... | collective-permute-start | bytes 393224 | tf_op jit(solution)/shard_map/ppermute | solution.py:341
  73.6 3.3 %shard_map.122 = (f32[32,2048]{1,0:T(8,128)S(1)}, f32[32,2048]{1,0:T(8,128)S(1)}, f32[32,2048]{1,0:T(8,128)S(1)}, f32[32,2048]{1,0:T(8,128)S(1)}, f32[32,2048]{1,0:T(8,128)S(1)}) custom-call(bf16[32,2048]{1,0:T(8,128)(2,1)S(1)} %collective-permute-done.15.refs_0_, bf16[32,2048]{1,0:T(8,128)(2,1)S(1)} %collective-permute-done.20.refs_1_, ...), custom_call_target="tpu_custom_call" | custom-call | flops 3019898880 | bytes 327680 | tf_op jit(solution)/shard_map/pallas_call | solution.py:299
  76.9 0.1 collective-permute-done.29
  77.1 0.4 collective-permute-start.30
  77.5 0.9 %collective-permute-done.25 = bf16[32,2048]{1,0:T(8,128)(2,1)S(1)} collective-permute-done((bf16[32,2048]{1,0:T(8,128)(2,1)S(1)}, bf16[32,2048]{1,0:T(8,128)(2,1)S(1)}, u32[]{:S(2)}, u32[]{:S(2)}) %collective-permute-start.25) | collective-permute-done | bytes 131104 | tf_op jit(solution)/shard_map/ppermute | solution.py:341
  78.5 0.6 collective-permute-start.26
  79.1 3.0 %collective-permute-done.30 = bf16[32,2048]{1,0:T(8,128)(2,1)S(1)} collective-permute-done((bf16[32,2048]{1,0:T(8,128)(2,1)S(1)}, bf16[32,2048]{1,0:T(8,128)(2,1)S(1)}, u32[]{:S(2)}, u32[]{:S(2)}) %collective-permute-start.30) | collective-permute-done | bytes 131104 | tf_op jit(solution)/shard_map/ppermute | solution.py:341
  82.1 0.4 collective-permute-start.31
  82.6 1.0 %collective-permute-done.26 = bf16[32,2048]{1,0:T(8,128)(2,1)S(1)} collective-permute-done((bf16[32,2048]{1,0:T(8,128)(2,1)S(1)}, bf16[32,2048]{1,0:T(8,128)(2,1)S(1)}, u32[]{:S(2)}, u32[]{:S(2)}) %collective-permute-start.26) | collective-permute-done | bytes 131104 | tf_op jit(solution)/shard_map/ppermute | solution.py:341
  83.5 0.6 collective-permute-start.27
  84.1 3.0 %collective-permute-done.31 = bf16[32,2048]{1,0:T(8,128)(2,1)S(1)} collective-permute-done((bf16[32,2048]{1,0:T(8,128)(2,1)S(1)}, bf16[32,2048]{1,0:T(8,128)(2,1)S(1)}, u32[]{:S(2)}, u32[]{:S(2)}) %collective-permute-start.31) | collective-permute-done | bytes 131104 | tf_op jit(solution)/shard_map/ppermute | solution.py:341
  87.1 1.4 %collective-permute-done.27 = bf16[32,2048]{1,0:T(8,128)(2,1)S(1)} collective-permute-done((bf16[32,2048]{1,0:T(8,128)(2,1)S(1)}, bf16[32,2048]{1,0:T(8,128)(2,1)S(1)}, u32[]{:S(2)}, u32[]{:S(2)}) %collective-permute-start.27) | collective-permute-done | bytes 131104 | tf_op jit(solution)/shard_map/ppermute | solution.py:341
  88.6 0.6 collective-permute-start.28
  89.2 4.4 %collective-permute-done.28 = bf16[32,2048]{1,0:T(8,128)(2,1)S(1)} collective-permute-done((bf16[32,2048]{1,0:T(8,128)(2,1)S(1)}, bf16[32,2048]{1,0:T(8,128)(2,1)S(1)}, u32[]{:S(2)}, u32[]{:S(2)}) %collective-permute-start.28) | collective-permute-done | bytes 131104 | tf_op jit(solution)/shard_map/ppermute | solution.py:341
  93.6 0.7 fusion.3
  (40 shorter events, 0.4 us)
Async XLA Ops:
  0.0 19.7 %copy-start.3 = (bf16[256,2048]{1,0:T(8,128)(2,1)S(1)}, bf16[256,2048]{1,0:T(8,128)(2,1)}, u32[]{:S(2)}) copy-start(bf16[256,2048]{1,0:T(8,128)(2,1)} %refs_3_.1) | copy-start | bytes 3145732
  0.0 19.7 %collective-permute-start.3 = (bf16[256,2048]{1,0:T(8,128)(2,1)}, bf16[256,2048]{1,0:T(8,128)(2,1)S(1)}, u32[]{:S(2)}, u32[]{:S(2)}) collective-permute-start(bf16[256,2048]{1,0:T(8,128)(2,1)} %refs_3_.1), channel_id=1, source_target_pairs={{0,1},{1,0},{2,3},{3,2},{4,5},{5,4},{6,7},{7,6},{8,9},{9,8},{10,11... | collective-permute-start | bytes 3145736 | tf_op jit(solution)/shard_map/ppermute | solution.py:344
  0.5 21.9 %copy-start = (bf16[1,2048,768]{2,1,0:T(8,128)(2,1)S(1)}, bf16[1,2048,768]{2,1,0:T(8,128)(2,1)}, u32[]{:S(2)}) copy-start(bf16[1,2048,768]{2,1,0:T(8,128)(2,1)} %refs_8_.1) | copy-start | bytes 9437188
  0.5 21.9 %copy-start.1 = (bf16[1,2048,768]{2,1,0:T(8,128)(2,1)S(1)}, bf16[1,2048,768]{2,1,0:T(8,128)(2,1)}, u32[]{:S(2)}) copy-start(bf16[1,2048,768]{2,1,0:T(8,128)(2,1)} %refs_9_.1) | copy-start | bytes 9437188
  5.5 20.0 %copy-start.4 = (bf16[32,640]{1,0:T(8,128)(2,1)S(1)}, bf16[32,640]{1,0:T(8,128)(2,1)}, u32[]{:S(2)}) copy-start(bf16[32,640]{1,0:T(8,128)(2,1)} %get-tuple-element.30.refs_2_.refs_7_) | copy-start | bytes 122884
  5.5 7.0 %collective-permute-start.1 = (bf16[3,32,640]{2,1,0:T(8,128)(2,1)}, bf16[3,32,640]{2,1,0:T(8,128)(2,1)S(1)}, u32[]{:S(2)}, u32[]{:S(2)}) collective-permute-start(bf16[3,32,640]{2,1,0:T(8,128)(2,1)} %get-tuple-element.27), channel_id=1, source_target_pairs={{0,1},{1,0},{2,3},{3,2},{4,5},{5,4},{6,7},{7,6},{8,9},{9,8},{10,11... | collective-permute-start | bytes 368648 | tf_op jit(solution)/shard_map/ppermute | solution.py:344
  5.6 8.7 %collective-permute-start = (bf16[32,640]{1,0:T(8,128)(2,1)}, bf16[32,640]{1,0:T(8,128)(2,1)S(1)}, u32[]{:S(2)}, u32[]{:S(2)}) collective-permute-start(bf16[32,640]{1,0:T(8,128)(2,1)} %get-tuple-element.25), channel_id=1, source_target_pairs={{0,14},{1,15},{4,10},{5,11},{8,6},{9,7},{12,2},{13,3},{14,0},{15,1... | collective-permute-start | bytes 122888 | tf_op jit(solution)/shard_map/ppermute | solution.py:341
  12.5 7.1 %collective-permute-start.2 = (bf16[64,640]{1,0:T(8,128)(2,1)S(1)}, bf16[64,640]{1,0:T(8,128)(2,1)S(1)}, u32[]{:S(2)}, u32[]{:S(2)}) collective-permute-start(bf16[64,640]{1,0:T(8,128)(2,1)S(1)} %pad_maximum_fusion), channel_id=1, source_target_pairs={{0,10},{1,13},{4,6},{5,15},{8,2},{9,11},{12,0},{13,7},{14,4},{15,3... | collective-permute-start | bytes 245768 | tf_op jit(solution)/shard_map/ppermute | solution.py:341
  12.6 34.3 %copy-start.5 = (bf16[32,2048]{1,0:T(8,128)(2,1)S(1)}, bf16[32,2048]{1,0:T(8,128)(2,1)}, u32[]{:S(2)}) copy-start(bf16[32,2048]{1,0:T(8,128)(2,1)} %param.16) | copy-start | bytes 393220
  12.6 10.2 %collective-permute-start.6 = (bf16[64,640]{1,0:T(8,128)(2,1)S(1)}, bf16[64,640]{1,0:T(8,128)(2,1)S(1)}, u32[]{:S(2)}, u32[]{:S(2)}) collective-permute-start(bf16[64,640]{1,0:T(8,128)(2,1)S(1)} %pad_maximum_fusion.1), channel_id=1, source_target_pairs={{0,6},{1,9},{4,2},{5,13},{8,0},{9,15},{12,4},{13,11},{14,8},{15,7}... | collective-permute-start | bytes 245768 | tf_op jit(solution)/shard_map/ppermute | solution.py:341
  20.1 27.0 %copy-start.6 = (f32[2048]{0:T(1024)S(1)}, f32[2048]{0:T(1024)}, u32[]{:S(2)}) copy-start(f32[2048]{0:T(1024)} %param.18) | copy-start | bytes 24580
  20.1 48.5 %copy-start.2 = (bf16[1,768,2048]{2,1,0:T(8,128)(2,1)S(1)}, bf16[1,768,2048]{2,1,0:T(8,128)(2,1)}, u32[]{:S(2)}) copy-start(bf16[1,768,2048]{2,1,0:T(8,128)(2,1)} %refs_10_.1) | copy-start | bytes 9437188
  20.2 5.8 %collective-permute-start.10 = (bf16[32,2048]{1,0:T(8,128)(2,1)S(1)}, bf16[32,2048]{1,0:T(8,128)(2,1)S(1)}, u32[]{:S(2)}, u32[]{:S(2)}) collective-permute-start(bf16[32,2048]{1,0:T(8,128)(2,1)S(1)} %get-tuple-element.34), channel_id=1, source_target_pairs={{0,4},{1,3},{4,8},{5,1},{8,12},{9,5},{12,14},{13,9},{14,10},{15,13... | collective-permute-start | bytes 393224 | tf_op jit(solution)/shard_map/ppermute | solution.py:341
  20.2 5.2 %collective-permute-start.7 = (bf16[64,640]{1,0:T(8,128)(2,1)S(1)}, bf16[64,640]{1,0:T(8,128)(2,1)S(1)}, u32[]{:S(2)}, u32[]{:S(2)}) collective-permute-start(bf16[64,640]{1,0:T(8,128)(2,1)S(1)} %pad_maximum_fusion.2), channel_id=1, source_target_pairs={{0,2},{1,5},{4,0},{5,9},{8,4},{9,13},{12,8},{13,15},{14,12},{15,11... | collective-permute-start | bytes 245768 | tf_op jit(solution)/shard_map/ppermute | solution.py:341
  22.3 46.3 %collective-permute-start.22 = (bf16[1,2048,768]{2,1,0:T(8,128)(2,1)S(1)}, bf16[1,2048,768]{2,1,0:T(8,128)(2,1)S(1)}, u32[]{:S(2)}, u32[]{:S(2)}) collective-permute-start(bf16[1,2048,768]{2,1,0:T(8,128)(2,1)S(1)} %copy-done), channel_id=1, source_target_pairs={{0,1},{1,0},{2,3},{3,2},{4,5},{5,4},{6,7},{7,6},{8,9},{9,8},{10,11... | collective-permute-start | bytes 9437192 | tf_op jit(solution)/shard_map/ppermute | solution.py:344
  22.3 46.3 %collective-permute-start.23 = (bf16[1,2048,768]{2,1,0:T(8,128)(2,1)S(1)}, bf16[1,2048,768]{2,1,0:T(8,128)(2,1)S(1)}, u32[]{:S(2)}, u32[]{:S(2)}) collective-permute-start(bf16[1,2048,768]{2,1,0:T(8,128)(2,1)S(1)} %copy-done.1), channel_id=1, source_target_pairs={{0,1},{1,0},{2,3},{3,2},{4,5},{5,4},{6,7},{7,6},{8,9},{9,8},{10,11... | collective-permute-start | bytes 9437192 | tf_op jit(solution)/shard_map/ppermute | solution.py:344
  22.8 45.8 %collective-permute-start.24 = (bf16[1,768,2048]{2,1,0:T(8,128)(2,1)}, bf16[1,768,2048]{2,1,0:T(8,128)(2,1)S(1)}, u32[]{:S(2)}, u32[]{:S(2)}) collective-permute-start(bf16[1,768,2048]{2,1,0:T(8,128)(2,1)} %refs_10_.1), channel_id=1, source_target_pairs={{0,1},{1,0},{2,3},{3,2},{4,5},{5,4},{6,7},{7,6},{8,9},{9,8},{10,11... | collective-permute-start | bytes 9437192 | tf_op jit(solution)/shard_map/ppermute | solution.py:344
  25.5 5.0 %collective-permute-start.4 = (bf16[32,2048]{1,0:T(8,128)(2,1)S(1)}, bf16[32,2048]{1,0:T(8,128)(2,1)S(1)}, u32[]{:S(2)}, u32[]{:S(2)}) collective-permute-start(bf16[32,2048]{1,0:T(8,128)(2,1)S(1)} %get-tuple-element.28), channel_id=1, source_target_pairs={{0,4},{1,3},{4,8},{5,1},{8,12},{9,5},{12,14},{13,9},{14,10},{15,13... | collective-permute-start | bytes 393224 | tf_op jit(solution)/shard_map/ppermute | solution.py:341
  26.0 5.8 %collective-permute-start.11 = (bf16[32,2048]{1,0:T(8,128)(2,1)S(1)}, bf16[32,2048]{1,0:T(8,128)(2,1)S(1)}, u32[]{:S(2)}, u32[]{:S(2)}) collective-permute-start(bf16[32,2048]{1,0:T(8,128)(2,1)S(1)} %add_convert_fusion.7), channel_id=1, source_target_pairs={{0,4},{1,3},{4,8},{5,1},{8,12},{9,5},{12,14},{13,9},{14,10},{15,13... | collective-permute-start | bytes 393224 | tf_op jit(solution)/shard_map/ppermute | solution.py:341
  30.5 5.0 %collective-permute-start.5 = (bf16[32,2048]{1,0:T(8,128)(2,1)S(1)}, bf16[32,2048]{1,0:T(8,128)(2,1)S(1)}, u32[]{:S(2)}, u32[]{:S(2)}) collective-permute-start(bf16[32,2048]{1,0:T(8,128)(2,1)S(1)} %add_convert_fusion.10), channel_id=1, source_target_pairs={{0,4},{1,3},{4,8},{5,1},{8,12},{9,5},{12,14},{13,9},{14,10},{15,13... | collective-permute-start | bytes 393224 | tf_op jit(solution)/shard_map/ppermute | solution.py:341
  31.9 5.0 %collective-permute-start.12 = (bf16[32,2048]{1,0:T(8,128)(2,1)S(1)}, bf16[32,2048]{1,0:T(8,128)(2,1)S(1)}, u32[]{:S(2)}, u32[]{:S(2)}) collective-permute-start(bf16[32,2048]{1,0:T(8,128)(2,1)S(1)} %add_convert_fusion.6), channel_id=1, source_target_pairs={{0,4},{1,3},{4,8},{5,1},{8,12},{9,5},{12,14},{13,9},{14,10},{15,13... | collective-permute-start | bytes 393224 | tf_op jit(solution)/shard_map/ppermute | solution.py:341
  35.5 5.0 %collective-permute-start.8 = (bf16[32,2048]{1,0:T(8,128)(2,1)S(1)}, bf16[32,2048]{1,0:T(8,128)(2,1)S(1)}, u32[]{:S(2)}, u32[]{:S(2)}) collective-permute-start(bf16[32,2048]{1,0:T(8,128)(2,1)S(1)} %add_convert_fusion.9), channel_id=1, source_target_pairs={{0,4},{1,3},{4,8},{5,1},{8,12},{9,5},{12,14},{13,9},{14,10},{15,13... | collective-permute-start | bytes 393224 | tf_op jit(solution)/shard_map/ppermute | solution.py:341
  36.9 3.7 %collective-permute-start.13 = (bf16[32,2048]{1,0:T(8,128)(2,1)S(1)}, bf16[32,2048]{1,0:T(8,128)(2,1)S(1)}, u32[]{:S(2)}, u32[]{:S(2)}) collective-permute-start(bf16[32,2048]{1,0:T(8,128)(2,1)S(1)} %collective-permute-done.12), channel_id=1, source_target_pairs={{0,1},{1,0},{2,3},{3,2},{4,5},{5,4},{6,7},{7,6},{8,9},{9,8},{10,11... | collective-permute-start | bytes 393224 | tf_op jit(solution)/shard_map/ppermute | solution.py:344
  40.6 6.3 %collective-permute-start.9 = (bf16[32,2048]{1,0:T(8,128)(2,1)S(1)}, bf16[32,2048]{1,0:T(8,128)(2,1)S(1)}, u32[]{:S(2)}, u32[]{:S(2)}) collective-permute-start(bf16[32,2048]{1,0:T(8,128)(2,1)S(1)} %add_convert_fusion.8), channel_id=1, source_target_pairs={{0,4},{1,3},{4,8},{5,1},{8,12},{9,5},{12,14},{13,9},{14,10},{15,13... | collective-permute-start | bytes 393224 | tf_op jit(solution)/shard_map/ppermute | solution.py:341
  47.2 5.0 %collective-permute-start.14 = (bf16[32,2048]{1,0:T(8,128)(2,1)S(1)}, bf16[32,2048]{1,0:T(8,128)(2,1)S(1)}, u32[]{:S(2)}, u32[]{:S(2)}) collective-permute-start(bf16[32,2048]{1,0:T(8,128)(2,1)S(1)} %fusion.2.refs_4_), channel_id=1, source_target_pairs={{0,2},{1,5},{4,0},{5,9},{8,4},{9,13},{12,8},{13,15},{14,12},{15,11... | collective-permute-start | bytes 393224 | tf_op jit(solution)/shard_map/ppermute | solution.py:341
  48.5 5.0 %collective-permute-start.18 = (bf16[32,2048]{1,0:T(8,128)(2,1)S(1)}, bf16[32,2048]{1,0:T(8,128)(2,1)S(1)}, u32[]{:S(2)}, u32[]{:S(2)}) collective-permute-start(bf16[32,2048]{1,0:T(8,128)(2,1)S(1)} %fusion.2.refs_4_), channel_id=1, source_target_pairs={{0,1},{1,0},{2,3},{3,2},{4,5},{5,4},{6,7},{7,6},{8,9},{9,8},{10,11... | collective-permute-start | bytes 393224 | tf_op jit(solution)/shard_map/ppermute | solution.py:344
  52.2 5.0 %collective-permute-start.15 = (bf16[32,2048]{1,0:T(8,128)(2,1)S(1)}, bf16[32,2048]{1,0:T(8,128)(2,1)S(1)}, u32[]{:S(2)}, u32[]{:S(2)}) collective-permute-start(bf16[32,2048]{1,0:T(8,128)(2,1)S(1)} %collective-permute-done.14.refs_2_), channel_id=1, source_target_pairs={{0,2},{1,5},{4,0},{5,9},{8,4},{9,13},{12,8},{13,15},{14,12},{15,11... | collective-permute-start | bytes 393224 | tf_op jit(solution)/shard_map/ppermute | solution.py:341
  53.5 5.1 %collective-permute-start.19 = (bf16[32,2048]{1,0:T(8,128)(2,1)S(1)}, bf16[32,2048]{1,0:T(8,128)(2,1)S(1)}, u32[]{:S(2)}, u32[]{:S(2)}) collective-permute-start(bf16[32,2048]{1,0:T(8,128)(2,1)S(1)} %collective-permute-done.18), channel_id=1, source_target_pairs={{0,2},{1,5},{4,0},{5,9},{8,4},{9,13},{12,8},{13,15},{14,12},{15,11... | collective-permute-start | bytes 393224 | tf_op jit(solution)/shard_map/ppermute | solution.py:341
  57.2 5.0 %collective-permute-start.16 = (bf16[32,2048]{1,0:T(8,128)(2,1)S(1)}, bf16[32,2048]{1,0:T(8,128)(2,1)S(1)}, u32[]{:S(2)}, u32[]{:S(2)}) collective-permute-start(bf16[32,2048]{1,0:T(8,128)(2,1)S(1)} %collective-permute-done.15.refs_0_), channel_id=1, source_target_pairs={{0,2},{1,5},{4,0},{5,9},{8,4},{9,13},{12,8},{13,15},{14,12},{15,11... | collective-permute-start | bytes 393224 | tf_op jit(solution)/shard_map/ppermute | solution.py:341
  58.6 5.0 %collective-permute-start.20 = (bf16[32,2048]{1,0:T(8,128)(2,1)S(1)}, bf16[32,2048]{1,0:T(8,128)(2,1)S(1)}, u32[]{:S(2)}, u32[]{:S(2)}) collective-permute-start(bf16[32,2048]{1,0:T(8,128)(2,1)S(1)} %collective-permute-done.19.refs_3_), channel_id=1, source_target_pairs={{0,2},{1,5},{4,0},{5,9},{8,4},{9,13},{12,8},{13,15},{14,12},{15,11... | collective-permute-start | bytes 393224 | tf_op jit(solution)/shard_map/ppermute | solution.py:341
  62.2 5.0 %collective-permute-start.17 = (bf16[32,2048]{1,0:T(8,128)(2,1)S(1)}, bf16[32,2048]{1,0:T(8,128)(2,1)S(1)}, u32[]{:S(2)}, u32[]{:S(2)}) collective-permute-start(bf16[32,2048]{1,0:T(8,128)(2,1)S(1)} %collective-permute-done.16.refs_1_), channel_id=1, source_target_pairs={{0,2},{1,5},{4,0},{5,9},{8,4},{9,13},{12,8},{13,15},{14,12},{15,11... | collective-permute-start | bytes 393224 | tf_op jit(solution)/shard_map/ppermute | solution.py:341
  63.6 5.1 %collective-permute-start.21 = (bf16[32,2048]{1,0:T(8,128)(2,1)S(1)}, bf16[32,2048]{1,0:T(8,128)(2,1)S(1)}, u32[]{:S(2)}, u32[]{:S(2)}) collective-permute-start(bf16[32,2048]{1,0:T(8,128)(2,1)S(1)} %collective-permute-done.20.refs_1_), channel_id=1, source_target_pairs={{0,2},{1,5},{4,0},{5,9},{8,4},{9,13},{12,8},{13,15},{14,12},{15,11... | collective-permute-start | bytes 393224 | tf_op jit(solution)/shard_map/ppermute | solution.py:341
  71.9 5.2 %collective-permute-start.29 = (bf16[32,2048]{1,0:T(8,128)(2,1)S(1)}, bf16[32,2048]{1,0:T(8,128)(2,1)S(1)}, u32[]{:S(2)}, u32[]{:S(2)}) collective-permute-start(bf16[32,2048]{1,0:T(8,128)(2,1)S(1)} %get-tuple-element.42), channel_id=1, source_target_pairs={{0,4},{1,3},{4,8},{5,1},{8,12},{9,5},{12,14},{13,9},{14,10},{15,13... | collective-permute-start | bytes 393224 | tf_op jit(solution)/shard_map/ppermute | solution.py:341
  72.5 6.0 %collective-permute-start.25 = (bf16[32,2048]{1,0:T(8,128)(2,1)S(1)}, bf16[32,2048]{1,0:T(8,128)(2,1)S(1)}, u32[]{:S(2)}, u32[]{:S(2)}) collective-permute-start(bf16[32,2048]{1,0:T(8,128)(2,1)S(1)} %get-tuple-element.37), channel_id=1, source_target_pairs={{0,4},{1,3},{4,8},{5,1},{8,12},{9,5},{12,14},{13,9},{14,10},{15,13... | collective-permute-start | bytes 393224 | tf_op jit(solution)/shard_map/ppermute | solution.py:341
  77.1 5.0 %collective-permute-start.30 = (bf16[32,2048]{1,0:T(8,128)(2,1)S(1)}, bf16[32,2048]{1,0:T(8,128)(2,1)S(1)}, u32[]{:S(2)}, u32[]{:S(2)}) collective-permute-start(bf16[32,2048]{1,0:T(8,128)(2,1)S(1)} %add_convert_fusion.1), channel_id=1, source_target_pairs={{0,4},{1,3},{4,8},{5,1},{8,12},{9,5},{12,14},{13,9},{14,10},{15,13... | collective-permute-start | bytes 393224 | tf_op jit(solution)/shard_map/ppermute | solution.py:341
  78.5 5.0 %collective-permute-start.26 = (bf16[32,2048]{1,0:T(8,128)(2,1)S(1)}, bf16[32,2048]{1,0:T(8,128)(2,1)S(1)}, u32[]{:S(2)}, u32[]{:S(2)}) collective-permute-start(bf16[32,2048]{1,0:T(8,128)(2,1)S(1)} %add_convert_fusion.4), channel_id=1, source_target_pairs={{0,4},{1,3},{4,8},{5,1},{8,12},{9,5},{12,14},{13,9},{14,10},{15,13... | collective-permute-start | bytes 393224 | tf_op jit(solution)/shard_map/ppermute | solution.py:341
  82.1 5.0 %collective-permute-start.31 = (bf16[32,2048]{1,0:T(8,128)(2,1)S(1)}, bf16[32,2048]{1,0:T(8,128)(2,1)S(1)}, u32[]{:S(2)}, u32[]{:S(2)}) collective-permute-start(bf16[32,2048]{1,0:T(8,128)(2,1)S(1)} %add_convert_fusion), channel_id=1, source_target_pairs={{0,4},{1,3},{4,8},{5,1},{8,12},{9,5},{12,14},{13,9},{14,10},{15,13... | collective-permute-start | bytes 393224 | tf_op jit(solution)/shard_map/ppermute | solution.py:341
  83.5 5.0 %collective-permute-start.27 = (bf16[32,2048]{1,0:T(8,128)(2,1)S(1)}, bf16[32,2048]{1,0:T(8,128)(2,1)S(1)}, u32[]{:S(2)}, u32[]{:S(2)}) collective-permute-start(bf16[32,2048]{1,0:T(8,128)(2,1)S(1)} %add_convert_fusion.3), channel_id=1, source_target_pairs={{0,4},{1,3},{4,8},{5,1},{8,12},{9,5},{12,14},{13,9},{14,10},{15,13... | collective-permute-start | bytes 393224 | tf_op jit(solution)/shard_map/ppermute | solution.py:341
  87.1 2.0 %collective-permute-start.32 = (bf16[32,2048]{1,0:T(8,128)(2,1)S(1)}, bf16[32,2048]{1,0:T(8,128)(2,1)S(1)}, u32[]{:S(2)}, u32[]{:S(2)}) collective-permute-start(bf16[32,2048]{1,0:T(8,128)(2,1)S(1)} %collective-permute-done.31), channel_id=1, source_target_pairs={{0,1},{1,0},{2,3},{3,2},{4,5},{5,4},{6,7},{7,6},{8,9},{9,8},{10,11... | collective-permute-start | bytes 393224 | tf_op jit(solution)/shard_map/ppermute | solution.py:344
  88.6 5.0 %collective-permute-start.28 = (bf16[32,2048]{1,0:T(8,128)(2,1)S(1)}, bf16[32,2048]{1,0:T(8,128)(2,1)S(1)}, u32[]{:S(2)}, u32[]{:S(2)}) collective-permute-start(bf16[32,2048]{1,0:T(8,128)(2,1)S(1)} %add_convert_fusion.2), channel_id=1, source_target_pairs={{0,4},{1,3},{4,8},{5,1},{8,12},{9,5},{12,14},{13,9},{14,10},{15,13... | collective-permute-start | bytes 393224 | tf_op jit(solution)/shard_map/ppermute | solution.py:341

commit v7 on v6

--- a/solution.py
+++ b/solution.py
@@ -64,14 +64,10 @@
     v_ref,
     ids_ref,
     numer_ref,
-    far_ref,
-    mine_ref,
-    give_ref,
-    own_ref,
-    q_rows,
-    out_rows,
-    tokens,
+    *refs,
 ):
+    far_ref, give_ref, own_ref = refs[:3]
+    mine_refs, (q_rows, out_rows, tokens) = refs[3 : hops + 2], refs[hops + 2 :]
     step, steps = pl.program_id(0), pl.num_programs(0)
     block, kv_count, cache_len, head_size = k_ref.shape
     rows, feats = q_ref.shape
@@ -150,7 +146,7 @@
         far_ref[...] = tokens[chip_at(-hops)]
         own_ref[...] = tokens[chip]
         for offset in range(1, hops):
-            mine_ref[offset - 1] = tokens[chip_at(-offset)]
+            mine_refs[offset - 1][...] = tokens[chip_at(-offset)]
             give_ref[offset - 1] = tokens[chip_at(offset)]
 
 
@@ -167,10 +163,10 @@
     several = jax.ShapeDtypeStruct((hops - 1, rows, wide), BF16)
     return pl.pallas_call(
         functools.partial(attend_kernel, chips, hops, chip_experts),
-        out_shape=(one, several, several, one),
+        out_shape=(one, several) + (one,) * hops,
         grid=(rows // block,),
         in_specs=[SMEM, VMEM, cache, cache, VMEM, VMEM],
-        out_specs=(VMEM,) * 4,
+        out_specs=(VMEM,) * (hops + 2),
         scratch_shapes=[
             pltpu.VMEM((rows * heads, head_size), F32),
             pltpu.VMEM((rows * heads, head_size), F32),
@@ -345,9 +341,8 @@
 
     weight_other = swapped(out_weight)
     own_experts = (w_gate, w_up, w_down)
-    other_experts = tuple(swapped(w) for w in own_experts)
-
-    far, mine, give, here = attend(
+
+    far, give, here, *mine = attend(
         devices,
         2 * local_experts,
         queries,
@@ -358,28 +353,37 @@
         gate_numer,
     )
     got = swapped(give)
+
+    def send(offset, mine, got):
+        return pass_on(jnp.concatenate([mine, got], axis=0), -offset)
+
+    kinds = [BF16, F32, BF16] + [F32] * (2 * hops - 3)
+    weights = (out_weight, weight_other)
     arrived = {0: here, hops: pass_on(far, -hops)}
-    for offset in range(hops - 1, 0, -1):
-        message = jnp.concatenate([mine[offset - 1], got[offset - 1]], axis=0)
-        arrived[offset] = pass_on(message, -offset)
-
-    kinds = [BF16, F32, BF16] + [F32] * (2 * hops - 3)
-    partial = project([arrived[hops], arrived[hops - 1]], kinds[:3], out_weight, weight_other)
+    arrived[hops - 1] = send(hops - 1, mine[hops - 2], got[hops - 2])
+    partial = project([arrived[hops], arrived[hops - 1]], kinds[:3], *weights)
+    first = pass_on(partial[0], 1)
+    first, mine, got, own_experts = lax.optimization_barrier((first, mine, got, own_experts))
+    for offset in range(hops - 2, 0, -1):
+        arrived[offset] = send(offset, mine[offset - 1], got[offset - 1])
     partial += project(
-        [arrived[offset] for offset in range(hops - 2, -1, -1)], kinds[3:], out_weight, weight_other
+        [arrived[offset] for offset in range(hops - 2, -1, -1)], kinds[3:], *weights
     )
-
-    def ring_sums(partial):
-        own, other = partial[0], partial[2]
+    other_experts = tuple(swapped(w) for w in own_experts)
+
+    def ring_sums(partial, first):
+        own, other = first, partial[2]
         for offset in range(hops - 1, 0, -1):
             spot = 1 + 2 * (hops - 1 - offset)
             if offset < hops - 1:
                 other = (pass_on(other, 1).astype(F32) + partial[spot + 1]).astype(BF16)
-            own = (pass_on(own, 1).astype(F32) + partial[spot]).astype(BF16)
+            if offset < hops - 1:
+                own = pass_on(own, 1)
+            own = (own.astype(F32) + partial[spot]).astype(BF16)
         other = swapped(pass_on(other, 1)).astype(F32)
         return pass_on(own, 1).astype(F32) + partial[-1] + other
 
-    residual = (hidden.astype(F32) + ring_sums(partial)).astype(BF16)
+    residual = (hidden.astype(F32) + ring_sums(partial, first)).astype(BF16)
     normed = rms_scale(residual.astype(F32), norm_gain).astype(BF16)
 
     def serve(pieces, kinds, digits):
@@ -398,7 +402,7 @@
     pieces = [pass_on(own, -1)] + pieces
     digits = [arrived[offset] for offset in range(hops, -1, -1)]
     total = serve(pieces[:3], kinds[:3], digits[:2]) + serve(pieces[3:], kinds[3:], digits[2:])
-    return (residual.astype(F32) + ring_sums(total)).astype(BF16)
+    return (residual.astype(F32) + ring_sums(total, pass_on(total[0], 1))).astype(BF16)
 
 
 def solution(mesh):

time: 94.5 us -> 93.5 us (0.989)
  waiting for transfers between devices: 54 us -> 49.8 us
  other arithmetic: 1.3 us -> 3.78 us
  starting transfers between devices: 25.3 us -> 26.8 us
    ppermute x25, waiting for transfers between devices: 54 us -> 48.3 us  [pass_on(): return lax.ppermute(array, 'rows', toward(step))]
    concatenate x3, other arithmetic: 0.03 us -> 2.51 us  [send(): return pass_on(jnp.concatenate([mine, got], axis=0), -offset)]
    ppermute x25, starting transfers between devices: 24.2 us -> 26.3 us  [pass_on(): return lax.ppermute(array, 'rows', toward(step))]
    ppermute x8, waiting for transfers between devices: 0.02 us -> 1.51 us  [swapped(): return lax.ppermute(array, 'rows', swap)]
  transfers between devices with their start and end apart: 33 -> 33, of which waited for: 22 -> 23; matrix products, arithmetic and copies ran while one was open for 2% -> 3% of each run, Pallas kernels for 10% -> 10%
where the time goes in v7:
time: 93.5 us; the launch traced here: 93.3 us
  waiting for transfers between devices  49.8 us (53%)
  starting transfers between devices  26.8 us (29%)
  Pallas kernels  12.6 us (13%)
  other arithmetic  3.78 us (4%)
    ppermute x25, waiting for transfers between devices, pass_on(): return lax.ppermute(array, 'rows', toward(step))  48.3 us
    ppermute x25, starting transfers between devices, pass_on(): return lax.ppermute(array, 'rows', toward(step))  26.3 us
    pallas_call x2, Pallas kernels, experts(): pl.pallas_call(functools.partial(expert_kernel, len(pieces), len(digits),...  6.55 us
    pallas_call x1, Pallas kernels, attend(): pl.pallas_call(functools.partial(attend_kernel, chips, hops, chip_experts...  5.04 us
    concatenate x3, other arithmetic, send(): return pass_on(jnp.concatenate([mine, got], axis=0), -offset)  2.51 us
  transfers between devices with their start and end apart: 33, of which 23 were waited for; matrix products, arithmetic and copies ran while one was open for 3% of the time, Pallas kernels for 10%

profile of v7, /device:TPU:0, one launch (start us, length us, event | category | flops | bytes accessed | tf_op | source)
XLA Modules:
  0.0 93.3 jit_solution(13491303826226086846)
XLA Ops:
  0.0 0.5 collective-permute-start.3
  0.5 5.0 %shard_map.118 = (bf16[32,640]{1,0:T(8,128)(2,1)}, bf16[3,32,640]{2,1,0:T(8,128)(2,1)}, bf16[32,640]{1,0:T(8,128)(2,1)}, bf16[32,640]{1,0:T(8,128)(2,1)}, bf16[3...) custom-call(s32[32]{0:T(128)} %lengths_ref.1, bf16[32,4096]{1,0:T(8,128)(2,1)} %q_ref.1, bf16[32,2,128,128]{3,2,1,0:T(8,128)(2,1)} %k_ref.1, ...), custom_call_target="tpu_custom_call" | custom-call | flops 67108864 | bytes 4194304 | tf_op jit(solution)/shard_map/pallas_call | solution.py:164
  5.5 0.1 collective-permute-start.1
  5.6 1.5 %collective-permute-done.1 = bf16[3,32,640]{2,1,0:T(8,128)(2,1)S(1)} collective-permute-done((bf16[3,32,640]{2,1,0:T(8,128)(2,1)}, bf16[3,32,640]{2,1,0:T(8,128)(2,1)S(1)}, u32[]{:S(2)}, u32[]{:S(2)}) %collective-permute-start.1) | collective-permute-done | bytes 122912 | tf_op jit(solution)/shard_map/ppermute | solution.py:340
  7.1 0.8 pad_maximum_fusion
  7.9 4.7 %collective-permute-start.2 = (bf16[64,640]{1,0:T(8,128)(2,1)S(1)}, bf16[64,640]{1,0:T(8,128)(2,1)S(1)}, u32[]{:S(2)}, u32[]{:S(2)}) collective-permute-start(bf16[64,640]{1,0:T(8,128)(2,1)S(1)} %pad_maximum_fusion), channel_id=1, source_target_pairs={{0,10},{1,13},{4,6},{5,15},{8,2},{9,11},{12,0},{13,7},{14,4},{15,3... | collective-permute-start | bytes 245768 | tf_op jit(solution)/shard_map/ppermute | solution.py:337
  12.6 1.3 %collective-permute-start = (bf16[32,640]{1,0:T(8,128)(2,1)}, bf16[32,640]{1,0:T(8,128)(2,1)S(1)}, u32[]{:S(2)}, u32[]{:S(2)}) collective-permute-start(bf16[32,640]{1,0:T(8,128)(2,1)} %get-tuple-element.34), channel_id=1, source_target_pairs={{0,14},{1,15},{4,10},{5,11},{8,6},{9,7},{12,2},{13,3},{14,0},{15,1... | collective-permute-start | bytes 122888 | tf_op jit(solution)/shard_map/ppermute | solution.py:337
  13.9 5.6 %collective-permute-done.refs_0_.refs_3_ = bf16[32,640]{1,0:T(8,128)(2,1)S(1)} collective-permute-done((bf16[32,640]{1,0:T(8,128)(2,1)}, bf16[32,640]{1,0:T(8,128)(2,1)S(1)}, u32[]{:S(2)}, u32[]{:S(2)}) %collective-permute-start) | collective-permute-done | bytes 40992 | tf_op jit(solution)/shard_map/ppermute | solution.py:337
  19.5 0.5 shard_map.119
  20.0 0.0 copy-start.5
  20.0 0.0 copy-start.6
  20.0 0.1 collective-permute-start.4
  20.1 1.8 %collective-permute-start.10 = (bf16[32,2048]{1,0:T(8,128)(2,1)S(1)}, bf16[32,2048]{1,0:T(8,128)(2,1)S(1)}, u32[]{:S(2)}, u32[]{:S(2)}) collective-permute-start(bf16[32,2048]{1,0:T(8,128)(2,1)S(1)} %get-tuple-element.49), channel_id=1, source_target_pairs={{0,4},{1,3},{4,8},{5,1},{8,12},{9,5},{12,14},{13,9},{14,10},{15,13... | collective-permute-start | bytes 393224 | tf_op jit(solution)/shard_map/ppermute | solution.py:337
  21.9 3.1 %collective-permute-done.4 = bf16[32,2048]{1,0:T(8,128)(2,1)S(1)} collective-permute-done((bf16[32,2048]{1,0:T(8,128)(2,1)S(1)}, bf16[32,2048]{1,0:T(8,128)(2,1)S(1)}, u32[]{:S(2)}, u32[]{:S(2)}) %collective-permute-start.4) | collective-permute-done | bytes 131104 | tf_op jit(solution)/shard_map/ppermute | solution.py:337
  25.1 0.0 copy-start.2
  25.1 0.9 %pad_maximum_fusion.1 = bf16[64,640]{1,0:T(8,128)(2,1)S(1)} fusion(bf16[32,640]{1,0:T(8,128)(2,1)S(1)} %get-tuple-element.66, bf16[32,640]{1,0:T(8,128)(2,1)} %get-tuple-element.42), kind=kLoop, calls=%fused_computation.19 | loop fusion | flops 163840 | bytes 163840 | tf_op jit(solution)/shard_map/concatenate | solution.py:358
  26.0 0.6 collective-permute-start.6
  26.6 0.8 pad_maximum_fusion.2
  27.4 1.4 %collective-permute-start.7 = (bf16[64,640]{1,0:T(8,128)(2,1)S(1)}, bf16[64,640]{1,0:T(8,128)(2,1)S(1)}, u32[]{:S(2)}, u32[]{:S(2)}) collective-permute-start(bf16[64,640]{1,0:T(8,128)(2,1)S(1)} %pad_maximum_fusion.2), channel_id=1, source_target_pairs={{0,2},{1,5},{4,0},{5,9},{8,4},{9,13},{12,8},{13,15},{14,12},{15,11... | collective-permute-start | bytes 245768 | tf_op jit(solution)/shard_map/ppermute | solution.py:337
  28.8 1.1 %collective-permute-start.5 = (bf16[32,2048]{1,0:T(8,128)(2,1)S(1)}, bf16[32,2048]{1,0:T(8,128)(2,1)S(1)}, u32[]{:S(2)}, u32[]{:S(2)}) collective-permute-start(bf16[32,2048]{1,0:T(8,128)(2,1)S(1)} %add_convert_fusion.10), channel_id=1, source_target_pairs={{0,4},{1,3},{4,8},{5,1},{8,12},{9,5},{12,14},{13,9},{14,10},{15,13... | collective-permute-start | bytes 393224 | tf_op jit(solution)/shard_map/ppermute | solution.py:337
  29.9 2.7 %collective-permute-done.6.refs_0_.refs_5_ = bf16[64,640]{1,0:T(8,128)(2,1)S(1)} collective-permute-done((bf16[64,640]{1,0:T(8,128)(2,1)S(1)}, bf16[64,640]{1,0:T(8,128)(2,1)S(1)}, u32[]{:S(2)}, u32[]{:S(2)}) %collective-permute-start.6) | collective-permute-done | bytes 81952 | tf_op jit(solution)/shard_map/ppermute | solution.py:337
  32.7 1.4 %collective-permute-done.7.refs_1_.refs_6_ = bf16[64,640]{1,0:T(8,128)(2,1)S(1)} collective-permute-done((bf16[64,640]{1,0:T(8,128)(2,1)S(1)}, bf16[64,640]{1,0:T(8,128)(2,1)S(1)}, u32[]{:S(2)}, u32[]{:S(2)}) %collective-permute-start.7) | collective-permute-done | bytes 81952 | tf_op jit(solution)/shard_map/ppermute | solution.py:337
  34.0 0.5 shard_map.120
  34.6 0.8 collective-permute-start.11
  35.4 0.3 collective-permute-start.8
  35.8 3.9 %collective-permute-done.11 = bf16[32,2048]{1,0:T(8,128)(2,1)S(1)} collective-permute-done((bf16[32,2048]{1,0:T(8,128)(2,1)S(1)}, bf16[32,2048]{1,0:T(8,128)(2,1)S(1)}, u32[]{:S(2)}, u32[]{:S(2)}) %collective-permute-start.11) | collective-permute-done | bytes 131104 | tf_op jit(solution)/shard_map/ppermute | solution.py:337
  39.7 0.8 collective-permute-start.12
  40.5 0.6 collective-permute-done.8
  41.1 0.8 collective-permute-start.9
  41.9 2.8 %collective-permute-done.12 = bf16[32,2048]{1,0:T(8,128)(2,1)S(1)} collective-permute-done((bf16[32,2048]{1,0:T(8,128)(2,1)S(1)}, bf16[32,2048]{1,0:T(8,128)(2,1)S(1)}, u32[]{:S(2)}, u32[]{:S(2)}) %collective-permute-start.12) | collective-permute-done | bytes 131104 | tf_op jit(solution)/shard_map/ppermute | solution.py:337
  44.7 1.4 %collective-permute-done.9 = bf16[32,2048]{1,0:T(8,128)(2,1)S(1)} collective-permute-done((bf16[32,2048]{1,0:T(8,128)(2,1)S(1)}, bf16[32,2048]{1,0:T(8,128)(2,1)S(1)}, u32[]{:S(2)}, u32[]{:S(2)}) %collective-permute-start.9) | collective-permute-done | bytes 131104 | tf_op jit(solution)/shard_map/ppermute | solution.py:337
  46.1 0.2 fusion
  46.3 0.1 fusion.2.refs_4_
  46.4 1.1 %collective-permute-start.14 = (bf16[32,2048]{1,0:T(8,128)(2,1)S(1)}, bf16[32,2048]{1,0:T(8,128)(2,1)S(1)}, u32[]{:S(2)}, u32[]{:S(2)}) collective-permute-start(bf16[32,2048]{1,0:T(8,128)(2,1)S(1)} %fusion.2.refs_4_), channel_id=1, source_target_pairs={{0,2},{1,5},{4,0},{5,9},{8,4},{9,13},{12,8},{13,15},{14,12},{15,11... | collective-permute-start | bytes 393224 | tf_op jit(solution)/shard_map/ppermute | solution.py:337
  47.5 3.9 %collective-permute-done.14.refs_2_ = bf16[32,2048]{1,0:T(8,128)(2,1)S(1)} collective-permute-done((bf16[32,2048]{1,0:T(8,128)(2,1)S(1)}, bf16[32,2048]{1,0:T(8,128)(2,1)S(1)}, u32[]{:S(2)}, u32[]{:S(2)}) %collective-permute-start.14) | collective-permute-done | bytes 131104 | tf_op jit(solution)/shard_map/ppermute | solution.py:337
  51.4 1.1 %collective-permute-start.15 = (bf16[32,2048]{1,0:T(8,128)(2,1)S(1)}, bf16[32,2048]{1,0:T(8,128)(2,1)S(1)}, u32[]{:S(2)}, u32[]{:S(2)}) collective-permute-start(bf16[32,2048]{1,0:T(8,128)(2,1)S(1)} %collective-permute-done.14.refs_2_), channel_id=1, source_target_pairs={{0,2},{1,5},{4,0},{5,9},{8,4},{9,13},{12,8},{13,15},{14,12},{15,11... | collective-permute-start | bytes 393224 | tf_op jit(solution)/shard_map/ppermute | solution.py:337
  52.5 0.7 collective-permute-start.19
  53.2 3.2 %collective-permute-done.15.refs_0_ = bf16[32,2048]{1,0:T(8,128)(2,1)S(1)} collective-permute-done((bf16[32,2048]{1,0:T(8,128)(2,1)S(1)}, bf16[32,2048]{1,0:T(8,128)(2,1)S(1)}, u32[]{:S(2)}, u32[]{:S(2)}) %collective-permute-start.15) | collective-permute-done | bytes 131104 | tf_op jit(solution)/shard_map/ppermute | solution.py:337
  56.4 1.1 %collective-permute-start.16 = (bf16[32,2048]{1,0:T(8,128)(2,1)S(1)}, bf16[32,2048]{1,0:T(8,128)(2,1)S(1)}, u32[]{:S(2)}, u32[]{:S(2)}) collective-permute-start(bf16[32,2048]{1,0:T(8,128)(2,1)S(1)} %collective-permute-done.15.refs_0_), channel_id=1, source_target_pairs={{0,2},{1,5},{4,0},{5,9},{8,4},{9,13},{12,8},{13,15},{14,12},{15,11... | collective-permute-start | bytes 393224 | tf_op jit(solution)/shard_map/ppermute | solution.py:337
  57.5 0.3 collective-permute-done.19.refs_3_
  57.8 1.1 %collective-permute-start.20 = (bf16[32,2048]{1,0:T(8,128)(2,1)S(1)}, bf16[32,2048]{1,0:T(8,128)(2,1)S(1)}, u32[]{:S(2)}, u32[]{:S(2)}) collective-permute-start(bf16[32,2048]{1,0:T(8,128)(2,1)S(1)} %collective-permute-done.19.refs_3_), channel_id=1, source_target_pairs={{0,2},{1,5},{4,0},{5,9},{8,4},{9,13},{12,8},{13,15},{14,12},{15,11... | collective-permute-start | bytes 393224 | tf_op jit(solution)/shard_map/ppermute | solution.py:337
  58.9 2.5 %collective-permute-done.16.refs_1_ = bf16[32,2048]{1,0:T(8,128)(2,1)S(1)} collective-permute-done((bf16[32,2048]{1,0:T(8,128)(2,1)S(1)}, bf16[32,2048]{1,0:T(8,128)(2,1)S(1)}, u32[]{:S(2)}, u32[]{:S(2)}) %collective-permute-start.16) | collective-permute-done | bytes 131104 | tf_op jit(solution)/shard_map/ppermute | solution.py:337
  61.4 1.1 %collective-permute-start.17 = (bf16[32,2048]{1,0:T(8,128)(2,1)S(1)}, bf16[32,2048]{1,0:T(8,128)(2,1)S(1)}, u32[]{:S(2)}, u32[]{:S(2)}) collective-permute-start(bf16[32,2048]{1,0:T(8,128)(2,1)S(1)} %collective-permute-done.16.refs_1_), channel_id=1, source_target_pairs={{0,2},{1,5},{4,0},{5,9},{8,4},{9,13},{12,8},{13,15},{14,12},{15,11... | collective-permute-start | bytes 393224 | tf_op jit(solution)/shard_map/ppermute | solution.py:337
  62.4 0.3 collective-permute-done.20.refs_1_
  62.8 1.1 %collective-permute-start.21 = (bf16[32,2048]{1,0:T(8,128)(2,1)S(1)}, bf16[32,2048]{1,0:T(8,128)(2,1)S(1)}, u32[]{:S(2)}, u32[]{:S(2)}) collective-permute-start(bf16[32,2048]{1,0:T(8,128)(2,1)S(1)} %collective-permute-done.20.refs_1_), channel_id=1, source_target_pairs={{0,2},{1,5},{4,0},{5,9},{8,4},{9,13},{12,8},{13,15},{14,12},{15,11... | collective-permute-start | bytes 393224 | tf_op jit(solution)/shard_map/ppermute | solution.py:337
  63.8 2.5 %collective-permute-done.17.refs_0_ = bf16[32,2048]{1,0:T(8,128)(2,1)S(1)} collective-permute-done((bf16[32,2048]{1,0:T(8,128)(2,1)S(1)}, bf16[32,2048]{1,0:T(8,128)(2,1)S(1)}, u32[]{:S(2)}, u32[]{:S(2)}) %collective-permute-start.17) | collective-permute-done | bytes 131104 | tf_op jit(solution)/shard_map/ppermute | solution.py:337
  66.3 1.4 %collective-permute-done.21.refs_2_ = bf16[32,2048]{1,0:T(8,128)(2,1)S(1)} collective-permute-done((bf16[32,2048]{1,0:T(8,128)(2,1)S(1)}, bf16[32,2048]{1,0:T(8,128)(2,1)S(1)}, u32[]{:S(2)}, u32[]{:S(2)}) %collective-permute-start.21) | collective-permute-done | bytes 131104 | tf_op jit(solution)/shard_map/ppermute | solution.py:337
  67.8 3.2 %shard_map.121 = (bf16[32,2048]{1,0:T(8,128)(2,1)S(1)}, f32[32,2048]{1,0:T(8,128)S(1)}, bf16[32,2048]{1,0:T(8,128)(2,1)S(1)}) custom-call(bf16[32,2048]{1,0:T(8,128)(2,1)S(1)} %collective-permute-done.17.refs_0_, bf16[32,2048]{1,0:T(8,128)(2,1)S(1)} %collective-permute-done.16.refs_1_, bf16[32,2048]{1,0:T(8,128)(2,1)S(1)} %collective-permute-done.21.refs_2_, ...), custom_call_target="tpu_custom_call" | custom-call | flops 1811939328 | bytes 196608 | tf_op jit(solution)/shard_map/pallas_call | solution.py:295
  71.0 0.8 collective-permute-start.29
  71.7 0.6 collective-permute-start.25
  72.4 3.3 %shard_map.122 = (f32[32,2048]{1,0:T(8,128)S(1)}, f32[32,2048]{1,0:T(8,128)S(1)}, f32[32,2048]{1,0:T(8,128)S(1)}, f32[32,2048]{1,0:T(8,128)S(1)}, f32[32,2048]{1,0:T(8,128)S(1)}) custom-call(bf16[32,2048]{1,0:T(8,128)(2,1)S(1)} %collective-permute-done.15.refs_0_, bf16[32,2048]{1,0:T(8,128)(2,1)S(1)} %collective-permute-done.20.refs_1_, ...), custom_call_target="tpu_custom_call" | custom-call | flops 3019898880 | bytes 327680 | tf_op jit(solution)/shard_map/pallas_call | solution.py:295
  75.7 0.3 collective-permute-done.29
  76.0 0.8 collective-permute-start.30
  76.8 0.6 collective-permute-done.25
  77.4 0.8 collective-permute-start.26
  78.2 2.8 %collective-permute-done.30 = bf16[32,2048]{1,0:T(8,128)(2,1)S(1)} collective-permute-done((bf16[32,2048]{1,0:T(8,128)(2,1)S(1)}, bf16[32,2048]{1,0:T(8,128)(2,1)S(1)}, u32[]{:S(2)}, u32[]{:S(2)}) %collective-permute-start.30) | collective-permute-done | bytes 131104 | tf_op jit(solution)/shard_map/ppermute | solution.py:337
  81.1 0.8 collective-permute-start.31
  81.9 0.6 collective-permute-done.26
  82.5 0.8 collective-permute-start.27
  83.3 2.8 %collective-permute-done.31 = bf16[32,2048]{1,0:T(8,128)(2,1)S(1)} collective-permute-done((bf16[32,2048]{1,0:T(8,128)(2,1)S(1)}, bf16[32,2048]{1,0:T(8,128)(2,1)S(1)}, u32[]{:S(2)}, u32[]{:S(2)}) %collective-permute-start.31) | collective-permute-done | bytes 131104 | tf_op jit(solution)/shard_map/ppermute | solution.py:337
  86.1 1.4 %collective-permute-done.27 = bf16[32,2048]{1,0:T(8,128)(2,1)S(1)} collective-permute-done((bf16[32,2048]{1,0:T(8,128)(2,1)S(1)}, bf16[32,2048]{1,0:T(8,128)(2,1)S(1)}, u32[]{:S(2)}, u32[]{:S(2)}) %collective-permute-start.27) | collective-permute-done | bytes 131104 | tf_op jit(solution)/shard_map/ppermute | solution.py:337
  87.5 0.8 collective-permute-start.28
  88.3 4.2 %collective-permute-done.28 = bf16[32,2048]{1,0:T(8,128)(2,1)S(1)} collective-permute-done((bf16[32,2048]{1,0:T(8,128)(2,1)S(1)}, bf16[32,2048]{1,0:T(8,128)(2,1)S(1)}, u32[]{:S(2)}, u32[]{:S(2)}) %collective-permute-start.28) | collective-permute-done | bytes 131104 | tf_op jit(solution)/shard_map/ppermute | solution.py:337
  92.5 0.7 fusion.3
  (40 shorter events, 0.4 us)
Async XLA Ops:
  0.0 19.5 %copy-start.3 = (bf16[256,2048]{1,0:T(8,128)(2,1)S(1)}, bf16[256,2048]{1,0:T(8,128)(2,1)}, u32[]{:S(2)}) copy-start(bf16[256,2048]{1,0:T(8,128)(2,1)} %refs_3_.1) | copy-start | bytes 3145732
  0.0 19.5 %collective-permute-start.3 = (bf16[256,2048]{1,0:T(8,128)(2,1)}, bf16[256,2048]{1,0:T(8,128)(2,1)S(1)}, u32[]{:S(2)}, u32[]{:S(2)}) collective-permute-start(bf16[256,2048]{1,0:T(8,128)(2,1)} %refs_3_.1), channel_id=1, source_target_pairs={{0,1},{1,0},{2,3},{3,2},{4,5},{5,4},{6,7},{7,6},{8,9},{9,8},{10,11... | collective-permute-start | bytes 3145736 | tf_op jit(solution)/shard_map/ppermute | solution.py:340
  0.5 29.5 %copy-start = (bf16[1,2048,768]{2,1,0:T(8,128)(2,1)S(1)}, bf16[1,2048,768]{2,1,0:T(8,128)(2,1)}, u32[]{:S(2)}) copy-start(bf16[1,2048,768]{2,1,0:T(8,128)(2,1)} %refs_8_) | copy-start | bytes 9437188
  0.5 32.2 %copy-start.1 = (bf16[1,2048,768]{2,1,0:T(8,128)(2,1)S(1)}, bf16[1,2048,768]{2,1,0:T(8,128)(2,1)}, u32[]{:S(2)}) copy-start(bf16[1,2048,768]{2,1,0:T(8,128)(2,1)} %refs_9_) | copy-start | bytes 9437188
  5.5 28.5 %copy-start.4 = (bf16[32,640]{1,0:T(8,128)(2,1)S(1)}, bf16[32,640]{1,0:T(8,128)(2,1)}, u32[]{:S(2)}) copy-start(bf16[32,640]{1,0:T(8,128)(2,1)} %get-tuple-element.45.refs_2_.refs_7_) | copy-start | bytes 122884
  5.5 1.6 %collective-permute-start.1 = (bf16[3,32,640]{2,1,0:T(8,128)(2,1)}, bf16[3,32,640]{2,1,0:T(8,128)(2,1)S(1)}, u32[]{:S(2)}, u32[]{:S(2)}) collective-permute-start(bf16[3,32,640]{2,1,0:T(8,128)(2,1)} %get-tuple-element.36), channel_id=1, source_target_pairs={{0,1},{1,0},{2,3},{3,2},{4,5},{5,4},{6,7},{7,6},{8,9},{9,8},{10,11... | collective-permute-start | bytes 368648 | tf_op jit(solution)/shard_map/ppermute | solution.py:340
  7.9 11.6 %collective-permute-start.2 = (bf16[64,640]{1,0:T(8,128)(2,1)S(1)}, bf16[64,640]{1,0:T(8,128)(2,1)S(1)}, u32[]{:S(2)}, u32[]{:S(2)}) collective-permute-start(bf16[64,640]{1,0:T(8,128)(2,1)S(1)} %pad_maximum_fusion), channel_id=1, source_target_pairs={{0,10},{1,13},{4,6},{5,15},{8,2},{9,11},{12,0},{13,7},{14,4},{15,3... | collective-permute-start | bytes 245768 | tf_op jit(solution)/shard_map/ppermute | solution.py:337
  12.6 6.9 %collective-permute-start = (bf16[32,640]{1,0:T(8,128)(2,1)}, bf16[32,640]{1,0:T(8,128)(2,1)S(1)}, u32[]{:S(2)}, u32[]{:S(2)}) collective-permute-start(bf16[32,640]{1,0:T(8,128)(2,1)} %get-tuple-element.34), channel_id=1, source_target_pairs={{0,14},{1,15},{4,10},{5,11},{8,6},{9,7},{12,2},{13,3},{14,0},{15,1... | collective-permute-start | bytes 122888 | tf_op jit(solution)/shard_map/ppermute | solution.py:337
  20.0 26.1 %copy-start.5 = (bf16[32,2048]{1,0:T(8,128)(2,1)S(1)}, bf16[32,2048]{1,0:T(8,128)(2,1)}, u32[]{:S(2)}) copy-start(bf16[32,2048]{1,0:T(8,128)(2,1)} %param.16) | copy-start | bytes 393220
  20.0 26.3 %copy-start.6 = (f32[2048]{0:T(1024)S(1)}, f32[2048]{0:T(1024)}, u32[]{:S(2)}) copy-start(f32[2048]{0:T(1024)} %param.18) | copy-start | bytes 24580
  20.0 5.0 %collective-permute-start.4 = (bf16[32,2048]{1,0:T(8,128)(2,1)S(1)}, bf16[32,2048]{1,0:T(8,128)(2,1)S(1)}, u32[]{:S(2)}, u32[]{:S(2)}) collective-permute-start(bf16[32,2048]{1,0:T(8,128)(2,1)S(1)} %get-tuple-element.37), channel_id=1, source_target_pairs={{0,4},{1,3},{4,8},{5,1},{8,12},{9,5},{12,14},{13,9},{14,10},{15,13... | collective-permute-start | bytes 393224 | tf_op jit(solution)/shard_map/ppermute | solution.py:337
  20.1 14.5 %collective-permute-start.10 = (bf16[32,2048]{1,0:T(8,128)(2,1)S(1)}, bf16[32,2048]{1,0:T(8,128)(2,1)S(1)}, u32[]{:S(2)}, u32[]{:S(2)}) collective-permute-start(bf16[32,2048]{1,0:T(8,128)(2,1)S(1)} %get-tuple-element.49), channel_id=1, source_target_pairs={{0,4},{1,3},{4,8},{5,1},{8,12},{9,5},{12,14},{13,9},{14,10},{15,13... | collective-permute-start | bytes 393224 | tf_op jit(solution)/shard_map/ppermute | solution.py:337
  25.1 42.7 %copy-start.2 = (bf16[1,768,2048]{2,1,0:T(8,128)(2,1)S(1)}, bf16[1,768,2048]{2,1,0:T(8,128)(2,1)}, u32[]{:S(2)}) copy-start(bf16[1,768,2048]{2,1,0:T(8,128)(2,1)} %refs_10_) | copy-start | bytes 9437188
  26.0 6.7 %collective-permute-start.6 = (bf16[64,640]{1,0:T(8,128)(2,1)S(1)}, bf16[64,640]{1,0:T(8,128)(2,1)S(1)}, u32[]{:S(2)}, u32[]{:S(2)}) collective-permute-start(bf16[64,640]{1,0:T(8,128)(2,1)S(1)} %pad_maximum_fusion.1), channel_id=1, source_target_pairs={{0,6},{1,9},{4,2},{5,13},{8,0},{9,15},{12,4},{13,11},{14,8},{15,7}... | collective-permute-start | bytes 245768 | tf_op jit(solution)/shard_map/ppermute | solution.py:337
  27.4 6.7 %collective-permute-start.7 = (bf16[64,640]{1,0:T(8,128)(2,1)S(1)}, bf16[64,640]{1,0:T(8,128)(2,1)S(1)}, u32[]{:S(2)}, u32[]{:S(2)}) collective-permute-start(bf16[64,640]{1,0:T(8,128)(2,1)S(1)} %pad_maximum_fusion.2), channel_id=1, source_target_pairs={{0,2},{1,5},{4,0},{5,9},{8,4},{9,13},{12,8},{13,15},{14,12},{15,11... | collective-permute-start | bytes 245768 | tf_op jit(solution)/shard_map/ppermute | solution.py:337
  28.8 6.6 %collective-permute-start.5 = (bf16[32,2048]{1,0:T(8,128)(2,1)S(1)}, bf16[32,2048]{1,0:T(8,128)(2,1)S(1)}, u32[]{:S(2)}, u32[]{:S(2)}) collective-permute-start(bf16[32,2048]{1,0:T(8,128)(2,1)S(1)} %add_convert_fusion.10), channel_id=1, source_target_pairs={{0,4},{1,3},{4,8},{5,1},{8,12},{9,5},{12,14},{13,9},{14,10},{15,13... | collective-permute-start | bytes 393224 | tf_op jit(solution)/shard_map/ppermute | solution.py:337
  29.9 37.8 %collective-permute-start.22 = (bf16[1,2048,768]{2,1,0:T(8,128)(2,1)S(1)}, bf16[1,2048,768]{2,1,0:T(8,128)(2,1)S(1)}, u32[]{:S(2)}, u32[]{:S(2)}) collective-permute-start(bf16[1,2048,768]{2,1,0:T(8,128)(2,1)S(1)} %copy-done), channel_id=1, source_target_pairs={{0,1},{1,0},{2,3},{3,2},{4,5},{5,4},{6,7},{7,6},{8,9},{9,8},{10,11... | collective-permute-start | bytes 9437192 | tf_op jit(solution)/shard_map/ppermute | solution.py:340
  32.7 35.1 %collective-permute-start.23 = (bf16[1,2048,768]{2,1,0:T(8,128)(2,1)S(1)}, bf16[1,2048,768]{2,1,0:T(8,128)(2,1)S(1)}, u32[]{:S(2)}, u32[]{:S(2)}) collective-permute-start(bf16[1,2048,768]{2,1,0:T(8,128)(2,1)S(1)} %copy-done.1), channel_id=1, source_target_pairs={{0,1},{1,0},{2,3},{3,2},{4,5},{5,4},{6,7},{7,6},{8,9},{9,8},{10,11... | collective-permute-start | bytes 9437192 | tf_op jit(solution)/shard_map/ppermute | solution.py:340
  34.0 33.7 %collective-permute-start.24 = (bf16[1,768,2048]{2,1,0:T(8,128)(2,1)}, bf16[1,768,2048]{2,1,0:T(8,128)(2,1)S(1)}, u32[]{:S(2)}, u32[]{:S(2)}) collective-permute-start(bf16[1,768,2048]{2,1,0:T(8,128)(2,1)} %refs_10_), channel_id=1, source_target_pairs={{0,1},{1,0},{2,3},{3,2},{4,5},{5,4},{6,7},{7,6},{8,9},{9,8},{10,11... | collective-permute-start | bytes 9437192 | tf_op jit(solution)/shard_map/ppermute | solution.py:340
  34.6 5.0 %collective-permute-start.11 = (bf16[32,2048]{1,0:T(8,128)(2,1)S(1)}, bf16[32,2048]{1,0:T(8,128)(2,1)S(1)}, u32[]{:S(2)}, u32[]{:S(2)}) collective-permute-start(bf16[32,2048]{1,0:T(8,128)(2,1)S(1)} %add_convert_fusion.7), channel_id=1, source_target_pairs={{0,4},{1,3},{4,8},{5,1},{8,12},{9,5},{12,14},{13,9},{14,10},{15,13... | collective-permute-start | bytes 393224 | tf_op jit(solution)/shard_map/ppermute | solution.py:337
  35.4 5.6 %collective-permute-start.8 = (bf16[32,2048]{1,0:T(8,128)(2,1)S(1)}, bf16[32,2048]{1,0:T(8,128)(2,1)S(1)}, u32[]{:S(2)}, u32[]{:S(2)}) collective-permute-start(bf16[32,2048]{1,0:T(8,128)(2,1)S(1)} %add_convert_fusion.9), channel_id=1, source_target_pairs={{0,4},{1,3},{4,8},{5,1},{8,12},{9,5},{12,14},{13,9},{14,10},{15,13... | collective-permute-start | bytes 393224 | tf_op jit(solution)/shard_map/ppermute | solution.py:337
  39.7 5.0 %collective-permute-start.12 = (bf16[32,2048]{1,0:T(8,128)(2,1)S(1)}, bf16[32,2048]{1,0:T(8,128)(2,1)S(1)}, u32[]{:S(2)}, u32[]{:S(2)}) collective-permute-start(bf16[32,2048]{1,0:T(8,128)(2,1)S(1)} %add_convert_fusion.6), channel_id=1, source_target_pairs={{0,4},{1,3},{4,8},{5,1},{8,12},{9,5},{12,14},{13,9},{14,10},{15,13... | collective-permute-start | bytes 393224 | tf_op jit(solution)/shard_map/ppermute | solution.py:337
  41.1 5.0 %collective-permute-start.9 = (bf16[32,2048]{1,0:T(8,128)(2,1)S(1)}, bf16[32,2048]{1,0:T(8,128)(2,1)S(1)}, u32[]{:S(2)}, u32[]{:S(2)}) collective-permute-start(bf16[32,2048]{1,0:T(8,128)(2,1)S(1)} %add_convert_fusion.8), channel_id=1, source_target_pairs={{0,4},{1,3},{4,8},{5,1},{8,12},{9,5},{12,14},{13,9},{14,10},{15,13... | collective-permute-start | bytes 393224 | tf_op jit(solution)/shard_map/ppermute | solution.py:337
  44.7 1.4 %collective-permute-start.13 = (bf16[32,2048]{1,0:T(8,128)(2,1)S(1)}, bf16[32,2048]{1,0:T(8,128)(2,1)S(1)}, u32[]{:S(2)}, u32[]{:S(2)}) collective-permute-start(bf16[32,2048]{1,0:T(8,128)(2,1)S(1)} %collective-permute-done.12), channel_id=1, source_target_pairs={{0,1},{1,0},{2,3},{3,2},{4,5},{5,4},{6,7},{7,6},{8,9},{9,8},{10,11... | collective-permute-start | bytes 393224 | tf_op jit(solution)/shard_map/ppermute | solution.py:340
  46.4 5.0 %collective-permute-start.14 = (bf16[32,2048]{1,0:T(8,128)(2,1)S(1)}, bf16[32,2048]{1,0:T(8,128)(2,1)S(1)}, u32[]{:S(2)}, u32[]{:S(2)}) collective-permute-start(bf16[32,2048]{1,0:T(8,128)(2,1)S(1)} %fusion.2.refs_4_), channel_id=1, source_target_pairs={{0,2},{1,5},{4,0},{5,9},{8,4},{9,13},{12,8},{13,15},{14,12},{15,11... | collective-permute-start | bytes 393224 | tf_op jit(solution)/shard_map/ppermute | solution.py:337
  47.5 5.0 %collective-permute-start.18 = (bf16[32,2048]{1,0:T(8,128)(2,1)S(1)}, bf16[32,2048]{1,0:T(8,128)(2,1)S(1)}, u32[]{:S(2)}, u32[]{:S(2)}) collective-permute-start(bf16[32,2048]{1,0:T(8,128)(2,1)S(1)} %fusion.2.refs_4_), channel_id=1, source_target_pairs={{0,1},{1,0},{2,3},{3,2},{4,5},{5,4},{6,7},{7,6},{8,9},{9,8},{10,11... | collective-permute-start | bytes 393224 | tf_op jit(solution)/shard_map/ppermute | solution.py:340
  51.4 5.0 %collective-permute-start.15 = (bf16[32,2048]{1,0:T(8,128)(2,1)S(1)}, bf16[32,2048]{1,0:T(8,128)(2,1)S(1)}, u32[]{:S(2)}, u32[]{:S(2)}) collective-permute-start(bf16[32,2048]{1,0:T(8,128)(2,1)S(1)} %collective-permute-done.14.refs_2_), channel_id=1, source_target_pairs={{0,2},{1,5},{4,0},{5,9},{8,4},{9,13},{12,8},{13,15},{14,12},{15,11... | collective-permute-start | bytes 393224 | tf_op jit(solution)/shard_map/ppermute | solution.py:337
  52.5 5.3 %collective-permute-start.19 = (bf16[32,2048]{1,0:T(8,128)(2,1)S(1)}, bf16[32,2048]{1,0:T(8,128)(2,1)S(1)}, u32[]{:S(2)}, u32[]{:S(2)}) collective-permute-start(bf16[32,2048]{1,0:T(8,128)(2,1)S(1)} %collective-permute-done.18), channel_id=1, source_target_pairs={{0,2},{1,5},{4,0},{5,9},{8,4},{9,13},{12,8},{13,15},{14,12},{15,11... | collective-permute-start | bytes 393224 | tf_op jit(solution)/shard_map/ppermute | solution.py:337
  56.4 5.0 %collective-permute-start.16 = (bf16[32,2048]{1,0:T(8,128)(2,1)S(1)}, bf16[32,2048]{1,0:T(8,128)(2,1)S(1)}, u32[]{:S(2)}, u32[]{:S(2)}) collective-permute-start(bf16[32,2048]{1,0:T(8,128)(2,1)S(1)} %collective-permute-done.15.refs_0_), channel_id=1, source_target_pairs={{0,2},{1,5},{4,0},{5,9},{8,4},{9,13},{12,8},{13,15},{14,12},{15,11... | collective-permute-start | bytes 393224 | tf_op jit(solution)/shard_map/ppermute | solution.py:337
  57.8 5.0 %collective-permute-start.20 = (bf16[32,2048]{1,0:T(8,128)(2,1)S(1)}, bf16[32,2048]{1,0:T(8,128)(2,1)S(1)}, u32[]{:S(2)}, u32[]{:S(2)}) collective-permute-start(bf16[32,2048]{1,0:T(8,128)(2,1)S(1)} %collective-permute-done.19.refs_3_), channel_id=1, source_target_pairs={{0,2},{1,5},{4,0},{5,9},{8,4},{9,13},{12,8},{13,15},{14,12},{15,11... | collective-permute-start | bytes 393224 | tf_op jit(solution)/shard_map/ppermute | solution.py:337
  61.4 5.0 %collective-permute-start.17 = (bf16[32,2048]{1,0:T(8,128)(2,1)S(1)}, bf16[32,2048]{1,0:T(8,128)(2,1)S(1)}, u32[]{:S(2)}, u32[]{:S(2)}) collective-permute-start(bf16[32,2048]{1,0:T(8,128)(2,1)S(1)} %collective-permute-done.16.refs_1_), channel_id=1, source_target_pairs={{0,2},{1,5},{4,0},{5,9},{8,4},{9,13},{12,8},{13,15},{14,12},{15,11... | collective-permute-start | bytes 393224 | tf_op jit(solution)/shard_map/ppermute | solution.py:337
  62.8 5.0 %collective-permute-start.21 = (bf16[32,2048]{1,0:T(8,128)(2,1)S(1)}, bf16[32,2048]{1,0:T(8,128)(2,1)S(1)}, u32[]{:S(2)}, u32[]{:S(2)}) collective-permute-start(bf16[32,2048]{1,0:T(8,128)(2,1)S(1)} %collective-permute-done.20.refs_1_), channel_id=1, source_target_pairs={{0,2},{1,5},{4,0},{5,9},{8,4},{9,13},{12,8},{13,15},{14,12},{15,11... | collective-permute-start | bytes 393224 | tf_op jit(solution)/shard_map/ppermute | solution.py:337
  71.0 5.0 %collective-permute-start.29 = (bf16[32,2048]{1,0:T(8,128)(2,1)S(1)}, bf16[32,2048]{1,0:T(8,128)(2,1)S(1)}, u32[]{:S(2)}, u32[]{:S(2)}) collective-permute-start(bf16[32,2048]{1,0:T(8,128)(2,1)S(1)} %get-tuple-element.60), channel_id=1, source_target_pairs={{0,4},{1,3},{4,8},{5,1},{8,12},{9,5},{12,14},{13,9},{14,10},{15,13... | collective-permute-start | bytes 393224 | tf_op jit(solution)/shard_map/ppermute | solution.py:337
  71.7 5.6 %collective-permute-start.25 = (bf16[32,2048]{1,0:T(8,128)(2,1)S(1)}, bf16[32,2048]{1,0:T(8,128)(2,1)S(1)}, u32[]{:S(2)}, u32[]{:S(2)}) collective-permute-start(bf16[32,2048]{1,0:T(8,128)(2,1)S(1)} %get-tuple-element.55), channel_id=1, source_target_pairs={{0,4},{1,3},{4,8},{5,1},{8,12},{9,5},{12,14},{13,9},{14,10},{15,13... | collective-permute-start | bytes 393224 | tf_op jit(solution)/shard_map/ppermute | solution.py:337
  76.0 5.0 %collective-permute-start.30 = (bf16[32,2048]{1,0:T(8,128)(2,1)S(1)}, bf16[32,2048]{1,0:T(8,128)(2,1)S(1)}, u32[]{:S(2)}, u32[]{:S(2)}) collective-permute-start(bf16[32,2048]{1,0:T(8,128)(2,1)S(1)} %add_convert_fusion.1), channel_id=1, source_target_pairs={{0,4},{1,3},{4,8},{5,1},{8,12},{9,5},{12,14},{13,9},{14,10},{15,13... | collective-permute-start | bytes 393224 | tf_op jit(solution)/shard_map/ppermute | solution.py:337
  77.4 5.0 %collective-permute-start.26 = (bf16[32,2048]{1,0:T(8,128)(2,1)S(1)}, bf16[32,2048]{1,0:T(8,128)(2,1)S(1)}, u32[]{:S(2)}, u32[]{:S(2)}) collective-permute-start(bf16[32,2048]{1,0:T(8,128)(2,1)S(1)} %add_convert_fusion.4), channel_id=1, source_target_pairs={{0,4},{1,3},{4,8},{5,1},{8,12},{9,5},{12,14},{13,9},{14,10},{15,13... | collective-permute-start | bytes 393224 | tf_op jit(solution)/shard_map/ppermute | solution.py:337
  81.1 5.0 %collective-permute-start.31 = (bf16[32,2048]{1,0:T(8,128)(2,1)S(1)}, bf16[32,2048]{1,0:T(8,128)(2,1)S(1)}, u32[]{:S(2)}, u32[]{:S(2)}) collective-permute-start(bf16[32,2048]{1,0:T(8,128)(2,1)S(1)} %add_convert_fusion), channel_id=1, source_target_pairs={{0,4},{1,3},{4,8},{5,1},{8,12},{9,5},{12,14},{13,9},{14,10},{15,13... | collective-permute-start | bytes 393224 | tf_op jit(solution)/shard_map/ppermute | solution.py:337
  82.5 5.0 %collective-permute-start.27 = (bf16[32,2048]{1,0:T(8,128)(2,1)S(1)}, bf16[32,2048]{1,0:T(8,128)(2,1)S(1)}, u32[]{:S(2)}, u32[]{:S(2)}) collective-permute-start(bf16[32,2048]{1,0:T(8,128)(2,1)S(1)} %add_convert_fusion.3), channel_id=1, source_target_pairs={{0,4},{1,3},{4,8},{5,1},{8,12},{9,5},{12,14},{13,9},{14,10},{15,13... | collective-permute-start | bytes 393224 | tf_op jit(solution)/shard_map/ppermute | solution.py:337
  86.1 2.2 %collective-permute-start.32 = (bf16[32,2048]{1,0:T(8,128)(2,1)S(1)}, bf16[32,2048]{1,0:T(8,128)(2,1)S(1)}, u32[]{:S(2)}, u32[]{:S(2)}) collective-permute-start(bf16[32,2048]{1,0:T(8,128)(2,1)S(1)} %collective-permute-done.31), channel_id=1, source_target_pairs={{0,1},{1,0},{2,3},{3,2},{4,5},{5,4},{6,7},{7,6},{8,9},{9,8},{10,11... | collective-permute-start | bytes 393224 | tf_op jit(solution)/shard_map/ppermute | solution.py:340
  87.5 5.0 %collective-permute-start.28 = (bf16[32,2048]{1,0:T(8,128)(2,1)S(1)}, bf16[32,2048]{1,0:T(8,128)(2,1)S(1)}, u32[]{:S(2)}, u32[]{:S(2)}) collective-permute-start(bf16[32,2048]{1,0:T(8,128)(2,1)S(1)} %add_convert_fusion.2), channel_id=1, source_target_pairs={{0,4},{1,3},{4,8},{5,1},{8,12},{9,5},{12,14},{13,9},{14,10},{15,13... | collective-permute-start | bytes 393224 | tf_op jit(solution)/shard_map/ppermute | solution.py:337

commit v8 on v7

--- a/solution.py
+++ b/solution.py
@@ -157,7 +157,7 @@
     heads = feats // head_size
     extra = -(-2 * chip_experts // 128) * 128
     wide = feats // chips + extra
-    block = 16
+    block = 32
     cache = pl.BlockSpec((block, kv_count, cache_len, head_size), lambda t: (t, 0, 0, 0))
     one = jax.ShapeDtypeStruct((rows, wide), BF16)
     several = jax.ShapeDtypeStruct((hops - 1, rows, wide), BF16)
@@ -357,13 +357,13 @@
     def send(offset, mine, got):
         return pass_on(jnp.concatenate([mine, got], axis=0), -offset)
 
-    kinds = [BF16, F32, BF16] + [F32] * (2 * hops - 3)
+    kinds = [BF16, BF16, BF16] + [F32] * (2 * hops - 3)
     weights = (out_weight, weight_other)
     arrived = {0: here, hops: pass_on(far, -hops)}
     arrived[hops - 1] = send(hops - 1, mine[hops - 2], got[hops - 2])
     partial = project([arrived[hops], arrived[hops - 1]], kinds[:3], *weights)
-    first = pass_on(partial[0], 1)
-    first, mine, got, own_experts = lax.optimization_barrier((first, mine, got, own_experts))
+    first = pass_on(partial[0], 2)
+    first, own_experts = lax.optimization_barrier((first, own_experts))
     for offset in range(hops - 2, 0, -1):
         arrived[offset] = send(offset, mine[offset - 1], got[offset - 1])
     partial += project(
@@ -371,15 +371,15 @@
     )
     other_experts = tuple(swapped(w) for w in own_experts)
 
-    def ring_sums(partial, first):
-        own, other = first, partial[2]
-        for offset in range(hops - 1, 0, -1):
+    def ring_sums(partial, far):
+        own, other = partial[1].astype(BF16), partial[2]
+        for offset in range(hops - 2, 0, -1):
             spot = 1 + 2 * (hops - 1 - offset)
-            if offset < hops - 1:
-                other = (pass_on(other, 1).astype(F32) + partial[spot + 1]).astype(BF16)
-            if offset < hops - 1:
-                own = pass_on(own, 1)
-            own = (own.astype(F32) + partial[spot]).astype(BF16)
+            own = pass_on(own, 1).astype(F32) + partial[spot]
+            if offset == hops - 2:
+                own = own + far.astype(F32)
+            own = own.astype(BF16)
+            other = (pass_on(other, 1).astype(F32) + partial[spot + 1]).astype(BF16)
         other = swapped(pass_on(other, 1)).astype(F32)
         return pass_on(own, 1).astype(F32) + partial[-1] + other
 
@@ -402,7 +402,7 @@
     pieces = [pass_on(own, -1)] + pieces
     digits = [arrived[offset] for offset in range(hops, -1, -1)]
     total = serve(pieces[:3], kinds[:3], digits[:2]) + serve(pieces[3:], kinds[3:], digits[2:])
-    return (residual.astype(F32) + ring_sums(total, pass_on(total[0], 1))).astype(BF16)
+    return (residual.astype(F32) + ring_sums(total, pass_on(total[0], 2))).astype(BF16)
 
 
 def solution(mesh):

time: 93.5 us -> 91.3 us (0.976)
  waiting for transfers between devices: 49.8 us -> 41.5 us
  starting transfers between devices: 26.8 us -> 30.1 us
  local copies, waits for them, and re-layouts: 0.05 us -> 3.26 us
    ppermute x25, waiting for transfers between devices: 48.3 us -> 38.7 us  [pass_on(): return lax.ppermute(array, 'rows', toward(step))]
    unnamed x14 -> x16, local copies, waits for them, and re-layouts: 0.03 us -> 3.25 us
    ppermute x25, starting transfers between devices: 26.3 us -> 28.9 us  [pass_on(): return lax.ppermute(array, 'rows', toward(step))]
    ppermute x8, waiting for transfers between devices: 1.51 us -> 2.74 us  [swapped(): return lax.ppermute(array, 'rows', swap)]
  transfers between devices with their start and end apart: 33 -> 33, of which waited for: 23 -> 19; matrix products, arithmetic and copies ran while one was open for 3% -> 3% of each run, Pallas kernels for 10% -> 10%
where the time goes in v8:
time: 91.3 us; the launch traced here: 90.9 us
  waiting for transfers between devices  41.5 us (45%)
  starting transfers between devices  30.1 us (33%)
  Pallas kernels  12.2 us (13%)
  other arithmetic  3.64 us (4%)
  local copies, waits for them, and re-layouts  3.26 us (4%)
    ppermute x25, waiting for transfers between devices, pass_on(): return lax.ppermute(array, 'rows', toward(step))  38.7 us
    ppermute x25, starting transfers between devices, pass_on(): return lax.ppermute(array, 'rows', toward(step))  28.9 us
    pallas_call x2, Pallas kernels, experts(): pl.pallas_call(functools.partial(expert_kernel, len(pieces), len(digits),...  6.56 us
    pallas_call x1, Pallas kernels, attend(): pl.pallas_call(functools.partial(attend_kernel, chips, hops, chip_experts...  4.67 us
    unnamed x16, local copies, waits for them, and re-layouts  3.25 us
    ppermute x8, waiting for transfers between devices, swapped(): return lax.ppermute(array, 'rows', swap)  2.74 us
    concatenate x3, other arithmetic, send(): return pass_on(jnp.concatenate([mine, got], axis=0), -offset)  2.36 us
  transfers between devices with their start and end apart: 33, of which 19 were waited for; matrix products, arithmetic and copies ran while one was open for 3% of the time, Pallas kernels for 10%

profile of v8, /device:TPU:0, one launch (start us, length us, event | category | flops | bytes accessed | tf_op | source)
XLA Modules:
  0.0 90.9 jit_solution(10984602836789385851)
XLA Ops:
  0.0 0.5 collective-permute-start.3
  0.5 4.7 %shard_map.118 = (bf16[32,640]{1,0:T(8,128)(2,1)}, bf16[3,32,640]{2,1,0:T(8,128)(2,1)}, bf16[32,640]{1,0:T(8,128)(2,1)}, bf16[32,640]{1,0:T(8,128)(2,1)}, bf16[3...) custom-call(s32[32]{0:T(128)} %lengths_ref.1, bf16[32,4096]{1,0:T(8,128)(2,1)} %q_ref.1, bf16[32,2,128,128]{3,2,1,0:T(8,128)(2,1)} %k_ref.1, ...), custom_call_target="tpu_custom_call" | custom-call | flops 67108864 | bytes 4194304 | tf_op jit(solution)/shard_map/pallas_call | solution.py:164
  5.1 0.1 collective-permute-start.1
  5.2 6.0 %collective-permute-start = (bf16[32,640]{1,0:T(8,128)(2,1)}, bf16[32,640]{1,0:T(8,128)(2,1)S(1)}, u32[]{:S(2)}, u32[]{:S(2)}) collective-permute-start(bf16[32,640]{1,0:T(8,128)(2,1)} %get-tuple-element.31), channel_id=1, source_target_pairs={{0,14},{1,15},{4,10},{5,11},{8,6},{9,7},{12,2},{13,3},{14,0},{15,1... | collective-permute-start | bytes 122888 | tf_op jit(solution)/shard_map/ppermute | solution.py:337
  11.3 0.8 pad_maximum_fusion
  12.1 0.2 collective-permute-start.2
  12.2 0.8 pad_maximum_fusion.1
  13.0 1.5 %collective-permute-start.5 = (bf16[64,640]{1,0:T(8,128)(2,1)S(1)}, bf16[64,640]{1,0:T(8,128)(2,1)S(1)}, u32[]{:S(2)}, u32[]{:S(2)}) collective-permute-start(bf16[64,640]{1,0:T(8,128)(2,1)S(1)} %pad_maximum_fusion.1), channel_id=1, source_target_pairs={{0,6},{1,9},{4,2},{5,13},{8,0},{9,15},{12,4},{13,11},{14,8},{15,7}... | collective-permute-start | bytes 245768 | tf_op jit(solution)/shard_map/ppermute | solution.py:337
  14.5 4.0 %collective-permute-done.2.refs_1_.refs_4_ = bf16[64,640]{1,0:T(8,128)(2,1)S(1)} collective-permute-done((bf16[64,640]{1,0:T(8,128)(2,1)S(1)}, bf16[64,640]{1,0:T(8,128)(2,1)S(1)}, u32[]{:S(2)}, u32[]{:S(2)}) %collective-permute-start.2) | collective-permute-done | bytes 81952 | tf_op jit(solution)/shard_map/ppermute | solution.py:337
  18.5 0.0 collective-permute-done.3.refs_3_.refs_4_
  18.5 1.2 %copy-done.3 = bf16[256,2048]{1,0:T(8,128)(2,1)S(1)} copy-done((bf16[256,2048]{1,0:T(8,128)(2,1)S(1)}, bf16[256,2048]{1,0:T(8,128)(2,1)}, u32[]{:S(2)}) %copy-start.3) | copy-done | bytes 1048600
  19.7 0.5 shard_map.119
  20.2 0.4 collective-permute-start.10
  20.6 2.4 %collective-permute-start.7 = (bf16[32,2048]{1,0:T(8,128)(2,1)S(1)}, bf16[32,2048]{1,0:T(8,128)(2,1)S(1)}, u32[]{:S(2)}, u32[]{:S(2)}) collective-permute-start(bf16[32,2048]{1,0:T(8,128)(2,1)S(1)} %get-tuple-element.39), channel_id=1, source_target_pairs={{0,8},{1,7},{4,12},{5,3},{8,14},{9,1},{12,10},{13,5},{14,6},{15,9}... | collective-permute-start | bytes 393224 | tf_op jit(solution)/shard_map/ppermute | solution.py:337
  23.0 0.8 pad_maximum_fusion.2
  23.7 0.0 collective-permute-start.6
  23.8 2.0 %collective-permute-start.4 = (bf16[32,2048]{1,0:T(8,128)(2,1)S(1)}, bf16[32,2048]{1,0:T(8,128)(2,1)S(1)}, u32[]{:S(2)}, u32[]{:S(2)}) collective-permute-start(bf16[32,2048]{1,0:T(8,128)(2,1)S(1)} %get-tuple-element.34), channel_id=1, source_target_pairs={{0,4},{1,3},{4,8},{5,1},{8,12},{9,5},{12,14},{13,9},{14,10},{15,13... | collective-permute-start | bytes 393224 | tf_op jit(solution)/shard_map/ppermute | solution.py:337
  25.8 3.5 %collective-permute-done.6.refs_1_.refs_6_ = bf16[64,640]{1,0:T(8,128)(2,1)S(1)} collective-permute-done((bf16[64,640]{1,0:T(8,128)(2,1)S(1)}, bf16[64,640]{1,0:T(8,128)(2,1)S(1)}, u32[]{:S(2)}, u32[]{:S(2)}) %collective-permute-start.6) | collective-permute-done | bytes 81952 | tf_op jit(solution)/shard_map/ppermute | solution.py:337
  29.3 1.2 %copy-done.4 = bf16[256,2048]{1,0:T(8,128)(2,1)S(1)} copy-done((bf16[256,2048]{1,0:T(8,128)(2,1)S(1)}, bf16[256,2048]{1,0:T(8,128)(2,1)}, u32[]{:S(2)}) %copy-start.4) | copy-done | bytes 1048600
  30.5 0.8 copy-done.5
  31.3 0.5 shard_map.120
  31.8 0.1 collective-permute-start.22
  31.9 0.5 collective-permute-start.23
  32.4 0.1 collective-permute-start.24
  32.5 0.6 collective-permute-start.11
  33.2 0.1 collective-permute-start.8
  33.3 4.3 %collective-permute-done.11 = bf16[32,2048]{1,0:T(8,128)(2,1)S(1)} collective-permute-done((bf16[32,2048]{1,0:T(8,128)(2,1)S(1)}, bf16[32,2048]{1,0:T(8,128)(2,1)S(1)}, u32[]{:S(2)}, u32[]{:S(2)}) %collective-permute-start.11) | collective-permute-done | bytes 131104 | tf_op jit(solution)/shard_map/ppermute | solution.py:337
  37.6 0.6 collective-permute-start.12
  38.2 0.8 collective-permute-done.8
  39.0 0.6 collective-permute-start.9
  39.6 3.0 %collective-permute-done.12 = bf16[32,2048]{1,0:T(8,128)(2,1)S(1)} collective-permute-done((bf16[32,2048]{1,0:T(8,128)(2,1)S(1)}, bf16[32,2048]{1,0:T(8,128)(2,1)S(1)}, u32[]{:S(2)}, u32[]{:S(2)}) %collective-permute-start.12) | collective-permute-done | bytes 131104 | tf_op jit(solution)/shard_map/ppermute | solution.py:337
  42.6 1.4 %collective-permute-done.9 = bf16[32,2048]{1,0:T(8,128)(2,1)S(1)} collective-permute-done((bf16[32,2048]{1,0:T(8,128)(2,1)S(1)}, bf16[32,2048]{1,0:T(8,128)(2,1)S(1)}, u32[]{:S(2)}, u32[]{:S(2)}) %collective-permute-start.9) | collective-permute-done | bytes 131104 | tf_op jit(solution)/shard_map/ppermute | solution.py:337
  44.0 2.7 %collective-permute-done.13 = bf16[32,2048]{1,0:T(8,128)(2,1)S(1)} collective-permute-done((bf16[32,2048]{1,0:T(8,128)(2,1)S(1)}, bf16[32,2048]{1,0:T(8,128)(2,1)S(1)}, u32[]{:S(2)}, u32[]{:S(2)}) %collective-permute-start.13) | collective-permute-done | bytes 131104 | tf_op jit(solution)/shard_map/ppermute | solution.py:340
  46.8 0.2 fusion
  47.0 0.1 fusion.2.refs_4_
  47.1 1.2 %collective-permute-start.14 = (bf16[32,2048]{1,0:T(8,128)(2,1)S(1)}, bf16[32,2048]{1,0:T(8,128)(2,1)S(1)}, u32[]{:S(2)}, u32[]{:S(2)}) collective-permute-start(bf16[32,2048]{1,0:T(8,128)(2,1)S(1)} %fusion.2.refs_4_), channel_id=1, source_target_pairs={{0,2},{1,5},{4,0},{5,9},{8,4},{9,13},{12,8},{13,15},{14,12},{15,11... | collective-permute-start | bytes 393224 | tf_op jit(solution)/shard_map/ppermute | solution.py:337
  48.3 3.8 %collective-permute-done.14.refs_2_ = bf16[32,2048]{1,0:T(8,128)(2,1)S(1)} collective-permute-done((bf16[32,2048]{1,0:T(8,128)(2,1)S(1)}, bf16[32,2048]{1,0:T(8,128)(2,1)S(1)}, u32[]{:S(2)}, u32[]{:S(2)}) %collective-permute-start.14) | collective-permute-done | bytes 131104 | tf_op jit(solution)/shard_map/ppermute | solution.py:337
  52.1 1.2 %collective-permute-start.15 = (bf16[32,2048]{1,0:T(8,128)(2,1)S(1)}, bf16[32,2048]{1,0:T(8,128)(2,1)S(1)}, u32[]{:S(2)}, u32[]{:S(2)}) collective-permute-start(bf16[32,2048]{1,0:T(8,128)(2,1)S(1)} %collective-permute-done.14.refs_2_), channel_id=1, source_target_pairs={{0,2},{1,5},{4,0},{5,9},{8,4},{9,13},{12,8},{13,15},{14,12},{15,11... | collective-permute-start | bytes 393224 | tf_op jit(solution)/shard_map/ppermute | solution.py:337
  53.3 0.0 collective-permute-start.19
  53.3 3.7 %collective-permute-done.15.refs_0_ = bf16[32,2048]{1,0:T(8,128)(2,1)S(1)} collective-permute-done((bf16[32,2048]{1,0:T(8,128)(2,1)S(1)}, bf16[32,2048]{1,0:T(8,128)(2,1)S(1)}, u32[]{:S(2)}, u32[]{:S(2)}) %collective-permute-start.15) | collective-permute-done | bytes 131104 | tf_op jit(solution)/shard_map/ppermute | solution.py:337
  57.1 1.2 %collective-permute-start.16 = (bf16[32,2048]{1,0:T(8,128)(2,1)S(1)}, bf16[32,2048]{1,0:T(8,128)(2,1)S(1)}, u32[]{:S(2)}, u32[]{:S(2)}) collective-permute-start(bf16[32,2048]{1,0:T(8,128)(2,1)S(1)} %collective-permute-done.15.refs_0_), channel_id=1, source_target_pairs={{0,2},{1,5},{4,0},{5,9},{8,4},{9,13},{12,8},{13,15},{14,12},{15,11... | collective-permute-start | bytes 393224 | tf_op jit(solution)/shard_map/ppermute | solution.py:337
  58.2 0.2 collective-permute-done.19.refs_3_
  58.5 1.2 %collective-permute-start.20 = (bf16[32,2048]{1,0:T(8,128)(2,1)S(1)}, bf16[32,2048]{1,0:T(8,128)(2,1)S(1)}, u32[]{:S(2)}, u32[]{:S(2)}) collective-permute-start(bf16[32,2048]{1,0:T(8,128)(2,1)S(1)} %collective-permute-done.19.refs_3_), channel_id=1, source_target_pairs={{0,2},{1,5},{4,0},{5,9},{8,4},{9,13},{12,8},{13,15},{14,12},{15,11... | collective-permute-start | bytes 393224 | tf_op jit(solution)/shard_map/ppermute | solution.py:337
  59.6 2.4 %collective-permute-done.16.refs_1_ = bf16[32,2048]{1,0:T(8,128)(2,1)S(1)} collective-permute-done((bf16[32,2048]{1,0:T(8,128)(2,1)S(1)}, bf16[32,2048]{1,0:T(8,128)(2,1)S(1)}, u32[]{:S(2)}, u32[]{:S(2)}) %collective-permute-start.16) | collective-permute-done | bytes 131104 | tf_op jit(solution)/shard_map/ppermute | solution.py:337
  62.0 1.2 %collective-permute-start.17 = (bf16[32,2048]{1,0:T(8,128)(2,1)S(1)}, bf16[32,2048]{1,0:T(8,128)(2,1)S(1)}, u32[]{:S(2)}, u32[]{:S(2)}) collective-permute-start(bf16[32,2048]{1,0:T(8,128)(2,1)S(1)} %collective-permute-done.16.refs_1_), channel_id=1, source_target_pairs={{0,2},{1,5},{4,0},{5,9},{8,4},{9,13},{12,8},{13,15},{14,12},{15,11... | collective-permute-start | bytes 393224 | tf_op jit(solution)/shard_map/ppermute | solution.py:337
  63.2 0.2 collective-permute-done.20.refs_1_
  63.4 1.2 %collective-permute-start.21 = (bf16[32,2048]{1,0:T(8,128)(2,1)S(1)}, bf16[32,2048]{1,0:T(8,128)(2,1)S(1)}, u32[]{:S(2)}, u32[]{:S(2)}) collective-permute-start(bf16[32,2048]{1,0:T(8,128)(2,1)S(1)} %collective-permute-done.20.refs_1_), channel_id=1, source_target_pairs={{0,2},{1,5},{4,0},{5,9},{8,4},{9,13},{12,8},{13,15},{14,12},{15,11... | collective-permute-start | bytes 393224 | tf_op jit(solution)/shard_map/ppermute | solution.py:337
  64.6 2.4 %collective-permute-done.17.refs_0_ = bf16[32,2048]{1,0:T(8,128)(2,1)S(1)} collective-permute-done((bf16[32,2048]{1,0:T(8,128)(2,1)S(1)}, bf16[32,2048]{1,0:T(8,128)(2,1)S(1)}, u32[]{:S(2)}, u32[]{:S(2)}) %collective-permute-start.17) | collective-permute-done | bytes 131104 | tf_op jit(solution)/shard_map/ppermute | solution.py:337
  67.0 1.4 %collective-permute-done.21.refs_2_ = bf16[32,2048]{1,0:T(8,128)(2,1)S(1)} collective-permute-done((bf16[32,2048]{1,0:T(8,128)(2,1)S(1)}, bf16[32,2048]{1,0:T(8,128)(2,1)S(1)}, u32[]{:S(2)}, u32[]{:S(2)}) %collective-permute-start.21) | collective-permute-done | bytes 131104 | tf_op jit(solution)/shard_map/ppermute | solution.py:337
  68.4 3.2 %shard_map.121 = (bf16[32,2048]{1,0:T(8,128)(2,1)S(1)}, bf16[32,2048]{1,0:T(8,128)(2,1)S(1)}, bf16[32,2048]{1,0:T(8,128)(2,1)S(1)}) custom-call(bf16[32,2048]{1,0:T(8,128)(2,1)S(1)} %collective-permute-done.17.refs_0_, bf16[32,2048]{1,0:T(8,128)(2,1)S(1)} %collective-permute-done.16.refs_1_, bf16[32,2048]{1,0:T(8,128)(2,1)S(1)} %collective-permute-done.21.refs_2_, ...), custom_call_target="tpu_custom_call" | custom-call | flops 1811939328 | bytes 196608 | tf_op jit(solution)/shard_map/pallas_call | solution.py:295
  71.6 0.7 collective-permute-start.29
  72.3 0.4 collective-permute-start.26
  72.7 1.4 %collective-permute-start.25 = (bf16[32,2048]{1,0:T(8,128)(2,1)S(1)}, bf16[32,2048]{1,0:T(8,128)(2,1)S(1)}, u32[]{:S(2)}, u32[]{:S(2)}) collective-permute-start(bf16[32,2048]{1,0:T(8,128)(2,1)S(1)} %get-tuple-element.49), channel_id=1, source_target_pairs={{0,4},{1,3},{4,8},{5,1},{8,12},{9,5},{12,14},{13,9},{14,10},{15,13... | collective-permute-start | bytes 393224 | tf_op jit(solution)/shard_map/ppermute | solution.py:337
  74.1 3.3 %shard_map.122 = (f32[32,2048]{1,0:T(8,128)S(1)}, f32[32,2048]{1,0:T(8,128)S(1)}, f32[32,2048]{1,0:T(8,128)S(1)}, f32[32,2048]{1,0:T(8,128)S(1)}, f32[32,2048]{1,0:T(8,128)S(1)}) custom-call(bf16[32,2048]{1,0:T(8,128)(2,1)S(1)} %collective-permute-done.15.refs_0_, bf16[32,2048]{1,0:T(8,128)(2,1)S(1)} %collective-permute-done.20.refs_1_, ...), custom_call_target="tpu_custom_call" | custom-call | flops 3019898880 | bytes 327680 | tf_op jit(solution)/shard_map/pallas_call | solution.py:295
  77.5 1.8 %collective-permute-start.30 = (bf16[32,2048]{1,0:T(8,128)(2,1)S(1)}, bf16[32,2048]{1,0:T(8,128)(2,1)S(1)}, u32[]{:S(2)}, u32[]{:S(2)}) collective-permute-start(bf16[32,2048]{1,0:T(8,128)(2,1)S(1)} %add_convert_fusion.1), channel_id=1, source_target_pairs={{0,4},{1,3},{4,8},{5,1},{8,12},{9,5},{12,14},{13,9},{14,10},{15,13... | collective-permute-start | bytes 393224 | tf_op jit(solution)/shard_map/ppermute | solution.py:337
  79.3 0.2 collective-permute-done.26
  79.5 0.7 collective-permute-start.27
  80.2 2.3 %collective-permute-done.30 = bf16[32,2048]{1,0:T(8,128)(2,1)S(1)} collective-permute-done((bf16[32,2048]{1,0:T(8,128)(2,1)S(1)}, bf16[32,2048]{1,0:T(8,128)(2,1)S(1)}, u32[]{:S(2)}, u32[]{:S(2)}) %collective-permute-start.30) | collective-permute-done | bytes 131104 | tf_op jit(solution)/shard_map/ppermute | solution.py:337
  82.5 1.8 %collective-permute-start.31 = (bf16[32,2048]{1,0:T(8,128)(2,1)S(1)}, bf16[32,2048]{1,0:T(8,128)(2,1)S(1)}, u32[]{:S(2)}, u32[]{:S(2)}) collective-permute-start(bf16[32,2048]{1,0:T(8,128)(2,1)S(1)} %add_convert_fusion), channel_id=1, source_target_pairs={{0,4},{1,3},{4,8},{5,1},{8,12},{9,5},{12,14},{13,9},{14,10},{15,13... | collective-permute-start | bytes 393224 | tf_op jit(solution)/shard_map/ppermute | solution.py:337
  84.3 0.8 collective-permute-done.27
  85.1 0.6 collective-permute-start.28
  85.7 1.8 %collective-permute-done.31 = bf16[32,2048]{1,0:T(8,128)(2,1)S(1)} collective-permute-done((bf16[32,2048]{1,0:T(8,128)(2,1)S(1)}, bf16[32,2048]{1,0:T(8,128)(2,1)S(1)}, u32[]{:S(2)}, u32[]{:S(2)}) %collective-permute-start.31) | collective-permute-done | bytes 131104 | tf_op jit(solution)/shard_map/ppermute | solution.py:337
  87.6 2.6 %collective-permute-done.28 = bf16[32,2048]{1,0:T(8,128)(2,1)S(1)} collective-permute-done((bf16[32,2048]{1,0:T(8,128)(2,1)S(1)}, bf16[32,2048]{1,0:T(8,128)(2,1)S(1)}, u32[]{:S(2)}, u32[]{:S(2)}) %collective-permute-start.28) | collective-permute-done | bytes 131104 | tf_op jit(solution)/shard_map/ppermute | solution.py:337
  90.1 0.7 fusion.3
  (39 shorter events, 0.4 us)
Async XLA Ops:
  0.0 18.5 %collective-permute-start.3 = (bf16[256,2048]{1,0:T(8,128)(2,1)}, bf16[256,2048]{1,0:T(8,128)(2,1)S(1)}, u32[]{:S(2)}, u32[]{:S(2)}) collective-permute-start(bf16[256,2048]{1,0:T(8,128)(2,1)} %refs_3_.1), channel_id=1, source_target_pairs={{0,1},{1,0},{2,3},{3,2},{4,5},{5,4},{6,7},{7,6},{8,9},{9,8},{10,11... | collective-permute-start | bytes 3145736 | tf_op jit(solution)/shard_map/ppermute | solution.py:340
  0.5 31.5 %copy-start.1 = (bf16[1,2048,768]{2,1,0:T(8,128)(2,1)S(1)}, bf16[1,2048,768]{2,1,0:T(8,128)(2,1)}, u32[]{:S(2)}) copy-start(bf16[1,2048,768]{2,1,0:T(8,128)(2,1)} %refs_9_) | copy-start | bytes 9437188
  0.5 32.0 %copy-start.2 = (bf16[1,768,2048]{2,1,0:T(8,128)(2,1)S(1)}, bf16[1,768,2048]{2,1,0:T(8,128)(2,1)}, u32[]{:S(2)}) copy-start(bf16[1,768,2048]{2,1,0:T(8,128)(2,1)} %refs_10_) | copy-start | bytes 9437188
  5.1 26.7 %copy-start = (bf16[1,2048,768]{2,1,0:T(8,128)(2,1)S(1)}, bf16[1,2048,768]{2,1,0:T(8,128)(2,1)}, u32[]{:S(2)}) copy-start(bf16[1,2048,768]{2,1,0:T(8,128)(2,1)} %refs_8_) | copy-start | bytes 9437188
  5.1 6.1 %collective-permute-start.1 = (bf16[3,32,640]{2,1,0:T(8,128)(2,1)}, bf16[3,32,640]{2,1,0:T(8,128)(2,1)S(1)}, u32[]{:S(2)}, u32[]{:S(2)}) collective-permute-start(bf16[3,32,640]{2,1,0:T(8,128)(2,1)} %get-tuple-element.33), channel_id=1, source_target_pairs={{0,1},{1,0},{2,3},{3,2},{4,5},{5,4},{6,7},{7,6},{8,9},{9,8},{10,11... | collective-permute-start | bytes 368648 | tf_op jit(solution)/shard_map/ppermute | solution.py:340
  5.2 9.3 %collective-permute-start = (bf16[32,640]{1,0:T(8,128)(2,1)}, bf16[32,640]{1,0:T(8,128)(2,1)S(1)}, u32[]{:S(2)}, u32[]{:S(2)}) collective-permute-start(bf16[32,640]{1,0:T(8,128)(2,1)} %get-tuple-element.31), channel_id=1, source_target_pairs={{0,14},{1,15},{4,10},{5,11},{8,6},{9,7},{12,2},{13,3},{14,0},{15,1... | collective-permute-start | bytes 122888 | tf_op jit(solution)/shard_map/ppermute | solution.py:337
  12.1 6.4 %collective-permute-start.2 = (bf16[64,640]{1,0:T(8,128)(2,1)S(1)}, bf16[64,640]{1,0:T(8,128)(2,1)S(1)}, u32[]{:S(2)}, u32[]{:S(2)}) collective-permute-start(bf16[64,640]{1,0:T(8,128)(2,1)S(1)} %pad_maximum_fusion), channel_id=1, source_target_pairs={{0,10},{1,13},{4,6},{5,15},{8,2},{9,11},{12,0},{13,7},{14,4},{15,3... | collective-permute-start | bytes 245768 | tf_op jit(solution)/shard_map/ppermute | solution.py:337
  13.0 12.8 %collective-permute-start.5 = (bf16[64,640]{1,0:T(8,128)(2,1)S(1)}, bf16[64,640]{1,0:T(8,128)(2,1)S(1)}, u32[]{:S(2)}, u32[]{:S(2)}) collective-permute-start(bf16[64,640]{1,0:T(8,128)(2,1)S(1)} %pad_maximum_fusion.1), channel_id=1, source_target_pairs={{0,6},{1,9},{4,2},{5,13},{8,0},{9,15},{12,4},{13,11},{14,8},{15,7}... | collective-permute-start | bytes 245768 | tf_op jit(solution)/shard_map/ppermute | solution.py:337
  18.5 1.2 %copy-start.3 = (bf16[256,2048]{1,0:T(8,128)(2,1)S(1)}, bf16[256,2048]{1,0:T(8,128)(2,1)}, u32[]{:S(2)}) copy-start(bf16[256,2048]{1,0:T(8,128)(2,1)} %refs_3_.1) | copy-start | bytes 3145732
  20.2 12.3 %collective-permute-start.10 = (bf16[32,2048]{1,0:T(8,128)(2,1)S(1)}, bf16[32,2048]{1,0:T(8,128)(2,1)S(1)}, u32[]{:S(2)}, u32[]{:S(2)}) collective-permute-start(bf16[32,2048]{1,0:T(8,128)(2,1)S(1)} %get-tuple-element.43), channel_id=1, source_target_pairs={{0,4},{1,3},{4,8},{5,1},{8,12},{9,5},{12,14},{13,9},{14,10},{15,13... | collective-permute-start | bytes 393224 | tf_op jit(solution)/shard_map/ppermute | solution.py:337
  20.6 11.2 %collective-permute-start.7 = (bf16[32,2048]{1,0:T(8,128)(2,1)S(1)}, bf16[32,2048]{1,0:T(8,128)(2,1)S(1)}, u32[]{:S(2)}, u32[]{:S(2)}) collective-permute-start(bf16[32,2048]{1,0:T(8,128)(2,1)S(1)} %get-tuple-element.39), channel_id=1, source_target_pairs={{0,8},{1,7},{4,12},{5,3},{8,14},{9,1},{12,10},{13,5},{14,6},{15,9}... | collective-permute-start | bytes 393224 | tf_op jit(solution)/shard_map/ppermute | solution.py:337
  23.7 5.5 %collective-permute-start.6 = (bf16[64,640]{1,0:T(8,128)(2,1)S(1)}, bf16[64,640]{1,0:T(8,128)(2,1)S(1)}, u32[]{:S(2)}, u32[]{:S(2)}) collective-permute-start(bf16[64,640]{1,0:T(8,128)(2,1)S(1)} %pad_maximum_fusion.2), channel_id=1, source_target_pairs={{0,2},{1,5},{4,0},{5,9},{8,4},{9,13},{12,8},{13,15},{14,12},{15,11... | collective-permute-start | bytes 245768 | tf_op jit(solution)/shard_map/ppermute | solution.py:337
  23.8 9.4 %collective-permute-start.4 = (bf16[32,2048]{1,0:T(8,128)(2,1)S(1)}, bf16[32,2048]{1,0:T(8,128)(2,1)S(1)}, u32[]{:S(2)}, u32[]{:S(2)}) collective-permute-start(bf16[32,2048]{1,0:T(8,128)(2,1)S(1)} %get-tuple-element.34), channel_id=1, source_target_pairs={{0,4},{1,3},{4,8},{5,1},{8,12},{9,5},{12,14},{13,9},{14,10},{15,13... | collective-permute-start | bytes 393224 | tf_op jit(solution)/shard_map/ppermute | solution.py:337
  29.3 1.2 %copy-start.4 = (bf16[256,2048]{1,0:T(8,128)(2,1)S(1)}, bf16[256,2048]{1,0:T(8,128)(2,1)}, u32[]{:S(2)}) copy-start(bf16[256,2048]{1,0:T(8,128)(2,1)} %refs_3_.1) | copy-start | bytes 3145732
  30.5 0.8 copy-start.5
  31.3 15.5 %copy-start.6 = (bf16[32,2048]{1,0:T(8,128)(2,1)S(1)}, bf16[32,2048]{1,0:T(8,128)(2,1)}, u32[]{:S(2)}) copy-start(bf16[32,2048]{1,0:T(8,128)(2,1)} %param.16) | copy-start | bytes 393220
  31.3 15.7 %copy-start.7 = (f32[2048]{0:T(1024)S(1)}, f32[2048]{0:T(1024)}, u32[]{:S(2)}) copy-start(f32[2048]{0:T(1024)} %param.18) | copy-start | bytes 24580
  31.8 36.6 %collective-permute-start.22 = (bf16[1,2048,768]{2,1,0:T(8,128)(2,1)S(1)}, bf16[1,2048,768]{2,1,0:T(8,128)(2,1)S(1)}, u32[]{:S(2)}, u32[]{:S(2)}) collective-permute-start(bf16[1,2048,768]{2,1,0:T(8,128)(2,1)S(1)} %copy-done), channel_id=1, source_target_pairs={{0,1},{1,0},{2,3},{3,2},{4,5},{5,4},{6,7},{7,6},{8,9},{9,8},{10,11... | collective-permute-start | bytes 9437192 | tf_op jit(solution)/shard_map/ppermute | solution.py:340
  31.9 36.5 %collective-permute-start.23 = (bf16[1,2048,768]{2,1,0:T(8,128)(2,1)S(1)}, bf16[1,2048,768]{2,1,0:T(8,128)(2,1)S(1)}, u32[]{:S(2)}, u32[]{:S(2)}) collective-permute-start(bf16[1,2048,768]{2,1,0:T(8,128)(2,1)S(1)} %copy-done.1), channel_id=1, source_target_pairs={{0,1},{1,0},{2,3},{3,2},{4,5},{5,4},{6,7},{7,6},{8,9},{9,8},{10,11... | collective-permute-start | bytes 9437192 | tf_op jit(solution)/shard_map/ppermute | solution.py:340
  32.4 36.0 %collective-permute-start.24 = (bf16[1,768,2048]{2,1,0:T(8,128)(2,1)S(1)}, bf16[1,768,2048]{2,1,0:T(8,128)(2,1)S(1)}, u32[]{:S(2)}, u32[]{:S(2)}) collective-permute-start(bf16[1,768,2048]{2,1,0:T(8,128)(2,1)S(1)} %copy-done.2), channel_id=1, source_target_pairs={{0,1},{1,0},{2,3},{3,2},{4,5},{5,4},{6,7},{7,6},{8,9},{9,8},{10,11... | collective-permute-start | bytes 9437192 | tf_op jit(solution)/shard_map/ppermute | solution.py:340
  32.5 5.0 %collective-permute-start.11 = (bf16[32,2048]{1,0:T(8,128)(2,1)S(1)}, bf16[32,2048]{1,0:T(8,128)(2,1)S(1)}, u32[]{:S(2)}, u32[]{:S(2)}) collective-permute-start(bf16[32,2048]{1,0:T(8,128)(2,1)S(1)} %add_convert_fusion.6), channel_id=1, source_target_pairs={{0,4},{1,3},{4,8},{5,1},{8,12},{9,5},{12,14},{13,9},{14,10},{15,13... | collective-permute-start | bytes 393224 | tf_op jit(solution)/shard_map/ppermute | solution.py:337
  33.2 5.8 %collective-permute-start.8 = (bf16[32,2048]{1,0:T(8,128)(2,1)S(1)}, bf16[32,2048]{1,0:T(8,128)(2,1)S(1)}, u32[]{:S(2)}, u32[]{:S(2)}) collective-permute-start(bf16[32,2048]{1,0:T(8,128)(2,1)S(1)} %add_convert_fusion.8), channel_id=1, source_target_pairs={{0,4},{1,3},{4,8},{5,1},{8,12},{9,5},{12,14},{13,9},{14,10},{15,13... | collective-permute-start | bytes 393224 | tf_op jit(solution)/shard_map/ppermute | solution.py:337
  37.6 5.0 %collective-permute-start.12 = (bf16[32,2048]{1,0:T(8,128)(2,1)S(1)}, bf16[32,2048]{1,0:T(8,128)(2,1)S(1)}, u32[]{:S(2)}, u32[]{:S(2)}) collective-permute-start(bf16[32,2048]{1,0:T(8,128)(2,1)S(1)} %add_convert_fusion.5), channel_id=1, source_target_pairs={{0,4},{1,3},{4,8},{5,1},{8,12},{9,5},{12,14},{13,9},{14,10},{15,13... | collective-permute-start | bytes 393224 | tf_op jit(solution)/shard_map/ppermute | solution.py:337
  39.0 5.0 %collective-permute-start.9 = (bf16[32,2048]{1,0:T(8,128)(2,1)S(1)}, bf16[32,2048]{1,0:T(8,128)(2,1)S(1)}, u32[]{:S(2)}, u32[]{:S(2)}) collective-permute-start(bf16[32,2048]{1,0:T(8,128)(2,1)S(1)} %add_convert_fusion.7), channel_id=1, source_target_pairs={{0,4},{1,3},{4,8},{5,1},{8,12},{9,5},{12,14},{13,9},{14,10},{15,13... | collective-permute-start | bytes 393224 | tf_op jit(solution)/shard_map/ppermute | solution.py:337
  42.6 4.1 %collective-permute-start.13 = (bf16[32,2048]{1,0:T(8,128)(2,1)S(1)}, bf16[32,2048]{1,0:T(8,128)(2,1)S(1)}, u32[]{:S(2)}, u32[]{:S(2)}) collective-permute-start(bf16[32,2048]{1,0:T(8,128)(2,1)S(1)} %collective-permute-done.12), channel_id=1, source_target_pairs={{0,1},{1,0},{2,3},{3,2},{4,5},{5,4},{6,7},{7,6},{8,9},{9,8},{10,11... | collective-permute-start | bytes 393224 | tf_op jit(solution)/shard_map/ppermute | solution.py:340
  47.1 5.0 %collective-permute-start.14 = (bf16[32,2048]{1,0:T(8,128)(2,1)S(1)}, bf16[32,2048]{1,0:T(8,128)(2,1)S(1)}, u32[]{:S(2)}, u32[]{:S(2)}) collective-permute-start(bf16[32,2048]{1,0:T(8,128)(2,1)S(1)} %fusion.2.refs_4_), channel_id=1, source_target_pairs={{0,2},{1,5},{4,0},{5,9},{8,4},{9,13},{12,8},{13,15},{14,12},{15,11... | collective-permute-start | bytes 393224 | tf_op jit(solution)/shard_map/ppermute | solution.py:337
  48.3 5.0 %collective-permute-start.18 = (bf16[32,2048]{1,0:T(8,128)(2,1)S(1)}, bf16[32,2048]{1,0:T(8,128)(2,1)S(1)}, u32[]{:S(2)}, u32[]{:S(2)}) collective-permute-start(bf16[32,2048]{1,0:T(8,128)(2,1)S(1)} %fusion.2.refs_4_), channel_id=1, source_target_pairs={{0,1},{1,0},{2,3},{3,2},{4,5},{5,4},{6,7},{7,6},{8,9},{9,8},{10,11... | collective-permute-start | bytes 393224 | tf_op jit(solution)/shard_map/ppermute | solution.py:340
  52.1 5.0 %collective-permute-start.15 = (bf16[32,2048]{1,0:T(8,128)(2,1)S(1)}, bf16[32,2048]{1,0:T(8,128)(2,1)S(1)}, u32[]{:S(2)}, u32[]{:S(2)}) collective-permute-start(bf16[32,2048]{1,0:T(8,128)(2,1)S(1)} %collective-permute-done.14.refs_2_), channel_id=1, source_target_pairs={{0,2},{1,5},{4,0},{5,9},{8,4},{9,13},{12,8},{13,15},{14,12},{15,11... | collective-permute-start | bytes 393224 | tf_op jit(solution)/shard_map/ppermute | solution.py:337
  53.3 5.2 %collective-permute-start.19 = (bf16[32,2048]{1,0:T(8,128)(2,1)S(1)}, bf16[32,2048]{1,0:T(8,128)(2,1)S(1)}, u32[]{:S(2)}, u32[]{:S(2)}) collective-permute-start(bf16[32,2048]{1,0:T(8,128)(2,1)S(1)} %collective-permute-done.18), channel_id=1, source_target_pairs={{0,2},{1,5},{4,0},{5,9},{8,4},{9,13},{12,8},{13,15},{14,12},{15,11... | collective-permute-start | bytes 393224 | tf_op jit(solution)/shard_map/ppermute | solution.py:337
  57.1 5.0 %collective-permute-start.16 = (bf16[32,2048]{1,0:T(8,128)(2,1)S(1)}, bf16[32,2048]{1,0:T(8,128)(2,1)S(1)}, u32[]{:S(2)}, u32[]{:S(2)}) collective-permute-start(bf16[32,2048]{1,0:T(8,128)(2,1)S(1)} %collective-permute-done.15.refs_0_), channel_id=1, source_target_pairs={{0,2},{1,5},{4,0},{5,9},{8,4},{9,13},{12,8},{13,15},{14,12},{15,11... | collective-permute-start | bytes 393224 | tf_op jit(solution)/shard_map/ppermute | solution.py:337
  58.5 5.0 %collective-permute-start.20 = (bf16[32,2048]{1,0:T(8,128)(2,1)S(1)}, bf16[32,2048]{1,0:T(8,128)(2,1)S(1)}, u32[]{:S(2)}, u32[]{:S(2)}) collective-permute-start(bf16[32,2048]{1,0:T(8,128)(2,1)S(1)} %collective-permute-done.19.refs_3_), channel_id=1, source_target_pairs={{0,2},{1,5},{4,0},{5,9},{8,4},{9,13},{12,8},{13,15},{14,12},{15,11... | collective-permute-start | bytes 393224 | tf_op jit(solution)/shard_map/ppermute | solution.py:337
  62.0 5.0 %collective-permute-start.17 = (bf16[32,2048]{1,0:T(8,128)(2,1)S(1)}, bf16[32,2048]{1,0:T(8,128)(2,1)S(1)}, u32[]{:S(2)}, u32[]{:S(2)}) collective-permute-start(bf16[32,2048]{1,0:T(8,128)(2,1)S(1)} %collective-permute-done.16.refs_1_), channel_id=1, source_target_pairs={{0,2},{1,5},{4,0},{5,9},{8,4},{9,13},{12,8},{13,15},{14,12},{15,11... | collective-permute-start | bytes 393224 | tf_op jit(solution)/shard_map/ppermute | solution.py:337
  63.4 5.0 %collective-permute-start.21 = (bf16[32,2048]{1,0:T(8,128)(2,1)S(1)}, bf16[32,2048]{1,0:T(8,128)(2,1)S(1)}, u32[]{:S(2)}, u32[]{:S(2)}) collective-permute-start(bf16[32,2048]{1,0:T(8,128)(2,1)S(1)} %collective-permute-done.20.refs_1_), channel_id=1, source_target_pairs={{0,2},{1,5},{4,0},{5,9},{8,4},{9,13},{12,8},{13,15},{14,12},{15,11... | collective-permute-start | bytes 393224 | tf_op jit(solution)/shard_map/ppermute | solution.py:337
  71.6 5.8 %collective-permute-start.29 = (bf16[32,2048]{1,0:T(8,128)(2,1)S(1)}, bf16[32,2048]{1,0:T(8,128)(2,1)S(1)}, u32[]{:S(2)}, u32[]{:S(2)}) collective-permute-start(bf16[32,2048]{1,0:T(8,128)(2,1)S(1)} %get-tuple-element.54), channel_id=1, source_target_pairs={{0,4},{1,3},{4,8},{5,1},{8,12},{9,5},{12,14},{13,9},{14,10},{15,13... | collective-permute-start | bytes 393224 | tf_op jit(solution)/shard_map/ppermute | solution.py:337
  72.3 7.2 %collective-permute-start.26 = (bf16[32,2048]{1,0:T(8,128)(2,1)S(1)}, bf16[32,2048]{1,0:T(8,128)(2,1)S(1)}, u32[]{:S(2)}, u32[]{:S(2)}) collective-permute-start(bf16[32,2048]{1,0:T(8,128)(2,1)S(1)} %get-tuple-element.51), channel_id=1, source_target_pairs={{0,8},{1,7},{4,12},{5,3},{8,14},{9,1},{12,10},{13,5},{14,6},{15,9}... | collective-permute-start | bytes 393224 | tf_op jit(solution)/shard_map/ppermute | solution.py:337
  72.7 6.8 %collective-permute-start.25 = (bf16[32,2048]{1,0:T(8,128)(2,1)S(1)}, bf16[32,2048]{1,0:T(8,128)(2,1)S(1)}, u32[]{:S(2)}, u32[]{:S(2)}) collective-permute-start(bf16[32,2048]{1,0:T(8,128)(2,1)S(1)} %get-tuple-element.49), channel_id=1, source_target_pairs={{0,4},{1,3},{4,8},{5,1},{8,12},{9,5},{12,14},{13,9},{14,10},{15,13... | collective-permute-start | bytes 393224 | tf_op jit(solution)/shard_map/ppermute | solution.py:337
  77.5 5.0 %collective-permute-start.30 = (bf16[32,2048]{1,0:T(8,128)(2,1)S(1)}, bf16[32,2048]{1,0:T(8,128)(2,1)S(1)}, u32[]{:S(2)}, u32[]{:S(2)}) collective-permute-start(bf16[32,2048]{1,0:T(8,128)(2,1)S(1)} %add_convert_fusion.1), channel_id=1, source_target_pairs={{0,4},{1,3},{4,8},{5,1},{8,12},{9,5},{12,14},{13,9},{14,10},{15,13... | collective-permute-start | bytes 393224 | tf_op jit(solution)/shard_map/ppermute | solution.py:337
  79.5 5.6 %collective-permute-start.27 = (bf16[32,2048]{1,0:T(8,128)(2,1)S(1)}, bf16[32,2048]{1,0:T(8,128)(2,1)S(1)}, u32[]{:S(2)}, u32[]{:S(2)}) collective-permute-start(bf16[32,2048]{1,0:T(8,128)(2,1)S(1)} %add_convert_fusion.3), channel_id=1, source_target_pairs={{0,4},{1,3},{4,8},{5,1},{8,12},{9,5},{12,14},{13,9},{14,10},{15,13... | collective-permute-start | bytes 393224 | tf_op jit(solution)/shard_map/ppermute | solution.py:337
  82.5 5.0 %collective-permute-start.31 = (bf16[32,2048]{1,0:T(8,128)(2,1)S(1)}, bf16[32,2048]{1,0:T(8,128)(2,1)S(1)}, u32[]{:S(2)}, u32[]{:S(2)}) collective-permute-start(bf16[32,2048]{1,0:T(8,128)(2,1)S(1)} %add_convert_fusion), channel_id=1, source_target_pairs={{0,4},{1,3},{4,8},{5,1},{8,12},{9,5},{12,14},{13,9},{14,10},{15,13... | collective-permute-start | bytes 393224 | tf_op jit(solution)/shard_map/ppermute | solution.py:337
  85.1 5.0 %collective-permute-start.28 = (bf16[32,2048]{1,0:T(8,128)(2,1)S(1)}, bf16[32,2048]{1,0:T(8,128)(2,1)S(1)}, u32[]{:S(2)}, u32[]{:S(2)}) collective-permute-start(bf16[32,2048]{1,0:T(8,128)(2,1)S(1)} %add_convert_fusion.2), channel_id=1, source_target_pairs={{0,4},{1,3},{4,8},{5,1},{8,12},{9,5},{12,14},{13,9},{14,10},{15,13... | collective-permute-start | bytes 393224 | tf_op jit(solution)/shard_map/ppermute | solution.py:337
  87.6 2.6 %collective-permute-start.32 = (bf16[32,2048]{1,0:T(8,128)(2,1)S(1)}, bf16[32,2048]{1,0:T(8,128)(2,1)S(1)}, u32[]{:S(2)}, u32[]{:S(2)}) collective-permute-start(bf16[32,2048]{1,0:T(8,128)(2,1)S(1)} %collective-permute-done.31), channel_id=1, source_target_pairs={{0,1},{1,0},{2,3},{3,2},{4,5},{5,4},{6,7},{7,6},{8,9},{9,8},{10,11... | collective-permute-start | bytes 393224 | tf_op jit(solution)/shard_map/ppermute | solution.py:340

commit v9 on v8

--- a/solution.py
+++ b/solution.py
@@ -181,9 +181,12 @@
     )(lengths, queries, cache_keys, cache_values, ids.T, numer.T)
 
 
-def project_kernel(pieces, *refs):
+def project_kernel(pieces, kept, *refs):
     piece_refs, own_ref, other_ref = refs[:pieces], refs[pieces], refs[pieces + 1]
     out_refs, x_ref = refs[pieces + 2 : -1], refs[-1]
+    if kept:
+        out_refs[-1][...] = own_ref[...]
+        out_refs = out_refs[:-1]
     feats, width = own_ref.shape
     start = 0
     for piece in piece_refs:
@@ -216,16 +219,17 @@
         both(other_ref, own_ref)
 
 
-def project(pieces, kinds, own, other):
+def project(pieces, kinds, own, other, kept=False):
     feats, width = own.shape
     rows = sum(piece.shape[0] for piece in pieces)
     return pl.pallas_call(
-        functools.partial(project_kernel, len(pieces)),
+        functools.partial(project_kernel, len(pieces), kept),
         out_shape=tuple(
             jax.ShapeDtypeStruct((rows // len(kinds), width), kind) for kind in kinds
-        ),
+        )
+        + (jax.ShapeDtypeStruct(own.shape, own.dtype),) * kept,
         in_specs=[VMEM] * (len(pieces) + 2),
-        out_specs=(VMEM,) * len(kinds),
+        out_specs=(VMEM,) * (len(kinds) + kept),
         scratch_shapes=[pltpu.VMEM((rows, 2 * feats), BF16)],
         compiler_params=pltpu.CompilerParams(vmem_limit_bytes=32 * 1024 * 1024),
         cost_estimate=pl.CostEstimate(
@@ -358,17 +362,19 @@
         return pass_on(jnp.concatenate([mine, got], axis=0), -offset)
 
     kinds = [BF16, BF16, BF16] + [F32] * (2 * hops - 3)
-    weights = (out_weight, weight_other)
     arrived = {0: here, hops: pass_on(far, -hops)}
     arrived[hops - 1] = send(hops - 1, mine[hops - 2], got[hops - 2])
-    partial = project([arrived[hops], arrived[hops - 1]], kinds[:3], *weights)
+    *partial, own_weight = project([arrived[hops]], kinds[:1], out_weight, weight_other, True)
+    weights = (own_weight, weight_other)
+    partial += project([arrived[hops - 1]], kinds[1:3], *weights)
     first = pass_on(partial[0], 2)
     first, own_experts = lax.optimization_barrier((first, own_experts))
     for offset in range(hops - 2, 0, -1):
         arrived[offset] = send(offset, mine[offset - 1], got[offset - 1])
-    partial += project(
-        [arrived[offset] for offset in range(hops - 2, -1, -1)], kinds[3:], *weights
-    )
+    nearer = [arrived[offset] for offset in range(hops - 2, 0, -1)]
+    partial += project(nearer, kinds[3:-1], *weights)
+    partial += project([here], kinds[-1:], *weights)
+    _, own_experts = lax.optimization_barrier((partial, own_experts))
     other_experts = tuple(swapped(w) for w in own_experts)
 
     def ring_sums(partial, far):

time: 91.3 us -> 87.1 us (0.954)
  local copies, waits for them, and re-layouts: 3.26 us -> 0.04 us
  waiting for transfers between devices: 41.5 us -> 39 us
  starting transfers between devices: 30.1 us -> 31.6 us
    unnamed x16, local copies, waits for them, and re-layouts: 3.25 us -> 0.03 us
    ppermute x25, waiting for transfers between devices: 38.7 us -> 36.3 us  [pass_on(): return lax.ppermute(array, 'rows', toward(step))]
    ppermute x25, starting transfers between devices: 28.9 us -> 30.3 us  [pass_on(): return lax.ppermute(array, 'rows', toward(step))]
    pallas_call x2 -> x4, Pallas kernels: 1 us -> 1.95 us  [project(): pl.pallas_call(functools.partial(project_kernel, len(pieces), kept), out_...]
  transfers between devices with their start and end apart: 33 -> 33, of which waited for: 19 -> 18; matrix products, arithmetic and copies ran while one was open for 3% -> 3% of each run, Pallas kernels for 10% -> 11%
where the time goes in v9:
time: 87.1 us; the launch traced here: 87 us
  waiting for transfers between devices  39 us (45%)
  starting transfers between devices  31.6 us (36%)
  Pallas kernels  13.1 us (15%)
  other arithmetic  3.01 us (3%)
    ppermute x25, waiting for transfers between devices, pass_on(): return lax.ppermute(array, 'rows', toward(step))  36.3 us
    ppermute x25, starting transfers between devices, pass_on(): return lax.ppermute(array, 'rows', toward(step))  30.3 us
    pallas_call x2, Pallas kernels, experts(): pl.pallas_call(functools.partial(expert_kernel, len(pieces), len(digits),...  6.59 us
    pallas_call x1, Pallas kernels, attend(): pl.pallas_call(functools.partial(attend_kernel, chips, hops, chip_experts...  4.52 us
    ppermute x8, waiting for transfers between devices, swapped(): return lax.ppermute(array, 'rows', swap)  2.74 us
    pallas_call x4, Pallas kernels, project(): pl.pallas_call(functools.partial(project_kernel, len(pieces), kept), out_...  1.95 us
  transfers between devices with their start and end apart: 33, of which 18 were waited for; matrix products, arithmetic and copies ran while one was open for 3% of the time, Pallas kernels for 11%

profile of v9, /device:TPU:0, one launch (start us, length us, event | category | flops | bytes accessed | tf_op | source)
XLA Modules:
  0.0 87.0 jit_solution(241335801983963852)
XLA Ops:
  0.0 0.5 collective-permute-start.3
  0.5 4.5 %shard_map.118 = (bf16[32,640]{1,0:T(8,128)(2,1)}, bf16[3,32,640]{2,1,0:T(8,128)(2,1)}, bf16[32,640]{1,0:T(8,128)(2,1)}, bf16[32,640]{1,0:T(8,128)(2,1)}, bf16[3...) custom-call(s32[32]{0:T(128)} %lengths_ref.1, bf16[32,4096]{1,0:T(8,128)(2,1)} %q_ref.1, bf16[32,2,128,128]{3,2,1,0:T(8,128)(2,1)} %k_ref.1, ...), custom_call_target="tpu_custom_call" | custom-call | flops 67108864 | bytes 4194304 | tf_op jit(solution)/shard_map/pallas_call | solution.py:164
  5.0 0.2 collective-permute-start
  5.2 5.9 %collective-permute-start.2 = (bf16[32,640]{1,0:T(8,128)(2,1)}, bf16[32,640]{1,0:T(8,128)(2,1)S(1)}, u32[]{:S(2)}, u32[]{:S(2)}) collective-permute-start(bf16[32,640]{1,0:T(8,128)(2,1)} %get-tuple-element.36), channel_id=1, source_target_pairs={{0,14},{1,15},{4,10},{5,11},{8,6},{9,7},{12,2},{13,3},{14,0},{15,1... | collective-permute-start | bytes 122888 | tf_op jit(solution)/shard_map/ppermute | solution.py:341
  11.1 0.0 copy-start.2
  11.1 0.9 %pad_maximum_fusion = bf16[64,640]{1,0:T(8,128)(2,1)S(1)} fusion(bf16[32,640]{1,0:T(8,128)(2,1)S(1)} %get-tuple-element.65, bf16[32,640]{1,0:T(8,128)(2,1)} %get-tuple-element.34), kind=kLoop, calls=%fused_computation.16 | loop fusion | flops 163840 | bytes 163840 | tf_op jit(solution)/shard_map/concatenate | solution.py:362
  12.1 0.2 collective-permute-start.1
  12.2 0.8 pad_maximum_fusion.1
  13.0 1.5 %collective-permute-start.5 = (bf16[64,640]{1,0:T(8,128)(2,1)S(1)}, bf16[64,640]{1,0:T(8,128)(2,1)S(1)}, u32[]{:S(2)}, u32[]{:S(2)}) collective-permute-start(bf16[64,640]{1,0:T(8,128)(2,1)S(1)} %pad_maximum_fusion.1), channel_id=1, source_target_pairs={{0,6},{1,9},{4,2},{5,13},{8,0},{9,15},{12,4},{13,11},{14,8},{15,7}... | collective-permute-start | bytes 245768 | tf_op jit(solution)/shard_map/ppermute | solution.py:341
  14.6 0.5 shard_map.119
  15.1 3.4 %collective-permute-done.1.refs_0_.refs_4_ = bf16[64,640]{1,0:T(8,128)(2,1)S(1)} collective-permute-done((bf16[64,640]{1,0:T(8,128)(2,1)S(1)}, bf16[64,640]{1,0:T(8,128)(2,1)S(1)}, u32[]{:S(2)}, u32[]{:S(2)}) %collective-permute-start.1) | collective-permute-done | bytes 81952 | tf_op jit(solution)/shard_map/ppermute | solution.py:341
  18.5 0.5 shard_map.120
  19.0 0.4 collective-permute-start.10
  19.4 2.0 %collective-permute-start.7 = (bf16[32,2048]{1,0:T(8,128)(2,1)S(1)}, bf16[32,2048]{1,0:T(8,128)(2,1)S(1)}, u32[]{:S(2)}, u32[]{:S(2)}) collective-permute-start(bf16[32,2048]{1,0:T(8,128)(2,1)S(1)} %get-tuple-element.42), channel_id=1, source_target_pairs={{0,8},{1,7},{4,12},{5,3},{8,14},{9,1},{12,10},{13,5},{14,6},{15,9}... | collective-permute-start | bytes 393224 | tf_op jit(solution)/shard_map/ppermute | solution.py:341
  21.5 0.1 collective-permute-start.6
  21.5 2.0 %collective-permute-start.4 = (bf16[32,2048]{1,0:T(8,128)(2,1)S(1)}, bf16[32,2048]{1,0:T(8,128)(2,1)S(1)}, u32[]{:S(2)}, u32[]{:S(2)}) collective-permute-start(bf16[32,2048]{1,0:T(8,128)(2,1)S(1)} %get-tuple-element.38), channel_id=1, source_target_pairs={{0,4},{1,3},{4,8},{5,1},{8,12},{9,5},{12,14},{13,9},{14,10},{15,13... | collective-permute-start | bytes 393224 | tf_op jit(solution)/shard_map/ppermute | solution.py:341
  23.5 0.5 shard_map.122
  24.0 0.0 collective-permute-done.5.refs_0_.refs_5_
  24.0 3.2 %collective-permute-done.6.refs_1_.refs_6_ = bf16[64,640]{1,0:T(8,128)(2,1)S(1)} collective-permute-done((bf16[64,640]{1,0:T(8,128)(2,1)S(1)}, bf16[64,640]{1,0:T(8,128)(2,1)S(1)}, u32[]{:S(2)}, u32[]{:S(2)}) %collective-permute-start.6) | collective-permute-done | bytes 81952 | tf_op jit(solution)/shard_map/ppermute | solution.py:341
  27.2 0.5 shard_map.121
  27.7 0.1 collective-permute-start.22
  27.8 0.5 collective-permute-start.23
  28.3 0.1 collective-permute-start.24
  28.5 1.1 %collective-permute-start.11 = (bf16[32,2048]{1,0:T(8,128)(2,1)S(1)}, bf16[32,2048]{1,0:T(8,128)(2,1)S(1)}, u32[]{:S(2)}, u32[]{:S(2)}) collective-permute-start(bf16[32,2048]{1,0:T(8,128)(2,1)S(1)} %add_convert_fusion.6), channel_id=1, source_target_pairs={{0,4},{1,3},{4,8},{5,1},{8,12},{9,5},{12,14},{13,9},{14,10},{15,13... | collective-permute-start | bytes 393224 | tf_op jit(solution)/shard_map/ppermute | solution.py:341
  29.5 0.1 add_convert_fusion.8
  29.6 0.8 collective-permute-start.8
  30.4 3.1 %collective-permute-done.11 = bf16[32,2048]{1,0:T(8,128)(2,1)S(1)} collective-permute-done((bf16[32,2048]{1,0:T(8,128)(2,1)S(1)}, bf16[32,2048]{1,0:T(8,128)(2,1)S(1)}, u32[]{:S(2)}, u32[]{:S(2)}) %collective-permute-start.11) | collective-permute-done | bytes 131104 | tf_op jit(solution)/shard_map/ppermute | solution.py:341
  33.5 1.1 %collective-permute-start.12 = (bf16[32,2048]{1,0:T(8,128)(2,1)S(1)}, bf16[32,2048]{1,0:T(8,128)(2,1)S(1)}, u32[]{:S(2)}, u32[]{:S(2)}) collective-permute-start(bf16[32,2048]{1,0:T(8,128)(2,1)S(1)} %add_convert_fusion.5), channel_id=1, source_target_pairs={{0,4},{1,3},{4,8},{5,1},{8,12},{9,5},{12,14},{13,9},{14,10},{15,13... | collective-permute-start | bytes 393224 | tf_op jit(solution)/shard_map/ppermute | solution.py:341
  34.6 0.3 collective-permute-done.8
  34.9 1.1 %collective-permute-start.9 = (bf16[32,2048]{1,0:T(8,128)(2,1)S(1)}, bf16[32,2048]{1,0:T(8,128)(2,1)S(1)}, u32[]{:S(2)}, u32[]{:S(2)}) collective-permute-start(bf16[32,2048]{1,0:T(8,128)(2,1)S(1)} %add_convert_fusion.7), channel_id=1, source_target_pairs={{0,4},{1,3},{4,8},{5,1},{8,12},{9,5},{12,14},{13,9},{14,10},{15,13... | collective-permute-start | bytes 393224 | tf_op jit(solution)/shard_map/ppermute | solution.py:341
  36.0 2.5 %collective-permute-done.12 = bf16[32,2048]{1,0:T(8,128)(2,1)S(1)} collective-permute-done((bf16[32,2048]{1,0:T(8,128)(2,1)S(1)}, bf16[32,2048]{1,0:T(8,128)(2,1)S(1)}, u32[]{:S(2)}, u32[]{:S(2)}) %collective-permute-start.12) | collective-permute-done | bytes 131104 | tf_op jit(solution)/shard_map/ppermute | solution.py:341
  38.5 1.4 %collective-permute-done.9 = bf16[32,2048]{1,0:T(8,128)(2,1)S(1)} collective-permute-done((bf16[32,2048]{1,0:T(8,128)(2,1)S(1)}, bf16[32,2048]{1,0:T(8,128)(2,1)S(1)}, u32[]{:S(2)}, u32[]{:S(2)}) %collective-permute-start.9) | collective-permute-done | bytes 131104 | tf_op jit(solution)/shard_map/ppermute | solution.py:341
  39.9 2.7 %collective-permute-done.13 = bf16[32,2048]{1,0:T(8,128)(2,1)S(1)} collective-permute-done((bf16[32,2048]{1,0:T(8,128)(2,1)S(1)}, bf16[32,2048]{1,0:T(8,128)(2,1)S(1)}, u32[]{:S(2)}, u32[]{:S(2)}) %collective-permute-start.13) | collective-permute-done | bytes 131104 | tf_op jit(solution)/shard_map/ppermute | solution.py:344
  42.7 0.2 fusion
  42.9 0.1 fusion.2.refs_4_
  43.0 1.0 %collective-permute-start.14 = (bf16[32,2048]{1,0:T(8,128)(2,1)S(1)}, bf16[32,2048]{1,0:T(8,128)(2,1)S(1)}, u32[]{:S(2)}, u32[]{:S(2)}) collective-permute-start(bf16[32,2048]{1,0:T(8,128)(2,1)S(1)} %fusion.2.refs_4_), channel_id=1, source_target_pairs={{0,2},{1,5},{4,0},{5,9},{8,4},{9,13},{12,8},{13,15},{14,12},{15,11... | collective-permute-start | bytes 393224 | tf_op jit(solution)/shard_map/ppermute | solution.py:341
  43.9 4.1 %collective-permute-done.14.refs_2_ = bf16[32,2048]{1,0:T(8,128)(2,1)S(1)} collective-permute-done((bf16[32,2048]{1,0:T(8,128)(2,1)S(1)}, bf16[32,2048]{1,0:T(8,128)(2,1)S(1)}, u32[]{:S(2)}, u32[]{:S(2)}) %collective-permute-start.14) | collective-permute-done | bytes 131104 | tf_op jit(solution)/shard_map/ppermute | solution.py:341
  48.0 0.9 %collective-permute-start.15 = (bf16[32,2048]{1,0:T(8,128)(2,1)S(1)}, bf16[32,2048]{1,0:T(8,128)(2,1)S(1)}, u32[]{:S(2)}, u32[]{:S(2)}) collective-permute-start(bf16[32,2048]{1,0:T(8,128)(2,1)S(1)} %collective-permute-done.14.refs_2_), channel_id=1, source_target_pairs={{0,2},{1,5},{4,0},{5,9},{8,4},{9,13},{12,8},{13,15},{14,12},{15,11... | collective-permute-start | bytes 393224 | tf_op jit(solution)/shard_map/ppermute | solution.py:341
  48.9 0.4 collective-permute-start.19
  49.3 3.6 %collective-permute-done.15.refs_0_ = bf16[32,2048]{1,0:T(8,128)(2,1)S(1)} collective-permute-done((bf16[32,2048]{1,0:T(8,128)(2,1)S(1)}, bf16[32,2048]{1,0:T(8,128)(2,1)S(1)}, u32[]{:S(2)}, u32[]{:S(2)}) %collective-permute-start.15) | collective-permute-done | bytes 131104 | tf_op jit(solution)/shard_map/ppermute | solution.py:341
  53.0 0.9 %collective-permute-start.16 = (bf16[32,2048]{1,0:T(8,128)(2,1)S(1)}, bf16[32,2048]{1,0:T(8,128)(2,1)S(1)}, u32[]{:S(2)}, u32[]{:S(2)}) collective-permute-start(bf16[32,2048]{1,0:T(8,128)(2,1)S(1)} %collective-permute-done.15.refs_0_), channel_id=1, source_target_pairs={{0,2},{1,5},{4,0},{5,9},{8,4},{9,13},{12,8},{13,15},{14,12},{15,11... | collective-permute-start | bytes 393224 | tf_op jit(solution)/shard_map/ppermute | solution.py:341
  53.9 0.5 collective-permute-done.19.refs_3_
  54.4 0.9 %collective-permute-start.20 = (bf16[32,2048]{1,0:T(8,128)(2,1)S(1)}, bf16[32,2048]{1,0:T(8,128)(2,1)S(1)}, u32[]{:S(2)}, u32[]{:S(2)}) collective-permute-start(bf16[32,2048]{1,0:T(8,128)(2,1)S(1)} %collective-permute-done.19.refs_3_), channel_id=1, source_target_pairs={{0,2},{1,5},{4,0},{5,9},{8,4},{9,13},{12,8},{13,15},{14,12},{15,11... | collective-permute-start | bytes 393224 | tf_op jit(solution)/shard_map/ppermute | solution.py:341
  55.3 2.7 %collective-permute-done.16.refs_1_ = bf16[32,2048]{1,0:T(8,128)(2,1)S(1)} collective-permute-done((bf16[32,2048]{1,0:T(8,128)(2,1)S(1)}, bf16[32,2048]{1,0:T(8,128)(2,1)S(1)}, u32[]{:S(2)}, u32[]{:S(2)}) %collective-permute-start.16) | collective-permute-done | bytes 131104 | tf_op jit(solution)/shard_map/ppermute | solution.py:341
  57.9 0.9 %collective-permute-start.17 = (bf16[32,2048]{1,0:T(8,128)(2,1)S(1)}, bf16[32,2048]{1,0:T(8,128)(2,1)S(1)}, u32[]{:S(2)}, u32[]{:S(2)}) collective-permute-start(bf16[32,2048]{1,0:T(8,128)(2,1)S(1)} %collective-permute-done.16.refs_1_), channel_id=1, source_target_pairs={{0,2},{1,5},{4,0},{5,9},{8,4},{9,13},{12,8},{13,15},{14,12},{15,11... | collective-permute-start | bytes 393224 | tf_op jit(solution)/shard_map/ppermute | solution.py:341
  58.8 0.5 collective-permute-done.20.refs_1_
  59.3 0.9 %collective-permute-start.21 = (bf16[32,2048]{1,0:T(8,128)(2,1)S(1)}, bf16[32,2048]{1,0:T(8,128)(2,1)S(1)}, u32[]{:S(2)}, u32[]{:S(2)}) collective-permute-start(bf16[32,2048]{1,0:T(8,128)(2,1)S(1)} %collective-permute-done.20.refs_1_), channel_id=1, source_target_pairs={{0,2},{1,5},{4,0},{5,9},{8,4},{9,13},{12,8},{13,15},{14,12},{15,11... | collective-permute-start | bytes 393224 | tf_op jit(solution)/shard_map/ppermute | solution.py:341
  60.2 2.7 %collective-permute-done.17.refs_0_ = bf16[32,2048]{1,0:T(8,128)(2,1)S(1)} collective-permute-done((bf16[32,2048]{1,0:T(8,128)(2,1)S(1)}, bf16[32,2048]{1,0:T(8,128)(2,1)S(1)}, u32[]{:S(2)}, u32[]{:S(2)}) %collective-permute-start.17) | collective-permute-done | bytes 131104 | tf_op jit(solution)/shard_map/ppermute | solution.py:341
  62.9 1.4 %collective-permute-done.21.refs_2_ = bf16[32,2048]{1,0:T(8,128)(2,1)S(1)} collective-permute-done((bf16[32,2048]{1,0:T(8,128)(2,1)S(1)}, bf16[32,2048]{1,0:T(8,128)(2,1)S(1)}, u32[]{:S(2)}, u32[]{:S(2)}) %collective-permute-start.21) | collective-permute-done | bytes 131104 | tf_op jit(solution)/shard_map/ppermute | solution.py:341
  64.3 3.2 %shard_map.123 = (bf16[32,2048]{1,0:T(8,128)(2,1)S(1)}, bf16[32,2048]{1,0:T(8,128)(2,1)S(1)}, bf16[32,2048]{1,0:T(8,128)(2,1)S(1)}) custom-call(bf16[32,2048]{1,0:T(8,128)(2,1)S(1)} %collective-permute-done.17.refs_0_, bf16[32,2048]{1,0:T(8,128)(2,1)S(1)} %collective-permute-done.16.refs_1_, bf16[32,2048]{1,0:T(8,128)(2,1)S(1)} %collective-permute-done.21.refs_2_, ...), custom_call_target="tpu_custom_call" | custom-call | flops 1811939328 | bytes 196608 | tf_op jit(solution)/shard_map/pallas_call | solution.py:299
  67.5 1.1 %collective-permute-start.29 = (bf16[32,2048]{1,0:T(8,128)(2,1)S(1)}, bf16[32,2048]{1,0:T(8,128)(2,1)S(1)}, u32[]{:S(2)}, u32[]{:S(2)}) collective-permute-start(bf16[32,2048]{1,0:T(8,128)(2,1)S(1)} %get-tuple-element.60), channel_id=1, source_target_pairs={{0,4},{1,3},{4,8},{5,1},{8,12},{9,5},{12,14},{13,9},{14,10},{15,13... | collective-permute-start | bytes 393224 | tf_op jit(solution)/shard_map/ppermute | solution.py:341
  68.6 0.9 collective-permute-start.26
  69.5 1.9 %collective-permute-start.25 = (bf16[32,2048]{1,0:T(8,128)(2,1)S(1)}, bf16[32,2048]{1,0:T(8,128)(2,1)S(1)}, u32[]{:S(2)}, u32[]{:S(2)}) collective-permute-start(bf16[32,2048]{1,0:T(8,128)(2,1)S(1)} %get-tuple-element.55), channel_id=1, source_target_pairs={{0,4},{1,3},{4,8},{5,1},{8,12},{9,5},{12,14},{13,9},{14,10},{15,13... | collective-permute-start | bytes 393224 | tf_op jit(solution)/shard_map/ppermute | solution.py:341
  71.4 3.4 %shard_map.124 = (f32[32,2048]{1,0:T(8,128)S(1)}, f32[32,2048]{1,0:T(8,128)S(1)}, f32[32,2048]{1,0:T(8,128)S(1)}, f32[32,2048]{1,0:T(8,128)S(1)}, f32[32,2048]{1,0:T(8,128)S(1)}) custom-call(bf16[32,2048]{1,0:T(8,128)(2,1)S(1)} %collective-permute-done.15.refs_0_, bf16[32,2048]{1,0:T(8,128)(2,1)S(1)} %collective-permute-done.20.refs_1_, ...), custom_call_target="tpu_custom_call" | custom-call | flops 3019898880 | bytes 327680 | tf_op jit(solution)/shard_map/pallas_call | solution.py:299
  74.8 1.2 %collective-permute-start.30 = (bf16[32,2048]{1,0:T(8,128)(2,1)S(1)}, bf16[32,2048]{1,0:T(8,128)(2,1)S(1)}, u32[]{:S(2)}, u32[]{:S(2)}) collective-permute-start(bf16[32,2048]{1,0:T(8,128)(2,1)S(1)} %add_convert_fusion.1), channel_id=1, source_target_pairs={{0,4},{1,3},{4,8},{5,1},{8,12},{9,5},{12,14},{13,9},{14,10},{15,13... | collective-permute-start | bytes 393224 | tf_op jit(solution)/shard_map/ppermute | solution.py:341
  76.0 0.1 add_convert_fusion.3
  76.1 0.7 collective-permute-start.27
  76.8 3.0 %collective-permute-done.30 = bf16[32,2048]{1,0:T(8,128)(2,1)S(1)} collective-permute-done((bf16[32,2048]{1,0:T(8,128)(2,1)S(1)}, bf16[32,2048]{1,0:T(8,128)(2,1)S(1)}, u32[]{:S(2)}, u32[]{:S(2)}) %collective-permute-start.30) | collective-permute-done | bytes 131104 | tf_op jit(solution)/shard_map/ppermute | solution.py:341
  79.8 1.2 %collective-permute-start.31 = (bf16[32,2048]{1,0:T(8,128)(2,1)S(1)}, bf16[32,2048]{1,0:T(8,128)(2,1)S(1)}, u32[]{:S(2)}, u32[]{:S(2)}) collective-permute-start(bf16[32,2048]{1,0:T(8,128)(2,1)S(1)} %add_convert_fusion), channel_id=1, source_target_pairs={{0,4},{1,3},{4,8},{5,1},{8,12},{9,5},{12,14},{13,9},{14,10},{15,13... | collective-permute-start | bytes 393224 | tf_op jit(solution)/shard_map/ppermute | solution.py:341
  81.0 0.1 collective-permute-done.27
  81.2 1.2 %collective-permute-start.28 = (bf16[32,2048]{1,0:T(8,128)(2,1)S(1)}, bf16[32,2048]{1,0:T(8,128)(2,1)S(1)}, u32[]{:S(2)}, u32[]{:S(2)}) collective-permute-start(bf16[32,2048]{1,0:T(8,128)(2,1)S(1)} %add_convert_fusion.2), channel_id=1, source_target_pairs={{0,4},{1,3},{4,8},{5,1},{8,12},{9,5},{12,14},{13,9},{14,10},{15,13... | collective-permute-start | bytes 393224 | tf_op jit(solution)/shard_map/ppermute | solution.py:341
  82.4 2.4 %collective-permute-done.31 = bf16[32,2048]{1,0:T(8,128)(2,1)S(1)} collective-permute-done((bf16[32,2048]{1,0:T(8,128)(2,1)S(1)}, bf16[32,2048]{1,0:T(8,128)(2,1)S(1)}, u32[]{:S(2)}, u32[]{:S(2)}) %collective-permute-start.31) | collective-permute-done | bytes 131104 | tf_op jit(solution)/shard_map/ppermute | solution.py:341
  84.8 1.4 %collective-permute-done.28 = bf16[32,2048]{1,0:T(8,128)(2,1)S(1)} collective-permute-done((bf16[32,2048]{1,0:T(8,128)(2,1)S(1)}, bf16[32,2048]{1,0:T(8,128)(2,1)S(1)}, u32[]{:S(2)}, u32[]{:S(2)}) %collective-permute-start.28) | collective-permute-done | bytes 131104 | tf_op jit(solution)/shard_map/ppermute | solution.py:341
  86.2 0.7 fusion.3
  (41 shorter events, 0.3 us)
Async XLA Ops:
  0.0 14.6 %copy-start.3 = (bf16[256,2048]{1,0:T(8,128)(2,1)S(1)}, bf16[256,2048]{1,0:T(8,128)(2,1)}, u32[]{:S(2)}) copy-start(bf16[256,2048]{1,0:T(8,128)(2,1)} %refs_1_.1) | copy-start | bytes 3145732
  0.0 14.6 %collective-permute-start.3 = (bf16[256,2048]{1,0:T(8,128)(2,1)}, bf16[256,2048]{1,0:T(8,128)(2,1)S(1)}, u32[]{:S(2)}, u32[]{:S(2)}) collective-permute-start(bf16[256,2048]{1,0:T(8,128)(2,1)} %refs_1_.1), channel_id=1, source_target_pairs={{0,1},{1,0},{2,3},{3,2},{4,5},{5,4},{6,7},{7,6},{8,9},{9,8},{10,11... | collective-permute-start | bytes 3145736 | tf_op jit(solution)/shard_map/ppermute | solution.py:344
  5.0 16.5 %copy-start.6 = (bf16[32,640]{1,0:T(8,128)(2,1)S(1)}, bf16[32,640]{1,0:T(8,128)(2,1)}, u32[]{:S(2)}) copy-start(bf16[32,640]{1,0:T(8,128)(2,1)} %get-tuple-element.40) | copy-start | bytes 122884
  5.0 18.6 %copy-start.4 = (bf16[32,640]{1,0:T(8,128)(2,1)S(1)}, bf16[32,640]{1,0:T(8,128)(2,1)}, u32[]{:S(2)}) copy-start(bf16[32,640]{1,0:T(8,128)(2,1)} %get-tuple-element.45.refs_0_.refs_7_) | copy-start | bytes 122884
  5.0 6.1 %collective-permute-start = (bf16[3,32,640]{2,1,0:T(8,128)(2,1)}, bf16[3,32,640]{2,1,0:T(8,128)(2,1)S(1)}, u32[]{:S(2)}, u32[]{:S(2)}) collective-permute-start(bf16[3,32,640]{2,1,0:T(8,128)(2,1)} %get-tuple-element.35), channel_id=1, source_target_pairs={{0,1},{1,0},{2,3},{3,2},{4,5},{5,4},{6,7},{7,6},{8,9},{9,8},{10,11... | collective-permute-start | bytes 368648 | tf_op jit(solution)/shard_map/ppermute | solution.py:344
  5.2 9.4 %collective-permute-start.2 = (bf16[32,640]{1,0:T(8,128)(2,1)}, bf16[32,640]{1,0:T(8,128)(2,1)S(1)}, u32[]{:S(2)}, u32[]{:S(2)}) collective-permute-start(bf16[32,640]{1,0:T(8,128)(2,1)} %get-tuple-element.36), channel_id=1, source_target_pairs={{0,14},{1,15},{4,10},{5,11},{8,6},{9,7},{12,2},{13,3},{14,0},{15,1... | collective-permute-start | bytes 122888 | tf_op jit(solution)/shard_map/ppermute | solution.py:341
  11.1 17.2 %copy-start.2 = (bf16[1,768,2048]{2,1,0:T(8,128)(2,1)S(1)}, bf16[1,768,2048]{2,1,0:T(8,128)(2,1)}, u32[]{:S(2)}) copy-start(bf16[1,768,2048]{2,1,0:T(8,128)(2,1)} %refs_10_) | copy-start | bytes 9437188
  12.1 6.4 %collective-permute-start.1 = (bf16[64,640]{1,0:T(8,128)(2,1)S(1)}, bf16[64,640]{1,0:T(8,128)(2,1)S(1)}, u32[]{:S(2)}, u32[]{:S(2)}) collective-permute-start(bf16[64,640]{1,0:T(8,128)(2,1)S(1)} %pad_maximum_fusion), channel_id=1, source_target_pairs={{0,10},{1,13},{4,6},{5,15},{8,2},{9,11},{12,0},{13,7},{14,4},{15,3... | collective-permute-start | bytes 245768 | tf_op jit(solution)/shard_map/ppermute | solution.py:341
  13.0 11.0 %collective-permute-start.5 = (bf16[64,640]{1,0:T(8,128)(2,1)S(1)}, bf16[64,640]{1,0:T(8,128)(2,1)S(1)}, u32[]{:S(2)}, u32[]{:S(2)}) collective-permute-start(bf16[64,640]{1,0:T(8,128)(2,1)S(1)} %pad_maximum_fusion.1), channel_id=1, source_target_pairs={{0,6},{1,9},{4,2},{5,13},{8,0},{9,15},{12,4},{13,11},{14,8},{15,7}... | collective-permute-start | bytes 245768 | tf_op jit(solution)/shard_map/ppermute | solution.py:341
  18.5 9.2 %copy-start = (bf16[1,2048,768]{2,1,0:T(8,128)(2,1)S(1)}, bf16[1,2048,768]{2,1,0:T(8,128)(2,1)}, u32[]{:S(2)}) copy-start(bf16[1,2048,768]{2,1,0:T(8,128)(2,1)} %refs_8_) | copy-start | bytes 9437188
  18.5 9.3 %copy-start.1 = (bf16[1,2048,768]{2,1,0:T(8,128)(2,1)S(1)}, bf16[1,2048,768]{2,1,0:T(8,128)(2,1)}, u32[]{:S(2)}) copy-start(bf16[1,2048,768]{2,1,0:T(8,128)(2,1)} %refs_9_) | copy-start | bytes 9437188
  19.0 9.4 %collective-permute-start.10 = (bf16[32,2048]{1,0:T(8,128)(2,1)S(1)}, bf16[32,2048]{1,0:T(8,128)(2,1)S(1)}, u32[]{:S(2)}, u32[]{:S(2)}) collective-permute-start(bf16[32,2048]{1,0:T(8,128)(2,1)S(1)} %get-tuple-element.46), channel_id=1, source_target_pairs={{0,4},{1,3},{4,8},{5,1},{8,12},{9,5},{12,14},{13,9},{14,10},{15,13... | collective-permute-start | bytes 393224 | tf_op jit(solution)/shard_map/ppermute | solution.py:341
  19.4 8.3 %collective-permute-start.7 = (bf16[32,2048]{1,0:T(8,128)(2,1)S(1)}, bf16[32,2048]{1,0:T(8,128)(2,1)S(1)}, u32[]{:S(2)}, u32[]{:S(2)}) collective-permute-start(bf16[32,2048]{1,0:T(8,128)(2,1)S(1)} %get-tuple-element.42), channel_id=1, source_target_pairs={{0,8},{1,7},{4,12},{5,3},{8,14},{9,1},{12,10},{13,5},{14,6},{15,9}... | collective-permute-start | bytes 393224 | tf_op jit(solution)/shard_map/ppermute | solution.py:341
  21.5 5.8 %collective-permute-start.6 = (bf16[64,640]{1,0:T(8,128)(2,1)S(1)}, bf16[64,640]{1,0:T(8,128)(2,1)S(1)}, u32[]{:S(2)}, u32[]{:S(2)}) collective-permute-start(bf16[64,640]{1,0:T(8,128)(2,1)S(1)} %pad_maximum_fusion.2), channel_id=1, source_target_pairs={{0,2},{1,5},{4,0},{5,9},{8,4},{9,13},{12,8},{13,15},{14,12},{15,11... | collective-permute-start | bytes 245768 | tf_op jit(solution)/shard_map/ppermute | solution.py:341
  21.5 8.0 %collective-permute-start.4 = (bf16[32,2048]{1,0:T(8,128)(2,1)S(1)}, bf16[32,2048]{1,0:T(8,128)(2,1)S(1)}, u32[]{:S(2)}, u32[]{:S(2)}) collective-permute-start(bf16[32,2048]{1,0:T(8,128)(2,1)S(1)} %get-tuple-element.38), channel_id=1, source_target_pairs={{0,4},{1,3},{4,8},{5,1},{8,12},{9,5},{12,14},{13,9},{14,10},{15,13... | collective-permute-start | bytes 393224 | tf_op jit(solution)/shard_map/ppermute | solution.py:341
  23.5 19.1 %copy-start.5 = (bf16[32,2048]{1,0:T(8,128)(2,1)S(1)}, bf16[32,2048]{1,0:T(8,128)(2,1)}, u32[]{:S(2)}) copy-start(bf16[32,2048]{1,0:T(8,128)(2,1)} %param.16) | copy-start | bytes 393220
  24.0 18.9 %copy-start.7 = (f32[2048]{0:T(1024)S(1)}, f32[2048]{0:T(1024)}, u32[]{:S(2)}) copy-start(f32[2048]{0:T(1024)} %param.18) | copy-start | bytes 24580
  27.7 36.6 %collective-permute-start.22 = (bf16[1,2048,768]{2,1,0:T(8,128)(2,1)S(1)}, bf16[1,2048,768]{2,1,0:T(8,128)(2,1)S(1)}, u32[]{:S(2)}, u32[]{:S(2)}) collective-permute-start(bf16[1,2048,768]{2,1,0:T(8,128)(2,1)S(1)} %copy-done), channel_id=1, source_target_pairs={{0,1},{1,0},{2,3},{3,2},{4,5},{5,4},{6,7},{7,6},{8,9},{9,8},{10,11... | collective-permute-start | bytes 9437192 | tf_op jit(solution)/shard_map/ppermute | solution.py:344
  27.8 36.5 %collective-permute-start.23 = (bf16[1,2048,768]{2,1,0:T(8,128)(2,1)S(1)}, bf16[1,2048,768]{2,1,0:T(8,128)(2,1)S(1)}, u32[]{:S(2)}, u32[]{:S(2)}) collective-permute-start(bf16[1,2048,768]{2,1,0:T(8,128)(2,1)S(1)} %copy-done.1), channel_id=1, source_target_pairs={{0,1},{1,0},{2,3},{3,2},{4,5},{5,4},{6,7},{7,6},{8,9},{9,8},{10,11... | collective-permute-start | bytes 9437192 | tf_op jit(solution)/shard_map/ppermute | solution.py:344
  28.3 36.0 %collective-permute-start.24 = (bf16[1,768,2048]{2,1,0:T(8,128)(2,1)S(1)}, bf16[1,768,2048]{2,1,0:T(8,128)(2,1)S(1)}, u32[]{:S(2)}, u32[]{:S(2)}) collective-permute-start(bf16[1,768,2048]{2,1,0:T(8,128)(2,1)S(1)} %copy-done.2), channel_id=1, source_target_pairs={{0,1},{1,0},{2,3},{3,2},{4,5},{5,4},{6,7},{7,6},{8,9},{9,8},{10,11... | collective-permute-start | bytes 9437192 | tf_op jit(solution)/shard_map/ppermute | solution.py:344
  28.5 5.0 %collective-permute-start.11 = (bf16[32,2048]{1,0:T(8,128)(2,1)S(1)}, bf16[32,2048]{1,0:T(8,128)(2,1)S(1)}, u32[]{:S(2)}, u32[]{:S(2)}) collective-permute-start(bf16[32,2048]{1,0:T(8,128)(2,1)S(1)} %add_convert_fusion.6), channel_id=1, source_target_pairs={{0,4},{1,3},{4,8},{5,1},{8,12},{9,5},{12,14},{13,9},{14,10},{15,13... | collective-permute-start | bytes 393224 | tf_op jit(solution)/shard_map/ppermute | solution.py:341
  29.6 5.3 %collective-permute-start.8 = (bf16[32,2048]{1,0:T(8,128)(2,1)S(1)}, bf16[32,2048]{1,0:T(8,128)(2,1)S(1)}, u32[]{:S(2)}, u32[]{:S(2)}) collective-permute-start(bf16[32,2048]{1,0:T(8,128)(2,1)S(1)} %add_convert_fusion.8), channel_id=1, source_target_pairs={{0,4},{1,3},{4,8},{5,1},{8,12},{9,5},{12,14},{13,9},{14,10},{15,13... | collective-permute-start | bytes 393224 | tf_op jit(solution)/shard_map/ppermute | solution.py:341
  33.5 5.0 %collective-permute-start.12 = (bf16[32,2048]{1,0:T(8,128)(2,1)S(1)}, bf16[32,2048]{1,0:T(8,128)(2,1)S(1)}, u32[]{:S(2)}, u32[]{:S(2)}) collective-permute-start(bf16[32,2048]{1,0:T(8,128)(2,1)S(1)} %add_convert_fusion.5), channel_id=1, source_target_pairs={{0,4},{1,3},{4,8},{5,1},{8,12},{9,5},{12,14},{13,9},{14,10},{15,13... | collective-permute-start | bytes 393224 | tf_op jit(solution)/shard_map/ppermute | solution.py:341
  34.9 5.0 %collective-permute-start.9 = (bf16[32,2048]{1,0:T(8,128)(2,1)S(1)}, bf16[32,2048]{1,0:T(8,128)(2,1)S(1)}, u32[]{:S(2)}, u32[]{:S(2)}) collective-permute-start(bf16[32,2048]{1,0:T(8,128)(2,1)S(1)} %add_convert_fusion.7), channel_id=1, source_target_pairs={{0,4},{1,3},{4,8},{5,1},{8,12},{9,5},{12,14},{13,9},{14,10},{15,13... | collective-permute-start | bytes 393224 | tf_op jit(solution)/shard_map/ppermute | solution.py:341
  38.5 4.1 %collective-permute-start.13 = (bf16[32,2048]{1,0:T(8,128)(2,1)S(1)}, bf16[32,2048]{1,0:T(8,128)(2,1)S(1)}, u32[]{:S(2)}, u32[]{:S(2)}) collective-permute-start(bf16[32,2048]{1,0:T(8,128)(2,1)S(1)} %collective-permute-done.12), channel_id=1, source_target_pairs={{0,1},{1,0},{2,3},{3,2},{4,5},{5,4},{6,7},{7,6},{8,9},{9,8},{10,11... | collective-permute-start | bytes 393224 | tf_op jit(solution)/shard_map/ppermute | solution.py:344
  43.0 5.0 %collective-permute-start.14 = (bf16[32,2048]{1,0:T(8,128)(2,1)S(1)}, bf16[32,2048]{1,0:T(8,128)(2,1)S(1)}, u32[]{:S(2)}, u32[]{:S(2)}) collective-permute-start(bf16[32,2048]{1,0:T(8,128)(2,1)S(1)} %fusion.2.refs_4_), channel_id=1, source_target_pairs={{0,2},{1,5},{4,0},{5,9},{8,4},{9,13},{12,8},{13,15},{14,12},{15,11... | collective-permute-start | bytes 393224 | tf_op jit(solution)/shard_map/ppermute | solution.py:341
  43.9 5.0 %collective-permute-start.18 = (bf16[32,2048]{1,0:T(8,128)(2,1)S(1)}, bf16[32,2048]{1,0:T(8,128)(2,1)S(1)}, u32[]{:S(2)}, u32[]{:S(2)}) collective-permute-start(bf16[32,2048]{1,0:T(8,128)(2,1)S(1)} %fusion.2.refs_4_), channel_id=1, source_target_pairs={{0,1},{1,0},{2,3},{3,2},{4,5},{5,4},{6,7},{7,6},{8,9},{9,8},{10,11... | collective-permute-start | bytes 393224 | tf_op jit(solution)/shard_map/ppermute | solution.py:344
  48.0 5.0 %collective-permute-start.15 = (bf16[32,2048]{1,0:T(8,128)(2,1)S(1)}, bf16[32,2048]{1,0:T(8,128)(2,1)S(1)}, u32[]{:S(2)}, u32[]{:S(2)}) collective-permute-start(bf16[32,2048]{1,0:T(8,128)(2,1)S(1)} %collective-permute-done.14.refs_2_), channel_id=1, source_target_pairs={{0,2},{1,5},{4,0},{5,9},{8,4},{9,13},{12,8},{13,15},{14,12},{15,11... | collective-permute-start | bytes 393224 | tf_op jit(solution)/shard_map/ppermute | solution.py:341
  48.9 5.5 %collective-permute-start.19 = (bf16[32,2048]{1,0:T(8,128)(2,1)S(1)}, bf16[32,2048]{1,0:T(8,128)(2,1)S(1)}, u32[]{:S(2)}, u32[]{:S(2)}) collective-permute-start(bf16[32,2048]{1,0:T(8,128)(2,1)S(1)} %collective-permute-done.18), channel_id=1, source_target_pairs={{0,2},{1,5},{4,0},{5,9},{8,4},{9,13},{12,8},{13,15},{14,12},{15,11... | collective-permute-start | bytes 393224 | tf_op jit(solution)/shard_map/ppermute | solution.py:341
  53.0 5.0 %collective-permute-start.16 = (bf16[32,2048]{1,0:T(8,128)(2,1)S(1)}, bf16[32,2048]{1,0:T(8,128)(2,1)S(1)}, u32[]{:S(2)}, u32[]{:S(2)}) collective-permute-start(bf16[32,2048]{1,0:T(8,128)(2,1)S(1)} %collective-permute-done.15.refs_0_), channel_id=1, source_target_pairs={{0,2},{1,5},{4,0},{5,9},{8,4},{9,13},{12,8},{13,15},{14,12},{15,11... | collective-permute-start | bytes 393224 | tf_op jit(solution)/shard_map/ppermute | solution.py:341
  54.4 5.0 %collective-permute-start.20 = (bf16[32,2048]{1,0:T(8,128)(2,1)S(1)}, bf16[32,2048]{1,0:T(8,128)(2,1)S(1)}, u32[]{:S(2)}, u32[]{:S(2)}) collective-permute-start(bf16[32,2048]{1,0:T(8,128)(2,1)S(1)} %collective-permute-done.19.refs_3_), channel_id=1, source_target_pairs={{0,2},{1,5},{4,0},{5,9},{8,4},{9,13},{12,8},{13,15},{14,12},{15,11... | collective-permute-start | bytes 393224 | tf_op jit(solution)/shard_map/ppermute | solution.py:341
  57.9 5.0 %collective-permute-start.17 = (bf16[32,2048]{1,0:T(8,128)(2,1)S(1)}, bf16[32,2048]{1,0:T(8,128)(2,1)S(1)}, u32[]{:S(2)}, u32[]{:S(2)}) collective-permute-start(bf16[32,2048]{1,0:T(8,128)(2,1)S(1)} %collective-permute-done.16.refs_1_), channel_id=1, source_target_pairs={{0,2},{1,5},{4,0},{5,9},{8,4},{9,13},{12,8},{13,15},{14,12},{15,11... | collective-permute-start | bytes 393224 | tf_op jit(solution)/shard_map/ppermute | solution.py:341
  59.3 5.0 %collective-permute-start.21 = (bf16[32,2048]{1,0:T(8,128)(2,1)S(1)}, bf16[32,2048]{1,0:T(8,128)(2,1)S(1)}, u32[]{:S(2)}, u32[]{:S(2)}) collective-permute-start(bf16[32,2048]{1,0:T(8,128)(2,1)S(1)} %collective-permute-done.20.refs_1_), channel_id=1, source_target_pairs={{0,2},{1,5},{4,0},{5,9},{8,4},{9,13},{12,8},{13,15},{14,12},{15,11... | collective-permute-start | bytes 393224 | tf_op jit(solution)/shard_map/ppermute | solution.py:341
  67.5 7.2 %collective-permute-start.29 = (bf16[32,2048]{1,0:T(8,128)(2,1)S(1)}, bf16[32,2048]{1,0:T(8,128)(2,1)S(1)}, u32[]{:S(2)}, u32[]{:S(2)}) collective-permute-start(bf16[32,2048]{1,0:T(8,128)(2,1)S(1)} %get-tuple-element.60), channel_id=1, source_target_pairs={{0,4},{1,3},{4,8},{5,1},{8,12},{9,5},{12,14},{13,9},{14,10},{15,13... | collective-permute-start | bytes 393224 | tf_op jit(solution)/shard_map/ppermute | solution.py:341
  68.6 7.4 %collective-permute-start.26 = (bf16[32,2048]{1,0:T(8,128)(2,1)S(1)}, bf16[32,2048]{1,0:T(8,128)(2,1)S(1)}, u32[]{:S(2)}, u32[]{:S(2)}) collective-permute-start(bf16[32,2048]{1,0:T(8,128)(2,1)S(1)} %get-tuple-element.57), channel_id=1, source_target_pairs={{0,8},{1,7},{4,12},{5,3},{8,14},{9,1},{12,10},{13,5},{14,6},{15,9}... | collective-permute-start | bytes 393224 | tf_op jit(solution)/shard_map/ppermute | solution.py:341
  69.5 6.5 %collective-permute-start.25 = (bf16[32,2048]{1,0:T(8,128)(2,1)S(1)}, bf16[32,2048]{1,0:T(8,128)(2,1)S(1)}, u32[]{:S(2)}, u32[]{:S(2)}) collective-permute-start(bf16[32,2048]{1,0:T(8,128)(2,1)S(1)} %get-tuple-element.55), channel_id=1, source_target_pairs={{0,4},{1,3},{4,8},{5,1},{8,12},{9,5},{12,14},{13,9},{14,10},{15,13... | collective-permute-start | bytes 393224 | tf_op jit(solution)/shard_map/ppermute | solution.py:341
  74.8 5.0 %collective-permute-start.30 = (bf16[32,2048]{1,0:T(8,128)(2,1)S(1)}, bf16[32,2048]{1,0:T(8,128)(2,1)S(1)}, u32[]{:S(2)}, u32[]{:S(2)}) collective-permute-start(bf16[32,2048]{1,0:T(8,128)(2,1)S(1)} %add_convert_fusion.1), channel_id=1, source_target_pairs={{0,4},{1,3},{4,8},{5,1},{8,12},{9,5},{12,14},{13,9},{14,10},{15,13... | collective-permute-start | bytes 393224 | tf_op jit(solution)/shard_map/ppermute | solution.py:341
  76.1 5.1 %collective-permute-start.27 = (bf16[32,2048]{1,0:T(8,128)(2,1)S(1)}, bf16[32,2048]{1,0:T(8,128)(2,1)S(1)}, u32[]{:S(2)}, u32[]{:S(2)}) collective-permute-start(bf16[32,2048]{1,0:T(8,128)(2,1)S(1)} %add_convert_fusion.3), channel_id=1, source_target_pairs={{0,4},{1,3},{4,8},{5,1},{8,12},{9,5},{12,14},{13,9},{14,10},{15,13... | collective-permute-start | bytes 393224 | tf_op jit(solution)/shard_map/ppermute | solution.py:341
  79.8 5.0 %collective-permute-start.31 = (bf16[32,2048]{1,0:T(8,128)(2,1)S(1)}, bf16[32,2048]{1,0:T(8,128)(2,1)S(1)}, u32[]{:S(2)}, u32[]{:S(2)}) collective-permute-start(bf16[32,2048]{1,0:T(8,128)(2,1)S(1)} %add_convert_fusion), channel_id=1, source_target_pairs={{0,4},{1,3},{4,8},{5,1},{8,12},{9,5},{12,14},{13,9},{14,10},{15,13... | collective-permute-start | bytes 393224 | tf_op jit(solution)/shard_map/ppermute | solution.py:341
  81.2 5.0 %collective-permute-start.28 = (bf16[32,2048]{1,0:T(8,128)(2,1)S(1)}, bf16[32,2048]{1,0:T(8,128)(2,1)S(1)}, u32[]{:S(2)}, u32[]{:S(2)}) collective-permute-start(bf16[32,2048]{1,0:T(8,128)(2,1)S(1)} %add_convert_fusion.2), channel_id=1, source_target_pairs={{0,4},{1,3},{4,8},{5,1},{8,12},{9,5},{12,14},{13,9},{14,10},{15,13... | collective-permute-start | bytes 393224 | tf_op jit(solution)/shard_map/ppermute | solution.py:341
  84.8 1.4 %collective-permute-start.32 = (bf16[32,2048]{1,0:T(8,128)(2,1)S(1)}, bf16[32,2048]{1,0:T(8,128)(2,1)S(1)}, u32[]{:S(2)}, u32[]{:S(2)}) collective-permute-start(bf16[32,2048]{1,0:T(8,128)(2,1)S(1)} %collective-permute-done.31), channel_id=1, source_target_pairs={{0,1},{1,0},{2,3},{3,2},{4,5},{5,4},{6,7},{7,6},{8,9},{9,8},{10,11... | collective-permute-start | bytes 393224 | tf_op jit(solution)/shard_map/ppermute | solution.py:344

commit v10 on v9

--- a/solution.py
+++ b/solution.py
@@ -407,7 +407,9 @@
         pieces = [own, other] + pieces
     pieces = [pass_on(own, -1)] + pieces
     digits = [arrived[offset] for offset in range(hops, -1, -1)]
-    total = serve(pieces[:3], kinds[:3], digits[:2]) + serve(pieces[3:], kinds[3:], digits[2:])
+    nearer = serve(pieces[3:], kinds[3:], digits[2:])
+    pieces[2], nearer = lax.optimization_barrier((pieces[2], nearer))
+    total = serve(pieces[:3], kinds[:3], digits[:2]) + nearer
     return (residual.astype(F32) + ring_sums(total, pass_on(total[0], 2))).astype(BF16)
 
 

time: 87.1 us -> 85.3 us (0.979)
  starting transfers between devices: 31.6 us -> 30 us
    ppermute x25, starting transfers between devices: 30.3 us -> 28.5 us  [pass_on(): return lax.ppermute(array, 'rows', toward(step))]
  transfers between devices with their start and end apart: 33 -> 33, of which waited for: 18 -> 17; matrix products, arithmetic and copies ran while one was open for 3% -> 3% of each run, Pallas kernels for 11% -> 12%
where the time goes in v10:
time: 85.3 us; the launch traced here: 85.2 us
  waiting for transfers between devices  38.9 us (46%)
  starting transfers between devices  30 us (35%)
  Pallas kernels  13.1 us (15%)
  other arithmetic  3.04 us (4%)
    ppermute x25, waiting for transfers between devices, pass_on(): return lax.ppermute(array, 'rows', toward(step))  36.1 us
    ppermute x25, starting transfers between devices, pass_on(): return lax.ppermute(array, 'rows', toward(step))  28.5 us
    pallas_call x2, Pallas kernels, experts(): pl.pallas_call(functools.partial(expert_kernel, len(pieces), len(digits),...  6.6 us
    pallas_call x1, Pallas kernels, attend(): pl.pallas_call(functools.partial(attend_kernel, chips, hops, chip_experts...  4.52 us
    ppermute x8, waiting for transfers between devices, swapped(): return lax.ppermute(array, 'rows', swap)  2.74 us
    pallas_call x4, Pallas kernels, project(): pl.pallas_call(functools.partial(project_kernel, len(pieces), kept), out_...  1.95 us
    concatenate x3, other arithmetic, send(): return pass_on(jnp.concatenate([mine, got], axis=0), -offset)  1.73 us
  transfers between devices with their start and end apart: 33, of which 17 were waited for; matrix products, arithmetic and copies ran while one was open for 3% of the time, Pallas kernels for 12%

profile of v10, /device:TPU:0, one launch (start us, length us, event | category | flops | bytes accessed | tf_op | source)
XLA Modules:
  0.0 85.2 jit_solution(15724670975816547360)
XLA Ops:
  0.0 0.5 collective-permute-start.3
  0.5 4.5 %shard_map.118 = (bf16[32,640]{1,0:T(8,128)(2,1)}, bf16[3,32,640]{2,1,0:T(8,128)(2,1)}, bf16[32,640]{1,0:T(8,128)(2,1)}, bf16[32,640]{1,0:T(8,128)(2,1)}, bf16[3...) custom-call(s32[32]{0:T(128)} %lengths_ref.1, bf16[32,4096]{1,0:T(8,128)(2,1)} %q_ref.1, bf16[32,2,128,128]{3,2,1,0:T(8,128)(2,1)} %k_ref.1, ...), custom_call_target="tpu_custom_call" | custom-call | flops 67108864 | bytes 4194304 | tf_op jit(solution)/shard_map/pallas_call | solution.py:164
  5.0 0.2 collective-permute-start
  5.2 5.9 %collective-permute-start.2 = (bf16[32,640]{1,0:T(8,128)(2,1)}, bf16[32,640]{1,0:T(8,128)(2,1)S(1)}, u32[]{:S(2)}, u32[]{:S(2)}) collective-permute-start(bf16[32,640]{1,0:T(8,128)(2,1)} %get-tuple-element.42), channel_id=1, source_target_pairs={{0,14},{1,15},{4,10},{5,11},{8,6},{9,7},{12,2},{13,3},{14,0},{15,1... | collective-permute-start | bytes 122888 | tf_op jit(solution)/shard_map/ppermute | solution.py:341
  11.1 0.0 copy-start.2
  11.1 0.9 %pad_maximum_fusion = bf16[64,640]{1,0:T(8,128)(2,1)S(1)} fusion(bf16[32,640]{1,0:T(8,128)(2,1)S(1)} %get-tuple-element.77, bf16[32,640]{1,0:T(8,128)(2,1)} %get-tuple-element.40), kind=kLoop, calls=%fused_computation.16 | loop fusion | flops 163840 | bytes 163840 | tf_op jit(solution)/shard_map/concatenate | solution.py:362
  12.1 0.2 collective-permute-start.1
  12.3 0.8 pad_maximum_fusion.2
  13.0 1.6 %collective-permute-start.6 = (bf16[64,640]{1,0:T(8,128)(2,1)S(1)}, bf16[64,640]{1,0:T(8,128)(2,1)S(1)}, u32[]{:S(2)}, u32[]{:S(2)}) collective-permute-start(bf16[64,640]{1,0:T(8,128)(2,1)S(1)} %pad_maximum_fusion.2), channel_id=1, source_target_pairs={{0,2},{1,5},{4,0},{5,9},{8,4},{9,13},{12,8},{13,15},{14,12},{15,11... | collective-permute-start | bytes 245768 | tf_op jit(solution)/shard_map/ppermute | solution.py:341
  14.6 0.5 shard_map.119
  15.2 1.2 %collective-permute-start.7 = (bf16[32,2048]{1,0:T(8,128)(2,1)S(1)}, bf16[32,2048]{1,0:T(8,128)(2,1)S(1)}, u32[]{:S(2)}, u32[]{:S(2)}) collective-permute-start(bf16[32,2048]{1,0:T(8,128)(2,1)S(1)} %get-tuple-element.48), channel_id=1, source_target_pairs={{0,8},{1,7},{4,12},{5,3},{8,14},{9,1},{12,10},{13,5},{14,6},{15,9}... | collective-permute-start | bytes 393224 | tf_op jit(solution)/shard_map/ppermute | solution.py:341
  16.3 2.2 %collective-permute-done.1.refs_0_.refs_4_ = bf16[64,640]{1,0:T(8,128)(2,1)S(1)} collective-permute-done((bf16[64,640]{1,0:T(8,128)(2,1)S(1)}, bf16[64,640]{1,0:T(8,128)(2,1)S(1)}, u32[]{:S(2)}, u32[]{:S(2)}) %collective-permute-start.1) | collective-permute-done | bytes 81952 | tf_op jit(solution)/shard_map/ppermute | solution.py:341
  18.6 0.5 shard_map.120
  19.1 0.1 collective-permute-start.10
  19.2 1.8 %collective-permute-start.5 = (bf16[64,640]{1,0:T(8,128)(2,1)S(1)}, bf16[64,640]{1,0:T(8,128)(2,1)S(1)}, u32[]{:S(2)}, u32[]{:S(2)}) collective-permute-start(bf16[64,640]{1,0:T(8,128)(2,1)S(1)} %pad_maximum_fusion.1), channel_id=1, source_target_pairs={{0,6},{1,9},{4,2},{5,13},{8,0},{9,15},{12,4},{13,11},{14,8},{15,7}... | collective-permute-start | bytes 245768 | tf_op jit(solution)/shard_map/ppermute | solution.py:341
  21.0 1.6 %collective-permute-start.4 = (bf16[32,2048]{1,0:T(8,128)(2,1)S(1)}, bf16[32,2048]{1,0:T(8,128)(2,1)S(1)}, u32[]{:S(2)}, u32[]{:S(2)}) collective-permute-start(bf16[32,2048]{1,0:T(8,128)(2,1)S(1)} %get-tuple-element.44), channel_id=1, source_target_pairs={{0,4},{1,3},{4,8},{5,1},{8,12},{9,5},{12,14},{13,9},{14,10},{15,13... | collective-permute-start | bytes 393224 | tf_op jit(solution)/shard_map/ppermute | solution.py:341
  22.7 0.5 shard_map.122
  23.1 0.0 collective-permute-done.6.refs_1_.refs_6_
  23.2 3.3 %collective-permute-done.5.refs_0_.refs_5_ = bf16[64,640]{1,0:T(8,128)(2,1)S(1)} collective-permute-done((bf16[64,640]{1,0:T(8,128)(2,1)S(1)}, bf16[64,640]{1,0:T(8,128)(2,1)S(1)}, u32[]{:S(2)}, u32[]{:S(2)}) %collective-permute-start.5) | collective-permute-done | bytes 81952 | tf_op jit(solution)/shard_map/ppermute | solution.py:341
  26.4 0.5 shard_map.121
  26.9 0.1 collective-permute-start.22
  27.0 0.5 collective-permute-start.23
  27.5 0.1 collective-permute-start.24
  27.6 0.4 collective-permute-start.11
  28.1 0.1 add_convert_fusion.8
  28.1 0.1 collective-permute-start.8
  28.2 4.5 %collective-permute-done.11 = bf16[32,2048]{1,0:T(8,128)(2,1)S(1)} collective-permute-done((bf16[32,2048]{1,0:T(8,128)(2,1)S(1)}, bf16[32,2048]{1,0:T(8,128)(2,1)S(1)}, u32[]{:S(2)}, u32[]{:S(2)}) %collective-permute-start.11) | collective-permute-done | bytes 131104 | tf_op jit(solution)/shard_map/ppermute | solution.py:341
  32.7 0.4 collective-permute-start.12
  33.1 0.9 %collective-permute-done.8 = bf16[32,2048]{1,0:T(8,128)(2,1)S(1)} collective-permute-done((bf16[32,2048]{1,0:T(8,128)(2,1)S(1)}, bf16[32,2048]{1,0:T(8,128)(2,1)S(1)}, u32[]{:S(2)}, u32[]{:S(2)}) %collective-permute-start.8) | collective-permute-done | bytes 131104 | tf_op jit(solution)/shard_map/ppermute | solution.py:341
  34.1 0.4 collective-permute-start.9
  34.5 3.2 %collective-permute-done.12 = bf16[32,2048]{1,0:T(8,128)(2,1)S(1)} collective-permute-done((bf16[32,2048]{1,0:T(8,128)(2,1)S(1)}, bf16[32,2048]{1,0:T(8,128)(2,1)S(1)}, u32[]{:S(2)}, u32[]{:S(2)}) %collective-permute-start.12) | collective-permute-done | bytes 131104 | tf_op jit(solution)/shard_map/ppermute | solution.py:341
  37.7 1.4 %collective-permute-done.9 = bf16[32,2048]{1,0:T(8,128)(2,1)S(1)} collective-permute-done((bf16[32,2048]{1,0:T(8,128)(2,1)S(1)}, bf16[32,2048]{1,0:T(8,128)(2,1)S(1)}, u32[]{:S(2)}, u32[]{:S(2)}) %collective-permute-start.9) | collective-permute-done | bytes 131104 | tf_op jit(solution)/shard_map/ppermute | solution.py:341
  39.1 2.7 %collective-permute-done.13 = bf16[32,2048]{1,0:T(8,128)(2,1)S(1)} collective-permute-done((bf16[32,2048]{1,0:T(8,128)(2,1)S(1)}, bf16[32,2048]{1,0:T(8,128)(2,1)S(1)}, u32[]{:S(2)}, u32[]{:S(2)}) %collective-permute-start.13) | collective-permute-done | bytes 131104 | tf_op jit(solution)/shard_map/ppermute | solution.py:344
  41.8 0.2 fusion
  42.0 0.1 fusion.2.refs_4_
  42.1 0.2 collective-permute-start.18
  42.3 1.5 %collective-permute-start.14 = (bf16[32,2048]{1,0:T(8,128)(2,1)S(1)}, bf16[32,2048]{1,0:T(8,128)(2,1)S(1)}, u32[]{:S(2)}, u32[]{:S(2)}) collective-permute-start(bf16[32,2048]{1,0:T(8,128)(2,1)S(1)} %fusion.2.refs_4_), channel_id=1, source_target_pairs={{0,2},{1,5},{4,0},{5,9},{8,4},{9,13},{12,8},{13,15},{14,12},{15,11... | collective-permute-start | bytes 393224 | tf_op jit(solution)/shard_map/ppermute | solution.py:341
  43.9 1.2 %collective-permute-start.19 = (bf16[32,2048]{1,0:T(8,128)(2,1)S(1)}, bf16[32,2048]{1,0:T(8,128)(2,1)S(1)}, u32[]{:S(2)}, u32[]{:S(2)}) collective-permute-start(bf16[32,2048]{1,0:T(8,128)(2,1)S(1)} %collective-permute-done.18), channel_id=1, source_target_pairs={{0,2},{1,5},{4,0},{5,9},{8,4},{9,13},{12,8},{13,15},{14,12},{15,11... | collective-permute-start | bytes 393224 | tf_op jit(solution)/shard_map/ppermute | solution.py:341
  45.1 2.2 %collective-permute-done.14.refs_2_ = bf16[32,2048]{1,0:T(8,128)(2,1)S(1)} collective-permute-done((bf16[32,2048]{1,0:T(8,128)(2,1)S(1)}, bf16[32,2048]{1,0:T(8,128)(2,1)S(1)}, u32[]{:S(2)}, u32[]{:S(2)}) %collective-permute-start.14) | collective-permute-done | bytes 131104 | tf_op jit(solution)/shard_map/ppermute | solution.py:341
  47.3 1.5 %collective-permute-start.15 = (bf16[32,2048]{1,0:T(8,128)(2,1)S(1)}, bf16[32,2048]{1,0:T(8,128)(2,1)S(1)}, u32[]{:S(2)}, u32[]{:S(2)}) collective-permute-start(bf16[32,2048]{1,0:T(8,128)(2,1)S(1)} %collective-permute-done.14.refs_2_), channel_id=1, source_target_pairs={{0,2},{1,5},{4,0},{5,9},{8,4},{9,13},{12,8},{13,15},{14,12},{15,11... | collective-permute-start | bytes 393224 | tf_op jit(solution)/shard_map/ppermute | solution.py:341
  48.8 1.4 %collective-permute-start.20 = (bf16[32,2048]{1,0:T(8,128)(2,1)S(1)}, bf16[32,2048]{1,0:T(8,128)(2,1)S(1)}, u32[]{:S(2)}, u32[]{:S(2)}) collective-permute-start(bf16[32,2048]{1,0:T(8,128)(2,1)S(1)} %collective-permute-done.19.refs_3_), channel_id=1, source_target_pairs={{0,2},{1,5},{4,0},{5,9},{8,4},{9,13},{12,8},{13,15},{14,12},{15,11... | collective-permute-start | bytes 393224 | tf_op jit(solution)/shard_map/ppermute | solution.py:341
  50.2 2.0 %collective-permute-done.15.refs_0_ = bf16[32,2048]{1,0:T(8,128)(2,1)S(1)} collective-permute-done((bf16[32,2048]{1,0:T(8,128)(2,1)S(1)}, bf16[32,2048]{1,0:T(8,128)(2,1)S(1)}, u32[]{:S(2)}, u32[]{:S(2)}) %collective-permute-start.15) | collective-permute-done | bytes 131104 | tf_op jit(solution)/shard_map/ppermute | solution.py:341
  52.3 1.5 %collective-permute-start.16 = (bf16[32,2048]{1,0:T(8,128)(2,1)S(1)}, bf16[32,2048]{1,0:T(8,128)(2,1)S(1)}, u32[]{:S(2)}, u32[]{:S(2)}) collective-permute-start(bf16[32,2048]{1,0:T(8,128)(2,1)S(1)} %collective-permute-done.15.refs_0_), channel_id=1, source_target_pairs={{0,2},{1,5},{4,0},{5,9},{8,4},{9,13},{12,8},{13,15},{14,12},{15,11... | collective-permute-start | bytes 393224 | tf_op jit(solution)/shard_map/ppermute | solution.py:341
  53.8 1.4 %collective-permute-start.21 = (bf16[32,2048]{1,0:T(8,128)(2,1)S(1)}, bf16[32,2048]{1,0:T(8,128)(2,1)S(1)}, u32[]{:S(2)}, u32[]{:S(2)}) collective-permute-start(bf16[32,2048]{1,0:T(8,128)(2,1)S(1)} %collective-permute-done.20.refs_1_), channel_id=1, source_target_pairs={{0,2},{1,5},{4,0},{5,9},{8,4},{9,13},{12,8},{13,15},{14,12},{15,11... | collective-permute-start | bytes 393224 | tf_op jit(solution)/shard_map/ppermute | solution.py:341
  55.2 2.0 %collective-permute-done.16.refs_1_ = bf16[32,2048]{1,0:T(8,128)(2,1)S(1)} collective-permute-done((bf16[32,2048]{1,0:T(8,128)(2,1)S(1)}, bf16[32,2048]{1,0:T(8,128)(2,1)S(1)}, u32[]{:S(2)}, u32[]{:S(2)}) %collective-permute-start.16) | collective-permute-done | bytes 131104 | tf_op jit(solution)/shard_map/ppermute | solution.py:341
  57.3 1.5 %collective-permute-start.17 = (bf16[32,2048]{1,0:T(8,128)(2,1)S(1)}, bf16[32,2048]{1,0:T(8,128)(2,1)S(1)}, u32[]{:S(2)}, u32[]{:S(2)}) collective-permute-start(bf16[32,2048]{1,0:T(8,128)(2,1)S(1)} %collective-permute-done.16.refs_1_), channel_id=1, source_target_pairs={{0,2},{1,5},{4,0},{5,9},{8,4},{9,13},{12,8},{13,15},{14,12},{15,11... | collective-permute-start | bytes 393224 | tf_op jit(solution)/shard_map/ppermute | solution.py:341
  58.8 3.4 %shard_map.123 = (f32[32,2048]{1,0:T(8,128)S(1)}, f32[32,2048]{1,0:T(8,128)S(1)}, f32[32,2048]{1,0:T(8,128)S(1)}, f32[32,2048]{1,0:T(8,128)S(1)}, f32[32,2048]{1,0:T(8,128)S(1)}) custom-call(bf16[32,2048]{1,0:T(8,128)(2,1)S(1)} %collective-permute-done.15.refs_0_, bf16[32,2048]{1,0:T(8,128)(2,1)S(1)} %collective-permute-done.20.refs_1_, ...), custom_call_target="tpu_custom_call" | custom-call | flops 3019898880 | bytes 327680 | tf_op jit(solution)/shard_map/pallas_call | solution.py:299
  62.2 0.0 collective-permute-done.17.refs_0_
  62.2 3.2 %shard_map.124 = (bf16[32,2048]{1,0:T(8,128)(2,1)S(1)}, bf16[32,2048]{1,0:T(8,128)(2,1)S(1)}, bf16[32,2048]{1,0:T(8,128)(2,1)S(1)}) custom-call(bf16[32,2048]{1,0:T(8,128)(2,1)S(1)} %collective-permute-done.17.refs_0_, bf16[32,2048]{1,0:T(8,128)(2,1)S(1)} %collective-permute-done.16.refs_1_, bf16[32,2048]{1,0:T(8,128)(2,1)S(1)} %collective-permute-done.21.refs_2_, ...), custom_call_target="tpu_custom_call" | custom-call | flops 1811939328 | bytes 196608 | tf_op jit(solution)/shard_map/pallas_call | solution.py:299
  65.5 0.5 collective-permute-start.29
  66.0 0.4 collective-permute-start.25
  66.3 2.1 %collective-permute-start.26 = (bf16[32,2048]{1,0:T(8,128)(2,1)S(1)}, bf16[32,2048]{1,0:T(8,128)(2,1)S(1)}, u32[]{:S(2)}, u32[]{:S(2)}) collective-permute-start(bf16[32,2048]{1,0:T(8,128)(2,1)S(1)} %get-tuple-element.69), channel_id=1, source_target_pairs={{0,8},{1,7},{4,12},{5,3},{8,14},{9,1},{12,10},{13,5},{14,6},{15,9}... | collective-permute-start | bytes 393224 | tf_op jit(solution)/shard_map/ppermute | solution.py:341
  68.4 2.1 %collective-permute-done.29 = bf16[32,2048]{1,0:T(8,128)(2,1)S(1)} collective-permute-done((bf16[32,2048]{1,0:T(8,128)(2,1)S(1)}, bf16[32,2048]{1,0:T(8,128)(2,1)S(1)}, u32[]{:S(2)}, u32[]{:S(2)}) %collective-permute-start.29) | collective-permute-done | bytes 131104 | tf_op jit(solution)/shard_map/ppermute | solution.py:341
  70.5 0.5 collective-permute-start.30
  71.0 0.8 collective-permute-done.25
  71.9 2.5 %collective-permute-done.26 = bf16[32,2048]{1,0:T(8,128)(2,1)S(1)} collective-permute-done((bf16[32,2048]{1,0:T(8,128)(2,1)S(1)}, bf16[32,2048]{1,0:T(8,128)(2,1)S(1)}, u32[]{:S(2)}, u32[]{:S(2)}) %collective-permute-start.26) | collective-permute-done | bytes 131104 | tf_op jit(solution)/shard_map/ppermute | solution.py:341
  74.4 0.4 collective-permute-start.27
  74.8 0.9 %collective-permute-done.30 = bf16[32,2048]{1,0:T(8,128)(2,1)S(1)} collective-permute-done((bf16[32,2048]{1,0:T(8,128)(2,1)S(1)}, bf16[32,2048]{1,0:T(8,128)(2,1)S(1)}, u32[]{:S(2)}, u32[]{:S(2)}) %collective-permute-start.30) | collective-permute-done | bytes 131104 | tf_op jit(solution)/shard_map/ppermute | solution.py:341
  75.8 0.3 collective-permute-start.31
  76.1 3.3 %collective-permute-done.27 = bf16[32,2048]{1,0:T(8,128)(2,1)S(1)} collective-permute-done((bf16[32,2048]{1,0:T(8,128)(2,1)S(1)}, bf16[32,2048]{1,0:T(8,128)(2,1)S(1)}, u32[]{:S(2)}, u32[]{:S(2)}) %collective-permute-start.27) | collective-permute-done | bytes 131104 | tf_op jit(solution)/shard_map/ppermute | solution.py:341
  79.5 0.4 collective-permute-start.28
  79.9 0.9 %collective-permute-done.31 = bf16[32,2048]{1,0:T(8,128)(2,1)S(1)} collective-permute-done((bf16[32,2048]{1,0:T(8,128)(2,1)S(1)}, bf16[32,2048]{1,0:T(8,128)(2,1)S(1)}, u32[]{:S(2)}, u32[]{:S(2)}) %collective-permute-start.31) | collective-permute-done | bytes 131104 | tf_op jit(solution)/shard_map/ppermute | solution.py:341
  80.8 3.6 %collective-permute-done.28 = bf16[32,2048]{1,0:T(8,128)(2,1)S(1)} collective-permute-done((bf16[32,2048]{1,0:T(8,128)(2,1)S(1)}, bf16[32,2048]{1,0:T(8,128)(2,1)S(1)}, u32[]{:S(2)}, u32[]{:S(2)}) %collective-permute-start.28) | collective-permute-done | bytes 131104 | tf_op jit(solution)/shard_map/ppermute | solution.py:341
  84.5 0.7 fusion.3
  (41 shorter events, 0.3 us)
Async XLA Ops:
  0.0 14.6 %copy-start.3 = (bf16[256,2048]{1,0:T(8,128)(2,1)S(1)}, bf16[256,2048]{1,0:T(8,128)(2,1)}, u32[]{:S(2)}) copy-start(bf16[256,2048]{1,0:T(8,128)(2,1)} %refs_1_.1) | copy-start | bytes 3145732
  0.0 14.6 %collective-permute-start.3 = (bf16[256,2048]{1,0:T(8,128)(2,1)}, bf16[256,2048]{1,0:T(8,128)(2,1)S(1)}, u32[]{:S(2)}, u32[]{:S(2)}) collective-permute-start(bf16[256,2048]{1,0:T(8,128)(2,1)} %refs_1_.1), channel_id=1, source_target_pairs={{0,1},{1,0},{2,3},{3,2},{4,5},{5,4},{6,7},{7,6},{8,9},{9,8},{10,11... | collective-permute-start | bytes 3145736 | tf_op jit(solution)/shard_map/ppermute | solution.py:344
  5.0 14.2 %copy-start.6 = (bf16[32,640]{1,0:T(8,128)(2,1)S(1)}, bf16[32,640]{1,0:T(8,128)(2,1)}, u32[]{:S(2)}) copy-start(bf16[32,640]{1,0:T(8,128)(2,1)} %get-tuple-element.45) | copy-start | bytes 122884
  5.0 17.7 %copy-start.4 = (bf16[32,640]{1,0:T(8,128)(2,1)S(1)}, bf16[32,640]{1,0:T(8,128)(2,1)}, u32[]{:S(2)}) copy-start(bf16[32,640]{1,0:T(8,128)(2,1)} %get-tuple-element.51.refs_0_.refs_7_) | copy-start | bytes 122884
  5.0 6.1 %collective-permute-start = (bf16[3,32,640]{2,1,0:T(8,128)(2,1)}, bf16[3,32,640]{2,1,0:T(8,128)(2,1)S(1)}, u32[]{:S(2)}, u32[]{:S(2)}) collective-permute-start(bf16[3,32,640]{2,1,0:T(8,128)(2,1)} %get-tuple-element.41), channel_id=1, source_target_pairs={{0,1},{1,0},{2,3},{3,2},{4,5},{5,4},{6,7},{7,6},{8,9},{9,8},{10,11... | collective-permute-start | bytes 368648 | tf_op jit(solution)/shard_map/ppermute | solution.py:344
  5.2 9.4 %collective-permute-start.2 = (bf16[32,640]{1,0:T(8,128)(2,1)}, bf16[32,640]{1,0:T(8,128)(2,1)S(1)}, u32[]{:S(2)}, u32[]{:S(2)}) collective-permute-start(bf16[32,640]{1,0:T(8,128)(2,1)} %get-tuple-element.42), channel_id=1, source_target_pairs={{0,14},{1,15},{4,10},{5,11},{8,6},{9,7},{12,2},{13,3},{14,0},{15,1... | collective-permute-start | bytes 122888 | tf_op jit(solution)/shard_map/ppermute | solution.py:341
  11.1 16.4 %copy-start.2 = (bf16[1,768,2048]{2,1,0:T(8,128)(2,1)S(1)}, bf16[1,768,2048]{2,1,0:T(8,128)(2,1)}, u32[]{:S(2)}) copy-start(bf16[1,768,2048]{2,1,0:T(8,128)(2,1)} %refs_7_) | copy-start | bytes 9437188
  12.1 6.5 %collective-permute-start.1 = (bf16[64,640]{1,0:T(8,128)(2,1)S(1)}, bf16[64,640]{1,0:T(8,128)(2,1)S(1)}, u32[]{:S(2)}, u32[]{:S(2)}) collective-permute-start(bf16[64,640]{1,0:T(8,128)(2,1)S(1)} %pad_maximum_fusion), channel_id=1, source_target_pairs={{0,10},{1,13},{4,6},{5,15},{8,2},{9,11},{12,0},{13,7},{14,4},{15,3... | collective-permute-start | bytes 245768 | tf_op jit(solution)/shard_map/ppermute | solution.py:341
  13.0 10.1 %collective-permute-start.6 = (bf16[64,640]{1,0:T(8,128)(2,1)S(1)}, bf16[64,640]{1,0:T(8,128)(2,1)S(1)}, u32[]{:S(2)}, u32[]{:S(2)}) collective-permute-start(bf16[64,640]{1,0:T(8,128)(2,1)S(1)} %pad_maximum_fusion.2), channel_id=1, source_target_pairs={{0,2},{1,5},{4,0},{5,9},{8,4},{9,13},{12,8},{13,15},{14,12},{15,11... | collective-permute-start | bytes 245768 | tf_op jit(solution)/shard_map/ppermute | solution.py:341
  15.2 11.8 %collective-permute-start.7 = (bf16[32,2048]{1,0:T(8,128)(2,1)S(1)}, bf16[32,2048]{1,0:T(8,128)(2,1)S(1)}, u32[]{:S(2)}, u32[]{:S(2)}) collective-permute-start(bf16[32,2048]{1,0:T(8,128)(2,1)S(1)} %get-tuple-element.48), channel_id=1, source_target_pairs={{0,8},{1,7},{4,12},{5,3},{8,14},{9,1},{12,10},{13,5},{14,6},{15,9}... | collective-permute-start | bytes 393224 | tf_op jit(solution)/shard_map/ppermute | solution.py:341
  18.6 8.4 %copy-start = (bf16[1,2048,768]{2,1,0:T(8,128)(2,1)S(1)}, bf16[1,2048,768]{2,1,0:T(8,128)(2,1)}, u32[]{:S(2)}) copy-start(bf16[1,2048,768]{2,1,0:T(8,128)(2,1)} %refs_5_) | copy-start | bytes 9437188
  18.6 8.4 %copy-start.1 = (bf16[1,2048,768]{2,1,0:T(8,128)(2,1)S(1)}, bf16[1,2048,768]{2,1,0:T(8,128)(2,1)}, u32[]{:S(2)}) copy-start(bf16[1,2048,768]{2,1,0:T(8,128)(2,1)} %refs_6_) | copy-start | bytes 9437188
  19.1 8.5 %collective-permute-start.10 = (bf16[32,2048]{1,0:T(8,128)(2,1)S(1)}, bf16[32,2048]{1,0:T(8,128)(2,1)S(1)}, u32[]{:S(2)}, u32[]{:S(2)}) collective-permute-start(bf16[32,2048]{1,0:T(8,128)(2,1)S(1)} %get-tuple-element.52), channel_id=1, source_target_pairs={{0,4},{1,3},{4,8},{5,1},{8,12},{9,5},{12,14},{13,9},{14,10},{15,13... | collective-permute-start | bytes 393224 | tf_op jit(solution)/shard_map/ppermute | solution.py:341
  19.2 7.2 %collective-permute-start.5 = (bf16[64,640]{1,0:T(8,128)(2,1)S(1)}, bf16[64,640]{1,0:T(8,128)(2,1)S(1)}, u32[]{:S(2)}, u32[]{:S(2)}) collective-permute-start(bf16[64,640]{1,0:T(8,128)(2,1)S(1)} %pad_maximum_fusion.1), channel_id=1, source_target_pairs={{0,6},{1,9},{4,2},{5,13},{8,0},{9,15},{12,4},{13,11},{14,8},{15,7}... | collective-permute-start | bytes 245768 | tf_op jit(solution)/shard_map/ppermute | solution.py:341
  21.0 7.0 %collective-permute-start.4 = (bf16[32,2048]{1,0:T(8,128)(2,1)S(1)}, bf16[32,2048]{1,0:T(8,128)(2,1)S(1)}, u32[]{:S(2)}, u32[]{:S(2)}) collective-permute-start(bf16[32,2048]{1,0:T(8,128)(2,1)S(1)} %get-tuple-element.44), channel_id=1, source_target_pairs={{0,4},{1,3},{4,8},{5,1},{8,12},{9,5},{12,14},{13,9},{14,10},{15,13... | collective-permute-start | bytes 393224 | tf_op jit(solution)/shard_map/ppermute | solution.py:341
  22.7 19.2 %copy-start.5 = (bf16[32,2048]{1,0:T(8,128)(2,1)S(1)}, bf16[32,2048]{1,0:T(8,128)(2,1)}, u32[]{:S(2)}) copy-start(bf16[32,2048]{1,0:T(8,128)(2,1)} %param.16) | copy-start | bytes 393220
  23.1 18.9 %copy-start.7 = (f32[2048]{0:T(1024)S(1)}, f32[2048]{0:T(1024)}, u32[]{:S(2)}) copy-start(f32[2048]{0:T(1024)} %param.18) | copy-start | bytes 24580
  26.9 31.9 %collective-permute-start.22 = (bf16[1,2048,768]{2,1,0:T(8,128)(2,1)S(1)}, bf16[1,2048,768]{2,1,0:T(8,128)(2,1)S(1)}, u32[]{:S(2)}, u32[]{:S(2)}) collective-permute-start(bf16[1,2048,768]{2,1,0:T(8,128)(2,1)S(1)} %copy-done), channel_id=1, source_target_pairs={{0,1},{1,0},{2,3},{3,2},{4,5},{5,4},{6,7},{7,6},{8,9},{9,8},{10,11... | collective-permute-start | bytes 9437192 | tf_op jit(solution)/shard_map/ppermute | solution.py:344
  27.0 31.8 %collective-permute-start.23 = (bf16[1,2048,768]{2,1,0:T(8,128)(2,1)S(1)}, bf16[1,2048,768]{2,1,0:T(8,128)(2,1)S(1)}, u32[]{:S(2)}, u32[]{:S(2)}) collective-permute-start(bf16[1,2048,768]{2,1,0:T(8,128)(2,1)S(1)} %copy-done.1), channel_id=1, source_target_pairs={{0,1},{1,0},{2,3},{3,2},{4,5},{5,4},{6,7},{7,6},{8,9},{9,8},{10,11... | collective-permute-start | bytes 9437192 | tf_op jit(solution)/shard_map/ppermute | solution.py:344
  27.5 31.3 %collective-permute-start.24 = (bf16[1,768,2048]{2,1,0:T(8,128)(2,1)S(1)}, bf16[1,768,2048]{2,1,0:T(8,128)(2,1)S(1)}, u32[]{:S(2)}, u32[]{:S(2)}) collective-permute-start(bf16[1,768,2048]{2,1,0:T(8,128)(2,1)S(1)} %copy-done.2), channel_id=1, source_target_pairs={{0,1},{1,0},{2,3},{3,2},{4,5},{5,4},{6,7},{7,6},{8,9},{9,8},{10,11... | collective-permute-start | bytes 9437192 | tf_op jit(solution)/shard_map/ppermute | solution.py:344
  27.6 5.0 %collective-permute-start.11 = (bf16[32,2048]{1,0:T(8,128)(2,1)S(1)}, bf16[32,2048]{1,0:T(8,128)(2,1)S(1)}, u32[]{:S(2)}, u32[]{:S(2)}) collective-permute-start(bf16[32,2048]{1,0:T(8,128)(2,1)S(1)} %add_convert_fusion.6), channel_id=1, source_target_pairs={{0,4},{1,3},{4,8},{5,1},{8,12},{9,5},{12,14},{13,9},{14,10},{15,13... | collective-permute-start | bytes 393224 | tf_op jit(solution)/shard_map/ppermute | solution.py:341
  28.1 5.9 %collective-permute-start.8 = (bf16[32,2048]{1,0:T(8,128)(2,1)S(1)}, bf16[32,2048]{1,0:T(8,128)(2,1)S(1)}, u32[]{:S(2)}, u32[]{:S(2)}) collective-permute-start(bf16[32,2048]{1,0:T(8,128)(2,1)S(1)} %add_convert_fusion.8), channel_id=1, source_target_pairs={{0,4},{1,3},{4,8},{5,1},{8,12},{9,5},{12,14},{13,9},{14,10},{15,13... | collective-permute-start | bytes 393224 | tf_op jit(solution)/shard_map/ppermute | solution.py:341
  32.7 5.0 %collective-permute-start.12 = (bf16[32,2048]{1,0:T(8,128)(2,1)S(1)}, bf16[32,2048]{1,0:T(8,128)(2,1)S(1)}, u32[]{:S(2)}, u32[]{:S(2)}) collective-permute-start(bf16[32,2048]{1,0:T(8,128)(2,1)S(1)} %add_convert_fusion.5), channel_id=1, source_target_pairs={{0,4},{1,3},{4,8},{5,1},{8,12},{9,5},{12,14},{13,9},{14,10},{15,13... | collective-permute-start | bytes 393224 | tf_op jit(solution)/shard_map/ppermute | solution.py:341
  34.1 5.0 %collective-permute-start.9 = (bf16[32,2048]{1,0:T(8,128)(2,1)S(1)}, bf16[32,2048]{1,0:T(8,128)(2,1)S(1)}, u32[]{:S(2)}, u32[]{:S(2)}) collective-permute-start(bf16[32,2048]{1,0:T(8,128)(2,1)S(1)} %add_convert_fusion.7), channel_id=1, source_target_pairs={{0,4},{1,3},{4,8},{5,1},{8,12},{9,5},{12,14},{13,9},{14,10},{15,13... | collective-permute-start | bytes 393224 | tf_op jit(solution)/shard_map/ppermute | solution.py:341
  37.7 4.1 %collective-permute-start.13 = (bf16[32,2048]{1,0:T(8,128)(2,1)S(1)}, bf16[32,2048]{1,0:T(8,128)(2,1)S(1)}, u32[]{:S(2)}, u32[]{:S(2)}) collective-permute-start(bf16[32,2048]{1,0:T(8,128)(2,1)S(1)} %collective-permute-done.12), channel_id=1, source_target_pairs={{0,1},{1,0},{2,3},{3,2},{4,5},{5,4},{6,7},{7,6},{8,9},{9,8},{10,11... | collective-permute-start | bytes 393224 | tf_op jit(solution)/shard_map/ppermute | solution.py:344
  42.1 1.7 %collective-permute-start.18 = (bf16[32,2048]{1,0:T(8,128)(2,1)S(1)}, bf16[32,2048]{1,0:T(8,128)(2,1)S(1)}, u32[]{:S(2)}, u32[]{:S(2)}) collective-permute-start(bf16[32,2048]{1,0:T(8,128)(2,1)S(1)} %fusion.2.refs_4_), channel_id=1, source_target_pairs={{0,1},{1,0},{2,3},{3,2},{4,5},{5,4},{6,7},{7,6},{8,9},{9,8},{10,11... | collective-permute-start | bytes 393224 | tf_op jit(solution)/shard_map/ppermute | solution.py:344
  42.3 5.0 %collective-permute-start.14 = (bf16[32,2048]{1,0:T(8,128)(2,1)S(1)}, bf16[32,2048]{1,0:T(8,128)(2,1)S(1)}, u32[]{:S(2)}, u32[]{:S(2)}) collective-permute-start(bf16[32,2048]{1,0:T(8,128)(2,1)S(1)} %fusion.2.refs_4_), channel_id=1, source_target_pairs={{0,2},{1,5},{4,0},{5,9},{8,4},{9,13},{12,8},{13,15},{14,12},{15,11... | collective-permute-start | bytes 393224 | tf_op jit(solution)/shard_map/ppermute | solution.py:341
  43.9 5.0 %collective-permute-start.19 = (bf16[32,2048]{1,0:T(8,128)(2,1)S(1)}, bf16[32,2048]{1,0:T(8,128)(2,1)S(1)}, u32[]{:S(2)}, u32[]{:S(2)}) collective-permute-start(bf16[32,2048]{1,0:T(8,128)(2,1)S(1)} %collective-permute-done.18), channel_id=1, source_target_pairs={{0,2},{1,5},{4,0},{5,9},{8,4},{9,13},{12,8},{13,15},{14,12},{15,11... | collective-permute-start | bytes 393224 | tf_op jit(solution)/shard_map/ppermute | solution.py:341
  47.3 5.0 %collective-permute-start.15 = (bf16[32,2048]{1,0:T(8,128)(2,1)S(1)}, bf16[32,2048]{1,0:T(8,128)(2,1)S(1)}, u32[]{:S(2)}, u32[]{:S(2)}) collective-permute-start(bf16[32,2048]{1,0:T(8,128)(2,1)S(1)} %collective-permute-done.14.refs_2_), channel_id=1, source_target_pairs={{0,2},{1,5},{4,0},{5,9},{8,4},{9,13},{12,8},{13,15},{14,12},{15,11... | collective-permute-start | bytes 393224 | tf_op jit(solution)/shard_map/ppermute | solution.py:341
  48.8 5.0 %collective-permute-start.20 = (bf16[32,2048]{1,0:T(8,128)(2,1)S(1)}, bf16[32,2048]{1,0:T(8,128)(2,1)S(1)}, u32[]{:S(2)}, u32[]{:S(2)}) collective-permute-start(bf16[32,2048]{1,0:T(8,128)(2,1)S(1)} %collective-permute-done.19.refs_3_), channel_id=1, source_target_pairs={{0,2},{1,5},{4,0},{5,9},{8,4},{9,13},{12,8},{13,15},{14,12},{15,11... | collective-permute-start | bytes 393224 | tf_op jit(solution)/shard_map/ppermute | solution.py:341
  52.3 5.0 %collective-permute-start.16 = (bf16[32,2048]{1,0:T(8,128)(2,1)S(1)}, bf16[32,2048]{1,0:T(8,128)(2,1)S(1)}, u32[]{:S(2)}, u32[]{:S(2)}) collective-permute-start(bf16[32,2048]{1,0:T(8,128)(2,1)S(1)} %collective-permute-done.15.refs_0_), channel_id=1, source_target_pairs={{0,2},{1,5},{4,0},{5,9},{8,4},{9,13},{12,8},{13,15},{14,12},{15,11... | collective-permute-start | bytes 393224 | tf_op jit(solution)/shard_map/ppermute | solution.py:341
  53.8 8.4 %collective-permute-start.21 = (bf16[32,2048]{1,0:T(8,128)(2,1)S(1)}, bf16[32,2048]{1,0:T(8,128)(2,1)S(1)}, u32[]{:S(2)}, u32[]{:S(2)}) collective-permute-start(bf16[32,2048]{1,0:T(8,128)(2,1)S(1)} %collective-permute-done.20.refs_1_), channel_id=1, source_target_pairs={{0,2},{1,5},{4,0},{5,9},{8,4},{9,13},{12,8},{13,15},{14,12},{15,11... | collective-permute-start | bytes 393224 | tf_op jit(solution)/shard_map/ppermute | solution.py:341
  57.3 5.0 %collective-permute-start.17 = (bf16[32,2048]{1,0:T(8,128)(2,1)S(1)}, bf16[32,2048]{1,0:T(8,128)(2,1)S(1)}, u32[]{:S(2)}, u32[]{:S(2)}) collective-permute-start(bf16[32,2048]{1,0:T(8,128)(2,1)S(1)} %collective-permute-done.16.refs_1_), channel_id=1, source_target_pairs={{0,2},{1,5},{4,0},{5,9},{8,4},{9,13},{12,8},{13,15},{14,12},{15,11... | collective-permute-start | bytes 393224 | tf_op jit(solution)/shard_map/ppermute | solution.py:341
  65.5 5.0 %collective-permute-start.29 = (bf16[32,2048]{1,0:T(8,128)(2,1)S(1)}, bf16[32,2048]{1,0:T(8,128)(2,1)S(1)}, u32[]{:S(2)}, u32[]{:S(2)}) collective-permute-start(bf16[32,2048]{1,0:T(8,128)(2,1)S(1)} %get-tuple-element.72), channel_id=1, source_target_pairs={{0,4},{1,3},{4,8},{5,1},{8,12},{9,5},{12,14},{13,9},{14,10},{15,13... | collective-permute-start | bytes 393224 | tf_op jit(solution)/shard_map/ppermute | solution.py:341
  66.0 5.9 %collective-permute-start.25 = (bf16[32,2048]{1,0:T(8,128)(2,1)S(1)}, bf16[32,2048]{1,0:T(8,128)(2,1)S(1)}, u32[]{:S(2)}, u32[]{:S(2)}) collective-permute-start(bf16[32,2048]{1,0:T(8,128)(2,1)S(1)} %get-tuple-element.67), channel_id=1, source_target_pairs={{0,4},{1,3},{4,8},{5,1},{8,12},{9,5},{12,14},{13,9},{14,10},{15,13... | collective-permute-start | bytes 393224 | tf_op jit(solution)/shard_map/ppermute | solution.py:341
  66.3 8.0 %collective-permute-start.26 = (bf16[32,2048]{1,0:T(8,128)(2,1)S(1)}, bf16[32,2048]{1,0:T(8,128)(2,1)S(1)}, u32[]{:S(2)}, u32[]{:S(2)}) collective-permute-start(bf16[32,2048]{1,0:T(8,128)(2,1)S(1)} %get-tuple-element.69), channel_id=1, source_target_pairs={{0,8},{1,7},{4,12},{5,3},{8,14},{9,1},{12,10},{13,5},{14,6},{15,9}... | collective-permute-start | bytes 393224 | tf_op jit(solution)/shard_map/ppermute | solution.py:341
  70.5 5.2 %collective-permute-start.30 = (bf16[32,2048]{1,0:T(8,128)(2,1)S(1)}, bf16[32,2048]{1,0:T(8,128)(2,1)S(1)}, u32[]{:S(2)}, u32[]{:S(2)}) collective-permute-start(bf16[32,2048]{1,0:T(8,128)(2,1)S(1)} %add_convert_fusion.1), channel_id=1, source_target_pairs={{0,4},{1,3},{4,8},{5,1},{8,12},{9,5},{12,14},{13,9},{14,10},{15,13... | collective-permute-start | bytes 393224 | tf_op jit(solution)/shard_map/ppermute | solution.py:341
  74.4 5.0 %collective-permute-start.27 = (bf16[32,2048]{1,0:T(8,128)(2,1)S(1)}, bf16[32,2048]{1,0:T(8,128)(2,1)S(1)}, u32[]{:S(2)}, u32[]{:S(2)}) collective-permute-start(bf16[32,2048]{1,0:T(8,128)(2,1)S(1)} %add_convert_fusion.3), channel_id=1, source_target_pairs={{0,4},{1,3},{4,8},{5,1},{8,12},{9,5},{12,14},{13,9},{14,10},{15,13... | collective-permute-start | bytes 393224 | tf_op jit(solution)/shard_map/ppermute | solution.py:341
  75.8 5.1 %collective-permute-start.31 = (bf16[32,2048]{1,0:T(8,128)(2,1)S(1)}, bf16[32,2048]{1,0:T(8,128)(2,1)S(1)}, u32[]{:S(2)}, u32[]{:S(2)}) collective-permute-start(bf16[32,2048]{1,0:T(8,128)(2,1)S(1)} %add_convert_fusion), channel_id=1, source_target_pairs={{0,4},{1,3},{4,8},{5,1},{8,12},{9,5},{12,14},{13,9},{14,10},{15,13... | collective-permute-start | bytes 393224 | tf_op jit(solution)/shard_map/ppermute | solution.py:341
  79.5 5.0 %collective-permute-start.28 = (bf16[32,2048]{1,0:T(8,128)(2,1)S(1)}, bf16[32,2048]{1,0:T(8,128)(2,1)S(1)}, u32[]{:S(2)}, u32[]{:S(2)}) collective-permute-start(bf16[32,2048]{1,0:T(8,128)(2,1)S(1)} %add_convert_fusion.2), channel_id=1, source_target_pairs={{0,4},{1,3},{4,8},{5,1},{8,12},{9,5},{12,14},{13,9},{14,10},{15,13... | collective-permute-start | bytes 393224 | tf_op jit(solution)/shard_map/ppermute | solution.py:341
  80.8 3.6 %collective-permute-start.32 = (bf16[32,2048]{1,0:T(8,128)(2,1)S(1)}, bf16[32,2048]{1,0:T(8,128)(2,1)S(1)}, u32[]{:S(2)}, u32[]{:S(2)}) collective-permute-start(bf16[32,2048]{1,0:T(8,128)(2,1)S(1)} %collective-permute-done.31), channel_id=1, source_target_pairs={{0,1},{1,0},{2,3},{3,2},{4,5},{5,4},{6,7},{7,6},{8,9},{9,8},{10,11... | collective-permute-start | bytes 393224 | tf_op jit(solution)/shard_map/ppermute | solution.py:344

commit v11 on v10

--- a/solution.py
+++ b/solution.py
@@ -371,8 +371,8 @@
     first, own_experts = lax.optimization_barrier((first, own_experts))
     for offset in range(hops - 2, 0, -1):
         arrived[offset] = send(offset, mine[offset - 1], got[offset - 1])
-    nearer = [arrived[offset] for offset in range(hops - 2, 0, -1)]
-    partial += project(nearer, kinds[3:-1], *weights)
+    for offset in range(hops - 2, 0, -1):
+        partial += project([arrived[offset]], kinds[3:5], *weights)
     partial += project([here], kinds[-1:], *weights)
     _, own_experts = lax.optimization_barrier((partial, own_experts))
     other_experts = tuple(swapped(w) for w in own_experts)
@@ -408,7 +408,7 @@
     pieces = [pass_on(own, -1)] + pieces
     digits = [arrived[offset] for offset in range(hops, -1, -1)]
     nearer = serve(pieces[3:], kinds[3:], digits[2:])
-    pieces[2], nearer = lax.optimization_barrier((pieces[2], nearer))
+    pieces[1], pieces[2], nearer = lax.optimization_barrier((pieces[1], pieces[2], nearer))
     total = serve(pieces[:3], kinds[:3], digits[:2]) + nearer
     return (residual.astype(F32) + ring_sums(total, pass_on(total[0], 2))).astype(BF16)
 

time: 85.3 us -> 84.3 us (0.988)
  waiting for transfers between devices: 38.9 us -> 35.4 us
  starting transfers between devices: 30 us -> 32 us
    ppermute x25, waiting for transfers between devices: 36.1 us -> 32.9 us  [pass_on(): return lax.ppermute(array, 'rows', toward(step))]
    ppermute x25, starting transfers between devices: 28.5 us -> 29.6 us  [pass_on(): return lax.ppermute(array, 'rows', toward(step))]
    ppermute x8, starting transfers between devices: 1.5 us -> 2.48 us  [swapped(): return lax.ppermute(array, 'rows', swap)]
    pallas_call x4 -> x5, Pallas kernels: 1.95 us -> 2.44 us  [project(): pl.pallas_call(functools.partial(project_kernel, len(pieces), kept), out_...]
  transfers between devices with their start and end apart: 33 -> 33, of which waited for: 17 -> 19; matrix products, arithmetic and copies ran while one was open for 3% -> 3% of each run, Pallas kernels for 12% -> 12%
where the time goes in v11:
time: 84.3 us; the launch traced here: 84.1 us
  waiting for transfers between devices  35.4 us (42%)
  starting transfers between devices  32 us (38%)
  Pallas kernels  13.6 us (16%)
  other arithmetic  2.88 us (3%)
    ppermute x25, waiting for transfers between devices, pass_on(): return lax.ppermute(array, 'rows', toward(step))  32.9 us
    ppermute x25, starting transfers between devices, pass_on(): return lax.ppermute(array, 'rows', toward(step))  29.6 us
    pallas_call x2, Pallas kernels, experts(): pl.pallas_call(functools.partial(expert_kernel, len(pieces), len(digits),...  6.59 us
    pallas_call x1, Pallas kernels, attend(): pl.pallas_call(functools.partial(attend_kernel, chips, hops, chip_experts...  4.53 us
    ppermute x8, starting transfers between devices, swapped(): return lax.ppermute(array, 'rows', swap)  2.48 us
    ppermute x8, waiting for transfers between devices, swapped(): return lax.ppermute(array, 'rows', swap)  2.45 us
    pallas_call x5, Pallas kernels, project(): pl.pallas_call(functools.partial(project_kernel, len(pieces), kept), out_...  2.44 us
  transfers between devices with their start and end apart: 33, of which 19 were waited for; matrix products, arithmetic and copies ran while one was open for 3% of the time, Pallas kernels for 12%

profile of v11, /device:TPU:0, one launch (start us, length us, event | category | flops | bytes accessed | tf_op | source)
XLA Modules:
  0.0 84.1 jit_solution(6390220269413889366)
XLA Ops:
  0.0 0.5 collective-permute-start.3
  0.5 4.5 %shard_map.118 = (bf16[32,640]{1,0:T(8,128)(2,1)}, bf16[3,32,640]{2,1,0:T(8,128)(2,1)}, bf16[32,640]{1,0:T(8,128)(2,1)}, bf16[32,640]{1,0:T(8,128)(2,1)}, bf16[3...) custom-call(s32[32]{0:T(128)} %lengths_ref.1, bf16[32,4096]{1,0:T(8,128)(2,1)} %q_ref.1, bf16[32,2,128,128]{3,2,1,0:T(8,128)(2,1)} %k_ref.1, ...), custom_call_target="tpu_custom_call" | custom-call | flops 67108864 | bytes 4194304 | tf_op jit(solution)/shard_map/pallas_call | solution.py:164
  5.0 0.2 collective-permute-start
  5.2 5.9 %collective-permute-start.2 = (bf16[32,640]{1,0:T(8,128)(2,1)}, bf16[32,640]{1,0:T(8,128)(2,1)S(1)}, u32[]{:S(2)}, u32[]{:S(2)}) collective-permute-start(bf16[32,640]{1,0:T(8,128)(2,1)} %get-tuple-element.43), channel_id=1, source_target_pairs={{0,14},{1,15},{4,10},{5,11},{8,6},{9,7},{12,2},{13,3},{14,0},{15,1... | collective-permute-start | bytes 122888 | tf_op jit(solution)/shard_map/ppermute | solution.py:341
  11.1 0.8 pad_maximum_fusion
  11.9 0.2 collective-permute-start.1
  12.1 0.8 pad_maximum_fusion.1
  12.9 1.5 %collective-permute-start.5 = (bf16[64,640]{1,0:T(8,128)(2,1)S(1)}, bf16[64,640]{1,0:T(8,128)(2,1)S(1)}, u32[]{:S(2)}, u32[]{:S(2)}) collective-permute-start(bf16[64,640]{1,0:T(8,128)(2,1)S(1)} %pad_maximum_fusion.1), channel_id=1, source_target_pairs={{0,6},{1,9},{4,2},{5,13},{8,0},{9,15},{12,4},{13,11},{14,8},{15,7}... | collective-permute-start | bytes 245768 | tf_op jit(solution)/shard_map/ppermute | solution.py:341
  14.4 0.5 shard_map.119
  15.0 1.4 %collective-permute-start.6 = (bf16[32,2048]{1,0:T(8,128)(2,1)S(1)}, bf16[32,2048]{1,0:T(8,128)(2,1)S(1)}, u32[]{:S(2)}, u32[]{:S(2)}) collective-permute-start(bf16[32,2048]{1,0:T(8,128)(2,1)S(1)} %get-tuple-element.48), channel_id=1, source_target_pairs={{0,8},{1,7},{4,12},{5,3},{8,14},{9,1},{12,10},{13,5},{14,6},{15,9}... | collective-permute-start | bytes 393224 | tf_op jit(solution)/shard_map/ppermute | solution.py:341
  16.4 2.0 %collective-permute-done.1.refs_0_.refs_4_ = bf16[64,640]{1,0:T(8,128)(2,1)S(1)} collective-permute-done((bf16[64,640]{1,0:T(8,128)(2,1)S(1)}, bf16[64,640]{1,0:T(8,128)(2,1)S(1)}, u32[]{:S(2)}, u32[]{:S(2)}) %collective-permute-start.1) | collective-permute-done | bytes 81952 | tf_op jit(solution)/shard_map/ppermute | solution.py:341
  18.3 0.5 shard_map.120
  18.8 0.4 collective-permute-start.10
  19.2 1.7 %collective-permute-start.8 = (bf16[64,640]{1,0:T(8,128)(2,1)S(1)}, bf16[64,640]{1,0:T(8,128)(2,1)S(1)}, u32[]{:S(2)}, u32[]{:S(2)}) collective-permute-start(bf16[64,640]{1,0:T(8,128)(2,1)S(1)} %pad_maximum_fusion.2), channel_id=1, source_target_pairs={{0,2},{1,5},{4,0},{5,9},{8,4},{9,13},{12,8},{13,15},{14,12},{15,11... | collective-permute-start | bytes 245768 | tf_op jit(solution)/shard_map/ppermute | solution.py:341
  21.0 0.3 collective-permute-start.4
  21.3 0.5 shard_map.123
  21.8 0.4 collective-permute-done.5.refs_0_.refs_5_
  22.2 0.5 shard_map.121
  22.7 1.9 %collective-permute-done.8.refs_0_.refs_6_ = bf16[64,640]{1,0:T(8,128)(2,1)S(1)} collective-permute-done((bf16[64,640]{1,0:T(8,128)(2,1)S(1)}, bf16[64,640]{1,0:T(8,128)(2,1)S(1)}, u32[]{:S(2)}, u32[]{:S(2)}) %collective-permute-start.8) | collective-permute-done | bytes 81952 | tf_op jit(solution)/shard_map/ppermute | solution.py:341
  24.6 0.5 shard_map.122
  25.1 0.9 %collective-permute-start.22 = (bf16[1,2048,768]{2,1,0:T(8,128)(2,1)S(1)}, bf16[1,2048,768]{2,1,0:T(8,128)(2,1)S(1)}, u32[]{:S(2)}, u32[]{:S(2)}) collective-permute-start(bf16[1,2048,768]{2,1,0:T(8,128)(2,1)S(1)} %copy-done), channel_id=1, source_target_pairs={{0,1},{1,0},{2,3},{3,2},{4,5},{5,4},{6,7},{7,6},{8,9},{9,8},{10,11... | collective-permute-start | bytes 9437192 | tf_op jit(solution)/shard_map/ppermute | solution.py:344
  26.0 0.1 collective-permute-start.23
  26.1 0.4 collective-permute-start.24
  26.6 0.7 collective-permute-start.11
  27.3 1.6 %collective-permute-start.7 = (bf16[32,2048]{1,0:T(8,128)(2,1)S(1)}, bf16[32,2048]{1,0:T(8,128)(2,1)S(1)}, u32[]{:S(2)}, u32[]{:S(2)}) collective-permute-start(bf16[32,2048]{1,0:T(8,128)(2,1)S(1)} %add_convert_fusion.8), channel_id=1, source_target_pairs={{0,4},{1,3},{4,8},{5,1},{8,12},{9,5},{12,14},{13,9},{14,10},{15,13... | collective-permute-start | bytes 393224 | tf_op jit(solution)/shard_map/ppermute | solution.py:341
  28.9 2.7 %collective-permute-done.11 = bf16[32,2048]{1,0:T(8,128)(2,1)S(1)} collective-permute-done((bf16[32,2048]{1,0:T(8,128)(2,1)S(1)}, bf16[32,2048]{1,0:T(8,128)(2,1)S(1)}, u32[]{:S(2)}, u32[]{:S(2)}) %collective-permute-start.11) | collective-permute-done | bytes 131104 | tf_op jit(solution)/shard_map/ppermute | solution.py:341
  31.6 0.7 collective-permute-start.12
  32.3 0.7 collective-permute-done.7
  33.0 1.0 %collective-permute-start.9 = (bf16[32,2048]{1,0:T(8,128)(2,1)S(1)}, bf16[32,2048]{1,0:T(8,128)(2,1)S(1)}, u32[]{:S(2)}, u32[]{:S(2)}) collective-permute-start(bf16[32,2048]{1,0:T(8,128)(2,1)S(1)} %add_convert_fusion.7), channel_id=1, source_target_pairs={{0,4},{1,3},{4,8},{5,1},{8,12},{9,5},{12,14},{13,9},{14,10},{15,13... | collective-permute-start | bytes 393224 | tf_op jit(solution)/shard_map/ppermute | solution.py:341
  34.0 2.7 %collective-permute-done.12 = bf16[32,2048]{1,0:T(8,128)(2,1)S(1)} collective-permute-done((bf16[32,2048]{1,0:T(8,128)(2,1)S(1)}, bf16[32,2048]{1,0:T(8,128)(2,1)S(1)}, u32[]{:S(2)}, u32[]{:S(2)}) %collective-permute-start.12) | collective-permute-done | bytes 131104 | tf_op jit(solution)/shard_map/ppermute | solution.py:341
  36.7 1.4 %collective-permute-done.9 = bf16[32,2048]{1,0:T(8,128)(2,1)S(1)} collective-permute-done((bf16[32,2048]{1,0:T(8,128)(2,1)S(1)}, bf16[32,2048]{1,0:T(8,128)(2,1)S(1)}, u32[]{:S(2)}, u32[]{:S(2)}) %collective-permute-start.9) | collective-permute-done | bytes 131104 | tf_op jit(solution)/shard_map/ppermute | solution.py:341
  38.1 2.4 %collective-permute-done.13 = bf16[32,2048]{1,0:T(8,128)(2,1)S(1)} collective-permute-done((bf16[32,2048]{1,0:T(8,128)(2,1)S(1)}, bf16[32,2048]{1,0:T(8,128)(2,1)S(1)}, u32[]{:S(2)}, u32[]{:S(2)}) %collective-permute-start.13) | collective-permute-done | bytes 131104 | tf_op jit(solution)/shard_map/ppermute | solution.py:344
  40.5 0.2 fusion
  40.7 0.1 fusion.2.refs_4_
  40.8 0.4 collective-permute-start.18
  41.2 1.0 %collective-permute-start.14 = (bf16[32,2048]{1,0:T(8,128)(2,1)S(1)}, bf16[32,2048]{1,0:T(8,128)(2,1)S(1)}, u32[]{:S(2)}, u32[]{:S(2)}) collective-permute-start(bf16[32,2048]{1,0:T(8,128)(2,1)S(1)} %fusion.2.refs_4_), channel_id=1, source_target_pairs={{0,2},{1,5},{4,0},{5,9},{8,4},{9,13},{12,8},{13,15},{14,12},{15,11... | collective-permute-start | bytes 393224 | tf_op jit(solution)/shard_map/ppermute | solution.py:341
  42.2 1.2 %collective-permute-start.19 = (bf16[32,2048]{1,0:T(8,128)(2,1)S(1)}, bf16[32,2048]{1,0:T(8,128)(2,1)S(1)}, u32[]{:S(2)}, u32[]{:S(2)}) collective-permute-start(bf16[32,2048]{1,0:T(8,128)(2,1)S(1)} %collective-permute-done.18), channel_id=1, source_target_pairs={{0,2},{1,5},{4,0},{5,9},{8,4},{9,13},{12,8},{13,15},{14,12},{15,11... | collective-permute-start | bytes 393224 | tf_op jit(solution)/shard_map/ppermute | solution.py:341
  43.4 2.8 %collective-permute-done.14.refs_2_ = bf16[32,2048]{1,0:T(8,128)(2,1)S(1)} collective-permute-done((bf16[32,2048]{1,0:T(8,128)(2,1)S(1)}, bf16[32,2048]{1,0:T(8,128)(2,1)S(1)}, u32[]{:S(2)}, u32[]{:S(2)}) %collective-permute-start.14) | collective-permute-done | bytes 131104 | tf_op jit(solution)/shard_map/ppermute | solution.py:341
  46.2 1.0 %collective-permute-start.15 = (bf16[32,2048]{1,0:T(8,128)(2,1)S(1)}, bf16[32,2048]{1,0:T(8,128)(2,1)S(1)}, u32[]{:S(2)}, u32[]{:S(2)}) collective-permute-start(bf16[32,2048]{1,0:T(8,128)(2,1)S(1)} %collective-permute-done.14.refs_2_), channel_id=1, source_target_pairs={{0,2},{1,5},{4,0},{5,9},{8,4},{9,13},{12,8},{13,15},{14,12},{15,11... | collective-permute-start | bytes 393224 | tf_op jit(solution)/shard_map/ppermute | solution.py:341
  47.2 0.4 collective-permute-done.19.refs_3_
  47.6 1.0 %collective-permute-start.20 = (bf16[32,2048]{1,0:T(8,128)(2,1)S(1)}, bf16[32,2048]{1,0:T(8,128)(2,1)S(1)}, u32[]{:S(2)}, u32[]{:S(2)}) collective-permute-start(bf16[32,2048]{1,0:T(8,128)(2,1)S(1)} %collective-permute-done.19.refs_3_), channel_id=1, source_target_pairs={{0,2},{1,5},{4,0},{5,9},{8,4},{9,13},{12,8},{13,15},{14,12},{15,11... | collective-permute-start | bytes 393224 | tf_op jit(solution)/shard_map/ppermute | solution.py:341
  48.6 2.6 %collective-permute-done.15.refs_0_ = bf16[32,2048]{1,0:T(8,128)(2,1)S(1)} collective-permute-done((bf16[32,2048]{1,0:T(8,128)(2,1)S(1)}, bf16[32,2048]{1,0:T(8,128)(2,1)S(1)}, u32[]{:S(2)}, u32[]{:S(2)}) %collective-permute-start.15) | collective-permute-done | bytes 131104 | tf_op jit(solution)/shard_map/ppermute | solution.py:341
  51.2 1.0 %collective-permute-start.16 = (bf16[32,2048]{1,0:T(8,128)(2,1)S(1)}, bf16[32,2048]{1,0:T(8,128)(2,1)S(1)}, u32[]{:S(2)}, u32[]{:S(2)}) collective-permute-start(bf16[32,2048]{1,0:T(8,128)(2,1)S(1)} %collective-permute-done.15.refs_0_), channel_id=1, source_target_pairs={{0,2},{1,5},{4,0},{5,9},{8,4},{9,13},{12,8},{13,15},{14,12},{15,11... | collective-permute-start | bytes 393224 | tf_op jit(solution)/shard_map/ppermute | solution.py:341
  52.2 0.4 collective-permute-done.20.refs_1_
  52.6 1.0 %collective-permute-start.21 = (bf16[32,2048]{1,0:T(8,128)(2,1)S(1)}, bf16[32,2048]{1,0:T(8,128)(2,1)S(1)}, u32[]{:S(2)}, u32[]{:S(2)}) collective-permute-start(bf16[32,2048]{1,0:T(8,128)(2,1)S(1)} %collective-permute-done.20.refs_1_), channel_id=1, source_target_pairs={{0,2},{1,5},{4,0},{5,9},{8,4},{9,13},{12,8},{13,15},{14,12},{15,11... | collective-permute-start | bytes 393224 | tf_op jit(solution)/shard_map/ppermute | solution.py:341
  53.6 2.6 %collective-permute-done.16.refs_1_ = bf16[32,2048]{1,0:T(8,128)(2,1)S(1)} collective-permute-done((bf16[32,2048]{1,0:T(8,128)(2,1)S(1)}, bf16[32,2048]{1,0:T(8,128)(2,1)S(1)}, u32[]{:S(2)}, u32[]{:S(2)}) %collective-permute-start.16) | collective-permute-done | bytes 131104 | tf_op jit(solution)/shard_map/ppermute | solution.py:341
  56.1 1.0 %collective-permute-start.17 = (bf16[32,2048]{1,0:T(8,128)(2,1)S(1)}, bf16[32,2048]{1,0:T(8,128)(2,1)S(1)}, u32[]{:S(2)}, u32[]{:S(2)}) collective-permute-start(bf16[32,2048]{1,0:T(8,128)(2,1)S(1)} %collective-permute-done.16.refs_1_), channel_id=1, source_target_pairs={{0,2},{1,5},{4,0},{5,9},{8,4},{9,13},{12,8},{13,15},{14,12},{15,11... | collective-permute-start | bytes 393224 | tf_op jit(solution)/shard_map/ppermute | solution.py:341
  57.1 3.4 %shard_map.124 = (f32[32,2048]{1,0:T(8,128)S(1)}, f32[32,2048]{1,0:T(8,128)S(1)}, f32[32,2048]{1,0:T(8,128)S(1)}, f32[32,2048]{1,0:T(8,128)S(1)}, f32[32,2048]{1,0:T(8,128)S(1)}) custom-call(bf16[32,2048]{1,0:T(8,128)(2,1)S(1)} %collective-permute-done.15.refs_0_, bf16[32,2048]{1,0:T(8,128)(2,1)S(1)} %collective-permute-done.20.refs_1_, ...), custom_call_target="tpu_custom_call" | custom-call | flops 3019898880 | bytes 327680 | tf_op jit(solution)/shard_map/pallas_call | solution.py:299
  60.5 0.6 collective-permute-done.17.refs_0_
  61.1 3.2 %shard_map.125 = (bf16[32,2048]{1,0:T(8,128)(2,1)S(1)}, bf16[32,2048]{1,0:T(8,128)(2,1)S(1)}, bf16[32,2048]{1,0:T(8,128)(2,1)S(1)}) custom-call(bf16[32,2048]{1,0:T(8,128)(2,1)S(1)} %collective-permute-done.17.refs_0_, bf16[32,2048]{1,0:T(8,128)(2,1)S(1)} %collective-permute-done.16.refs_1_, bf16[32,2048]{1,0:T(8,128)(2,1)S(1)} %collective-permute-done.21.refs_2_, ...), custom_call_target="tpu_custom_call" | custom-call | flops 1811939328 | bytes 196608 | tf_op jit(solution)/shard_map/pallas_call | solution.py:299
  64.3 0.7 collective-permute-start.29
  65.1 1.6 %collective-permute-start.25 = (bf16[32,2048]{1,0:T(8,128)(2,1)S(1)}, bf16[32,2048]{1,0:T(8,128)(2,1)S(1)}, u32[]{:S(2)}, u32[]{:S(2)}) collective-permute-start(bf16[32,2048]{1,0:T(8,128)(2,1)S(1)} %get-tuple-element.69), channel_id=1, source_target_pairs={{0,4},{1,3},{4,8},{5,1},{8,12},{9,5},{12,14},{13,9},{14,10},{15,13... | collective-permute-start | bytes 393224 | tf_op jit(solution)/shard_map/ppermute | solution.py:341
  66.6 0.7 collective-permute-start.26
  67.3 2.0 %collective-permute-done.29 = bf16[32,2048]{1,0:T(8,128)(2,1)S(1)} collective-permute-done((bf16[32,2048]{1,0:T(8,128)(2,1)S(1)}, bf16[32,2048]{1,0:T(8,128)(2,1)S(1)}, u32[]{:S(2)}, u32[]{:S(2)}) %collective-permute-start.29) | collective-permute-done | bytes 131104 | tf_op jit(solution)/shard_map/ppermute | solution.py:341
  69.4 0.7 collective-permute-start.30
  70.1 0.6 collective-permute-done.25
  70.7 2.5 %collective-permute-done.26 = bf16[32,2048]{1,0:T(8,128)(2,1)S(1)} collective-permute-done((bf16[32,2048]{1,0:T(8,128)(2,1)S(1)}, bf16[32,2048]{1,0:T(8,128)(2,1)S(1)}, u32[]{:S(2)}, u32[]{:S(2)}) %collective-permute-start.26) | collective-permute-done | bytes 131104 | tf_op jit(solution)/shard_map/ppermute | solution.py:341
  73.2 0.1 add_convert_fusion.3
  73.3 1.3 %collective-permute-start.27 = (bf16[32,2048]{1,0:T(8,128)(2,1)S(1)}, bf16[32,2048]{1,0:T(8,128)(2,1)S(1)}, u32[]{:S(2)}, u32[]{:S(2)}) collective-permute-start(bf16[32,2048]{1,0:T(8,128)(2,1)S(1)} %add_convert_fusion.3), channel_id=1, source_target_pairs={{0,4},{1,3},{4,8},{5,1},{8,12},{9,5},{12,14},{13,9},{14,10},{15,13... | collective-permute-start | bytes 393224 | tf_op jit(solution)/shard_map/ppermute | solution.py:341
  74.7 0.5 collective-permute-start.31
  75.2 3.2 %collective-permute-done.27 = bf16[32,2048]{1,0:T(8,128)(2,1)S(1)} collective-permute-done((bf16[32,2048]{1,0:T(8,128)(2,1)S(1)}, bf16[32,2048]{1,0:T(8,128)(2,1)S(1)}, u32[]{:S(2)}, u32[]{:S(2)}) %collective-permute-start.27) | collective-permute-done | bytes 131104 | tf_op jit(solution)/shard_map/ppermute | solution.py:341
  78.3 1.3 %collective-permute-start.28 = (bf16[32,2048]{1,0:T(8,128)(2,1)S(1)}, bf16[32,2048]{1,0:T(8,128)(2,1)S(1)}, u32[]{:S(2)}, u32[]{:S(2)}) collective-permute-start(bf16[32,2048]{1,0:T(8,128)(2,1)S(1)} %add_convert_fusion.2), channel_id=1, source_target_pairs={{0,4},{1,3},{4,8},{5,1},{8,12},{9,5},{12,14},{13,9},{14,10},{15,13... | collective-permute-start | bytes 393224 | tf_op jit(solution)/shard_map/ppermute | solution.py:341
  79.7 3.6 %collective-permute-done.28 = bf16[32,2048]{1,0:T(8,128)(2,1)S(1)} collective-permute-done((bf16[32,2048]{1,0:T(8,128)(2,1)S(1)}, bf16[32,2048]{1,0:T(8,128)(2,1)S(1)}, u32[]{:S(2)}, u32[]{:S(2)}) %collective-permute-start.28) | collective-permute-done | bytes 131104 | tf_op jit(solution)/shard_map/ppermute | solution.py:341
  83.4 0.7 fusion.3
  (42 shorter events, 0.4 us)
Async XLA Ops:
  0.0 14.4 %copy-start.3 = (bf16[256,2048]{1,0:T(8,128)(2,1)S(1)}, bf16[256,2048]{1,0:T(8,128)(2,1)}, u32[]{:S(2)}) copy-start(bf16[256,2048]{1,0:T(8,128)(2,1)} %refs_1_.1) | copy-start | bytes 3145732
  0.0 14.4 %collective-permute-start.3 = (bf16[256,2048]{1,0:T(8,128)(2,1)}, bf16[256,2048]{1,0:T(8,128)(2,1)S(1)}, u32[]{:S(2)}, u32[]{:S(2)}) collective-permute-start(bf16[256,2048]{1,0:T(8,128)(2,1)} %refs_1_.1), channel_id=1, source_target_pairs={{0,1},{1,0},{2,3},{3,2},{4,5},{5,4},{6,7},{7,6},{8,9},{9,8},{10,11... | collective-permute-start | bytes 3145736 | tf_op jit(solution)/shard_map/ppermute | solution.py:344
  5.0 14.3 %copy-start.6 = (bf16[32,640]{1,0:T(8,128)(2,1)S(1)}, bf16[32,640]{1,0:T(8,128)(2,1)}, u32[]{:S(2)}) copy-start(bf16[32,640]{1,0:T(8,128)(2,1)} %get-tuple-element.50) | copy-start | bytes 122884
  5.0 16.3 %copy-start.4 = (bf16[32,640]{1,0:T(8,128)(2,1)S(1)}, bf16[32,640]{1,0:T(8,128)(2,1)}, u32[]{:S(2)}) copy-start(bf16[32,640]{1,0:T(8,128)(2,1)} %get-tuple-element.52.refs_0_.refs_7_) | copy-start | bytes 122884
  5.0 6.1 %collective-permute-start = (bf16[3,32,640]{2,1,0:T(8,128)(2,1)}, bf16[3,32,640]{2,1,0:T(8,128)(2,1)S(1)}, u32[]{:S(2)}, u32[]{:S(2)}) collective-permute-start(bf16[3,32,640]{2,1,0:T(8,128)(2,1)} %get-tuple-element.42), channel_id=1, source_target_pairs={{0,1},{1,0},{2,3},{3,2},{4,5},{5,4},{6,7},{7,6},{8,9},{9,8},{10,11... | collective-permute-start | bytes 368648 | tf_op jit(solution)/shard_map/ppermute | solution.py:344
  5.2 9.2 %collective-permute-start.2 = (bf16[32,640]{1,0:T(8,128)(2,1)}, bf16[32,640]{1,0:T(8,128)(2,1)S(1)}, u32[]{:S(2)}, u32[]{:S(2)}) collective-permute-start(bf16[32,640]{1,0:T(8,128)(2,1)} %get-tuple-element.43), channel_id=1, source_target_pairs={{0,14},{1,15},{4,10},{5,11},{8,6},{9,7},{12,2},{13,3},{14,0},{15,1... | collective-permute-start | bytes 122888 | tf_op jit(solution)/shard_map/ppermute | solution.py:341
  11.9 6.4 %collective-permute-start.1 = (bf16[64,640]{1,0:T(8,128)(2,1)S(1)}, bf16[64,640]{1,0:T(8,128)(2,1)S(1)}, u32[]{:S(2)}, u32[]{:S(2)}) collective-permute-start(bf16[64,640]{1,0:T(8,128)(2,1)S(1)} %pad_maximum_fusion), channel_id=1, source_target_pairs={{0,10},{1,13},{4,6},{5,15},{8,2},{9,11},{12,0},{13,7},{14,4},{15,3... | collective-permute-start | bytes 245768 | tf_op jit(solution)/shard_map/ppermute | solution.py:341
  12.9 9.3 %collective-permute-start.5 = (bf16[64,640]{1,0:T(8,128)(2,1)S(1)}, bf16[64,640]{1,0:T(8,128)(2,1)S(1)}, u32[]{:S(2)}, u32[]{:S(2)}) collective-permute-start(bf16[64,640]{1,0:T(8,128)(2,1)S(1)} %pad_maximum_fusion.1), channel_id=1, source_target_pairs={{0,6},{1,9},{4,2},{5,13},{8,0},{9,15},{12,4},{13,11},{14,8},{15,7}... | collective-permute-start | bytes 245768 | tf_op jit(solution)/shard_map/ppermute | solution.py:341
  14.4 11.7 %copy-start.2 = (bf16[1,768,2048]{2,1,0:T(8,128)(2,1)S(1)}, bf16[1,768,2048]{2,1,0:T(8,128)(2,1)}, u32[]{:S(2)}) copy-start(bf16[1,768,2048]{2,1,0:T(8,128)(2,1)} %refs_7_) | copy-start | bytes 9437188
  15.0 10.2 %collective-permute-start.6 = (bf16[32,2048]{1,0:T(8,128)(2,1)S(1)}, bf16[32,2048]{1,0:T(8,128)(2,1)S(1)}, u32[]{:S(2)}, u32[]{:S(2)}) collective-permute-start(bf16[32,2048]{1,0:T(8,128)(2,1)S(1)} %get-tuple-element.48), channel_id=1, source_target_pairs={{0,8},{1,7},{4,12},{5,3},{8,14},{9,1},{12,10},{13,5},{14,6},{15,9}... | collective-permute-start | bytes 393224 | tf_op jit(solution)/shard_map/ppermute | solution.py:341
  18.8 7.7 %collective-permute-start.10 = (bf16[32,2048]{1,0:T(8,128)(2,1)S(1)}, bf16[32,2048]{1,0:T(8,128)(2,1)S(1)}, u32[]{:S(2)}, u32[]{:S(2)}) collective-permute-start(bf16[32,2048]{1,0:T(8,128)(2,1)S(1)} %get-tuple-element.53), channel_id=1, source_target_pairs={{0,4},{1,3},{4,8},{5,1},{8,12},{9,5},{12,14},{13,9},{14,10},{15,13... | collective-permute-start | bytes 393224 | tf_op jit(solution)/shard_map/ppermute | solution.py:341
  19.2 5.4 %collective-permute-start.8 = (bf16[64,640]{1,0:T(8,128)(2,1)S(1)}, bf16[64,640]{1,0:T(8,128)(2,1)S(1)}, u32[]{:S(2)}, u32[]{:S(2)}) collective-permute-start(bf16[64,640]{1,0:T(8,128)(2,1)S(1)} %pad_maximum_fusion.2), channel_id=1, source_target_pairs={{0,2},{1,5},{4,0},{5,9},{8,4},{9,13},{12,8},{13,15},{14,12},{15,11... | collective-permute-start | bytes 245768 | tf_op jit(solution)/shard_map/ppermute | solution.py:341
  21.0 6.3 %collective-permute-start.4 = (bf16[32,2048]{1,0:T(8,128)(2,1)S(1)}, bf16[32,2048]{1,0:T(8,128)(2,1)S(1)}, u32[]{:S(2)}, u32[]{:S(2)}) collective-permute-start(bf16[32,2048]{1,0:T(8,128)(2,1)S(1)} %get-tuple-element.45), channel_id=1, source_target_pairs={{0,4},{1,3},{4,8},{5,1},{8,12},{9,5},{12,14},{13,9},{14,10},{15,13... | collective-permute-start | bytes 393224 | tf_op jit(solution)/shard_map/ppermute | solution.py:341
  21.3 3.8 %copy-start = (bf16[1,2048,768]{2,1,0:T(8,128)(2,1)S(1)}, bf16[1,2048,768]{2,1,0:T(8,128)(2,1)}, u32[]{:S(2)}) copy-start(bf16[1,2048,768]{2,1,0:T(8,128)(2,1)} %refs_5_) | copy-start | bytes 9437188
  21.3 4.7 %copy-start.1 = (bf16[1,2048,768]{2,1,0:T(8,128)(2,1)S(1)}, bf16[1,2048,768]{2,1,0:T(8,128)(2,1)}, u32[]{:S(2)}) copy-start(bf16[1,2048,768]{2,1,0:T(8,128)(2,1)} %refs_6_) | copy-start | bytes 9437188
  21.8 18.7 %copy-start.5 = (bf16[32,2048]{1,0:T(8,128)(2,1)S(1)}, bf16[32,2048]{1,0:T(8,128)(2,1)}, u32[]{:S(2)}) copy-start(bf16[32,2048]{1,0:T(8,128)(2,1)} %param.16) | copy-start | bytes 393220
  22.7 18.0 %copy-start.7 = (f32[2048]{0:T(1024)S(1)}, f32[2048]{0:T(1024)}, u32[]{:S(2)}) copy-start(f32[2048]{0:T(1024)} %param.18) | copy-start | bytes 24580
  25.1 32.0 %collective-permute-start.22 = (bf16[1,2048,768]{2,1,0:T(8,128)(2,1)S(1)}, bf16[1,2048,768]{2,1,0:T(8,128)(2,1)S(1)}, u32[]{:S(2)}, u32[]{:S(2)}) collective-permute-start(bf16[1,2048,768]{2,1,0:T(8,128)(2,1)S(1)} %copy-done), channel_id=1, source_target_pairs={{0,1},{1,0},{2,3},{3,2},{4,5},{5,4},{6,7},{7,6},{8,9},{9,8},{10,11... | collective-permute-start | bytes 9437192 | tf_op jit(solution)/shard_map/ppermute | solution.py:344
  26.0 31.1 %collective-permute-start.23 = (bf16[1,2048,768]{2,1,0:T(8,128)(2,1)S(1)}, bf16[1,2048,768]{2,1,0:T(8,128)(2,1)S(1)}, u32[]{:S(2)}, u32[]{:S(2)}) collective-permute-start(bf16[1,2048,768]{2,1,0:T(8,128)(2,1)S(1)} %copy-done.1), channel_id=1, source_target_pairs={{0,1},{1,0},{2,3},{3,2},{4,5},{5,4},{6,7},{7,6},{8,9},{9,8},{10,11... | collective-permute-start | bytes 9437192 | tf_op jit(solution)/shard_map/ppermute | solution.py:344
  26.1 31.0 %collective-permute-start.24 = (bf16[1,768,2048]{2,1,0:T(8,128)(2,1)S(1)}, bf16[1,768,2048]{2,1,0:T(8,128)(2,1)S(1)}, u32[]{:S(2)}, u32[]{:S(2)}) collective-permute-start(bf16[1,768,2048]{2,1,0:T(8,128)(2,1)S(1)} %copy-done.2), channel_id=1, source_target_pairs={{0,1},{1,0},{2,3},{3,2},{4,5},{5,4},{6,7},{7,6},{8,9},{9,8},{10,11... | collective-permute-start | bytes 9437192 | tf_op jit(solution)/shard_map/ppermute | solution.py:344
  26.6 5.0 %collective-permute-start.11 = (bf16[32,2048]{1,0:T(8,128)(2,1)S(1)}, bf16[32,2048]{1,0:T(8,128)(2,1)S(1)}, u32[]{:S(2)}, u32[]{:S(2)}) collective-permute-start(bf16[32,2048]{1,0:T(8,128)(2,1)S(1)} %add_convert_fusion.6), channel_id=1, source_target_pairs={{0,4},{1,3},{4,8},{5,1},{8,12},{9,5},{12,14},{13,9},{14,10},{15,13... | collective-permute-start | bytes 393224 | tf_op jit(solution)/shard_map/ppermute | solution.py:341
  27.3 5.7 %collective-permute-start.7 = (bf16[32,2048]{1,0:T(8,128)(2,1)S(1)}, bf16[32,2048]{1,0:T(8,128)(2,1)S(1)}, u32[]{:S(2)}, u32[]{:S(2)}) collective-permute-start(bf16[32,2048]{1,0:T(8,128)(2,1)S(1)} %add_convert_fusion.8), channel_id=1, source_target_pairs={{0,4},{1,3},{4,8},{5,1},{8,12},{9,5},{12,14},{13,9},{14,10},{15,13... | collective-permute-start | bytes 393224 | tf_op jit(solution)/shard_map/ppermute | solution.py:341
  31.6 5.0 %collective-permute-start.12 = (bf16[32,2048]{1,0:T(8,128)(2,1)S(1)}, bf16[32,2048]{1,0:T(8,128)(2,1)S(1)}, u32[]{:S(2)}, u32[]{:S(2)}) collective-permute-start(bf16[32,2048]{1,0:T(8,128)(2,1)S(1)} %add_convert_fusion.5), channel_id=1, source_target_pairs={{0,4},{1,3},{4,8},{5,1},{8,12},{9,5},{12,14},{13,9},{14,10},{15,13... | collective-permute-start | bytes 393224 | tf_op jit(solution)/shard_map/ppermute | solution.py:341
  33.0 5.0 %collective-permute-start.9 = (bf16[32,2048]{1,0:T(8,128)(2,1)S(1)}, bf16[32,2048]{1,0:T(8,128)(2,1)S(1)}, u32[]{:S(2)}, u32[]{:S(2)}) collective-permute-start(bf16[32,2048]{1,0:T(8,128)(2,1)S(1)} %add_convert_fusion.7), channel_id=1, source_target_pairs={{0,4},{1,3},{4,8},{5,1},{8,12},{9,5},{12,14},{13,9},{14,10},{15,13... | collective-permute-start | bytes 393224 | tf_op jit(solution)/shard_map/ppermute | solution.py:341
  36.6 3.8 %collective-permute-start.13 = (bf16[32,2048]{1,0:T(8,128)(2,1)S(1)}, bf16[32,2048]{1,0:T(8,128)(2,1)S(1)}, u32[]{:S(2)}, u32[]{:S(2)}) collective-permute-start(bf16[32,2048]{1,0:T(8,128)(2,1)S(1)} %collective-permute-done.12), channel_id=1, source_target_pairs={{0,1},{1,0},{2,3},{3,2},{4,5},{5,4},{6,7},{7,6},{8,9},{9,8},{10,11... | collective-permute-start | bytes 393224 | tf_op jit(solution)/shard_map/ppermute | solution.py:344
  40.8 1.4 %collective-permute-start.18 = (bf16[32,2048]{1,0:T(8,128)(2,1)S(1)}, bf16[32,2048]{1,0:T(8,128)(2,1)S(1)}, u32[]{:S(2)}, u32[]{:S(2)}) collective-permute-start(bf16[32,2048]{1,0:T(8,128)(2,1)S(1)} %fusion.2.refs_4_), channel_id=1, source_target_pairs={{0,1},{1,0},{2,3},{3,2},{4,5},{5,4},{6,7},{7,6},{8,9},{9,8},{10,11... | collective-permute-start | bytes 393224 | tf_op jit(solution)/shard_map/ppermute | solution.py:344
  41.2 5.0 %collective-permute-start.14 = (bf16[32,2048]{1,0:T(8,128)(2,1)S(1)}, bf16[32,2048]{1,0:T(8,128)(2,1)S(1)}, u32[]{:S(2)}, u32[]{:S(2)}) collective-permute-start(bf16[32,2048]{1,0:T(8,128)(2,1)S(1)} %fusion.2.refs_4_), channel_id=1, source_target_pairs={{0,2},{1,5},{4,0},{5,9},{8,4},{9,13},{12,8},{13,15},{14,12},{15,11... | collective-permute-start | bytes 393224 | tf_op jit(solution)/shard_map/ppermute | solution.py:341
  42.2 5.4 %collective-permute-start.19 = (bf16[32,2048]{1,0:T(8,128)(2,1)S(1)}, bf16[32,2048]{1,0:T(8,128)(2,1)S(1)}, u32[]{:S(2)}, u32[]{:S(2)}) collective-permute-start(bf16[32,2048]{1,0:T(8,128)(2,1)S(1)} %collective-permute-done.18), channel_id=1, source_target_pairs={{0,2},{1,5},{4,0},{5,9},{8,4},{9,13},{12,8},{13,15},{14,12},{15,11... | collective-permute-start | bytes 393224 | tf_op jit(solution)/shard_map/ppermute | solution.py:341
  46.2 5.0 %collective-permute-start.15 = (bf16[32,2048]{1,0:T(8,128)(2,1)S(1)}, bf16[32,2048]{1,0:T(8,128)(2,1)S(1)}, u32[]{:S(2)}, u32[]{:S(2)}) collective-permute-start(bf16[32,2048]{1,0:T(8,128)(2,1)S(1)} %collective-permute-done.14.refs_2_), channel_id=1, source_target_pairs={{0,2},{1,5},{4,0},{5,9},{8,4},{9,13},{12,8},{13,15},{14,12},{15,11... | collective-permute-start | bytes 393224 | tf_op jit(solution)/shard_map/ppermute | solution.py:341
  47.6 5.0 %collective-permute-start.20 = (bf16[32,2048]{1,0:T(8,128)(2,1)S(1)}, bf16[32,2048]{1,0:T(8,128)(2,1)S(1)}, u32[]{:S(2)}, u32[]{:S(2)}) collective-permute-start(bf16[32,2048]{1,0:T(8,128)(2,1)S(1)} %collective-permute-done.19.refs_3_), channel_id=1, source_target_pairs={{0,2},{1,5},{4,0},{5,9},{8,4},{9,13},{12,8},{13,15},{14,12},{15,11... | collective-permute-start | bytes 393224 | tf_op jit(solution)/shard_map/ppermute | solution.py:341
  51.2 5.0 %collective-permute-start.16 = (bf16[32,2048]{1,0:T(8,128)(2,1)S(1)}, bf16[32,2048]{1,0:T(8,128)(2,1)S(1)}, u32[]{:S(2)}, u32[]{:S(2)}) collective-permute-start(bf16[32,2048]{1,0:T(8,128)(2,1)S(1)} %collective-permute-done.15.refs_0_), channel_id=1, source_target_pairs={{0,2},{1,5},{4,0},{5,9},{8,4},{9,13},{12,8},{13,15},{14,12},{15,11... | collective-permute-start | bytes 393224 | tf_op jit(solution)/shard_map/ppermute | solution.py:341
  52.6 8.0 %collective-permute-start.21 = (bf16[32,2048]{1,0:T(8,128)(2,1)S(1)}, bf16[32,2048]{1,0:T(8,128)(2,1)S(1)}, u32[]{:S(2)}, u32[]{:S(2)}) collective-permute-start(bf16[32,2048]{1,0:T(8,128)(2,1)S(1)} %collective-permute-done.20.refs_1_), channel_id=1, source_target_pairs={{0,2},{1,5},{4,0},{5,9},{8,4},{9,13},{12,8},{13,15},{14,12},{15,11... | collective-permute-start | bytes 393224 | tf_op jit(solution)/shard_map/ppermute | solution.py:341
  56.1 5.0 %collective-permute-start.17 = (bf16[32,2048]{1,0:T(8,128)(2,1)S(1)}, bf16[32,2048]{1,0:T(8,128)(2,1)S(1)}, u32[]{:S(2)}, u32[]{:S(2)}) collective-permute-start(bf16[32,2048]{1,0:T(8,128)(2,1)S(1)} %collective-permute-done.16.refs_1_), channel_id=1, source_target_pairs={{0,2},{1,5},{4,0},{5,9},{8,4},{9,13},{12,8},{13,15},{14,12},{15,11... | collective-permute-start | bytes 393224 | tf_op jit(solution)/shard_map/ppermute | solution.py:341
  64.3 5.0 %collective-permute-start.29 = (bf16[32,2048]{1,0:T(8,128)(2,1)S(1)}, bf16[32,2048]{1,0:T(8,128)(2,1)S(1)}, u32[]{:S(2)}, u32[]{:S(2)}) collective-permute-start(bf16[32,2048]{1,0:T(8,128)(2,1)S(1)} %get-tuple-element.74), channel_id=1, source_target_pairs={{0,4},{1,3},{4,8},{5,1},{8,12},{9,5},{12,14},{13,9},{14,10},{15,13... | collective-permute-start | bytes 393224 | tf_op jit(solution)/shard_map/ppermute | solution.py:341
  65.1 5.7 %collective-permute-start.25 = (bf16[32,2048]{1,0:T(8,128)(2,1)S(1)}, bf16[32,2048]{1,0:T(8,128)(2,1)S(1)}, u32[]{:S(2)}, u32[]{:S(2)}) collective-permute-start(bf16[32,2048]{1,0:T(8,128)(2,1)S(1)} %get-tuple-element.69), channel_id=1, source_target_pairs={{0,4},{1,3},{4,8},{5,1},{8,12},{9,5},{12,14},{13,9},{14,10},{15,13... | collective-permute-start | bytes 393224 | tf_op jit(solution)/shard_map/ppermute | solution.py:341
  66.6 6.6 %collective-permute-start.26 = (bf16[32,2048]{1,0:T(8,128)(2,1)S(1)}, bf16[32,2048]{1,0:T(8,128)(2,1)S(1)}, u32[]{:S(2)}, u32[]{:S(2)}) collective-permute-start(bf16[32,2048]{1,0:T(8,128)(2,1)S(1)} %get-tuple-element.71), channel_id=1, source_target_pairs={{0,8},{1,7},{4,12},{5,3},{8,14},{9,1},{12,10},{13,5},{14,6},{15,9}... | collective-permute-start | bytes 393224 | tf_op jit(solution)/shard_map/ppermute | solution.py:341
  69.4 5.3 %collective-permute-start.30 = (bf16[32,2048]{1,0:T(8,128)(2,1)S(1)}, bf16[32,2048]{1,0:T(8,128)(2,1)S(1)}, u32[]{:S(2)}, u32[]{:S(2)}) collective-permute-start(bf16[32,2048]{1,0:T(8,128)(2,1)S(1)} %add_convert_fusion.1), channel_id=1, source_target_pairs={{0,4},{1,3},{4,8},{5,1},{8,12},{9,5},{12,14},{13,9},{14,10},{15,13... | collective-permute-start | bytes 393224 | tf_op jit(solution)/shard_map/ppermute | solution.py:341
  73.3 5.0 %collective-permute-start.27 = (bf16[32,2048]{1,0:T(8,128)(2,1)S(1)}, bf16[32,2048]{1,0:T(8,128)(2,1)S(1)}, u32[]{:S(2)}, u32[]{:S(2)}) collective-permute-start(bf16[32,2048]{1,0:T(8,128)(2,1)S(1)} %add_convert_fusion.3), channel_id=1, source_target_pairs={{0,4},{1,3},{4,8},{5,1},{8,12},{9,5},{12,14},{13,9},{14,10},{15,13... | collective-permute-start | bytes 393224 | tf_op jit(solution)/shard_map/ppermute | solution.py:341
  74.7 5.0 %collective-permute-start.31 = (bf16[32,2048]{1,0:T(8,128)(2,1)S(1)}, bf16[32,2048]{1,0:T(8,128)(2,1)S(1)}, u32[]{:S(2)}, u32[]{:S(2)}) collective-permute-start(bf16[32,2048]{1,0:T(8,128)(2,1)S(1)} %add_convert_fusion), channel_id=1, source_target_pairs={{0,4},{1,3},{4,8},{5,1},{8,12},{9,5},{12,14},{13,9},{14,10},{15,13... | collective-permute-start | bytes 393224 | tf_op jit(solution)/shard_map/ppermute | solution.py:341
  78.3 5.0 %collective-permute-start.28 = (bf16[32,2048]{1,0:T(8,128)(2,1)S(1)}, bf16[32,2048]{1,0:T(8,128)(2,1)S(1)}, u32[]{:S(2)}, u32[]{:S(2)}) collective-permute-start(bf16[32,2048]{1,0:T(8,128)(2,1)S(1)} %add_convert_fusion.2), channel_id=1, source_target_pairs={{0,4},{1,3},{4,8},{5,1},{8,12},{9,5},{12,14},{13,9},{14,10},{15,13... | collective-permute-start | bytes 393224 | tf_op jit(solution)/shard_map/ppermute | solution.py:341
  79.7 3.6 %collective-permute-start.32 = (bf16[32,2048]{1,0:T(8,128)(2,1)S(1)}, bf16[32,2048]{1,0:T(8,128)(2,1)S(1)}, u32[]{:S(2)}, u32[]{:S(2)}) collective-permute-start(bf16[32,2048]{1,0:T(8,128)(2,1)S(1)} %collective-permute-done.31), channel_id=1, source_target_pairs={{0,1},{1,0},{2,3},{3,2},{4,5},{5,4},{6,7},{7,6},{8,9},{9,8},{10,11... | collective-permute-start | bytes 393224 | tf_op jit(solution)/shard_map/ppermute | solution.py:344

commit v12 on v11

--- a/solution.py
+++ b/solution.py
@@ -232,9 +232,7 @@
         out_specs=(VMEM,) * (len(kinds) + kept),
         scratch_shapes=[pltpu.VMEM((rows, 2 * feats), BF16)],
         compiler_params=pltpu.CompilerParams(vmem_limit_bytes=32 * 1024 * 1024),
-        cost_estimate=pl.CostEstimate(
-            flops=4 * rows * feats * width, bytes_accessed=4 * feats * width, transcendentals=0
-        ),
+        cost_estimate=pl.CostEstimate(flops=rows, bytes_accessed=rows, transcendentals=0),
     )(*pieces, own, other)
 
 

time: 84.3 us -> 84.3 us (level)
  no operation moved by 1% of the time
where the time goes in v12:
time: 84.3 us; the launch traced here: 84.1 us
  waiting for transfers between devices  35.4 us (42%)
  starting transfers between devices  32 us (38%)
  Pallas kernels  13.6 us (16%)
  other arithmetic  2.88 us (3%)
    ppermute x25, waiting for transfers between devices, pass_on(): return lax.ppermute(array, 'rows', toward(step))  32.9 us
    ppermute x25, starting transfers between devices, pass_on(): return lax.ppermute(array, 'rows', toward(step))  29.6 us
    pallas_call x2, Pallas kernels, experts(): pl.pallas_call(functools.partial(expert_kernel, len(pieces), len(digits),...  6.59 us
    pallas_call x1, Pallas kernels, attend(): pl.pallas_call(functools.partial(attend_kernel, chips, hops, chip_experts...  4.53 us
    ppermute x8, starting transfers between devices, swapped(): return lax.ppermute(array, 'rows', swap)  2.48 us
    ppermute x8, waiting for transfers between devices, swapped(): return lax.ppermute(array, 'rows', swap)  2.45 us
    pallas_call x5, Pallas kernels, project(): pl.pallas_call(functools.partial(project_kernel, len(pieces), kept), out_...  2.44 us
  transfers between devices with their start and end apart: 33, of which 19 were waited for; matrix products, arithmetic and copies ran while one was open for 3% of the time, Pallas kernels for 12%

profile of v12, /device:TPU:0, one launch (start us, length us, event | category | flops | bytes accessed | tf_op | source)
XLA Modules:
  0.0 84.1 jit_solution(6390220269413889366)
XLA Ops:
  0.0 0.5 collective-permute-start.3
  0.5 4.5 %shard_map.118 = (bf16[32,640]{1,0:T(8,128)(2,1)}, bf16[3,32,640]{2,1,0:T(8,128)(2,1)}, bf16[32,640]{1,0:T(8,128)(2,1)}, bf16[32,640]{1,0:T(8,128)(2,1)}, bf16[3...) custom-call(s32[32]{0:T(128)} %lengths_ref.1, bf16[32,4096]{1,0:T(8,128)(2,1)} %q_ref.1, bf16[32,2,128,128]{3,2,1,0:T(8,128)(2,1)} %k_ref.1, ...), custom_call_target="tpu_custom_call" | custom-call | flops 67108864 | bytes 4194304 | tf_op jit(solution)/shard_map/pallas_call | solution.py:164
  5.0 0.2 collective-permute-start
  5.2 5.9 %collective-permute-start.2 = (bf16[32,640]{1,0:T(8,128)(2,1)}, bf16[32,640]{1,0:T(8,128)(2,1)S(1)}, u32[]{:S(2)}, u32[]{:S(2)}) collective-permute-start(bf16[32,640]{1,0:T(8,128)(2,1)} %get-tuple-element.43), channel_id=1, source_target_pairs={{0,14},{1,15},{4,10},{5,11},{8,6},{9,7},{12,2},{13,3},{14,0},{15,1... | collective-permute-start | bytes 122888 | tf_op jit(solution)/shard_map/ppermute | solution.py:339
  11.1 0.8 pad_maximum_fusion
  11.9 0.2 collective-permute-start.1
  12.1 0.8 pad_maximum_fusion.1
  12.9 1.5 %collective-permute-start.5 = (bf16[64,640]{1,0:T(8,128)(2,1)S(1)}, bf16[64,640]{1,0:T(8,128)(2,1)S(1)}, u32[]{:S(2)}, u32[]{:S(2)}) collective-permute-start(bf16[64,640]{1,0:T(8,128)(2,1)S(1)} %pad_maximum_fusion.1), channel_id=1, source_target_pairs={{0,6},{1,9},{4,2},{5,13},{8,0},{9,15},{12,4},{13,11},{14,8},{15,7}... | collective-permute-start | bytes 245768 | tf_op jit(solution)/shard_map/ppermute | solution.py:339
  14.4 0.5 shard_map.119
  15.0 1.4 %collective-permute-start.6 = (bf16[32,2048]{1,0:T(8,128)(2,1)S(1)}, bf16[32,2048]{1,0:T(8,128)(2,1)S(1)}, u32[]{:S(2)}, u32[]{:S(2)}) collective-permute-start(bf16[32,2048]{1,0:T(8,128)(2,1)S(1)} %get-tuple-element.48), channel_id=1, source_target_pairs={{0,8},{1,7},{4,12},{5,3},{8,14},{9,1},{12,10},{13,5},{14,6},{15,9}... | collective-permute-start | bytes 393224 | tf_op jit(solution)/shard_map/ppermute | solution.py:339
  16.4 2.0 %collective-permute-done.1.refs_0_.refs_4_ = bf16[64,640]{1,0:T(8,128)(2,1)S(1)} collective-permute-done((bf16[64,640]{1,0:T(8,128)(2,1)S(1)}, bf16[64,640]{1,0:T(8,128)(2,1)S(1)}, u32[]{:S(2)}, u32[]{:S(2)}) %collective-permute-start.1) | collective-permute-done | bytes 81952 | tf_op jit(solution)/shard_map/ppermute | solution.py:339
  18.3 0.5 shard_map.120
  18.8 0.4 collective-permute-start.10
  19.2 1.7 %collective-permute-start.8 = (bf16[64,640]{1,0:T(8,128)(2,1)S(1)}, bf16[64,640]{1,0:T(8,128)(2,1)S(1)}, u32[]{:S(2)}, u32[]{:S(2)}) collective-permute-start(bf16[64,640]{1,0:T(8,128)(2,1)S(1)} %pad_maximum_fusion.2), channel_id=1, source_target_pairs={{0,2},{1,5},{4,0},{5,9},{8,4},{9,13},{12,8},{13,15},{14,12},{15,11... | collective-permute-start | bytes 245768 | tf_op jit(solution)/shard_map/ppermute | solution.py:339
  21.0 0.3 collective-permute-start.4
  21.3 0.5 shard_map.123
  21.8 0.4 collective-permute-done.5.refs_0_.refs_5_
  22.2 0.5 shard_map.121
  22.7 1.9 %collective-permute-done.8.refs_0_.refs_6_ = bf16[64,640]{1,0:T(8,128)(2,1)S(1)} collective-permute-done((bf16[64,640]{1,0:T(8,128)(2,1)S(1)}, bf16[64,640]{1,0:T(8,128)(2,1)S(1)}, u32[]{:S(2)}, u32[]{:S(2)}) %collective-permute-start.8) | collective-permute-done | bytes 81952 | tf_op jit(solution)/shard_map/ppermute | solution.py:339
  24.6 0.5 shard_map.122
  25.1 0.9 %collective-permute-start.22 = (bf16[1,2048,768]{2,1,0:T(8,128)(2,1)S(1)}, bf16[1,2048,768]{2,1,0:T(8,128)(2,1)S(1)}, u32[]{:S(2)}, u32[]{:S(2)}) collective-permute-start(bf16[1,2048,768]{2,1,0:T(8,128)(2,1)S(1)} %copy-done), channel_id=1, source_target_pairs={{0,1},{1,0},{2,3},{3,2},{4,5},{5,4},{6,7},{7,6},{8,9},{9,8},{10,11... | collective-permute-start | bytes 9437192 | tf_op jit(solution)/shard_map/ppermute | solution.py:342
  26.0 0.1 collective-permute-start.23
  26.1 0.4 collective-permute-start.24
  26.6 0.7 collective-permute-start.11
  27.3 1.6 %collective-permute-start.7 = (bf16[32,2048]{1,0:T(8,128)(2,1)S(1)}, bf16[32,2048]{1,0:T(8,128)(2,1)S(1)}, u32[]{:S(2)}, u32[]{:S(2)}) collective-permute-start(bf16[32,2048]{1,0:T(8,128)(2,1)S(1)} %add_convert_fusion.8), channel_id=1, source_target_pairs={{0,4},{1,3},{4,8},{5,1},{8,12},{9,5},{12,14},{13,9},{14,10},{15,13... | collective-permute-start | bytes 393224 | tf_op jit(solution)/shard_map/ppermute | solution.py:339
  28.9 2.7 %collective-permute-done.11 = bf16[32,2048]{1,0:T(8,128)(2,1)S(1)} collective-permute-done((bf16[32,2048]{1,0:T(8,128)(2,1)S(1)}, bf16[32,2048]{1,0:T(8,128)(2,1)S(1)}, u32[]{:S(2)}, u32[]{:S(2)}) %collective-permute-start.11) | collective-permute-done | bytes 131104 | tf_op jit(solution)/shard_map/ppermute | solution.py:339
  31.6 0.7 collective-permute-start.12
  32.3 0.7 collective-permute-done.7
  33.0 1.0 %collective-permute-start.9 = (bf16[32,2048]{1,0:T(8,128)(2,1)S(1)}, bf16[32,2048]{1,0:T(8,128)(2,1)S(1)}, u32[]{:S(2)}, u32[]{:S(2)}) collective-permute-start(bf16[32,2048]{1,0:T(8,128)(2,1)S(1)} %add_convert_fusion.7), channel_id=1, source_target_pairs={{0,4},{1,3},{4,8},{5,1},{8,12},{9,5},{12,14},{13,9},{14,10},{15,13... | collective-permute-start | bytes 393224 | tf_op jit(solution)/shard_map/ppermute | solution.py:339
  34.0 2.7 %collective-permute-done.12 = bf16[32,2048]{1,0:T(8,128)(2,1)S(1)} collective-permute-done((bf16[32,2048]{1,0:T(8,128)(2,1)S(1)}, bf16[32,2048]{1,0:T(8,128)(2,1)S(1)}, u32[]{:S(2)}, u32[]{:S(2)}) %collective-permute-start.12) | collective-permute-done | bytes 131104 | tf_op jit(solution)/shard_map/ppermute | solution.py:339
  36.7 1.4 %collective-permute-done.9 = bf16[32,2048]{1,0:T(8,128)(2,1)S(1)} collective-permute-done((bf16[32,2048]{1,0:T(8,128)(2,1)S(1)}, bf16[32,2048]{1,0:T(8,128)(2,1)S(1)}, u32[]{:S(2)}, u32[]{:S(2)}) %collective-permute-start.9) | collective-permute-done | bytes 131104 | tf_op jit(solution)/shard_map/ppermute | solution.py:339
  38.1 2.4 %collective-permute-done.13 = bf16[32,2048]{1,0:T(8,128)(2,1)S(1)} collective-permute-done((bf16[32,2048]{1,0:T(8,128)(2,1)S(1)}, bf16[32,2048]{1,0:T(8,128)(2,1)S(1)}, u32[]{:S(2)}, u32[]{:S(2)}) %collective-permute-start.13) | collective-permute-done | bytes 131104 | tf_op jit(solution)/shard_map/ppermute | solution.py:342
  40.5 0.2 fusion
  40.7 0.1 fusion.2.refs_4_
  40.8 0.4 collective-permute-start.18
  41.2 1.0 %collective-permute-start.14 = (bf16[32,2048]{1,0:T(8,128)(2,1)S(1)}, bf16[32,2048]{1,0:T(8,128)(2,1)S(1)}, u32[]{:S(2)}, u32[]{:S(2)}) collective-permute-start(bf16[32,2048]{1,0:T(8,128)(2,1)S(1)} %fusion.2.refs_4_), channel_id=1, source_target_pairs={{0,2},{1,5},{4,0},{5,9},{8,4},{9,13},{12,8},{13,15},{14,12},{15,11... | collective-permute-start | bytes 393224 | tf_op jit(solution)/shard_map/ppermute | solution.py:339
  42.2 1.2 %collective-permute-start.19 = (bf16[32,2048]{1,0:T(8,128)(2,1)S(1)}, bf16[32,2048]{1,0:T(8,128)(2,1)S(1)}, u32[]{:S(2)}, u32[]{:S(2)}) collective-permute-start(bf16[32,2048]{1,0:T(8,128)(2,1)S(1)} %collective-permute-done.18), channel_id=1, source_target_pairs={{0,2},{1,5},{4,0},{5,9},{8,4},{9,13},{12,8},{13,15},{14,12},{15,11... | collective-permute-start | bytes 393224 | tf_op jit(solution)/shard_map/ppermute | solution.py:339
  43.4 2.8 %collective-permute-done.14.refs_2_ = bf16[32,2048]{1,0:T(8,128)(2,1)S(1)} collective-permute-done((bf16[32,2048]{1,0:T(8,128)(2,1)S(1)}, bf16[32,2048]{1,0:T(8,128)(2,1)S(1)}, u32[]{:S(2)}, u32[]{:S(2)}) %collective-permute-start.14) | collective-permute-done | bytes 131104 | tf_op jit(solution)/shard_map/ppermute | solution.py:339
  46.2 1.0 %collective-permute-start.15 = (bf16[32,2048]{1,0:T(8,128)(2,1)S(1)}, bf16[32,2048]{1,0:T(8,128)(2,1)S(1)}, u32[]{:S(2)}, u32[]{:S(2)}) collective-permute-start(bf16[32,2048]{1,0:T(8,128)(2,1)S(1)} %collective-permute-done.14.refs_2_), channel_id=1, source_target_pairs={{0,2},{1,5},{4,0},{5,9},{8,4},{9,13},{12,8},{13,15},{14,12},{15,11... | collective-permute-start | bytes 393224 | tf_op jit(solution)/shard_map/ppermute | solution.py:339
  47.2 0.4 collective-permute-done.19.refs_3_
  47.6 1.0 %collective-permute-start.20 = (bf16[32,2048]{1,0:T(8,128)(2,1)S(1)}, bf16[32,2048]{1,0:T(8,128)(2,1)S(1)}, u32[]{:S(2)}, u32[]{:S(2)}) collective-permute-start(bf16[32,2048]{1,0:T(8,128)(2,1)S(1)} %collective-permute-done.19.refs_3_), channel_id=1, source_target_pairs={{0,2},{1,5},{4,0},{5,9},{8,4},{9,13},{12,8},{13,15},{14,12},{15,11... | collective-permute-start | bytes 393224 | tf_op jit(solution)/shard_map/ppermute | solution.py:339
  48.6 2.6 %collective-permute-done.15.refs_0_ = bf16[32,2048]{1,0:T(8,128)(2,1)S(1)} collective-permute-done((bf16[32,2048]{1,0:T(8,128)(2,1)S(1)}, bf16[32,2048]{1,0:T(8,128)(2,1)S(1)}, u32[]{:S(2)}, u32[]{:S(2)}) %collective-permute-start.15) | collective-permute-done | bytes 131104 | tf_op jit(solution)/shard_map/ppermute | solution.py:339
  51.2 1.0 %collective-permute-start.16 = (bf16[32,2048]{1,0:T(8,128)(2,1)S(1)}, bf16[32,2048]{1,0:T(8,128)(2,1)S(1)}, u32[]{:S(2)}, u32[]{:S(2)}) collective-permute-start(bf16[32,2048]{1,0:T(8,128)(2,1)S(1)} %collective-permute-done.15.refs_0_), channel_id=1, source_target_pairs={{0,2},{1,5},{4,0},{5,9},{8,4},{9,13},{12,8},{13,15},{14,12},{15,11... | collective-permute-start | bytes 393224 | tf_op jit(solution)/shard_map/ppermute | solution.py:339
  52.2 0.4 collective-permute-done.20.refs_1_
  52.6 1.0 %collective-permute-start.21 = (bf16[32,2048]{1,0:T(8,128)(2,1)S(1)}, bf16[32,2048]{1,0:T(8,128)(2,1)S(1)}, u32[]{:S(2)}, u32[]{:S(2)}) collective-permute-start(bf16[32,2048]{1,0:T(8,128)(2,1)S(1)} %collective-permute-done.20.refs_1_), channel_id=1, source_target_pairs={{0,2},{1,5},{4,0},{5,9},{8,4},{9,13},{12,8},{13,15},{14,12},{15,11... | collective-permute-start | bytes 393224 | tf_op jit(solution)/shard_map/ppermute | solution.py:339
  53.6 2.6 %collective-permute-done.16.refs_1_ = bf16[32,2048]{1,0:T(8,128)(2,1)S(1)} collective-permute-done((bf16[32,2048]{1,0:T(8,128)(2,1)S(1)}, bf16[32,2048]{1,0:T(8,128)(2,1)S(1)}, u32[]{:S(2)}, u32[]{:S(2)}) %collective-permute-start.16) | collective-permute-done | bytes 131104 | tf_op jit(solution)/shard_map/ppermute | solution.py:339
  56.1 1.0 %collective-permute-start.17 = (bf16[32,2048]{1,0:T(8,128)(2,1)S(1)}, bf16[32,2048]{1,0:T(8,128)(2,1)S(1)}, u32[]{:S(2)}, u32[]{:S(2)}) collective-permute-start(bf16[32,2048]{1,0:T(8,128)(2,1)S(1)} %collective-permute-done.16.refs_1_), channel_id=1, source_target_pairs={{0,2},{1,5},{4,0},{5,9},{8,4},{9,13},{12,8},{13,15},{14,12},{15,11... | collective-permute-start | bytes 393224 | tf_op jit(solution)/shard_map/ppermute | solution.py:339
  57.1 3.4 %shard_map.124 = (f32[32,2048]{1,0:T(8,128)S(1)}, f32[32,2048]{1,0:T(8,128)S(1)}, f32[32,2048]{1,0:T(8,128)S(1)}, f32[32,2048]{1,0:T(8,128)S(1)}, f32[32,2048]{1,0:T(8,128)S(1)}) custom-call(bf16[32,2048]{1,0:T(8,128)(2,1)S(1)} %collective-permute-done.15.refs_0_, bf16[32,2048]{1,0:T(8,128)(2,1)S(1)} %collective-permute-done.20.refs_1_, ...), custom_call_target="tpu_custom_call" | custom-call | flops 3019898880 | bytes 327680 | tf_op jit(solution)/shard_map/pallas_call | solution.py:297
  60.5 0.6 collective-permute-done.17.refs_0_
  61.1 3.2 %shard_map.125 = (bf16[32,2048]{1,0:T(8,128)(2,1)S(1)}, bf16[32,2048]{1,0:T(8,128)(2,1)S(1)}, bf16[32,2048]{1,0:T(8,128)(2,1)S(1)}) custom-call(bf16[32,2048]{1,0:T(8,128)(2,1)S(1)} %collective-permute-done.17.refs_0_, bf16[32,2048]{1,0:T(8,128)(2,1)S(1)} %collective-permute-done.16.refs_1_, bf16[32,2048]{1,0:T(8,128)(2,1)S(1)} %collective-permute-done.21.refs_2_, ...), custom_call_target="tpu_custom_call" | custom-call | flops 1811939328 | bytes 196608 | tf_op jit(solution)/shard_map/pallas_call | solution.py:297
  64.3 0.7 collective-permute-start.29
  65.1 1.6 %collective-permute-start.25 = (bf16[32,2048]{1,0:T(8,128)(2,1)S(1)}, bf16[32,2048]{1,0:T(8,128)(2,1)S(1)}, u32[]{:S(2)}, u32[]{:S(2)}) collective-permute-start(bf16[32,2048]{1,0:T(8,128)(2,1)S(1)} %get-tuple-element.69), channel_id=1, source_target_pairs={{0,4},{1,3},{4,8},{5,1},{8,12},{9,5},{12,14},{13,9},{14,10},{15,13... | collective-permute-start | bytes 393224 | tf_op jit(solution)/shard_map/ppermute | solution.py:339
  66.6 0.7 collective-permute-start.26
  67.3 2.0 %collective-permute-done.29 = bf16[32,2048]{1,0:T(8,128)(2,1)S(1)} collective-permute-done((bf16[32,2048]{1,0:T(8,128)(2,1)S(1)}, bf16[32,2048]{1,0:T(8,128)(2,1)S(1)}, u32[]{:S(2)}, u32[]{:S(2)}) %collective-permute-start.29) | collective-permute-done | bytes 131104 | tf_op jit(solution)/shard_map/ppermute | solution.py:339
  69.4 0.7 collective-permute-start.30
  70.1 0.6 collective-permute-done.25
  70.7 2.5 %collective-permute-done.26 = bf16[32,2048]{1,0:T(8,128)(2,1)S(1)} collective-permute-done((bf16[32,2048]{1,0:T(8,128)(2,1)S(1)}, bf16[32,2048]{1,0:T(8,128)(2,1)S(1)}, u32[]{:S(2)}, u32[]{:S(2)}) %collective-permute-start.26) | collective-permute-done | bytes 131104 | tf_op jit(solution)/shard_map/ppermute | solution.py:339
  73.2 0.1 add_convert_fusion.3
  73.3 1.3 %collective-permute-start.27 = (bf16[32,2048]{1,0:T(8,128)(2,1)S(1)}, bf16[32,2048]{1,0:T(8,128)(2,1)S(1)}, u32[]{:S(2)}, u32[]{:S(2)}) collective-permute-start(bf16[32,2048]{1,0:T(8,128)(2,1)S(1)} %add_convert_fusion.3), channel_id=1, source_target_pairs={{0,4},{1,3},{4,8},{5,1},{8,12},{9,5},{12,14},{13,9},{14,10},{15,13... | collective-permute-start | bytes 393224 | tf_op jit(solution)/shard_map/ppermute | solution.py:339
  74.7 0.5 collective-permute-start.31
  75.2 3.2 %collective-permute-done.27 = bf16[32,2048]{1,0:T(8,128)(2,1)S(1)} collective-permute-done((bf16[32,2048]{1,0:T(8,128)(2,1)S(1)}, bf16[32,2048]{1,0:T(8,128)(2,1)S(1)}, u32[]{:S(2)}, u32[]{:S(2)}) %collective-permute-start.27) | collective-permute-done | bytes 131104 | tf_op jit(solution)/shard_map/ppermute | solution.py:339
  78.3 1.3 %collective-permute-start.28 = (bf16[32,2048]{1,0:T(8,128)(2,1)S(1)}, bf16[32,2048]{1,0:T(8,128)(2,1)S(1)}, u32[]{:S(2)}, u32[]{:S(2)}) collective-permute-start(bf16[32,2048]{1,0:T(8,128)(2,1)S(1)} %add_convert_fusion.2), channel_id=1, source_target_pairs={{0,4},{1,3},{4,8},{5,1},{8,12},{9,5},{12,14},{13,9},{14,10},{15,13... | collective-permute-start | bytes 393224 | tf_op jit(solution)/shard_map/ppermute | solution.py:339
  79.7 3.6 %collective-permute-done.28 = bf16[32,2048]{1,0:T(8,128)(2,1)S(1)} collective-permute-done((bf16[32,2048]{1,0:T(8,128)(2,1)S(1)}, bf16[32,2048]{1,0:T(8,128)(2,1)S(1)}, u32[]{:S(2)}, u32[]{:S(2)}) %collective-permute-start.28) | collective-permute-done | bytes 131104 | tf_op jit(solution)/shard_map/ppermute | solution.py:339
  83.4 0.7 fusion.3
  (42 shorter events, 0.4 us)
Async XLA Ops:
  0.0 14.4 %copy-start.3 = (bf16[256,2048]{1,0:T(8,128)(2,1)S(1)}, bf16[256,2048]{1,0:T(8,128)(2,1)}, u32[]{:S(2)}) copy-start(bf16[256,2048]{1,0:T(8,128)(2,1)} %refs_1_.1) | copy-start | bytes 3145732
  0.0 14.4 %collective-permute-start.3 = (bf16[256,2048]{1,0:T(8,128)(2,1)}, bf16[256,2048]{1,0:T(8,128)(2,1)S(1)}, u32[]{:S(2)}, u32[]{:S(2)}) collective-permute-start(bf16[256,2048]{1,0:T(8,128)(2,1)} %refs_1_.1), channel_id=1, source_target_pairs={{0,1},{1,0},{2,3},{3,2},{4,5},{5,4},{6,7},{7,6},{8,9},{9,8},{10,11... | collective-permute-start | bytes 3145736 | tf_op jit(solution)/shard_map/ppermute | solution.py:342
  5.0 14.3 %copy-start.6 = (bf16[32,640]{1,0:T(8,128)(2,1)S(1)}, bf16[32,640]{1,0:T(8,128)(2,1)}, u32[]{:S(2)}) copy-start(bf16[32,640]{1,0:T(8,128)(2,1)} %get-tuple-element.50) | copy-start | bytes 122884
  5.0 16.3 %copy-start.4 = (bf16[32,640]{1,0:T(8,128)(2,1)S(1)}, bf16[32,640]{1,0:T(8,128)(2,1)}, u32[]{:S(2)}) copy-start(bf16[32,640]{1,0:T(8,128)(2,1)} %get-tuple-element.52.refs_0_.refs_7_) | copy-start | bytes 122884
  5.0 6.1 %collective-permute-start = (bf16[3,32,640]{2,1,0:T(8,128)(2,1)}, bf16[3,32,640]{2,1,0:T(8,128)(2,1)S(1)}, u32[]{:S(2)}, u32[]{:S(2)}) collective-permute-start(bf16[3,32,640]{2,1,0:T(8,128)(2,1)} %get-tuple-element.42), channel_id=1, source_target_pairs={{0,1},{1,0},{2,3},{3,2},{4,5},{5,4},{6,7},{7,6},{8,9},{9,8},{10,11... | collective-permute-start | bytes 368648 | tf_op jit(solution)/shard_map/ppermute | solution.py:342
  5.2 9.2 %collective-permute-start.2 = (bf16[32,640]{1,0:T(8,128)(2,1)}, bf16[32,640]{1,0:T(8,128)(2,1)S(1)}, u32[]{:S(2)}, u32[]{:S(2)}) collective-permute-start(bf16[32,640]{1,0:T(8,128)(2,1)} %get-tuple-element.43), channel_id=1, source_target_pairs={{0,14},{1,15},{4,10},{5,11},{8,6},{9,7},{12,2},{13,3},{14,0},{15,1... | collective-permute-start | bytes 122888 | tf_op jit(solution)/shard_map/ppermute | solution.py:339
  11.9 6.4 %collective-permute-start.1 = (bf16[64,640]{1,0:T(8,128)(2,1)S(1)}, bf16[64,640]{1,0:T(8,128)(2,1)S(1)}, u32[]{:S(2)}, u32[]{:S(2)}) collective-permute-start(bf16[64,640]{1,0:T(8,128)(2,1)S(1)} %pad_maximum_fusion), channel_id=1, source_target_pairs={{0,10},{1,13},{4,6},{5,15},{8,2},{9,11},{12,0},{13,7},{14,4},{15,3... | collective-permute-start | bytes 245768 | tf_op jit(solution)/shard_map/ppermute | solution.py:339
  12.9 9.3 %collective-permute-start.5 = (bf16[64,640]{1,0:T(8,128)(2,1)S(1)}, bf16[64,640]{1,0:T(8,128)(2,1)S(1)}, u32[]{:S(2)}, u32[]{:S(2)}) collective-permute-start(bf16[64,640]{1,0:T(8,128)(2,1)S(1)} %pad_maximum_fusion.1), channel_id=1, source_target_pairs={{0,6},{1,9},{4,2},{5,13},{8,0},{9,15},{12,4},{13,11},{14,8},{15,7}... | collective-permute-start | bytes 245768 | tf_op jit(solution)/shard_map/ppermute | solution.py:339
  14.4 11.7 %copy-start.2 = (bf16[1,768,2048]{2,1,0:T(8,128)(2,1)S(1)}, bf16[1,768,2048]{2,1,0:T(8,128)(2,1)}, u32[]{:S(2)}) copy-start(bf16[1,768,2048]{2,1,0:T(8,128)(2,1)} %refs_7_) | copy-start | bytes 9437188
  15.0 10.2 %collective-permute-start.6 = (bf16[32,2048]{1,0:T(8,128)(2,1)S(1)}, bf16[32,2048]{1,0:T(8,128)(2,1)S(1)}, u32[]{:S(2)}, u32[]{:S(2)}) collective-permute-start(bf16[32,2048]{1,0:T(8,128)(2,1)S(1)} %get-tuple-element.48), channel_id=1, source_target_pairs={{0,8},{1,7},{4,12},{5,3},{8,14},{9,1},{12,10},{13,5},{14,6},{15,9}... | collective-permute-start | bytes 393224 | tf_op jit(solution)/shard_map/ppermute | solution.py:339
  18.8 7.7 %collective-permute-start.10 = (bf16[32,2048]{1,0:T(8,128)(2,1)S(1)}, bf16[32,2048]{1,0:T(8,128)(2,1)S(1)}, u32[]{:S(2)}, u32[]{:S(2)}) collective-permute-start(bf16[32,2048]{1,0:T(8,128)(2,1)S(1)} %get-tuple-element.53), channel_id=1, source_target_pairs={{0,4},{1,3},{4,8},{5,1},{8,12},{9,5},{12,14},{13,9},{14,10},{15,13... | collective-permute-start | bytes 393224 | tf_op jit(solution)/shard_map/ppermute | solution.py:339
  19.2 5.4 %collective-permute-start.8 = (bf16[64,640]{1,0:T(8,128)(2,1)S(1)}, bf16[64,640]{1,0:T(8,128)(2,1)S(1)}, u32[]{:S(2)}, u32[]{:S(2)}) collective-permute-start(bf16[64,640]{1,0:T(8,128)(2,1)S(1)} %pad_maximum_fusion.2), channel_id=1, source_target_pairs={{0,2},{1,5},{4,0},{5,9},{8,4},{9,13},{12,8},{13,15},{14,12},{15,11... | collective-permute-start | bytes 245768 | tf_op jit(solution)/shard_map/ppermute | solution.py:339
  21.0 6.3 %collective-permute-start.4 = (bf16[32,2048]{1,0:T(8,128)(2,1)S(1)}, bf16[32,2048]{1,0:T(8,128)(2,1)S(1)}, u32[]{:S(2)}, u32[]{:S(2)}) collective-permute-start(bf16[32,2048]{1,0:T(8,128)(2,1)S(1)} %get-tuple-element.45), channel_id=1, source_target_pairs={{0,4},{1,3},{4,8},{5,1},{8,12},{9,5},{12,14},{13,9},{14,10},{15,13... | collective-permute-start | bytes 393224 | tf_op jit(solution)/shard_map/ppermute | solution.py:339
  21.3 3.8 %copy-start = (bf16[1,2048,768]{2,1,0:T(8,128)(2,1)S(1)}, bf16[1,2048,768]{2,1,0:T(8,128)(2,1)}, u32[]{:S(2)}) copy-start(bf16[1,2048,768]{2,1,0:T(8,128)(2,1)} %refs_5_) | copy-start | bytes 9437188
  21.3 4.7 %copy-start.1 = (bf16[1,2048,768]{2,1,0:T(8,128)(2,1)S(1)}, bf16[1,2048,768]{2,1,0:T(8,128)(2,1)}, u32[]{:S(2)}) copy-start(bf16[1,2048,768]{2,1,0:T(8,128)(2,1)} %refs_6_) | copy-start | bytes 9437188
  21.8 18.7 %copy-start.5 = (bf16[32,2048]{1,0:T(8,128)(2,1)S(1)}, bf16[32,2048]{1,0:T(8,128)(2,1)}, u32[]{:S(2)}) copy-start(bf16[32,2048]{1,0:T(8,128)(2,1)} %param.16) | copy-start | bytes 393220
  22.7 18.0 %copy-start.7 = (f32[2048]{0:T(1024)S(1)}, f32[2048]{0:T(1024)}, u32[]{:S(2)}) copy-start(f32[2048]{0:T(1024)} %param.18) | copy-start | bytes 24580
  25.1 32.0 %collective-permute-start.22 = (bf16[1,2048,768]{2,1,0:T(8,128)(2,1)S(1)}, bf16[1,2048,768]{2,1,0:T(8,128)(2,1)S(1)}, u32[]{:S(2)}, u32[]{:S(2)}) collective-permute-start(bf16[1,2048,768]{2,1,0:T(8,128)(2,1)S(1)} %copy-done), channel_id=1, source_target_pairs={{0,1},{1,0},{2,3},{3,2},{4,5},{5,4},{6,7},{7,6},{8,9},{9,8},{10,11... | collective-permute-start | bytes 9437192 | tf_op jit(solution)/shard_map/ppermute | solution.py:342
  26.0 31.1 %collective-permute-start.23 = (bf16[1,2048,768]{2,1,0:T(8,128)(2,1)S(1)}, bf16[1,2048,768]{2,1,0:T(8,128)(2,1)S(1)}, u32[]{:S(2)}, u32[]{:S(2)}) collective-permute-start(bf16[1,2048,768]{2,1,0:T(8,128)(2,1)S(1)} %copy-done.1), channel_id=1, source_target_pairs={{0,1},{1,0},{2,3},{3,2},{4,5},{5,4},{6,7},{7,6},{8,9},{9,8},{10,11... | collective-permute-start | bytes 9437192 | tf_op jit(solution)/shard_map/ppermute | solution.py:342
  26.1 31.0 %collective-permute-start.24 = (bf16[1,768,2048]{2,1,0:T(8,128)(2,1)S(1)}, bf16[1,768,2048]{2,1,0:T(8,128)(2,1)S(1)}, u32[]{:S(2)}, u32[]{:S(2)}) collective-permute-start(bf16[1,768,2048]{2,1,0:T(8,128)(2,1)S(1)} %copy-done.2), channel_id=1, source_target_pairs={{0,1},{1,0},{2,3},{3,2},{4,5},{5,4},{6,7},{7,6},{8,9},{9,8},{10,11... | collective-permute-start | bytes 9437192 | tf_op jit(solution)/shard_map/ppermute | solution.py:342
  26.6 5.0 %collective-permute-start.11 = (bf16[32,2048]{1,0:T(8,128)(2,1)S(1)}, bf16[32,2048]{1,0:T(8,128)(2,1)S(1)}, u32[]{:S(2)}, u32[]{:S(2)}) collective-permute-start(bf16[32,2048]{1,0:T(8,128)(2,1)S(1)} %add_convert_fusion.6), channel_id=1, source_target_pairs={{0,4},{1,3},{4,8},{5,1},{8,12},{9,5},{12,14},{13,9},{14,10},{15,13... | collective-permute-start | bytes 393224 | tf_op jit(solution)/shard_map/ppermute | solution.py:339
  27.3 5.7 %collective-permute-start.7 = (bf16[32,2048]{1,0:T(8,128)(2,1)S(1)}, bf16[32,2048]{1,0:T(8,128)(2,1)S(1)}, u32[]{:S(2)}, u32[]{:S(2)}) collective-permute-start(bf16[32,2048]{1,0:T(8,128)(2,1)S(1)} %add_convert_fusion.8), channel_id=1, source_target_pairs={{0,4},{1,3},{4,8},{5,1},{8,12},{9,5},{12,14},{13,9},{14,10},{15,13... | collective-permute-start | bytes 393224 | tf_op jit(solution)/shard_map/ppermute | solution.py:339
  31.6 5.0 %collective-permute-start.12 = (bf16[32,2048]{1,0:T(8,128)(2,1)S(1)}, bf16[32,2048]{1,0:T(8,128)(2,1)S(1)}, u32[]{:S(2)}, u32[]{:S(2)}) collective-permute-start(bf16[32,2048]{1,0:T(8,128)(2,1)S(1)} %add_convert_fusion.5), channel_id=1, source_target_pairs={{0,4},{1,3},{4,8},{5,1},{8,12},{9,5},{12,14},{13,9},{14,10},{15,13... | collective-permute-start | bytes 393224 | tf_op jit(solution)/shard_map/ppermute | solution.py:339
  33.0 5.0 %collective-permute-start.9 = (bf16[32,2048]{1,0:T(8,128)(2,1)S(1)}, bf16[32,2048]{1,0:T(8,128)(2,1)S(1)}, u32[]{:S(2)}, u32[]{:S(2)}) collective-permute-start(bf16[32,2048]{1,0:T(8,128)(2,1)S(1)} %add_convert_fusion.7), channel_id=1, source_target_pairs={{0,4},{1,3},{4,8},{5,1},{8,12},{9,5},{12,14},{13,9},{14,10},{15,13... | collective-permute-start | bytes 393224 | tf_op jit(solution)/shard_map/ppermute | solution.py:339
  36.6 3.8 %collective-permute-start.13 = (bf16[32,2048]{1,0:T(8,128)(2,1)S(1)}, bf16[32,2048]{1,0:T(8,128)(2,1)S(1)}, u32[]{:S(2)}, u32[]{:S(2)}) collective-permute-start(bf16[32,2048]{1,0:T(8,128)(2,1)S(1)} %collective-permute-done.12), channel_id=1, source_target_pairs={{0,1},{1,0},{2,3},{3,2},{4,5},{5,4},{6,7},{7,6},{8,9},{9,8},{10,11... | collective-permute-start | bytes 393224 | tf_op jit(solution)/shard_map/ppermute | solution.py:342
  40.8 1.4 %collective-permute-start.18 = (bf16[32,2048]{1,0:T(8,128)(2,1)S(1)}, bf16[32,2048]{1,0:T(8,128)(2,1)S(1)}, u32[]{:S(2)}, u32[]{:S(2)}) collective-permute-start(bf16[32,2048]{1,0:T(8,128)(2,1)S(1)} %fusion.2.refs_4_), channel_id=1, source_target_pairs={{0,1},{1,0},{2,3},{3,2},{4,5},{5,4},{6,7},{7,6},{8,9},{9,8},{10,11... | collective-permute-start | bytes 393224 | tf_op jit(solution)/shard_map/ppermute | solution.py:342
  41.2 5.0 %collective-permute-start.14 = (bf16[32,2048]{1,0:T(8,128)(2,1)S(1)}, bf16[32,2048]{1,0:T(8,128)(2,1)S(1)}, u32[]{:S(2)}, u32[]{:S(2)}) collective-permute-start(bf16[32,2048]{1,0:T(8,128)(2,1)S(1)} %fusion.2.refs_4_), channel_id=1, source_target_pairs={{0,2},{1,5},{4,0},{5,9},{8,4},{9,13},{12,8},{13,15},{14,12},{15,11... | collective-permute-start | bytes 393224 | tf_op jit(solution)/shard_map/ppermute | solution.py:339
  42.2 5.4 %collective-permute-start.19 = (bf16[32,2048]{1,0:T(8,128)(2,1)S(1)}, bf16[32,2048]{1,0:T(8,128)(2,1)S(1)}, u32[]{:S(2)}, u32[]{:S(2)}) collective-permute-start(bf16[32,2048]{1,0:T(8,128)(2,1)S(1)} %collective-permute-done.18), channel_id=1, source_target_pairs={{0,2},{1,5},{4,0},{5,9},{8,4},{9,13},{12,8},{13,15},{14,12},{15,11... | collective-permute-start | bytes 393224 | tf_op jit(solution)/shard_map/ppermute | solution.py:339
  46.2 5.0 %collective-permute-start.15 = (bf16[32,2048]{1,0:T(8,128)(2,1)S(1)}, bf16[32,2048]{1,0:T(8,128)(2,1)S(1)}, u32[]{:S(2)}, u32[]{:S(2)}) collective-permute-start(bf16[32,2048]{1,0:T(8,128)(2,1)S(1)} %collective-permute-done.14.refs_2_), channel_id=1, source_target_pairs={{0,2},{1,5},{4,0},{5,9},{8,4},{9,13},{12,8},{13,15},{14,12},{15,11... | collective-permute-start | bytes 393224 | tf_op jit(solution)/shard_map/ppermute | solution.py:339
  47.6 5.0 %collective-permute-start.20 = (bf16[32,2048]{1,0:T(8,128)(2,1)S(1)}, bf16[32,2048]{1,0:T(8,128)(2,1)S(1)}, u32[]{:S(2)}, u32[]{:S(2)}) collective-permute-start(bf16[32,2048]{1,0:T(8,128)(2,1)S(1)} %collective-permute-done.19.refs_3_), channel_id=1, source_target_pairs={{0,2},{1,5},{4,0},{5,9},{8,4},{9,13},{12,8},{13,15},{14,12},{15,11... | collective-permute-start | bytes 393224 | tf_op jit(solution)/shard_map/ppermute | solution.py:339
  51.2 5.0 %collective-permute-start.16 = (bf16[32,2048]{1,0:T(8,128)(2,1)S(1)}, bf16[32,2048]{1,0:T(8,128)(2,1)S(1)}, u32[]{:S(2)}, u32[]{:S(2)}) collective-permute-start(bf16[32,2048]{1,0:T(8,128)(2,1)S(1)} %collective-permute-done.15.refs_0_), channel_id=1, source_target_pairs={{0,2},{1,5},{4,0},{5,9},{8,4},{9,13},{12,8},{13,15},{14,12},{15,11... | collective-permute-start | bytes 393224 | tf_op jit(solution)/shard_map/ppermute | solution.py:339
  52.6 8.0 %collective-permute-start.21 = (bf16[32,2048]{1,0:T(8,128)(2,1)S(1)}, bf16[32,2048]{1,0:T(8,128)(2,1)S(1)}, u32[]{:S(2)}, u32[]{:S(2)}) collective-permute-start(bf16[32,2048]{1,0:T(8,128)(2,1)S(1)} %collective-permute-done.20.refs_1_), channel_id=1, source_target_pairs={{0,2},{1,5},{4,0},{5,9},{8,4},{9,13},{12,8},{13,15},{14,12},{15,11... | collective-permute-start | bytes 393224 | tf_op jit(solution)/shard_map/ppermute | solution.py:339
  56.1 5.0 %collective-permute-start.17 = (bf16[32,2048]{1,0:T(8,128)(2,1)S(1)}, bf16[32,2048]{1,0:T(8,128)(2,1)S(1)}, u32[]{:S(2)}, u32[]{:S(2)}) collective-permute-start(bf16[32,2048]{1,0:T(8,128)(2,1)S(1)} %collective-permute-done.16.refs_1_), channel_id=1, source_target_pairs={{0,2},{1,5},{4,0},{5,9},{8,4},{9,13},{12,8},{13,15},{14,12},{15,11... | collective-permute-start | bytes 393224 | tf_op jit(solution)/shard_map/ppermute | solution.py:339
  64.3 5.0 %collective-permute-start.29 = (bf16[32,2048]{1,0:T(8,128)(2,1)S(1)}, bf16[32,2048]{1,0:T(8,128)(2,1)S(1)}, u32[]{:S(2)}, u32[]{:S(2)}) collective-permute-start(bf16[32,2048]{1,0:T(8,128)(2,1)S(1)} %get-tuple-element.74), channel_id=1, source_target_pairs={{0,4},{1,3},{4,8},{5,1},{8,12},{9,5},{12,14},{13,9},{14,10},{15,13... | collective-permute-start | bytes 393224 | tf_op jit(solution)/shard_map/ppermute | solution.py:339
  65.1 5.7 %collective-permute-start.25 = (bf16[32,2048]{1,0:T(8,128)(2,1)S(1)}, bf16[32,2048]{1,0:T(8,128)(2,1)S(1)}, u32[]{:S(2)}, u32[]{:S(2)}) collective-permute-start(bf16[32,2048]{1,0:T(8,128)(2,1)S(1)} %get-tuple-element.69), channel_id=1, source_target_pairs={{0,4},{1,3},{4,8},{5,1},{8,12},{9,5},{12,14},{13,9},{14,10},{15,13... | collective-permute-start | bytes 393224 | tf_op jit(solution)/shard_map/ppermute | solution.py:339
  66.6 6.6 %collective-permute-start.26 = (bf16[32,2048]{1,0:T(8,128)(2,1)S(1)}, bf16[32,2048]{1,0:T(8,128)(2,1)S(1)}, u32[]{:S(2)}, u32[]{:S(2)}) collective-permute-start(bf16[32,2048]{1,0:T(8,128)(2,1)S(1)} %get-tuple-element.71), channel_id=1, source_target_pairs={{0,8},{1,7},{4,12},{5,3},{8,14},{9,1},{12,10},{13,5},{14,6},{15,9}... | collective-permute-start | bytes 393224 | tf_op jit(solution)/shard_map/ppermute | solution.py:339
  69.4 5.3 %collective-permute-start.30 = (bf16[32,2048]{1,0:T(8,128)(2,1)S(1)}, bf16[32,2048]{1,0:T(8,128)(2,1)S(1)}, u32[]{:S(2)}, u32[]{:S(2)}) collective-permute-start(bf16[32,2048]{1,0:T(8,128)(2,1)S(1)} %add_convert_fusion.1), channel_id=1, source_target_pairs={{0,4},{1,3},{4,8},{5,1},{8,12},{9,5},{12,14},{13,9},{14,10},{15,13... | collective-permute-start | bytes 393224 | tf_op jit(solution)/shard_map/ppermute | solution.py:339
  73.3 5.0 %collective-permute-start.27 = (bf16[32,2048]{1,0:T(8,128)(2,1)S(1)}, bf16[32,2048]{1,0:T(8,128)(2,1)S(1)}, u32[]{:S(2)}, u32[]{:S(2)}) collective-permute-start(bf16[32,2048]{1,0:T(8,128)(2,1)S(1)} %add_convert_fusion.3), channel_id=1, source_target_pairs={{0,4},{1,3},{4,8},{5,1},{8,12},{9,5},{12,14},{13,9},{14,10},{15,13... | collective-permute-start | bytes 393224 | tf_op jit(solution)/shard_map/ppermute | solution.py:339
  74.7 5.0 %collective-permute-start.31 = (bf16[32,2048]{1,0:T(8,128)(2,1)S(1)}, bf16[32,2048]{1,0:T(8,128)(2,1)S(1)}, u32[]{:S(2)}, u32[]{:S(2)}) collective-permute-start(bf16[32,2048]{1,0:T(8,128)(2,1)S(1)} %add_convert_fusion), channel_id=1, source_target_pairs={{0,4},{1,3},{4,8},{5,1},{8,12},{9,5},{12,14},{13,9},{14,10},{15,13... | collective-permute-start | bytes 393224 | tf_op jit(solution)/shard_map/ppermute | solution.py:339
  78.3 5.0 %collective-permute-start.28 = (bf16[32,2048]{1,0:T(8,128)(2,1)S(1)}, bf16[32,2048]{1,0:T(8,128)(2,1)S(1)}, u32[]{:S(2)}, u32[]{:S(2)}) collective-permute-start(bf16[32,2048]{1,0:T(8,128)(2,1)S(1)} %add_convert_fusion.2), channel_id=1, source_target_pairs={{0,4},{1,3},{4,8},{5,1},{8,12},{9,5},{12,14},{13,9},{14,10},{15,13... | collective-permute-start | bytes 393224 | tf_op jit(solution)/shard_map/ppermute | solution.py:339
  79.7 3.6 %collective-permute-start.32 = (bf16[32,2048]{1,0:T(8,128)(2,1)S(1)}, bf16[32,2048]{1,0:T(8,128)(2,1)S(1)}, u32[]{:S(2)}, u32[]{:S(2)}) collective-permute-start(bf16[32,2048]{1,0:T(8,128)(2,1)S(1)} %collective-permute-done.31), channel_id=1, source_target_pairs={{0,1},{1,0},{2,3},{3,2},{4,5},{5,4},{6,7},{7,6},{8,9},{9,8},{10,11... | collective-permute-start | bytes 393224 | tf_op jit(solution)/shard_map/ppermute | solution.py:342
